TPU v7x, 32 devices: a whole 2x2x4 slice. The times are simulated.
32 devices in a mesh: dom: 8 (over y, x, core), band: 4 (over z).
Axes of the slice: x: 2, y: 2, z: 4, core: 2. Of those that a mesh axis runs over, the one named last changes fastest.
Arguments:
- wave_block: float32 [4, 96, 16, 128], P('band', 'dom'), may hold values from -6 to 6
- potential: float32 [96, 16, 128], P('dom'), may hold values from -1.5 to 1
- projectors: float32 [256, 8, 2048], P('dom', None, 'band'), may hold values from -0.25 to 0.25
- kb_energy: float32 [128, 8], P('dom'), may hold values from 1 to 6
- slot_atom: int32 [256], P('dom'), may hold values from 0 to 127, as said below
- slot_corner: int32 [3, 256], P(None, 'dom'), may hold values from 0 to 112, as said below
Outputs:
- filtered: float32 [4, 96, 16, 128], P('band', 'dom')
Inputs may be any that keep to these rules, and one draw needn't show every extreme that they name: `slot_atom`: the slots of slab t are rows t * 32 to (t + 1) * 32 - 1; each names an atom owned by slab t - 1, t or t + 1, where atom a is owned by slab a // 16. `slot_corner`: rows 0, 1, 2 give the box's first cell inside its slab along the three dimensions, at most 4, 0 and 112.
All inputs are finite; a program needn't handle non-finite values.
Results may differ from a plain program's by a relative error of at most 0.00024.
Values sent between devices are 32-bit elements; how exact they have to be, the bound alone decides.
No kernel may reach another device: no remote copies, remote signals or barrier semaphores. Data moves between devices by JAX's collectives and lax.ppermute only.
A program may use at most 64 MiB of HBM per device.

v0:
```python
import functools

import jax
import jax.numpy as jnp
from jax import lax
from jax.experimental import pallas as pl
from jax.experimental.pallas import tpu as pltpu
from jax.sharding import PartitionSpec as P

SX = 8
SY = 16
SZ = 16
DEGREE = 3
LANES = 128
ROWS = 8
TILES = SX * SY * SZ // LANES
HALVES = SY // ROWS

STENCIL_WEIGHTS = (
    -5369.0 / 1800.0,
    12.0 / 7.0,
    -15.0 / 56.0,
    10.0 / 189.0,
    -1.0 / 112.0,
    2.0 / 1925.0,
    -1.0 / 16632.0,
)
REACH = len(STENCIL_WEIGHTS) - 1
LOWER_EDGE = 3.0
UPPER_EDGE = 30.0
ANCHOR_POINT = 0.5
EXACT = lax.Precision.HIGHEST
HALF_WIDTH = (UPPER_EDGE - LOWER_EDGE) / 2.0
CENTRE = (UPPER_EDGE + LOWER_EDGE) / 2.0
SIGMA_FIRST = HALF_WIDTH / (ANCHOR_POINT - CENTRE)
COPIES = 4


def step_factors():
    sigma_now = SIGMA_FIRST
    factors = [(SIGMA_FIRST / HALF_WIDTH, 0.0)]
    for _ in range(2, DEGREE + 1):
        sigma_next = 1.0 / (2.0 / SIGMA_FIRST - sigma_now)
        factors.append((2.0 * sigma_next / HALF_WIDTH, sigma_now * sigma_next))
        sigma_now = sigma_next
    return factors


def iota(shape, dim):
    return lax.broadcasted_iota(jnp.int32, shape, dim)


def fold_rows(blocks):
    row = iota((ROWS, LANES), 0)
    distance = 1
    while len(blocks) > 1:
        first = (row // distance) % 2 == 0
        blocks = [
            jnp.where(first, a, b) + pltpu.roll(jnp.where(first, b, a), distance, 0)
            for a, b in zip(blocks[::2], blocks[1::2])
        ]
        distance *= 2
    return blocks[0]


def choose(masks, values):
    result = values[-1]
    for mask, value in zip(masks[:-1], values[:-1]):
        result = jnp.where(mask, value, result)
    return result


def pack_kernel(first_tile, proj_ref, out_ref):
    tiles, groups = out_ref.shape[:2]
    row = iota((ROWS, LANES), 0)
    block = iota((ROWS, LANES), 1) // SZ
    apart = (row - block + ROWS) % ROWS
    block_is = [block == b for b in range(ROWS)]
    row_is = [row == r for r in range(ROWS)]
    apart_is = [apart == d for d in range(ROWS)]

    def one(index, carry):
        tile, group = index // groups, index % groups
        cells = pl.ds(pl.multiple_of((first_tile + tile) * LANES, LANES), LANES)
        given = [proj_ref[group * ROWS + u, :, cells] for u in range(ROWS)]
        by_lane = []
        for d in range(ROWS):
            mixed = choose(block_is, [given[(b - d) % ROWS] for b in range(ROWS)])
            by_lane.append(pltpu.roll(mixed, (LANES - d * SZ) % LANES, 1) if d else mixed)
        by_row = []
        for e in range(ROWS):
            mixed = choose(apart_is, [by_lane[(d + e) % ROWS] for d in range(ROWS)])
            by_row.append(pltpu.roll(mixed, e, 0) if e else mixed)
        for p in range(ROWS):
            out_ref[tile, group, p] = choose(row_is, [by_row[(j - p) % ROWS] for j in range(ROWS)])
        return carry

    lax.fori_loop(0, tiles * groups, one, 0)


def member(atom_row, atoms):
    return (iota((atoms, atom_row.shape[1]), 0) == atom_row).astype(jnp.float32)


def total_of(products):
    while len(products) > 1:
        pairs = [a + b for a, b in zip(products[::2], products[1::2])]
        products = pairs + products[len(pairs) * 2 :]
    return products[0]


def project(field, chunks, corner_ref, flat_ref, start_ref=None):
    groups = flat_ref.shape[0]
    lane_block = iota((ROWS, LANES), 1) // SZ

    def one(group, carry):
        corners = [corner_ref[0, group * ROWS + u] for u in range(ROWS)]
        shifts = [
            lax.rem(LANES + u * SZ - corner_ref[2, group * ROWS + u], LANES) for u in range(ROWS)
        ]
        sums = [[] for _ in range(ROWS)]
        for plane, ref in chunks:
            for half in range(HALVES):
                box = None
                for u in range(ROWS):
                    turned = pltpu.roll(field(corners[u] + plane, half), shifts[u], 1)
                    box = turned if u == 0 else jnp.where(lane_block == u, turned, box)
                for p in range(ROWS):
                    sums[p].append(ref[half, group, p] * box)
        flat = fold_rows([total_of(products) for products in sums])
        flat_ref[group] = flat if start_ref is None else flat + start_ref[group]
        return carry

    lax.fori_loop(0, groups, one, 0)


def sum_atoms(flat_ref, atom_row_ref, atoms):
    flat = jnp.concatenate([flat_ref[g] for g in range(flat_ref.shape[0])], axis=1)
    return lax.dot_general(
        flat, member(atom_row_ref[...], atoms), (((1,), (1,)), ((), ())),
        precision=EXACT, preferred_element_type=jnp.float32,
    )


def deposit(scaled, chunks, corner_ref, atom_row_ref, flat_ref, box_ref, parts_ref):
    groups = chunks[0][1].shape[1]
    copies = parts_ref.shape[0]
    lane_block = iota((ROWS, LANES), 1) // SZ
    flat = jnp.dot(
        scaled, member(atom_row_ref[...], scaled.shape[1]),
        precision=EXACT, preferred_element_type=jnp.float32,
    )
    for g in range(groups):
        flat_ref[g] = flat[:, g * LANES : (g + 1) * LANES]
    parts_ref[...] = jnp.zeros(parts_ref.shape, jnp.float32)

    def one(group, carry):
        factors = [
            jnp.broadcast_to(flat_ref[group, pl.ds(p, 1), :], (ROWS, LANES)) for p in range(ROWS)
        ]
        for plane, ref in chunks:
            for half in range(HALVES):
                box_ref[plane * HALVES + half] = total_of(
                    [ref[half, group, p] * factors[p] for p in range(ROWS)]
                )
        for u in range(ROWS):
            slot = group * ROWS + u
            planes = pl.ds(corner_ref[0, slot], SX)
            shift = lax.rem(LANES + corner_ref[2, slot] - u * SZ, LANES)
            for half in range(HALVES):
                at = (u % copies, planes, pl.ds(half * ROWS, ROWS), slice(None))
                added = [
                    pltpu.roll(
                        jnp.where(lane_block == u, box_ref[x * HALVES + half], 0.0), shift, 1
                    )
                    for x in range(SX)
                ]
                parts_ref[at] = parts_ref[at] + jnp.stack(added)
        return carry

    lax.fori_loop(0, groups, one, 0)


def band_matrix(size, block, centre):
    row = iota((size, size), 0)
    column = iota((size, size), 1)
    apart = jnp.abs(row - column)
    table = jnp.where(apart == 0, centre, 0.0)
    for k in range(1, REACH + 1):
        table = jnp.where(apart == k, STENCIL_WEIGHTS[k], table)
    return jnp.where(row // block == column // block, table, 0.0)


def laplacian(padded_ref, extent):
    inner = padded_ref[REACH : REACH + extent]
    flat = inner.reshape(extent * SY, LANES)
    along_z = jnp.dot(
        flat, band_matrix(LANES, LANES, 3.0 * STENCIL_WEIGHTS[0]),
        precision=EXACT, preferred_element_type=jnp.float32,
    )
    along_y = jnp.dot(
        band_matrix(extent * SY, SY, 0.0), flat,
        precision=EXACT, preferred_element_type=jnp.float32,
    )
    total = (along_z + along_y).reshape(inner.shape)
    for k in range(1, REACH + 1):
        total = total + STENCIL_WEIGHTS[k] * (
            padded_ref[REACH + k : REACH + k + extent] + padded_ref[REACH - k : REACH - k + extent]
        )
    return total


HALO_ROWS = REACH * SY


def to_rows(table):
    blocks = [table[:, at : at + LANES] for at in range(0, table.shape[1], LANES)]
    return jnp.concatenate(blocks, axis=0)


def from_rows(rows):
    blocks = [rows[at : at + ROWS] for at in range(0, rows.shape[0], ROWS)]
    return jnp.concatenate(blocks, axis=1)


def write_sends(field_ref, table, odd, mate_ref, cross_ref):
    extent = field_ref.shape[0]
    mate_start = (1 - odd) * (extent - REACH)
    cross_start = odd * (extent - REACH)
    for start, ref in ((mate_start, mate_ref), (cross_start, cross_ref)):
        ref[:HALO_ROWS] = field_ref[pl.ds(start, REACH)].reshape(HALO_ROWS, LANES)
        ref[HALO_ROWS:] = table


def all_planes(ref):
    return [(x, ref.at[pl.ds(x * HALVES, HALVES)]) for x in range(SX)]


def part_planes(where_ref, parts, refs):
    return [
        (where_ref[2 + part] * 2 + h, refs[2 * i + h]) for i, part in enumerate(parts) for h in range(2)
    ]


def field_reader(ref):
    return lambda x, half: ref[x, pl.ds(half * ROWS, ROWS), :]


def early_kernel(parts, has_start, corner_ref, where_ref, field_ref, other_ref, *refs):
    refs = list(refs)
    outs = refs[-2:]
    starts = [refs.pop(0), refs.pop(0)] if has_start else [None, None]
    chunks = part_planes(where_ref, parts, refs[:-2])

    @pl.when(where_ref[1] == 0)
    def _():
        for source_ref, start_ref, out_ref in zip((field_ref, other_ref), starts, outs):
            project(field_reader(source_ref), chunks, corner_ref, out_ref, start_ref)


def first_kernel(where_ref, atom_row_ref, field_ref, energy_ref, inner_ref, end_ref,
                 mate_ref, cross_ref, flat_ref):
    flat_ref[...] = jnp.where(where_ref[1] == 0, inner_ref[...], end_ref[...])
    energy = energy_ref[...]
    sums = sum_atoms(flat_ref, atom_row_ref, energy.shape[1])
    table = jnp.concatenate([to_rows(sums), to_rows(energy)], axis=0)
    write_sends(field_ref, table, where_ref[0], mate_ref, cross_ref)


def whole_kernel(corner_ref, where_ref, atom_row_ref, field_ref, energy_ref, whole_ref,
                 mate_ref, cross_ref, flat_ref):
    project(field_reader(field_ref), all_planes(whole_ref), corner_ref, flat_ref)
    energy = energy_ref[...]
    sums = sum_atoms(flat_ref, atom_row_ref, energy.shape[1])
    table = jnp.concatenate([to_rows(sums), to_rows(energy)], axis=0)
    write_sends(field_ref, table, where_ref[0], mate_ref, cross_ref)


def assemble(where_ref, shared, inner, end, whole_ref):
    def put(part, pair):
        for h in range(2):
            at = pl.ds((where_ref[2 + part] * 2 + h) * HALVES, HALVES)
            whole_ref[at] = pair[h][...]

    put(0, shared[:2])
    put(1, shared[2:])

    @pl.when(where_ref[1] == 0)
    def _():
        put(2, inner[:2])
        put(3, inner[2:])

    @pl.when(where_ref[1] != 0)
    def _():
        put(2, end[:2])
        put(3, [end[2].at[:HALVES], end[2].at[HALVES:]])


def step_kernel(index, chunk_count, corner_ref, where_ref, atom_row_ref, field_ref, potential_ref,
                own_ref, mate_ref, cross_ref, far_ref, *refs):
    factors = step_factors()
    is_first, is_last = index == 0, index + 1 == len(factors)
    given = refs[:chunk_count]
    refs = list(refs[chunk_count:])
    energy_ref = None if is_first else refs.pop(0)
    before_ref = None if is_first else refs.pop(0)
    next_ref = refs.pop(0)
    if not is_last:
        next_mate_ref, next_cross_ref = refs.pop(0), refs.pop(0)
    if is_first:
        energy_ref = refs.pop(0)
    if chunk_count > 1:
        whole_ref = refs.pop(0)
        assemble(where_ref, given[:4], given[4:8], given[8:], whole_ref)
    else:
        whole_ref = given[0]
    chunks = all_planes(whole_ref)
    flat_ref, box_ref, parts_ref, padded_ref = refs
    extent = field_ref.shape[0]
    odd = where_ref[0]

    table = from_rows(own_ref[HALO_ROWS:] + cross_ref[HALO_ROWS:] + far_ref[...])
    if is_first:
        atoms = table.shape[1] // 2
        energy_ref[...] = table[:, atoms:]
        table = table[:, :atoms]
    scaled = table * energy_ref[...]
    deposit(scaled, chunks, corner_ref, atom_row_ref, flat_ref, box_ref, parts_ref)

    cells = field_ref[...]
    padded_ref[REACH : REACH + extent] = cells
    mate_at = (1 - odd) * (extent + REACH)
    cross_at = odd * (extent + REACH)
    padded_ref[pl.ds(mate_at, REACH)] = mate_ref[:HALO_ROWS].reshape(REACH, SY, LANES)
    padded_ref[pl.ds(cross_at, REACH)] = cross_ref[:HALO_ROWS].reshape(REACH, SY, LANES)
    value = -0.5 * laplacian(padded_ref, extent) + (potential_ref[...] - CENTRE) * cells
    for u in range(parts_ref.shape[0]):
        value = value + parts_ref[u]
    value = factors[index][0] * value
    if not is_first:
        value = value - factors[index][1] * before_ref[...]
    next_ref[...] = value
    if not is_last:
        project(field_reader(next_ref), chunks, corner_ref, flat_ref)
        sums = sum_atoms(flat_ref, atom_row_ref, scaled.shape[1])
        write_sends(next_ref, to_rows(sums), odd, next_mate_ref, next_cross_ref)


VMEM = pl.BlockSpec(memory_space=pltpu.VMEM)
SMEM = pl.BlockSpec(memory_space=pltpu.SMEM)
ANY = pl.BlockSpec(memory_space=pl.ANY)


def swap(values, axis, first):
    count = lax.axis_size(axis)
    pairs = []
    for i in range(first, count - 1, 2):
        pairs += [(i, i + 1), (i + 1, i)]
    return lax.ppermute(values, axis, pairs)


def exchange(to_mate, to_cross):
    mate = swap(to_mate, "dom", 0)
    own = to_cross.at[HALO_ROWS:].add(mate[HALO_ROWS:])
    cross = swap(own, "dom", 1)
    far = swap(cross[HALO_ROWS:], "dom", 0)
    return own, mate, cross, far


def on_device(wave_block, potential, projectors, kb_energy, slot_atom, slot_corner):
    bands, planes, cells_y, cells_z = wave_block.shape
    assert bands == 1 and cells_y == SY and cells_z == LANES
    slots, proj_count = projectors.shape[:2]
    atom_own = kb_energy.shape[0]
    atoms = atom_own * lax.axis_size("dom")
    groups = slots // ROWS
    tiles = projectors.shape[2] // LANES
    assert proj_count == ROWS and slots % ROWS == 0
    place = lax.axis_index("dom")
    field = wave_block[0]

    def shaped(*shape):
        return jax.ShapeDtypeStruct(shape, jnp.float32)

    def call(kernel, name, out_shape, scalars, operands, scratch, after=()):
        inputs = len(scalars) + len(operands)

        def body(*refs):
            kernel(*refs[:inputs], *refs[inputs + len(after) :])

        return pl.pallas_call(
            body,
            out_shape=out_shape,
            in_specs=[SMEM] * len(scalars) + [VMEM] * len(operands) + [ANY] * len(after),
            out_specs=jax.tree.map(lambda _: VMEM, out_shape),
            scratch_shapes=[pltpu.VMEM(shape, jnp.float32) for shape in scratch],
            compiler_params=pltpu.CompilerParams(vmem_limit_bytes=16 * 2**20),
            cost_estimate=pl.CostEstimate(flops=0, bytes_accessed=0, transcendentals=0),
            name=name,
        )(*scalars, *operands, *after)

    atom_row = jnp.repeat(slot_atom, SZ)[None, :]
    own_atoms = (jnp.arange(atoms) // atom_own) == place
    energy = jnp.where(own_atoms[None, :], jnp.tile(kb_energy.T, (1, atoms // atom_own)), 0.0)
    flat = (groups, ROWS, LANES)
    boxes = (TILES, ROWS, LANES)
    parts = (COPIES, planes, SY, LANES)
    padded = (planes + 2 * REACH, SY, LANES)
    table_rows = ROWS * atoms // LANES
    sends = [shaped(HALO_ROWS + table_rows, LANES)] * 2

    def pack(first_tile, count):
        return call(
            functools.partial(pack_kernel, first_tile), "pack_projectors",
            shaped(count, groups, ROWS, ROWS, LANES), [], [projectors], [],
        )

    odd = (place % 2).astype(jnp.int32)
    first_sends = [shaped(HALO_ROWS + 2 * table_rows, LANES)] * 2
    if lax.axis_size("band") == 4 and tiles == 2 * HALVES:
        at = lax.axis_index("band").astype(jnp.int32)
        inner = (at == 1) | (at == 2)
        second = jnp.where(at < 2, 2, 1)
        third = jnp.where(at < 2, 3, 0)
        neighbour = at + 1 - 2 * (at % 2)
        where = jnp.stack([odd, 1 - inner.astype(jnp.int32), at, neighbour, second, third])
        at_ends = [(0, 1), (1, 0), (2, 3), (3, 2)]
        middle = [(1, 2), (2, 1)]
        outward = [(1, 0), (2, 3)]
        inward = [(0, 1), (3, 2)]

        def move(values, pairs):
            return [lax.ppermute(value, "band", pairs) for value in values]

        own_part = [pack(0, HALVES), pack(HALVES, HALVES)]
        beside = move(own_part, at_ends)
        across = move(own_part, middle)
        (other,) = move([field], inward)
        end_across = move(across, outward)
        beyond = move(beside, middle)
        end_beyond = move([jnp.concatenate(beyond)], outward)
        flats = call(
            functools.partial(early_kernel, (0, 1, 2), False), "project_early",
            [shaped(*flat)] * 2, [slot_corner, where],
            [field, other, *own_part, *beside, *across], [],
        )
        flats = call(
            functools.partial(early_kernel, (3,), True), "project_late",
            [shaped(*flat)] * 2, [slot_corner, where], [field, other, *flats, *beyond], [], end_across,
        )
        (returned,) = move(flats[1:], outward)
        sent = call(
            first_kernel, "first_sums", first_sends, [where],
            [atom_row, field, energy, flats[0], returned], [flat],
        )
        chunks = [*own_part, *beside, *across, *beyond, *end_across, *end_beyond]
    else:
        where = jnp.stack([odd, jnp.int32(0)])
        chunks = [lax.all_gather(pack(0, tiles), "band", axis=0, tiled=True)]
        sent = call(
            whole_kernel, "project_first", first_sends, [slot_corner, where],
            [atom_row, field, energy, *chunks], [flat],
        )
    before = None
    for index in range(DEGREE):
        own, mate, cross, far = exchange(*sent)
        operands = [atom_row, field, potential, own, mate, cross, far, *chunks]
        out_shape = [shaped(planes, SY, LANES)]
        if index > 0:
            operands += [energy, before]
        if index + 1 < DEGREE:
            out_shape += sends
        if index == 0:
            out_shape += [shaped(ROWS, atoms)]
        if len(chunks) > 1:
            out_shape += [shaped(TILES, groups, ROWS, ROWS, LANES)]
        result = call(
            functools.partial(step_kernel, index, len(chunks)), f"filter_step_{index + 1}",
            out_shape, [slot_corner, where], operands, [flat, boxes, parts, padded],
        )
        before, field = field, result[0]
        sent = result[1:3]
        if index == 0:
            energy = result[3]
            chunks = chunks if len(chunks) == 1 else [result[4]]
    return field[None]


def solution(mesh):
    placed = (
        P("band", "dom", None, None),
        P("dom", None, None),
        P("dom", None, "band"),
        P("dom", None),
        P("dom"),
        P(None, "dom"),
    )
    return jax.shard_map(
        on_device,
        mesh=mesh,
        in_specs=placed,
        out_specs=P("band", "dom", None, None),
        check_vma=False,
    )
```

profile of v0, /device:TPU:5, one launch (start us, length us, event | category | flops | bytes accessed | tf_op | source)
XLA Modules:
  0.0 78.3 jit_solution(11966155631054443117)
XLA Ops:
  0.0 1.1 %copy-done.2 = f32[32,8,512]{2,1,0:T(8,128)S(1)} copy-done((f32[32,8,512]{2,1,0:T(8,128)S(1)}, f32[32,8,512]{2,1,0:T(8,128)}, u32[]{:S(2)}) %copy-start.2) | copy-done | bytes 524312
  1.1 0.9 %pack_projectors.2.refs_4_.refs_9_ = f32[2,4,8,8,128]{4,3,2,1,0:T(8,128)S(1)} custom-call(f32[32,8,512]{2,1,0:T(8,128)S(1)} %copy-done.2), custom_call_target="tpu_custom_call" | custom-call | tf_op jit(solution)/shard_map/pack_projectors/pallas_call | solution.py:391
  2.7 3.9 %collective-permute-start.1 = (f32[2,4,8,8,128]{4,3,2,1,0:T(8,128)S(1)}, f32[2,4,8,8,128]{4,3,2,1,0:T(8,128)S(1)}, u32[]{:S(2)}, u32[]{:S(2)}) collective-permute-start(f32[2,4,8,8,128]{4,3,2,1,0:T(8,128)S(1)} %pack_projectors.2.refs_4_.refs_9_), channel_id=1, source_target_pairs={{0,1},{1,0},{2,3},{3,2},{4,5},{5,4},{6,7},{7,6},{8,9},{9,8},{10,11... | collective-permute-start | bytes 786440 | tf_op jit(solution)/shard_map/ppermute | solution.py:433
  6.6 0.9 %pack_projectors.3.refs_5_.refs_10_ = f32[2,4,8,8,128]{4,3,2,1,0:T(8,128)S(1)} custom-call(f32[32,8,512]{2,1,0:T(8,128)S(1)} %copy-done.2), custom_call_target="tpu_custom_call" | custom-call | tf_op jit(solution)/shard_map/pack_projectors/pallas_call | solution.py:391
  8.2 1.5 %collective-permute-start.2 = (f32[2,4,8,8,128]{4,3,2,1,0:T(8,128)S(1)}, f32[2,4,8,8,128]{4,3,2,1,0:T(8,128)S(1)}, u32[]{:S(2)}, u32[]{:S(2)}) collective-permute-start(f32[2,4,8,8,128]{4,3,2,1,0:T(8,128)S(1)} %pack_projectors.3.refs_5_.refs_10_), channel_id=1, source_target_pairs={{0,1},{1,0},{2,3},{3,2},{4,5},{5,4},{6,7},{7,6},{8,9},{9,8},{10,11... | collective-permute-start | bytes 786440 | tf_op jit(solution)/shard_map/ppermute | solution.py:433
  9.6 1.3 %collective-permute-start.7 = (f32[2,4,8,8,128]{4,3,2,1,0:T(8,128)S(1)}, f32[2,4,8,8,128]{4,3,2,1,0:T(8,128)S(1)}, u32[]{:S(2)}, u32[]{:S(2)}) collective-permute-start(f32[2,4,8,8,128]{4,3,2,1,0:T(8,128)S(1)} %collective-permute-done.3.refs_8_.refs_13_), channel_id=1, source_target_pairs={{1,0},{2,3},{5,4},{6,7},{9,8},{10,11},{13,12},{14,15},{17,16},{18,... | collective-permute-start | bytes 786440 | tf_op jit(solution)/shard_map/ppermute | solution.py:433
  10.9 1.3 %collective-permute-done.1.refs_6_.refs_11_ = f32[2,4,8,8,128]{4,3,2,1,0:T(8,128)S(1)} collective-permute-done((f32[2,4,8,8,128]{4,3,2,1,0:T(8,128)S(1)}, f32[2,4,8,8,128]{4,3,2,1,0:T(8,128)S(1)}, u32[]{:S(2)}, u32[]{:S(2)}) %collective-permute-start.1) | collective-permute-done | bytes 262176 | tf_op jit(solution)/shard_map/ppermute | solution.py:433
  13.0 1.3 %collective-permute-start.8 = (f32[2,4,8,8,128]{4,3,2,1,0:T(8,128)S(1)}, f32[2,4,8,8,128]{4,3,2,1,0:T(8,128)S(1)}, u32[]{:S(2)}, u32[]{:S(2)}) collective-permute-start(f32[2,4,8,8,128]{4,3,2,1,0:T(8,128)S(1)} %collective-permute-done.4.refs_9_.refs_14_), channel_id=1, source_target_pairs={{1,0},{2,3},{5,4},{6,7},{9,8},{10,11},{13,12},{14,15},{17,16},{18,... | collective-permute-start | bytes 786440 | tf_op jit(solution)/shard_map/ppermute | solution.py:433
  14.3 3.6 %collective-permute-done.2.refs_7_.refs_12_ = f32[2,4,8,8,128]{4,3,2,1,0:T(8,128)S(1)} collective-permute-done((f32[2,4,8,8,128]{4,3,2,1,0:T(8,128)S(1)}, f32[2,4,8,8,128]{4,3,2,1,0:T(8,128)S(1)}, u32[]{:S(2)}, u32[]{:S(2)}) %collective-permute-start.2) | collective-permute-done | bytes 262176 | tf_op jit(solution)/shard_map/ppermute | solution.py:433
  18.6 5.8 %collective-permute-start = (f32[12,16,128]{2,1,0:T(8,128)}, f32[12,16,128]{2,1,0:T(8,128)S(1)}, u32[]{:S(2)}, u32[]{:S(2)}) collective-permute-start(f32[12,16,128]{2,1,0:T(8,128)} %bitcast.9), channel_id=1, source_target_pairs={{0,1},{3,2},{4,5},{7,6},{8,9},{11,10},{12,13},{15,14},{16,17},{19,... | collective-permute-start | bytes 294920 | tf_op jit(solution)/shard_map/ppermute | solution.py:433
  25.3 1.0 %collective-permute-done.refs_3_ = f32[12,16,128]{2,1,0:T(8,128)S(1)} collective-permute-done((f32[12,16,128]{2,1,0:T(8,128)}, f32[12,16,128]{2,1,0:T(8,128)S(1)}, u32[]{:S(2)}, u32[]{:S(2)}) %collective-permute-start) | collective-permute-done | bytes 98336 | tf_op jit(solution)/shard_map/ppermute | solution.py:433
  26.3 0.9 %copy-done = f32[1,12,16,128]{3,2,1,0:T(8,128)S(1)} copy-done((f32[1,12,16,128]{3,2,1,0:T(8,128)S(1)}, f32[1,12,16,128]{3,2,1,0:T(8,128)}, u32[]{:S(2)}) %copy-start) | copy-done | bytes 98328
  29.7 1.3 %collective-permute-start.9 = (f32[4,8,128]{2,1,0:T(8,128)S(1)}, f32[4,8,128]{2,1,0:T(8,128)S(1)}, u32[]{:S(2)}, u32[]{:S(2)}) collective-permute-start(f32[4,8,128]{2,1,0:T(8,128)S(1)} %get-tuple-element.58), channel_id=1, source_target_pairs={{1,0},{2,3},{5,4},{6,7},{9,8},{10,11},{13,12},{14,15},{17,16},{18,... | collective-permute-start | bytes 49160 | tf_op jit(solution)/shard_map/ppermute | solution.py:433
  31.9 1.3 %collective-permute-start.13 = (f32[4,4,8,8,128]{4,3,2,1,0:T(8,128)}, f32[4,4,8,8,128]{4,3,2,1,0:T(8,128)S(1)}, u32[]{:S(2)}, u32[]{:S(2)}) collective-permute-start(f32[4,4,8,8,128]{4,3,2,1,0:T(8,128)} %pad_maximum_fusion), channel_id=1, source_target_pairs={{1,0},{2,3},{5,4},{6,7},{9,8},{10,11},{13,12},{14,15},{17,16},{18,... | collective-permute-start | bytes 1572872 | tf_op jit(solution)/shard_map/ppermute | solution.py:433
  33.3 3.0 %collective-permute-done.9.refs_5_ = f32[4,8,128]{2,1,0:T(8,128)S(1)} collective-permute-done((f32[4,8,128]{2,1,0:T(8,128)S(1)}, f32[4,8,128]{2,1,0:T(8,128)S(1)}, u32[]{:S(2)}, u32[]{:S(2)}) %collective-permute-start.9) | collective-permute-done | bytes 16416 | tf_op jit(solution)/shard_map/ppermute | solution.py:433
  36.3 0.9 %first_sums.1 = (f32[112,128]{1,0:T(8,128)S(1)}, f32[112,128]{1,0:T(8,128)S(1)}) custom-call(s32[6]{0:T(128)S(1)} %stack.27.refs_1_.refs_0_, s32[1,512]{1,0:T(1,128)S(1)} %broadcast_in_dim_reshape.3.refs_1_.refs_2_, f32[12,16,128]{2,1,0:T(8,128)S(1)} %bitcast.12, f32[8,128]{1,0:T(8,128)S(1)} %broadcast_select_fusion.refs_3_, ...), custom_call_target="tpu_custom_call" | custom-call | tf_op jit(solution)/shard_map/first_sums/pallas_call | solution.py:391
  37.1 4.6 %collective-permute-start.10 = (f32[112,128]{1,0:T(8,128)S(1)}, f32[112,128]{1,0:T(8,128)S(1)}, u32[]{:S(2)}, u32[]{:S(2)}) collective-permute-start(f32[112,128]{1,0:T(8,128)S(1)} %get-tuple-element.60), channel_id=1, source_target_pairs={{0,4},{4,0},{8,12},{12,8},{16,20},{20,16},{24,28},{28,24},{1,5},{5... | collective-permute-start | bytes 172040 | tf_op jit(solution)/shard_map/ppermute | solution.py:359
  41.7 0.9 %collective-permute-done.10.refs_6_ = f32[112,128]{1,0:T(8,128)S(1)} collective-permute-done((f32[112,128]{1,0:T(8,128)S(1)}, f32[112,128]{1,0:T(8,128)S(1)}, u32[]{:S(2)}, u32[]{:S(2)}) %collective-permute-start.10) | collective-permute-done | bytes 57376 | tf_op jit(solution)/shard_map/ppermute | solution.py:359
  42.6 3.3 %collective-permute-start.11 = (f32[112,128]{1,0:T(8,128)S(1)}, f32[112,128]{1,0:T(8,128)S(1)}, u32[]{:S(2)}, u32[]{:S(2)}) collective-permute-start(f32[112,128]{1,0:T(8,128)S(1)} %fusion.refs_5_), channel_id=1, source_target_pairs={{4,8},{8,4},{12,16},{16,12},{20,24},{24,20},{5,9},{9,5},{13,17},{1... | collective-permute-start | bytes 172040 | tf_op jit(solution)/shard_map/ppermute | solution.py:359
  46.0 2.4 %collective-permute-done.11.refs_7_ = f32[112,128]{1,0:T(8,128)S(1)} collective-permute-done((f32[112,128]{1,0:T(8,128)S(1)}, f32[112,128]{1,0:T(8,128)S(1)}, u32[]{:S(2)}, u32[]{:S(2)}) %collective-permute-start.11) | collective-permute-done | bytes 57376 | tf_op jit(solution)/shard_map/ppermute | solution.py:359
  48.4 1.0 %collective-permute-start.12 = (f32[16,128]{1,0:T(8,128)S(1)}, f32[16,128]{1,0:T(8,128)S(1)}, u32[]{:S(2)}, u32[]{:S(2)}) collective-permute-start(f32[16,128]{1,0:T(8,128)S(1)} %slice.85), channel_id=1, source_target_pairs={{0,4},{4,0},{8,12},{12,8},{16,20},{20,16},{24,28},{28,24},{1,5},{5... | collective-permute-start | bytes 24584 | tf_op jit(solution)/shard_map/ppermute | solution.py:359
  50.2 3.9 %filter_step_1.1 = (f32[12,16,128]{2,1,0:T(8,128)S(1)}, f32[104,128]{1,0:T(8,128)S(1)}, f32[104,128]{1,0:T(8,128)S(1)}, f32[8,128]{1,0:T(8,128)S(1)}, f32[16,4,8,8,128]{4,3,2,1,0:T(8,128)S(1)}) custom-call(s32[3,32]{1,0:T(4,128)S(1)} %copy-done.5, s32[6]{0:T(128)S(1)} %stack.27.refs_1_.refs_0_, s32[1,512]{1,0:T(1,128)S(1)} %broadcast_in_dim_reshape.3.refs_1_.refs_2_, ...), custom_call_target="tpu_custom_call" | custom-call | tf_op jit(solution)/shard_map/filter_step_1/pallas_call | solution.py:391
  54.5 0.9 %collective-permute-done.14.refs_6_ = f32[104,128]{1,0:T(8,128)S(1)} collective-permute-done((f32[104,128]{1,0:T(8,128)S(1)}, f32[104,128]{1,0:T(8,128)S(1)}, u32[]{:S(2)}, u32[]{:S(2)}) %collective-permute-start.14) | collective-permute-done | bytes 53280 | tf_op jit(solution)/shard_map/ppermute | solution.py:359
  55.4 3.3 %collective-permute-start.15 = (f32[104,128]{1,0:T(8,128)S(1)}, f32[104,128]{1,0:T(8,128)S(1)}, u32[]{:S(2)}, u32[]{:S(2)}) collective-permute-start(f32[104,128]{1,0:T(8,128)S(1)} %fusion.2.refs_5_), channel_id=1, source_target_pairs={{4,8},{8,4},{12,16},{16,12},{20,24},{24,20},{5,9},{9,5},{13,17},{1... | collective-permute-start | bytes 159752 | tf_op jit(solution)/shard_map/ppermute | solution.py:359
  58.7 2.4 %collective-permute-done.15.refs_7_ = f32[104,128]{1,0:T(8,128)S(1)} collective-permute-done((f32[104,128]{1,0:T(8,128)S(1)}, f32[104,128]{1,0:T(8,128)S(1)}, u32[]{:S(2)}, u32[]{:S(2)}) %collective-permute-start.15) | collective-permute-done | bytes 53280 | tf_op jit(solution)/shard_map/ppermute | solution.py:359
  61.1 1.0 %collective-permute-start.16 = (f32[8,128]{1,0:T(8,128)S(1)}, f32[8,128]{1,0:T(8,128)S(1)}, u32[]{:S(2)}, u32[]{:S(2)}) collective-permute-start(f32[8,128]{1,0:T(8,128)S(1)} %slice.87), channel_id=1, source_target_pairs={{0,4},{4,0},{8,12},{12,8},{16,20},{20,16},{24,28},{28,24},{1,5},{5... | collective-permute-start | bytes 12296 | tf_op jit(solution)/shard_map/ppermute | solution.py:359
  62.9 3.7 %filter_step_2.1 = (f32[12,16,128]{2,1,0:T(8,128)S(1)}, f32[104,128]{1,0:T(8,128)S(1)}, f32[104,128]{1,0:T(8,128)S(1)}) custom-call(s32[3,32]{1,0:T(4,128)S(1)} %copy-done.5, s32[6]{0:T(128)S(1)} %stack.27.refs_1_.refs_0_, s32[1,512]{1,0:T(1,128)S(1)} %broadcast_in_dim_reshape.3.refs_1_.refs_2_, f32[12,16,128]{2,1,0:T(8,128)S(1)} %get-tuple-element.61.refs_3_.refs_11_, ...), custom_call_target="tpu_custom_call" | custom-call | tf_op jit(solution)/shard_map/filter_step_2/pallas_call | solution.py:391
  67.0 0.9 %collective-permute-done.17.refs_6_ = f32[104,128]{1,0:T(8,128)S(1)} collective-permute-done((f32[104,128]{1,0:T(8,128)S(1)}, f32[104,128]{1,0:T(8,128)S(1)}, u32[]{:S(2)}, u32[]{:S(2)}) %collective-permute-start.17) | collective-permute-done | bytes 53280 | tf_op jit(solution)/shard_map/ppermute | solution.py:359
  67.9 2.4 %collective-permute-start.18 = (f32[104,128]{1,0:T(8,128)S(1)}, f32[104,128]{1,0:T(8,128)S(1)}, u32[]{:S(2)}, u32[]{:S(2)}) collective-permute-start(f32[104,128]{1,0:T(8,128)S(1)} %fusion.1.refs_5_), channel_id=1, source_target_pairs={{4,8},{8,4},{12,16},{16,12},{20,24},{24,20},{5,9},{9,5},{13,17},{1... | collective-permute-start | bytes 159752 | tf_op jit(solution)/shard_map/ppermute | solution.py:359
  70.3 3.3 %collective-permute-done.18.refs_7_ = f32[104,128]{1,0:T(8,128)S(1)} collective-permute-done((f32[104,128]{1,0:T(8,128)S(1)}, f32[104,128]{1,0:T(8,128)S(1)}, u32[]{:S(2)}, u32[]{:S(2)}) %collective-permute-start.18) | collective-permute-done | bytes 53280 | tf_op jit(solution)/shard_map/ppermute | solution.py:359
  73.6 0.9 %collective-permute-start.19 = (f32[8,128]{1,0:T(8,128)S(1)}, f32[8,128]{1,0:T(8,128)S(1)}, u32[]{:S(2)}, u32[]{:S(2)}) collective-permute-start(f32[8,128]{1,0:T(8,128)S(1)} %slice.89), channel_id=1, source_target_pairs={{0,4},{4,0},{8,12},{12,8},{16,20},{20,16},{24,28},{28,24},{1,5},{5... | collective-permute-start | bytes 12296 | tf_op jit(solution)/shard_map/ppermute | solution.py:359
  75.4 2.9 %filter_step_3.1 = f32[12,16,128]{2,1,0:T(8,128)} custom-call(s32[3,32]{1,0:T(4,128)S(1)} %copy-done.5, s32[6]{0:T(128)S(1)} %stack.27.refs_1_.refs_0_, s32[1,512]{1,0:T(1,128)S(1)} %broadcast_in_dim_reshape.3.refs_1_.refs_2_, f32[12,16,128]{2,1,0:T(8,128)S(1)} %get-tuple-element.66.refs_3_, f32[12,16,128]{2,1,0:T(8,128)S(1)} %copy-done.3, ...), custom_call_target="tpu_custom_call" | custom-call | tf_op jit(solution)/shard_map/filter_step_3/pallas_call | solution.py:391
  (44 shorter events, 10.3 us)
Async XLA Ops:
  0.0 29.1 %copy-start.1 = (f32[1,12,16,128]{3,2,1,0:T(8,128)S(1)}, f32[1,12,16,128]{3,2,1,0:T(8,128)}, u32[]{:S(2)}) copy-start(f32[1,12,16,128]{3,2,1,0:T(8,128)} %param.12) | copy-start | bytes 294916
  0.0 1.1 %copy-start.2 = (f32[32,8,512]{2,1,0:T(8,128)S(1)}, f32[32,8,512]{2,1,0:T(8,128)}, u32[]{:S(2)}) copy-start(f32[32,8,512]{2,1,0:T(8,128)} %refs_0_.8) | copy-start | bytes 1572868
  2.0 7.7 %collective-permute-start.3 = (f32[2,4,8,8,128]{4,3,2,1,0:T(8,128)S(1)}, f32[2,4,8,8,128]{4,3,2,1,0:T(8,128)S(1)}, u32[]{:S(2)}, u32[]{:S(2)}) collective-permute-start(f32[2,4,8,8,128]{4,3,2,1,0:T(8,128)S(1)} %pack_projectors.2.refs_4_.refs_9_), channel_id=1, source_target_pairs={{1,2},{2,1},{5,6},{6,5},{9,10},{10,9},{13,14},{14,13},{17,18},{18,... | collective-permute-start | bytes 786440 | tf_op jit(solution)/shard_map/ppermute | solution.py:433
  2.7 9.6 %collective-permute-start.1 = (f32[2,4,8,8,128]{4,3,2,1,0:T(8,128)S(1)}, f32[2,4,8,8,128]{4,3,2,1,0:T(8,128)S(1)}, u32[]{:S(2)}, u32[]{:S(2)}) collective-permute-start(f32[2,4,8,8,128]{4,3,2,1,0:T(8,128)S(1)} %pack_projectors.2.refs_4_.refs_9_), channel_id=1, source_target_pairs={{0,1},{1,0},{2,3},{3,2},{4,5},{5,4},{6,7},{7,6},{8,9},{9,8},{10,11... | collective-permute-start | bytes 786440 | tf_op jit(solution)/shard_map/ppermute | solution.py:433
  7.5 5.5 %collective-permute-start.4 = (f32[2,4,8,8,128]{4,3,2,1,0:T(8,128)S(1)}, f32[2,4,8,8,128]{4,3,2,1,0:T(8,128)S(1)}, u32[]{:S(2)}, u32[]{:S(2)}) collective-permute-start(f32[2,4,8,8,128]{4,3,2,1,0:T(8,128)S(1)} %pack_projectors.3.refs_5_.refs_10_), channel_id=1, source_target_pairs={{1,2},{2,1},{5,6},{6,5},{9,10},{10,9},{13,14},{14,13},{17,18},{18,... | collective-permute-start | bytes 786440 | tf_op jit(solution)/shard_map/ppermute | solution.py:433
  8.2 9.7 %collective-permute-start.2 = (f32[2,4,8,8,128]{4,3,2,1,0:T(8,128)S(1)}, f32[2,4,8,8,128]{4,3,2,1,0:T(8,128)S(1)}, u32[]{:S(2)}, u32[]{:S(2)}) collective-permute-start(f32[2,4,8,8,128]{4,3,2,1,0:T(8,128)S(1)} %pack_projectors.3.refs_5_.refs_10_), channel_id=1, source_target_pairs={{0,1},{1,0},{2,3},{3,2},{4,5},{5,4},{6,7},{7,6},{8,9},{9,8},{10,11... | collective-permute-start | bytes 786440 | tf_op jit(solution)/shard_map/ppermute | solution.py:433
  9.6 18.9 %collective-permute-start.7 = (f32[2,4,8,8,128]{4,3,2,1,0:T(8,128)S(1)}, f32[2,4,8,8,128]{4,3,2,1,0:T(8,128)S(1)}, u32[]{:S(2)}, u32[]{:S(2)}) collective-permute-start(f32[2,4,8,8,128]{4,3,2,1,0:T(8,128)S(1)} %collective-permute-done.3.refs_8_.refs_13_), channel_id=1, source_target_pairs={{1,0},{2,3},{5,4},{6,7},{9,8},{10,11},{13,12},{14,15},{17,16},{18,... | collective-permute-start | bytes 786440 | tf_op jit(solution)/shard_map/ppermute | solution.py:433
  12.3 16.2 %collective-permute-start.5 = (f32[2,4,8,8,128]{4,3,2,1,0:T(8,128)S(1)}, f32[2,4,8,8,128]{4,3,2,1,0:T(8,128)S(1)}, u32[]{:S(2)}, u32[]{:S(2)}) collective-permute-start(f32[2,4,8,8,128]{4,3,2,1,0:T(8,128)S(1)} %collective-permute-done.1.refs_6_.refs_11_), channel_id=1, source_target_pairs={{1,2},{2,1},{5,6},{6,5},{9,10},{10,9},{13,14},{14,13},{17,18},{18,... | collective-permute-start | bytes 786440 | tf_op jit(solution)/shard_map/ppermute | solution.py:433
  13.0 16.2 %collective-permute-start.8 = (f32[2,4,8,8,128]{4,3,2,1,0:T(8,128)S(1)}, f32[2,4,8,8,128]{4,3,2,1,0:T(8,128)S(1)}, u32[]{:S(2)}, u32[]{:S(2)}) collective-permute-start(f32[2,4,8,8,128]{4,3,2,1,0:T(8,128)S(1)} %collective-permute-done.4.refs_9_.refs_14_), channel_id=1, source_target_pairs={{1,0},{2,3},{5,4},{6,7},{9,8},{10,11},{13,12},{14,15},{17,16},{18,... | collective-permute-start | bytes 786440 | tf_op jit(solution)/shard_map/ppermute | solution.py:433
  17.9 11.2 %collective-permute-start.6 = (f32[2,4,8,8,128]{4,3,2,1,0:T(8,128)S(1)}, f32[2,4,8,8,128]{4,3,2,1,0:T(8,128)S(1)}, u32[]{:S(2)}, u32[]{:S(2)}) collective-permute-start(f32[2,4,8,8,128]{4,3,2,1,0:T(8,128)S(1)} %collective-permute-done.2.refs_7_.refs_12_), channel_id=1, source_target_pairs={{1,2},{2,1},{5,6},{6,5},{9,10},{10,9},{13,14},{14,13},{17,18},{18,... | collective-permute-start | bytes 786440 | tf_op jit(solution)/shard_map/ppermute | solution.py:433
  18.6 7.8 %collective-permute-start = (f32[12,16,128]{2,1,0:T(8,128)}, f32[12,16,128]{2,1,0:T(8,128)S(1)}, u32[]{:S(2)}, u32[]{:S(2)}) collective-permute-start(f32[12,16,128]{2,1,0:T(8,128)} %bitcast.9), channel_id=1, source_target_pairs={{0,1},{3,2},{4,5},{7,6},{8,9},{11,10},{12,13},{15,14},{16,17},{19,... | collective-permute-start | bytes 294920 | tf_op jit(solution)/shard_map/ppermute | solution.py:433
  24.4 8.7 %copy-start.6 = (s32[32]{0:T(128)S(1)}, s32[32]{0:T(128)}, u32[]{:S(2)}) copy-start(s32[32]{0:T(128)} %param.16) | copy-start | bytes 388
  26.3 0.9 %copy-start = (f32[1,12,16,128]{3,2,1,0:T(8,128)S(1)}, f32[1,12,16,128]{3,2,1,0:T(8,128)}, u32[]{:S(2)}) copy-start(f32[1,12,16,128]{3,2,1,0:T(8,128)} %param.12) | copy-start | bytes 294916
  27.2 0.7 copy-start.4
  27.9 22.3 %copy-start.3 = (f32[12,16,128]{2,1,0:T(8,128)S(1)}, f32[12,16,128]{2,1,0:T(8,128)}, u32[]{:S(2)}) copy-start(f32[12,16,128]{2,1,0:T(8,128)} %refs_4_.5) | copy-start | bytes 294916
  27.9 22.3 %copy-start.5 = (s32[3,32]{1,0:T(4,128)S(1)}, s32[3,32]{1,0:T(4,128)}, u32[]{:S(2)}) copy-start(s32[3,32]{1,0:T(4,128)} %refs_0_.13) | copy-start | bytes 1156
  29.7 6.6 %collective-permute-start.9 = (f32[4,8,128]{2,1,0:T(8,128)S(1)}, f32[4,8,128]{2,1,0:T(8,128)S(1)}, u32[]{:S(2)}, u32[]{:S(2)}) collective-permute-start(f32[4,8,128]{2,1,0:T(8,128)S(1)} %get-tuple-element.58), channel_id=1, source_target_pairs={{1,0},{2,3},{5,4},{6,7},{9,8},{10,11},{13,12},{14,15},{17,16},{18,... | collective-permute-start | bytes 49160 | tf_op jit(solution)/shard_map/ppermute | solution.py:433
  31.9 18.3 %collective-permute-start.13 = (f32[4,4,8,8,128]{4,3,2,1,0:T(8,128)}, f32[4,4,8,8,128]{4,3,2,1,0:T(8,128)S(1)}, u32[]{:S(2)}, u32[]{:S(2)}) collective-permute-start(f32[4,4,8,8,128]{4,3,2,1,0:T(8,128)} %pad_maximum_fusion), channel_id=1, source_target_pairs={{1,0},{2,3},{5,4},{6,7},{9,8},{10,11},{13,12},{14,15},{17,16},{18,... | collective-permute-start | bytes 1572872 | tf_op jit(solution)/shard_map/ppermute | solution.py:433
  37.1 5.5 %collective-permute-start.10 = (f32[112,128]{1,0:T(8,128)S(1)}, f32[112,128]{1,0:T(8,128)S(1)}, u32[]{:S(2)}, u32[]{:S(2)}) collective-permute-start(f32[112,128]{1,0:T(8,128)S(1)} %get-tuple-element.60), channel_id=1, source_target_pairs={{0,4},{4,0},{8,12},{12,8},{16,20},{20,16},{24,28},{28,24},{1,5},{5... | collective-permute-start | bytes 172040 | tf_op jit(solution)/shard_map/ppermute | solution.py:359
  42.6 5.8 %collective-permute-start.11 = (f32[112,128]{1,0:T(8,128)S(1)}, f32[112,128]{1,0:T(8,128)S(1)}, u32[]{:S(2)}, u32[]{:S(2)}) collective-permute-start(f32[112,128]{1,0:T(8,128)S(1)} %fusion.refs_5_), channel_id=1, source_target_pairs={{4,8},{8,4},{12,16},{16,12},{20,24},{24,20},{5,9},{9,5},{13,17},{1... | collective-permute-start | bytes 172040 | tf_op jit(solution)/shard_map/ppermute | solution.py:359
  48.4 1.8 %collective-permute-start.12 = (f32[16,128]{1,0:T(8,128)S(1)}, f32[16,128]{1,0:T(8,128)S(1)}, u32[]{:S(2)}, u32[]{:S(2)}) collective-permute-start(f32[16,128]{1,0:T(8,128)S(1)} %slice.85), channel_id=1, source_target_pairs={{0,4},{4,0},{8,12},{12,8},{16,20},{20,16},{24,28},{28,24},{1,5},{5... | collective-permute-start | bytes 24584 | tf_op jit(solution)/shard_map/ppermute | solution.py:359
  54.1 1.3 %collective-permute-start.14 = (f32[104,128]{1,0:T(8,128)S(1)}, f32[104,128]{1,0:T(8,128)S(1)}, u32[]{:S(2)}, u32[]{:S(2)}) collective-permute-start(f32[104,128]{1,0:T(8,128)S(1)} %get-tuple-element.63), channel_id=1, source_target_pairs={{0,4},{4,0},{8,12},{12,8},{16,20},{20,16},{24,28},{28,24},{1,5},{5... | collective-permute-start | bytes 159752 | tf_op jit(solution)/shard_map/ppermute | solution.py:359
  55.4 5.7 %collective-permute-start.15 = (f32[104,128]{1,0:T(8,128)S(1)}, f32[104,128]{1,0:T(8,128)S(1)}, u32[]{:S(2)}, u32[]{:S(2)}) collective-permute-start(f32[104,128]{1,0:T(8,128)S(1)} %fusion.2.refs_5_), channel_id=1, source_target_pairs={{4,8},{8,4},{12,16},{16,12},{20,24},{24,20},{5,9},{9,5},{13,17},{1... | collective-permute-start | bytes 159752 | tf_op jit(solution)/shard_map/ppermute | solution.py:359
  61.1 1.8 %collective-permute-start.16 = (f32[8,128]{1,0:T(8,128)S(1)}, f32[8,128]{1,0:T(8,128)S(1)}, u32[]{:S(2)}, u32[]{:S(2)}) collective-permute-start(f32[8,128]{1,0:T(8,128)S(1)} %slice.87), channel_id=1, source_target_pairs={{0,4},{4,0},{8,12},{12,8},{16,20},{20,16},{24,28},{28,24},{1,5},{5... | collective-permute-start | bytes 12296 | tf_op jit(solution)/shard_map/ppermute | solution.py:359
  66.6 1.3 %collective-permute-start.17 = (f32[104,128]{1,0:T(8,128)S(1)}, f32[104,128]{1,0:T(8,128)S(1)}, u32[]{:S(2)}, u32[]{:S(2)}) collective-permute-start(f32[104,128]{1,0:T(8,128)S(1)} %get-tuple-element.68), channel_id=1, source_target_pairs={{0,4},{4,0},{8,12},{12,8},{16,20},{20,16},{24,28},{28,24},{1,5},{5... | collective-permute-start | bytes 159752 | tf_op jit(solution)/shard_map/ppermute | solution.py:359
  67.9 5.7 %collective-permute-start.18 = (f32[104,128]{1,0:T(8,128)S(1)}, f32[104,128]{1,0:T(8,128)S(1)}, u32[]{:S(2)}, u32[]{:S(2)}) collective-permute-start(f32[104,128]{1,0:T(8,128)S(1)} %fusion.1.refs_5_), channel_id=1, source_target_pairs={{4,8},{8,4},{12,16},{16,12},{20,24},{24,20},{5,9},{9,5},{13,17},{1... | collective-permute-start | bytes 159752 | tf_op jit(solution)/shard_map/ppermute | solution.py:359
  73.6 1.8 %collective-permute-start.19 = (f32[8,128]{1,0:T(8,128)S(1)}, f32[8,128]{1,0:T(8,128)S(1)}, u32[]{:S(2)}, u32[]{:S(2)}) collective-permute-start(f32[8,128]{1,0:T(8,128)S(1)} %slice.89), channel_id=1, source_target_pairs={{0,4},{4,0},{8,12},{12,8},{16,20},{20,16},{24,28},{28,24},{1,5},{5... | collective-permute-start | bytes 12296 | tf_op jit(solution)/shard_map/ppermute | solution.py:359
where the time goes:
time: 79.1 us; the launch traced here: 78.3 us
  starting transfers between devices  36.4 us (46%)
  waiting for transfers between devices  22.8 us (29%)
  Pallas kernels  14.3 us (18%)
  local copies, waits for them, and re-layouts  3.68 us (5%)
  other arithmetic  0.87 us (1%)
    ppermute x11, starting transfers between devices, move(): return [lax.ppermute(value, 'band', pairs) for value in values]  19 us
    ppermute x9, starting transfers between devices, swap(): return lax.ppermute(values, axis, pairs)  17.3 us
    pallas_call x8, Pallas kernels, call(): pl.pallas_call(body, out_shape=out_shape, in_specs=[SMEM] * len(scalars)...  14.3 us
    ppermute x9, waiting for transfers between devices, swap(): return lax.ppermute(values, axis, pairs)  13.2 us
    ppermute x11, waiting for transfers between devices, move(): return [lax.ppermute(value, 'band', pairs) for value in values]  9.57 us
    unnamed x14, local copies, waits for them, and re-layouts  2.67 us
  transfers between devices with their start and end apart: 20, of which 14 were waited for; matrix products, arithmetic and copies ran while one was open for 2% of the time, Pallas kernels for 3%

commit v1 on v0

--- a/solution.py
+++ b/solution.py
@@ -34,6 +34,7 @@
 CENTRE = (UPPER_EDGE + LOWER_EDGE) / 2.0
 SIGMA_FIRST = HALF_WIDTH / (ANCHOR_POINT - CENTRE)
 COPIES = 4
+FIRST_CHUNK = 1
 
 
 def step_factors():
@@ -223,85 +224,87 @@
     return jnp.concatenate(blocks, axis=1)
 
 
-def write_sends(field_ref, table, odd, mate_ref, cross_ref):
+def write_halos(field_ref, odd, mate_ref, cross_ref):
     extent = field_ref.shape[0]
     mate_start = (1 - odd) * (extent - REACH)
     cross_start = odd * (extent - REACH)
     for start, ref in ((mate_start, mate_ref), (cross_start, cross_ref)):
         ref[:HALO_ROWS] = field_ref[pl.ds(start, REACH)].reshape(HALO_ROWS, LANES)
-        ref[HALO_ROWS:] = table
 
 
 def all_planes(ref):
     return [(x, ref.at[pl.ds(x * HALVES, HALVES)]) for x in range(SX)]
 
 
-def part_planes(where_ref, parts, refs):
-    return [
-        (where_ref[2 + part] * 2 + h, refs[2 * i + h]) for i, part in enumerate(parts) for h in range(2)
-    ]
-
-
 def field_reader(ref):
     return lambda x, half: ref[x, pl.ds(half * ROWS, ROWS), :]
 
 
-def early_kernel(parts, has_start, corner_ref, where_ref, field_ref, other_ref, *refs):
-    refs = list(refs)
-    outs = refs[-2:]
-    starts = [refs.pop(0), refs.pop(0)] if has_start else [None, None]
-    chunks = part_planes(where_ref, parts, refs[:-2])
-
-    @pl.when(where_ref[1] == 0)
-    def _():
-        for source_ref, start_ref, out_ref in zip((field_ref, other_ref), starts, outs):
-            project(field_reader(source_ref), chunks, corner_ref, out_ref, start_ref)
-
-
-def first_kernel(where_ref, atom_row_ref, field_ref, energy_ref, inner_ref, end_ref,
-                 mate_ref, cross_ref, flat_ref):
-    flat_ref[...] = jnp.where(where_ref[1] == 0, inner_ref[...], end_ref[...])
+def halo_kernel(where_ref, field_ref, mate_ref, cross_ref):
+    write_halos(field_ref, where_ref[0], mate_ref, cross_ref)
+
+
+def opening_kernel(where_ref, field_hbm, proj_hbm, mate_ref, cross_ref, window_ref, low_ref,
+                   field_ref, proj_ref, field_sem, proj_sem):
+    field_copy = pltpu.make_async_copy(field_hbm, field_ref, field_sem)
+    cells = pl.ds(0, proj_ref.shape[2])
+    proj_copy = pltpu.make_async_copy(proj_hbm.at[:, :, cells], proj_ref, proj_sem)
+    field_copy.start()
+    proj_copy.start()
+    field_copy.wait()
+    window_ref[...] = field_ref[pl.ds(where_ref[FIRST_CHUNK + 6], REACH)]
+    write_halos(field_ref, where_ref[0], mate_ref, cross_ref)
+    proj_copy.wait()
+    pack_kernel(0, proj_ref, low_ref)
+
+
+def own_planes_kernel(corner_ref, where_ref, field_ref, window_ref, low_ref, high_ref,
+                      own_ref, opposite_ref):
+    chunks = [low_ref, high_ref]
+    here = [(where_ref[FIRST_CHUNK + h], ref) for h, ref in enumerate(chunks)]
+    project(field_reader(field_ref), here, corner_ref, own_ref)
+    project(field_reader(window_ref), list(enumerate(chunks)), corner_ref, opposite_ref)
+
+
+def forward_kernel(above_ref, below_ref, above_out_ref, below_out_ref):
+    pass
+
+
+def beside_kernel(corner_ref, where_ref, field_ref, own_ref, returned_ref, *refs):
+    flat_ref = refs[-1]
+    flat_ref[...] = own_ref[...] + returned_ref[...]
+    chunks = [(where_ref[FIRST_CHUNK + 2 + i], ref) for i, ref in enumerate(refs[:-1])]
+    project(field_reader(field_ref), chunks, corner_ref, flat_ref, flat_ref)
+
+
+def table_kernel(atom_row_ref, energy_ref, *refs):
+    flat_refs, out_ref, flat_ref = refs[:-2], refs[-2], refs[-1]
+    flat_ref[...] = total_of([ref[...] for ref in flat_refs])
     energy = energy_ref[...]
     sums = sum_atoms(flat_ref, atom_row_ref, energy.shape[1])
-    table = jnp.concatenate([to_rows(sums), to_rows(energy)], axis=0)
-    write_sends(field_ref, table, where_ref[0], mate_ref, cross_ref)
-
-
-def whole_kernel(corner_ref, where_ref, atom_row_ref, field_ref, energy_ref, whole_ref,
-                 mate_ref, cross_ref, flat_ref):
-    project(field_reader(field_ref), all_planes(whole_ref), corner_ref, flat_ref)
-    energy = energy_ref[...]
-    sums = sum_atoms(flat_ref, atom_row_ref, energy.shape[1])
-    table = jnp.concatenate([to_rows(sums), to_rows(energy)], axis=0)
-    write_sends(field_ref, table, where_ref[0], mate_ref, cross_ref)
-
-
-def assemble(where_ref, shared, inner, end, whole_ref):
-    def put(part, pair):
-        for h in range(2):
-            at = pl.ds((where_ref[2 + part] * 2 + h) * HALVES, HALVES)
-            whole_ref[at] = pair[h][...]
-
-    put(0, shared[:2])
-    put(1, shared[2:])
-
-    @pl.when(where_ref[1] == 0)
-    def _():
-        put(2, inner[:2])
-        put(3, inner[2:])
-
-    @pl.when(where_ref[1] != 0)
-    def _():
-        put(2, end[:2])
-        put(3, [end[2].at[:HALVES], end[2].at[HALVES:]])
+    out_ref[...] = jnp.concatenate([to_rows(sums), to_rows(energy)], axis=0)
+
+
+def whole_kernel(corner_ref, field_ref, whole_ref, out_ref):
+    project(field_reader(field_ref), all_planes(whole_ref), corner_ref, out_ref)
 
 
 def step_kernel(index, chunk_count, corner_ref, where_ref, atom_row_ref, field_ref, potential_ref,
-                own_ref, mate_ref, cross_ref, far_ref, *refs):
+                mate_ref, cross_ref, *refs):
     factors = step_factors()
     is_first, is_last = index == 0, index + 1 == len(factors)
-    given = refs[:chunk_count]
-    refs = list(refs[chunk_count:])
+    refs = list(refs)
+    odd = where_ref[0]
+    own_ref, far_ref = refs.pop(0), refs.pop(0)
+    if is_first:
+        table = from_rows(own_ref[...] + refs.pop(0)[...] + far_ref[...])
+    else:
+        table = from_rows(own_ref[HALO_ROWS:] + cross_ref[HALO_ROWS:] + far_ref[...])
+    if chunk_count > 1:
+        chunks = [(where_ref[FIRST_CHUNK + i], refs[i]) for i in range(chunk_count)]
+    else:
+        chunks = all_planes(refs[0])
+    refs = refs[chunk_count:]
     energy_ref = None if is_first else refs.pop(0)
     before_ref = None if is_first else refs.pop(0)
     next_ref = refs.pop(0)
@@ -309,17 +312,8 @@
         next_mate_ref, next_cross_ref = refs.pop(0), refs.pop(0)
     if is_first:
         energy_ref = refs.pop(0)
-    if chunk_count > 1:
-        whole_ref = refs.pop(0)
-        assemble(where_ref, given[:4], given[4:8], given[8:], whole_ref)
-    else:
-        whole_ref = given[0]
-    chunks = all_planes(whole_ref)
     flat_ref, box_ref, parts_ref, padded_ref = refs
     extent = field_ref.shape[0]
-    odd = where_ref[0]
-
-    table = from_rows(own_ref[HALO_ROWS:] + cross_ref[HALO_ROWS:] + far_ref[...])
     if is_first:
         atoms = table.shape[1] // 2
         energy_ref[...] = table[:, atoms:]
@@ -343,7 +337,9 @@
     if not is_last:
         project(field_reader(next_ref), chunks, corner_ref, flat_ref)
         sums = sum_atoms(flat_ref, atom_row_ref, scaled.shape[1])
-        write_sends(next_ref, to_rows(sums), odd, next_mate_ref, next_cross_ref)
+        write_halos(next_ref, odd, next_mate_ref, next_cross_ref)
+        next_mate_ref[HALO_ROWS:] = to_rows(sums)
+        next_cross_ref[HALO_ROWS:] = to_rows(sums)
 
 
 VMEM = pl.BlockSpec(memory_space=pltpu.VMEM)
@@ -359,12 +355,9 @@
     return lax.ppermute(values, axis, pairs)
 
 
-def exchange(to_mate, to_cross):
-    mate = swap(to_mate, "dom", 0)
-    own = to_cross.at[HALO_ROWS:].add(mate[HALO_ROWS:])
-    cross = swap(own, "dom", 1)
-    far = swap(cross[HALO_ROWS:], "dom", 0)
-    return own, mate, cross, far
+def turn(values, axis, step):
+    count = lax.axis_size(axis)
+    return lax.ppermute(values, axis, [(i, (i + step) % count) for i in range(count)])
 
 
 def on_device(wave_block, potential, projectors, kb_energy, slot_atom, slot_corner):
@@ -382,7 +375,7 @@
     def shaped(*shape):
         return jax.ShapeDtypeStruct(shape, jnp.float32)
 
-    def call(kernel, name, out_shape, scalars, operands, scratch, after=()):
+    def call(kernel, name, out_shape, scalars, operands, scratch, after=(), in_place={}):
         inputs = len(scalars) + len(operands)
 
         def body(*refs):
@@ -395,6 +388,7 @@
             out_specs=jax.tree.map(lambda _: VMEM, out_shape),
             scratch_shapes=[pltpu.VMEM(shape, jnp.float32) for shape in scratch],
             compiler_params=pltpu.CompilerParams(vmem_limit_bytes=16 * 2**20),
+            input_output_aliases=in_place,
             cost_estimate=pl.CostEstimate(flops=0, bytes_accessed=0, transcendentals=0),
             name=name,
         )(*scalars, *operands, *after)
@@ -409,62 +403,87 @@
     table_rows = ROWS * atoms // LANES
     sends = [shaped(HALO_ROWS + table_rows, LANES)] * 2
 
-    def pack(first_tile, count):
+    def pack(first_tile, count, after=()):
         return call(
             functools.partial(pack_kernel, first_tile), "pack_projectors",
-            shaped(count, groups, ROWS, ROWS, LANES), [], [projectors], [],
+            shaped(count, groups, ROWS, ROWS, LANES), [], [projectors], [], after,
         )
 
     odd = (place % 2).astype(jnp.int32)
-    first_sends = [shaped(HALO_ROWS + 2 * table_rows, LANES)] * 2
+    halos = [shaped(HALO_ROWS, LANES)] * 2
     if lax.axis_size("band") == 4 and tiles == 2 * HALVES:
         at = lax.axis_index("band").astype(jnp.int32)
-        inner = (at == 1) | (at == 2)
-        second = jnp.where(at < 2, 2, 1)
-        third = jnp.where(at < 2, 3, 0)
-        neighbour = at + 1 - 2 * (at % 2)
-        where = jnp.stack([odd, 1 - inner.astype(jnp.int32), at, neighbour, second, third])
-        at_ends = [(0, 1), (1, 0), (2, 3), (3, 2)]
-        middle = [(1, 2), (2, 1)]
-        outward = [(1, 0), (2, 3)]
-        inward = [(0, 1), (3, 2)]
-
-        def move(values, pairs):
-            return [lax.ppermute(value, "band", pairs) for value in values]
-
-        own_part = [pack(0, HALVES), pack(HALVES, HALVES)]
-        beside = move(own_part, at_ends)
-        across = move(own_part, middle)
-        (other,) = move([field], inward)
-        end_across = move(across, outward)
-        beyond = move(beside, middle)
-        end_beyond = move([jnp.concatenate(beyond)], outward)
-        flats = call(
-            functools.partial(early_kernel, (0, 1, 2), False), "project_early",
-            [shaped(*flat)] * 2, [slot_corner, where],
-            [field, other, *own_part, *beside, *across], [],
+        owners = [at, (at + 1) % 4, (at + 3) % 4, (at + 2) % 4]
+        where = jnp.stack([odd] + [2 * part + h for part in owners for h in range(2)])
+        window = shaped(REACH, SY, LANES)
+        packed_plane = shaped(HALVES, groups, ROWS, ROWS, LANES)
+        mate, cross, opposite, low = pl.pallas_call(
+            opening_kernel,
+            out_shape=halos + [window, packed_plane],
+            in_specs=[SMEM, ANY, ANY],
+            out_specs=[VMEM] * 4,
+            scratch_shapes=[
+                pltpu.VMEM(field.shape, jnp.float32),
+                pltpu.VMEM((slots, ROWS, HALVES * LANES), jnp.float32),
+                pltpu.SemaphoreType.DMA,
+                pltpu.SemaphoreType.DMA,
+            ],
+            compiler_params=pltpu.CompilerParams(vmem_limit_bytes=16 * 2**20),
+            cost_estimate=pl.CostEstimate(flops=0, bytes_accessed=0, transcendentals=0),
+            name="open",
+        )(where, field, projectors)
+        opposite = turn(opposite, "band", 2)
+        below_low = turn(low, "band", 1)
+        high = pack(HALVES, HALVES, [opposite])
+        above_high = turn(high, "band", -1)
+        below_high = turn(high, "band", 1)
+        above_low = turn(low, "band", -1)
+        own, returned = call(
+            own_planes_kernel, "project_own", [shaped(*flat)] * 2, [slot_corner, where],
+            [field, opposite, low, high], [],
         )
-        flats = call(
-            functools.partial(early_kernel, (3,), True), "project_late",
-            [shaped(*flat)] * 2, [slot_corner, where], [field, other, *flats, *beyond], [], end_across,
+        returned = turn(returned, "band", 2)
+        above_high, below_low = call(
+            forward_kernel, "forward", [packed_plane] * 2, [], [above_high, below_low], [],
+            [returned, above_low, below_high], {0: 0, 1: 1},
         )
-        (returned,) = move(flats[1:], outward)
-        sent = call(
-            first_kernel, "first_sums", first_sends, [where],
-            [atom_row, field, energy, flats[0], returned], [flat],
-        )
-        chunks = [*own_part, *beside, *across, *beyond, *end_across, *end_beyond]
+        far_low = turn(below_low, "band", 1)
+        far_high = turn(above_high, "band", -1)
+        beside = [above_low, above_high, below_low, below_high]
+        flats = [
+            call(
+                beside_kernel, "project_beside", shaped(*flat), [slot_corner, where],
+                [field, own, returned, *beside], [],
+            )
+        ]
+        chunks = [low, high, *beside, far_low, far_high]
     else:
-        where = jnp.stack([odd, jnp.int32(0)])
+        where = odd[None]
+        mate, cross = call(halo_kernel, "cut_halos", halos, [where], [field], [])
         chunks = [lax.all_gather(pack(0, tiles), "band", axis=0, tiled=True)]
-        sent = call(
-            whole_kernel, "project_first", first_sends, [slot_corner, where],
-            [atom_row, field, energy, *chunks], [flat],
-        )
+        flats = [
+            call(whole_kernel, "project_first", shaped(*flat), [slot_corner], [field, *chunks], [])
+        ]
+    mate, cross = swap(mate, "dom", 0), swap(cross, "dom", 1)
+    own = call(
+        table_kernel, "first_sums", shaped(2 * table_rows, LANES), [],
+        [atom_row, energy, *flats], [flat],
+    )
+    own = own + swap(own, "dom", 0)
+    other = swap(own, "dom", 1)
+    far = swap(other, "dom", 0)
     before = None
     for index in range(DEGREE):
-        own, mate, cross, far = exchange(*sent)
-        operands = [atom_row, field, potential, own, mate, cross, far, *chunks]
+        if index > 0:
+            to_mate, to_cross = sent
+            mate = swap(to_mate, "dom", 0)
+            own = to_cross.at[HALO_ROWS:].add(mate[HALO_ROWS:])
+            cross = swap(own, "dom", 1)
+            far = swap(cross[HALO_ROWS:], "dom", 0)
+        operands = [atom_row, field, potential, mate, cross, own, far]
+        if index == 0:
+            operands.append(other)
+        operands += chunks
         out_shape = [shaped(planes, SY, LANES)]
         if index > 0:
             operands += [energy, before]
@@ -472,8 +491,6 @@
             out_shape += sends
         if index == 0:
             out_shape += [shaped(ROWS, atoms)]
-        if len(chunks) > 1:
-            out_shape += [shaped(TILES, groups, ROWS, ROWS, LANES)]
         result = call(
             functools.partial(step_kernel, index, len(chunks)), f"filter_step_{index + 1}",
             out_shape, [slot_corner, where], operands, [flat, boxes, parts, padded],
@@ -482,7 +499,6 @@
         sent = result[1:3]
         if index == 0:
             energy = result[3]
-            chunks = chunks if len(chunks) == 1 else [result[4]]
     return field[None]
 
 

time: 79.1 us -> 80.4 us (1.016)
  waiting for transfers between devices: 22.8 us -> 33.1 us
  starting transfers between devices: 36.4 us -> 27.5 us
  Pallas kernels: 14.3 us -> 16.3 us
  local copies, waits for them, and re-layouts: 3.68 us -> 2.83 us
  other arithmetic: 0.87 us -> 0.02 us
    ppermute x11 -> x8, waiting for transfers between devices: 9.57 us -> 17.6 us  [turn(): lax.ppermute(values, axis, [(i, (i + step) % count) for i in range(count)])]
    ppermute x11 -> x8, starting transfers between devices: 19 us -> 11.9 us  [turn(): lax.ppermute(values, axis, [(i, (i + step) % count) for i in range(count)])]
    ppermute x9 -> x11, waiting for transfers between devices: 13.2 us -> 15.5 us  [swap(): return lax.ppermute(values, axis, pairs)]
    ppermute x9 -> x11, starting transfers between devices: 17.3 us -> 15.6 us  [swap(): return lax.ppermute(values, axis, pairs)]
    pallas_call x0 -> x1, Pallas kernels: none -> 1.61 us  [on_device(): pl.pallas_call(opening_kernel, out_shape=halos + [window, packed_plane],...]
    concatenate x1 -> x0, other arithmetic: 0.85 us -> none  [on_device(): end_beyond = move([jnp.concatenate(beyond)], outward)]
  transfers between devices with their start and end apart: 20 -> 19, of which waited for: 14 -> 11; matrix products, arithmetic and copies ran while one was open for 2% -> 0% of each run, Pallas kernels for 3% -> 5%
where the time goes in v1:
time: 80.4 us; the launch traced here: 79.9 us
  waiting for transfers between devices  33.1 us (41%)
  starting transfers between devices  27.5 us (34%)
  Pallas kernels  16.3 us (20%)
  local copies, waits for them, and re-layouts  2.83 us (4%)
    ppermute x8, waiting for transfers between devices, turn(): lax.ppermute(values, axis, [(i, (i + step) % count) for i in range(count)])  17.6 us
    ppermute x11, starting transfers between devices, swap(): return lax.ppermute(values, axis, pairs)  15.6 us
    ppermute x11, waiting for transfers between devices, swap(): return lax.ppermute(values, axis, pairs)  15.5 us
    pallas_call x8, Pallas kernels, call(): pl.pallas_call(body, out_shape=out_shape, in_specs=[SMEM] * len(scalars)...  14.7 us
    ppermute x8, starting transfers between devices, turn(): lax.ppermute(values, axis, [(i, (i + step) % count) for i in range(count)])  11.9 us
    unnamed x14, local copies, waits for them, and re-layouts  2.51 us
    pallas_call x1, Pallas kernels, on_device(): pl.pallas_call(opening_kernel, out_shape=halos + [window, packed_plane],...  1.61 us
  transfers between devices with their start and end apart: 19, of which 11 were waited for; matrix products, arithmetic and copies ran while one was open for 0% of the time, Pallas kernels for 5%

profile of v1, /device:TPU:5, one launch (start us, length us, event | category | flops | bytes accessed | tf_op | source)
XLA Modules:
  0.0 79.9 jit_solution(2647124979003215525)
XLA Ops:
  0.9 1.0 %copy-done.1 = f32[32,8,512]{2,1,0:T(8,128)S(1)} copy-done((f32[32,8,512]{2,1,0:T(8,128)S(1)}, f32[32,8,512]{2,1,0:T(8,128)}, u32[]{:S(2)}) %copy-start.1) | copy-done | bytes 524312
  1.9 1.6 %open.1 = (f32[96,128]{1,0:T(8,128)S(1)}, f32[96,128]{1,0:T(8,128)S(1)}, f32[6,16,128]{2,1,0:T(8,128)S(1)}, f32[2,4,8,8,128]{4,3,2,1,0:T(8,128)S(1)}) custom-call(s32[9]{0:T(128)S(1)} %stack.39.where_ref.refs_1_, f32[12,16,128]{2,1,0:T(8,128)S(1)} %bitcast.12, f32[32,8,512]{2,1,0:T(8,128)S(1)} %copy-done.1), custom_call_target="tpu_custom_call" | custom-call | tf_op jit(solution)/shard_map/open/pallas_call | solution.py:420
  3.6 2.4 %collective-permute-start.2 = (f32[6,16,128]{2,1,0:T(8,128)S(1)}, f32[6,16,128]{2,1,0:T(8,128)S(1)}, u32[]{:S(2)}, u32[]{:S(2)}) collective-permute-start(f32[6,16,128]{2,1,0:T(8,128)S(1)} %get-tuple-element.46), channel_id=1, source_target_pairs={{0,2},{1,3},{2,0},{3,1},{4,6},{5,7},{6,4},{7,5},{8,10},{9,11},{10,... | collective-permute-start | bytes 147464 | tf_op jit(solution)/shard_map/ppermute | solution.py:360
  5.9 1.3 %collective-permute-start.6 = (f32[2,4,8,8,128]{4,3,2,1,0:T(8,128)S(1)}, f32[2,4,8,8,128]{4,3,2,1,0:T(8,128)S(1)}, u32[]{:S(2)}, u32[]{:S(2)}) collective-permute-start(f32[2,4,8,8,128]{4,3,2,1,0:T(8,128)S(1)} %get-tuple-element.47.refs_4_.refs_10_.refs_9_), channel_id=1, source_target_pairs={{0,1},{1,2},{2,3},{3,0},{4,5},{5,6},{6,7},{7,4},{8,9},{9,10},{10,1... | collective-permute-start | bytes 786440 | tf_op jit(solution)/shard_map/ppermute | solution.py:360
  7.2 2.0 %collective-permute-start.4 = (f32[2,4,8,8,128]{4,3,2,1,0:T(8,128)S(1)}, f32[2,4,8,8,128]{4,3,2,1,0:T(8,128)S(1)}, u32[]{:S(2)}, u32[]{:S(2)}) collective-permute-start(f32[2,4,8,8,128]{4,3,2,1,0:T(8,128)S(1)} %get-tuple-element.47.refs_4_.refs_10_.refs_9_), channel_id=1, source_target_pairs={{0,3},{1,0},{2,1},{3,2},{4,7},{5,4},{6,5},{7,6},{8,11},{9,8},{10,9... | collective-permute-start | bytes 786440 | tf_op jit(solution)/shard_map/ppermute | solution.py:360
  9.2 0.9 %pack_projectors.1.refs_5_.refs_11_.refs_10_ = f32[2,4,8,8,128]{4,3,2,1,0:T(8,128)S(1)} custom-call(f32[32,8,512]{2,1,0:T(8,128)S(1)} %copy-done.2, f32[6,16,128]{2,1,0:T(8,128)S(1)} %collective-permute-done.2.refs_1_.refs_3_), custom_call_target="tpu_custom_call" | custom-call | tf_op jit(solution)/shard_map/pack_projectors/pallas_call | solution.py:384
  10.2 3.3 %collective-permute-start.5 = (f32[2,4,8,8,128]{4,3,2,1,0:T(8,128)S(1)}, f32[2,4,8,8,128]{4,3,2,1,0:T(8,128)S(1)}, u32[]{:S(2)}, u32[]{:S(2)}) collective-permute-start(f32[2,4,8,8,128]{4,3,2,1,0:T(8,128)S(1)} %pack_projectors.1.refs_5_.refs_11_.refs_10_), channel_id=1, source_target_pairs={{0,3},{1,0},{2,1},{3,2},{4,7},{5,4},{6,5},{7,6},{8,11},{9,8},{10,9... | collective-permute-start | bytes 786440 | tf_op jit(solution)/shard_map/ppermute | solution.py:360
  13.4 1.6 %project_own.1 = (f32[4,8,128]{2,1,0:T(8,128)S(1)}, f32[4,8,128]{2,1,0:T(8,128)S(1)}) custom-call(s32[3,32]{1,0:T(4,128)S(1)} %copy-done.4, s32[9]{0:T(128)S(1)} %stack.39.where_ref.refs_1_, f32[12,16,128]{2,1,0:T(8,128)S(1)} %bitcast.13, f32[6,16,128]{2,1,0:T(8,128)S(1)} %collective-permute-done.2.refs_1_.refs_3_, ...), custom_call_target="tpu_custom_call" | custom-call | tf_op jit(solution)/shard_map/project_own/pallas_call | solution.py:384
  15.1 16.8 %collective-permute-done.3.refs_2_.refs_4_ = f32[4,8,128]{2,1,0:T(8,128)S(1)} collective-permute-done((f32[4,8,128]{2,1,0:T(8,128)S(1)}, f32[4,8,128]{2,1,0:T(8,128)S(1)}, u32[]{:S(2)}, u32[]{:S(2)}) %collective-permute-start.3) | collective-permute-done | bytes 16416 | tf_op jit(solution)/shard_map/ppermute | solution.py:360
  31.9 1.4 %collective-permute-start = (f32[96,128]{1,0:T(8,128)S(1)}, f32[96,128]{1,0:T(8,128)S(1)}, u32[]{:S(2)}, u32[]{:S(2)}) collective-permute-start(f32[96,128]{1,0:T(8,128)S(1)} %get-tuple-element.44), channel_id=1, source_target_pairs={{0,4},{4,0},{8,12},{12,8},{16,20},{20,16},{24,28},{28,24},{1,5},{5... | collective-permute-start | bytes 147464 | tf_op jit(solution)/shard_map/ppermute | solution.py:355
  33.3 3.0 %collective-permute-start.1 = (f32[96,128]{1,0:T(8,128)S(1)}, f32[96,128]{1,0:T(8,128)S(1)}, u32[]{:S(2)}, u32[]{:S(2)}) collective-permute-start(f32[96,128]{1,0:T(8,128)S(1)} %get-tuple-element.45), channel_id=1, source_target_pairs={{4,8},{8,4},{12,16},{16,12},{20,24},{24,20},{5,9},{9,5},{13,17},{1... | collective-permute-start | bytes 147464 | tf_op jit(solution)/shard_map/ppermute | solution.py:355
  36.4 2.9 %collective-permute-start.12 = (f32[2,4,8,8,128]{4,3,2,1,0:T(8,128)S(1)}, f32[2,4,8,8,128]{4,3,2,1,0:T(8,128)S(1)}, u32[]{:S(2)}, u32[]{:S(2)}) collective-permute-start(f32[2,4,8,8,128]{4,3,2,1,0:T(8,128)S(1)} %get-tuple-element.50.refs_6_.refs_13_.refs_12_), channel_id=1, source_target_pairs={{0,3},{1,0},{2,1},{3,2},{4,7},{5,4},{6,5},{7,6},{8,11},{9,8},{10,9... | collective-permute-start | bytes 786440 | tf_op jit(solution)/shard_map/ppermute | solution.py:360
  40.2 1.3 %project_beside.1.refs_2_ = f32[4,8,128]{2,1,0:T(8,128)S(1)} custom-call(s32[3,32]{1,0:T(4,128)S(1)} %copy-done.4, s32[9]{0:T(128)S(1)} %stack.39.where_ref.refs_1_, f32[12,16,128]{2,1,0:T(8,128)S(1)} %bitcast.14, f32[4,8,128]{2,1,0:T(8,128)S(1)} %get-tuple-element.48.refs_3_, f32[4,8,128]{2,1,0:T(8,128)S(1)} %collective-permute-done.3.refs_2_.refs_4_, ...), custom_call_target="tpu_custom_call" | custom-call | tf_op jit(solution)/shard_map/project_beside/pallas_call | solution.py:384
  42.5 0.8 %collective-permute-done.8 = f32[16,128]{1,0:T(8,128)S(1)} collective-permute-done((f32[16,128]{1,0:T(8,128)S(1)}, f32[16,128]{1,0:T(8,128)S(1)}, u32[]{:S(2)}, u32[]{:S(2)}) %collective-permute-start.8) | collective-permute-done | bytes 8224 | tf_op jit(solution)/shard_map/ppermute | solution.py:355
  43.4 2.4 %collective-permute-start.9 = (f32[16,128]{1,0:T(8,128)S(1)}, f32[16,128]{1,0:T(8,128)S(1)}, u32[]{:S(2)}, u32[]{:S(2)}) collective-permute-start(f32[16,128]{1,0:T(8,128)S(1)} %add.67.refs_7_), channel_id=1, source_target_pairs={{4,8},{8,4},{12,16},{16,12},{20,24},{24,20},{5,9},{9,5},{13,17},{1... | collective-permute-start | bytes 24584 | tf_op jit(solution)/shard_map/ppermute | solution.py:355
  45.8 2.8 %collective-permute-done.9.refs_9_ = f32[16,128]{1,0:T(8,128)S(1)} collective-permute-done((f32[16,128]{1,0:T(8,128)S(1)}, f32[16,128]{1,0:T(8,128)S(1)}, u32[]{:S(2)}, u32[]{:S(2)}) %collective-permute-start.9) | collective-permute-done | bytes 8224 | tf_op jit(solution)/shard_map/ppermute | solution.py:355
  48.6 0.9 %collective-permute-start.10 = (f32[16,128]{1,0:T(8,128)S(1)}, f32[16,128]{1,0:T(8,128)S(1)}, u32[]{:S(2)}, u32[]{:S(2)}) collective-permute-start(f32[16,128]{1,0:T(8,128)S(1)} %collective-permute-done.9.refs_9_), channel_id=1, source_target_pairs={{0,4},{4,0},{8,12},{12,8},{16,20},{20,16},{24,28},{28,24},{1,5},{5... | collective-permute-start | bytes 24584 | tf_op jit(solution)/shard_map/ppermute | solution.py:355
  49.6 0.8 %collective-permute-done.10.refs_8_ = f32[16,128]{1,0:T(8,128)S(1)} collective-permute-done((f32[16,128]{1,0:T(8,128)S(1)}, f32[16,128]{1,0:T(8,128)S(1)}, u32[]{:S(2)}, u32[]{:S(2)}) %collective-permute-start.10) | collective-permute-done | bytes 8224 | tf_op jit(solution)/shard_map/ppermute | solution.py:355
  51.1 3.8 %filter_step_1.1 = (f32[12,16,128]{2,1,0:T(8,128)S(1)}, f32[104,128]{1,0:T(8,128)S(1)}, f32[104,128]{1,0:T(8,128)S(1)}, f32[8,128]{1,0:T(8,128)S(1)}) custom-call(s32[3,32]{1,0:T(4,128)S(1)} %copy-done.4, s32[9]{0:T(128)S(1)} %stack.39.where_ref.refs_1_, s32[1,512]{1,0:T(1,128)S(1)} %broadcast_in_dim_reshape.3.refs_0_.refs_2_, f32[12,16,128]{2,1,0:T(8,128)S(1)} %bitcast.15, ...), custom_call_target="tpu_custom_call" | custom-call | tf_op jit(solution)/shard_map/filter_step_1/pallas_call | solution.py:384
  54.9 1.0 %collective-permute-start.13 = (f32[104,128]{1,0:T(8,128)S(1)}, f32[104,128]{1,0:T(8,128)S(1)}, u32[]{:S(2)}, u32[]{:S(2)}) collective-permute-start(f32[104,128]{1,0:T(8,128)S(1)} %get-tuple-element.53), channel_id=1, source_target_pairs={{0,4},{4,0},{8,12},{12,8},{16,20},{20,16},{24,28},{28,24},{1,5},{5... | collective-permute-start | bytes 159752 | tf_op jit(solution)/shard_map/ppermute | solution.py:355
  55.9 0.9 %collective-permute-done.13.refs_5_ = f32[104,128]{1,0:T(8,128)S(1)} collective-permute-done((f32[104,128]{1,0:T(8,128)S(1)}, f32[104,128]{1,0:T(8,128)S(1)}, u32[]{:S(2)}, u32[]{:S(2)}) %collective-permute-start.13) | collective-permute-done | bytes 53280 | tf_op jit(solution)/shard_map/ppermute | solution.py:355
  56.8 1.9 %collective-permute-start.14 = (f32[104,128]{1,0:T(8,128)S(1)}, f32[104,128]{1,0:T(8,128)S(1)}, u32[]{:S(2)}, u32[]{:S(2)}) collective-permute-start(f32[104,128]{1,0:T(8,128)S(1)} %fusion.1.refs_7_), channel_id=1, source_target_pairs={{4,8},{8,4},{12,16},{16,12},{20,24},{24,20},{5,9},{9,5},{13,17},{1... | collective-permute-start | bytes 159752 | tf_op jit(solution)/shard_map/ppermute | solution.py:355
  58.7 3.8 %collective-permute-done.14.refs_6_ = f32[104,128]{1,0:T(8,128)S(1)} collective-permute-done((f32[104,128]{1,0:T(8,128)S(1)}, f32[104,128]{1,0:T(8,128)S(1)}, u32[]{:S(2)}, u32[]{:S(2)}) %collective-permute-start.14) | collective-permute-done | bytes 53280 | tf_op jit(solution)/shard_map/ppermute | solution.py:355
  62.6 1.0 %collective-permute-start.15 = (f32[8,128]{1,0:T(8,128)S(1)}, f32[8,128]{1,0:T(8,128)S(1)}, u32[]{:S(2)}, u32[]{:S(2)}) collective-permute-start(f32[8,128]{1,0:T(8,128)S(1)} %slice.57), channel_id=1, source_target_pairs={{0,4},{4,0},{8,12},{12,8},{16,20},{20,16},{24,28},{28,24},{1,5},{5... | collective-permute-start | bytes 12296 | tf_op jit(solution)/shard_map/ppermute | solution.py:355
  63.5 0.8 %collective-permute-done.15.refs_8_ = f32[8,128]{1,0:T(8,128)S(1)} collective-permute-done((f32[8,128]{1,0:T(8,128)S(1)}, f32[8,128]{1,0:T(8,128)S(1)}, u32[]{:S(2)}, u32[]{:S(2)}) %collective-permute-start.15) | collective-permute-done | bytes 4128 | tf_op jit(solution)/shard_map/ppermute | solution.py:355
  64.3 3.8 %filter_step_2.1 = (f32[12,16,128]{2,1,0:T(8,128)S(1)}, f32[104,128]{1,0:T(8,128)S(1)}, f32[104,128]{1,0:T(8,128)S(1)}) custom-call(s32[3,32]{1,0:T(4,128)S(1)} %copy-done.4, s32[9]{0:T(128)S(1)} %stack.39.where_ref.refs_1_, s32[1,512]{1,0:T(1,128)S(1)} %broadcast_in_dim_reshape.3.refs_0_.refs_2_, f32[12,16,128]{2,1,0:T(8,128)S(1)} %get-tuple-element.52.refs_3_.refs_18_, ...), custom_call_target="tpu_custom_call" | custom-call | tf_op jit(solution)/shard_map/filter_step_2/pallas_call | solution.py:384
  68.5 0.9 %collective-permute-done.16.refs_5_ = f32[104,128]{1,0:T(8,128)S(1)} collective-permute-done((f32[104,128]{1,0:T(8,128)S(1)}, f32[104,128]{1,0:T(8,128)S(1)}, u32[]{:S(2)}, u32[]{:S(2)}) %collective-permute-start.16) | collective-permute-done | bytes 53280 | tf_op jit(solution)/shard_map/ppermute | solution.py:355
  69.4 1.9 %collective-permute-start.17 = (f32[104,128]{1,0:T(8,128)S(1)}, f32[104,128]{1,0:T(8,128)S(1)}, u32[]{:S(2)}, u32[]{:S(2)}) collective-permute-start(f32[104,128]{1,0:T(8,128)S(1)} %fusion.refs_7_), channel_id=1, source_target_pairs={{4,8},{8,4},{12,16},{16,12},{20,24},{24,20},{5,9},{9,5},{13,17},{1... | collective-permute-start | bytes 159752 | tf_op jit(solution)/shard_map/ppermute | solution.py:355
  71.3 3.8 %collective-permute-done.17.refs_6_ = f32[104,128]{1,0:T(8,128)S(1)} collective-permute-done((f32[104,128]{1,0:T(8,128)S(1)}, f32[104,128]{1,0:T(8,128)S(1)}, u32[]{:S(2)}, u32[]{:S(2)}) %collective-permute-start.17) | collective-permute-done | bytes 53280 | tf_op jit(solution)/shard_map/ppermute | solution.py:355
  75.2 0.9 %collective-permute-start.18 = (f32[8,128]{1,0:T(8,128)S(1)}, f32[8,128]{1,0:T(8,128)S(1)}, u32[]{:S(2)}, u32[]{:S(2)}) collective-permute-start(f32[8,128]{1,0:T(8,128)S(1)} %slice.59), channel_id=1, source_target_pairs={{0,4},{4,0},{8,12},{12,8},{16,20},{20,16},{24,28},{28,24},{1,5},{5... | collective-permute-start | bytes 12296 | tf_op jit(solution)/shard_map/ppermute | solution.py:355
  76.1 0.8 %collective-permute-done.18.refs_8_ = f32[8,128]{1,0:T(8,128)S(1)} collective-permute-done((f32[8,128]{1,0:T(8,128)S(1)}, f32[8,128]{1,0:T(8,128)S(1)}, u32[]{:S(2)}, u32[]{:S(2)}) %collective-permute-start.18) | collective-permute-done | bytes 4128 | tf_op jit(solution)/shard_map/ppermute | solution.py:355
  76.9 3.0 %filter_step_3.1 = f32[12,16,128]{2,1,0:T(8,128)} custom-call(s32[3,32]{1,0:T(4,128)S(1)} %copy-done.4, s32[9]{0:T(128)S(1)} %stack.39.where_ref.refs_1_, s32[1,512]{1,0:T(1,128)S(1)} %broadcast_in_dim_reshape.3.refs_0_.refs_2_, f32[12,16,128]{2,1,0:T(8,128)S(1)} %get-tuple-element.56.refs_3_, f32[12,16,128]{2,1,0:T(8,128)S(1)} %copy-done.3, ...), custom_call_target="tpu_custom_call" | custom-call | tf_op jit(solution)/shard_map/filter_step_3/pallas_call | solution.py:384
  (41 shorter events, 4.1 us)
Async XLA Ops:
  0.0 0.9 %copy-start = (f32[1,12,16,128]{3,2,1,0:T(8,128)S(1)}, f32[1,12,16,128]{3,2,1,0:T(8,128)}, u32[]{:S(2)}) copy-start(f32[1,12,16,128]{3,2,1,0:T(8,128)} %param.10) | copy-start | bytes 294916
  0.9 1.0 %copy-start.1 = (f32[32,8,512]{2,1,0:T(8,128)S(1)}, f32[32,8,512]{2,1,0:T(8,128)}, u32[]{:S(2)}) copy-start(f32[32,8,512]{2,1,0:T(8,128)} %refs_0_.6) | copy-start | bytes 1572868
  1.9 7.3 %copy-start.2 = (f32[32,8,512]{2,1,0:T(8,128)S(1)}, f32[32,8,512]{2,1,0:T(8,128)}, u32[]{:S(2)}) copy-start(f32[32,8,512]{2,1,0:T(8,128)} %refs_0_.6) | copy-start | bytes 1572868
  3.6 5.6 %collective-permute-start.2 = (f32[6,16,128]{2,1,0:T(8,128)S(1)}, f32[6,16,128]{2,1,0:T(8,128)S(1)}, u32[]{:S(2)}, u32[]{:S(2)}) collective-permute-start(f32[6,16,128]{2,1,0:T(8,128)S(1)} %get-tuple-element.46), channel_id=1, source_target_pairs={{0,2},{1,3},{2,0},{3,1},{4,6},{5,7},{6,4},{7,5},{8,10},{9,11},{10,... | collective-permute-start | bytes 147464 | tf_op jit(solution)/shard_map/ppermute | solution.py:360
  5.9 7.5 %copy-start.4 = (s32[3,32]{1,0:T(4,128)S(1)}, s32[3,32]{1,0:T(4,128)}, u32[]{:S(2)}) copy-start(s32[3,32]{1,0:T(4,128)} %refs_0_.11) | copy-start | bytes 1156
  5.9 27.4 %collective-permute-start.6 = (f32[2,4,8,8,128]{4,3,2,1,0:T(8,128)S(1)}, f32[2,4,8,8,128]{4,3,2,1,0:T(8,128)S(1)}, u32[]{:S(2)}, u32[]{:S(2)}) collective-permute-start(f32[2,4,8,8,128]{4,3,2,1,0:T(8,128)S(1)} %get-tuple-element.47.refs_4_.refs_10_.refs_9_), channel_id=1, source_target_pairs={{0,1},{1,2},{2,3},{3,0},{4,5},{5,6},{6,7},{7,4},{8,9},{9,10},{10,1... | collective-permute-start | bytes 786440 | tf_op jit(solution)/shard_map/ppermute | solution.py:360
  7.2 29.1 %collective-permute-start.4 = (f32[2,4,8,8,128]{4,3,2,1,0:T(8,128)S(1)}, f32[2,4,8,8,128]{4,3,2,1,0:T(8,128)S(1)}, u32[]{:S(2)}, u32[]{:S(2)}) collective-permute-start(f32[2,4,8,8,128]{4,3,2,1,0:T(8,128)S(1)} %get-tuple-element.47.refs_4_.refs_10_.refs_9_), channel_id=1, source_target_pairs={{0,3},{1,0},{2,1},{3,2},{4,7},{5,4},{6,5},{7,6},{8,11},{9,8},{10,9... | collective-permute-start | bytes 786440 | tf_op jit(solution)/shard_map/ppermute | solution.py:360
  10.1 26.2 %collective-permute-start.7 = (f32[2,4,8,8,128]{4,3,2,1,0:T(8,128)S(1)}, f32[2,4,8,8,128]{4,3,2,1,0:T(8,128)S(1)}, u32[]{:S(2)}, u32[]{:S(2)}) collective-permute-start(f32[2,4,8,8,128]{4,3,2,1,0:T(8,128)S(1)} %pack_projectors.1.refs_5_.refs_11_.refs_10_), channel_id=1, source_target_pairs={{0,1},{1,2},{2,3},{3,0},{4,5},{5,6},{6,7},{7,4},{8,9},{9,10},{10,1... | collective-permute-start | bytes 786440 | tf_op jit(solution)/shard_map/ppermute | solution.py:360
  10.2 26.1 %collective-permute-start.5 = (f32[2,4,8,8,128]{4,3,2,1,0:T(8,128)S(1)}, f32[2,4,8,8,128]{4,3,2,1,0:T(8,128)S(1)}, u32[]{:S(2)}, u32[]{:S(2)}) collective-permute-start(f32[2,4,8,8,128]{4,3,2,1,0:T(8,128)S(1)} %pack_projectors.1.refs_5_.refs_11_.refs_10_), channel_id=1, source_target_pairs={{0,3},{1,0},{2,1},{3,2},{4,7},{5,4},{6,5},{7,6},{8,11},{9,8},{10,9... | collective-permute-start | bytes 786440 | tf_op jit(solution)/shard_map/ppermute | solution.py:360
  15.0 16.9 %collective-permute-start.3 = (f32[4,8,128]{2,1,0:T(8,128)S(1)}, f32[4,8,128]{2,1,0:T(8,128)S(1)}, u32[]{:S(2)}, u32[]{:S(2)}) collective-permute-start(f32[4,8,128]{2,1,0:T(8,128)S(1)} %get-tuple-element.49), channel_id=1, source_target_pairs={{0,2},{1,3},{2,0},{3,1},{4,6},{5,7},{6,4},{7,5},{8,10},{9,11},{10,... | collective-permute-start | bytes 49160 | tf_op jit(solution)/shard_map/ppermute | solution.py:360
  31.9 17.6 %collective-permute-start = (f32[96,128]{1,0:T(8,128)S(1)}, f32[96,128]{1,0:T(8,128)S(1)}, u32[]{:S(2)}, u32[]{:S(2)}) collective-permute-start(f32[96,128]{1,0:T(8,128)S(1)} %get-tuple-element.44), channel_id=1, source_target_pairs={{0,4},{4,0},{8,12},{12,8},{16,20},{20,16},{24,28},{28,24},{1,5},{5... | collective-permute-start | bytes 147464 | tf_op jit(solution)/shard_map/ppermute | solution.py:355
  33.3 16.3 %collective-permute-start.1 = (f32[96,128]{1,0:T(8,128)S(1)}, f32[96,128]{1,0:T(8,128)S(1)}, u32[]{:S(2)}, u32[]{:S(2)}) collective-permute-start(f32[96,128]{1,0:T(8,128)S(1)} %get-tuple-element.45), channel_id=1, source_target_pairs={{4,8},{8,4},{12,16},{16,12},{20,24},{24,20},{5,9},{9,5},{13,17},{1... | collective-permute-start | bytes 147464 | tf_op jit(solution)/shard_map/ppermute | solution.py:355
  36.3 2.9 %copy-start.5 = (f32[16,8]{0,1:T(8,128)S(1)}, f32[16,8]{0,1:T(8,128)}, u32[]{:S(2)}) copy-start(f32[16,8]{0,1:T(8,128)} %param.13) | copy-start | bytes 1540
  36.4 14.0 %collective-permute-start.12 = (f32[2,4,8,8,128]{4,3,2,1,0:T(8,128)S(1)}, f32[2,4,8,8,128]{4,3,2,1,0:T(8,128)S(1)}, u32[]{:S(2)}, u32[]{:S(2)}) collective-permute-start(f32[2,4,8,8,128]{4,3,2,1,0:T(8,128)S(1)} %get-tuple-element.50.refs_6_.refs_13_.refs_12_), channel_id=1, source_target_pairs={{0,3},{1,0},{2,1},{3,2},{4,7},{5,4},{6,5},{7,6},{8,11},{9,8},{10,9... | collective-permute-start | bytes 786440 | tf_op jit(solution)/shard_map/ppermute | solution.py:360
  39.2 11.9 %collective-permute-start.11 = (f32[2,4,8,8,128]{4,3,2,1,0:T(8,128)S(1)}, f32[2,4,8,8,128]{4,3,2,1,0:T(8,128)S(1)}, u32[]{:S(2)}, u32[]{:S(2)}) collective-permute-start(f32[2,4,8,8,128]{4,3,2,1,0:T(8,128)S(1)} %get-tuple-element.51.refs_7_.refs_14_.refs_13_), channel_id=1, source_target_pairs={{0,1},{1,2},{2,3},{3,0},{4,5},{5,6},{6,7},{7,4},{8,9},{9,10},{10,1... | collective-permute-start | bytes 786440 | tf_op jit(solution)/shard_map/ppermute | solution.py:360
  39.3 0.7 copy-start.6
  40.1 11.0 %copy-start.3 = (f32[12,16,128]{2,1,0:T(8,128)S(1)}, f32[12,16,128]{2,1,0:T(8,128)}, u32[]{:S(2)}) copy-start(f32[12,16,128]{2,1,0:T(8,128)} %refs_4_.5) | copy-start | bytes 294916
  41.8 1.6 %collective-permute-start.8 = (f32[16,128]{1,0:T(8,128)S(1)}, f32[16,128]{1,0:T(8,128)S(1)}, u32[]{:S(2)}, u32[]{:S(2)}) collective-permute-start(f32[16,128]{1,0:T(8,128)S(1)} %first_sums.1), channel_id=1, source_target_pairs={{0,4},{4,0},{8,12},{12,8},{16,20},{20,16},{24,28},{28,24},{1,5},{5... | collective-permute-start | bytes 24584 | tf_op jit(solution)/shard_map/ppermute | solution.py:355
  43.4 5.3 %collective-permute-start.9 = (f32[16,128]{1,0:T(8,128)S(1)}, f32[16,128]{1,0:T(8,128)S(1)}, u32[]{:S(2)}, u32[]{:S(2)}) collective-permute-start(f32[16,128]{1,0:T(8,128)S(1)} %add.67.refs_7_), channel_id=1, source_target_pairs={{4,8},{8,4},{12,16},{16,12},{20,24},{24,20},{5,9},{9,5},{13,17},{1... | collective-permute-start | bytes 24584 | tf_op jit(solution)/shard_map/ppermute | solution.py:355
  48.6 1.8 %collective-permute-start.10 = (f32[16,128]{1,0:T(8,128)S(1)}, f32[16,128]{1,0:T(8,128)S(1)}, u32[]{:S(2)}, u32[]{:S(2)}) collective-permute-start(f32[16,128]{1,0:T(8,128)S(1)} %collective-permute-done.9.refs_9_), channel_id=1, source_target_pairs={{0,4},{4,0},{8,12},{12,8},{16,20},{20,16},{24,28},{28,24},{1,5},{5... | collective-permute-start | bytes 24584 | tf_op jit(solution)/shard_map/ppermute | solution.py:355
  54.9 1.9 %collective-permute-start.13 = (f32[104,128]{1,0:T(8,128)S(1)}, f32[104,128]{1,0:T(8,128)S(1)}, u32[]{:S(2)}, u32[]{:S(2)}) collective-permute-start(f32[104,128]{1,0:T(8,128)S(1)} %get-tuple-element.53), channel_id=1, source_target_pairs={{0,4},{4,0},{8,12},{12,8},{16,20},{20,16},{24,28},{28,24},{1,5},{5... | collective-permute-start | bytes 159752 | tf_op jit(solution)/shard_map/ppermute | solution.py:355
  56.8 5.7 %collective-permute-start.14 = (f32[104,128]{1,0:T(8,128)S(1)}, f32[104,128]{1,0:T(8,128)S(1)}, u32[]{:S(2)}, u32[]{:S(2)}) collective-permute-start(f32[104,128]{1,0:T(8,128)S(1)} %fusion.1.refs_7_), channel_id=1, source_target_pairs={{4,8},{8,4},{12,16},{16,12},{20,24},{24,20},{5,9},{9,5},{13,17},{1... | collective-permute-start | bytes 159752 | tf_op jit(solution)/shard_map/ppermute | solution.py:355
  62.6 1.8 %collective-permute-start.15 = (f32[8,128]{1,0:T(8,128)S(1)}, f32[8,128]{1,0:T(8,128)S(1)}, u32[]{:S(2)}, u32[]{:S(2)}) collective-permute-start(f32[8,128]{1,0:T(8,128)S(1)} %slice.57), channel_id=1, source_target_pairs={{0,4},{4,0},{8,12},{12,8},{16,20},{20,16},{24,28},{28,24},{1,5},{5... | collective-permute-start | bytes 12296 | tf_op jit(solution)/shard_map/ppermute | solution.py:355
  68.2 1.3 %collective-permute-start.16 = (f32[104,128]{1,0:T(8,128)S(1)}, f32[104,128]{1,0:T(8,128)S(1)}, u32[]{:S(2)}, u32[]{:S(2)}) collective-permute-start(f32[104,128]{1,0:T(8,128)S(1)} %get-tuple-element.57), channel_id=1, source_target_pairs={{0,4},{4,0},{8,12},{12,8},{16,20},{20,16},{24,28},{28,24},{1,5},{5... | collective-permute-start | bytes 159752 | tf_op jit(solution)/shard_map/ppermute | solution.py:355
  69.4 5.7 %collective-permute-start.17 = (f32[104,128]{1,0:T(8,128)S(1)}, f32[104,128]{1,0:T(8,128)S(1)}, u32[]{:S(2)}, u32[]{:S(2)}) collective-permute-start(f32[104,128]{1,0:T(8,128)S(1)} %fusion.refs_7_), channel_id=1, source_target_pairs={{4,8},{8,4},{12,16},{16,12},{20,24},{24,20},{5,9},{9,5},{13,17},{1... | collective-permute-start | bytes 159752 | tf_op jit(solution)/shard_map/ppermute | solution.py:355
  75.2 1.8 %collective-permute-start.18 = (f32[8,128]{1,0:T(8,128)S(1)}, f32[8,128]{1,0:T(8,128)S(1)}, u32[]{:S(2)}, u32[]{:S(2)}) collective-permute-start(f32[8,128]{1,0:T(8,128)S(1)} %slice.59), channel_id=1, source_target_pairs={{0,4},{4,0},{8,12},{12,8},{16,20},{20,16},{24,28},{28,24},{1,5},{5... | collective-permute-start | bytes 12296 | tf_op jit(solution)/shard_map/ppermute | solution.py:355

commit v2 on v1

--- a/solution.py
+++ b/solution.py
@@ -29,7 +29,6 @@
 LOWER_EDGE = 3.0
 UPPER_EDGE = 30.0
 ANCHOR_POINT = 0.5
-EXACT = lax.Precision.HIGHEST
 HALF_WIDTH = (UPPER_EDGE - LOWER_EDGE) / 2.0
 CENTRE = (UPPER_EDGE + LOWER_EDGE) / 2.0
 SIGMA_FIRST = HALF_WIDTH / (ANCHOR_POINT - CENTRE)
@@ -99,8 +98,31 @@
     lax.fori_loop(0, tiles * groups, one, 0)
 
 
-def member(atom_row, atoms):
-    return (iota((atoms, atom_row.shape[1]), 0) == atom_row).astype(jnp.float32)
+def halves_of(value):
+    high = value.astype(jnp.bfloat16)
+    return high, (value - high.astype(jnp.float32)).astype(jnp.bfloat16)
+
+
+def thirds_of(value):
+    rest, parts = value, []
+    for _ in range(3):
+        high = rest.astype(jnp.bfloat16).astype(jnp.float32)
+        parts.append(high)
+        rest = rest - high
+    return jnp.concatenate(parts, axis=0).astype(jnp.bfloat16)
+
+
+def sum_thirds(value):
+    return value[:ROWS] + value[ROWS : 2 * ROWS] + value[2 * ROWS :]
+
+
+def table_kernel(atom_row_ref, member_ref, along_z_ref, along_y_ref):
+    atoms = iota(member_ref.shape, 0)
+    member_ref[...] = (atoms == atom_row_ref[...]).astype(jnp.float32).astype(jnp.bfloat16)
+    high, low = halves_of(band_matrix(LANES, LANES, 3.0 * STENCIL_WEIGHTS[0]))
+    along_z_ref[...] = jnp.concatenate([high, low, high], axis=0)
+    high, low = halves_of(band_matrix(along_y_ref.shape[0], SY, 0.0))
+    along_y_ref[...] = jnp.concatenate([high, high, low], axis=1)
 
 
 def total_of(products):
@@ -132,24 +154,26 @@
         flat_ref[group] = flat if start_ref is None else flat + start_ref[group]
         return carry
 
-    lax.fori_loop(0, groups, one, 0)
-
-
-def sum_atoms(flat_ref, atom_row_ref, atoms):
+    for group in range(groups):
+        one(group, 0)
+
+
+def sum_atoms(flat_ref, member_ref):
     flat = jnp.concatenate([flat_ref[g] for g in range(flat_ref.shape[0])], axis=1)
-    return lax.dot_general(
-        flat, member(atom_row_ref[...], atoms), (((1,), (1,)), ((), ())),
-        precision=EXACT, preferred_element_type=jnp.float32,
-    )
-
-
-def deposit(scaled, chunks, corner_ref, atom_row_ref, flat_ref, box_ref, parts_ref):
+    return sum_thirds(
+        lax.dot_general(
+            thirds_of(flat), member_ref[...], (((1,), (1,)), ((), ())),
+            preferred_element_type=jnp.float32,
+        )
+    )
+
+
+def deposit(scaled, chunks, corner_ref, member_ref, flat_ref, box_ref, parts_ref):
     groups = chunks[0][1].shape[1]
     copies = parts_ref.shape[0]
     lane_block = iota((ROWS, LANES), 1) // SZ
-    flat = jnp.dot(
-        scaled, member(atom_row_ref[...], scaled.shape[1]),
-        precision=EXACT, preferred_element_type=jnp.float32,
+    flat = sum_thirds(
+        jnp.dot(thirds_of(scaled), member_ref[...], preferred_element_type=jnp.float32)
     )
     for g in range(groups):
         flat_ref[g] = flat[:, g * LANES : (g + 1) * LANES]
@@ -179,7 +203,8 @@
                 parts_ref[at] = parts_ref[at] + jnp.stack(added)
         return carry
 
-    lax.fori_loop(0, groups, one, 0)
+    for group in range(groups):
+        one(group, 0)
 
 
 def band_matrix(size, block, centre):
@@ -192,16 +217,16 @@
     return jnp.where(row // block == column // block, table, 0.0)
 
 
-def laplacian(padded_ref, extent):
+def laplacian(padded_ref, extent, along_z_ref, along_y_ref):
     inner = padded_ref[REACH : REACH + extent]
-    flat = inner.reshape(extent * SY, LANES)
+    high, low = halves_of(inner.reshape(extent * SY, LANES))
     along_z = jnp.dot(
-        flat, band_matrix(LANES, LANES, 3.0 * STENCIL_WEIGHTS[0]),
-        precision=EXACT, preferred_element_type=jnp.float32,
+        jnp.concatenate([high, high, low], axis=1), along_z_ref[...],
+        preferred_element_type=jnp.float32,
     )
     along_y = jnp.dot(
-        band_matrix(extent * SY, SY, 0.0), flat,
-        precision=EXACT, preferred_element_type=jnp.float32,
+        along_y_ref[...], jnp.concatenate([high, low, high], axis=0),
+        preferred_element_type=jnp.float32,
     )
     total = (along_z + along_y).reshape(inner.shape)
     for k in range(1, REACH + 1):
@@ -240,22 +265,10 @@
     return lambda x, half: ref[x, pl.ds(half * ROWS, ROWS), :]
 
 
-def halo_kernel(where_ref, field_ref, mate_ref, cross_ref):
+def window_kernel(where_ref, field_ref, mate_ref, cross_ref, *window_refs):
     write_halos(field_ref, where_ref[0], mate_ref, cross_ref)
-
-
-def opening_kernel(where_ref, field_hbm, proj_hbm, mate_ref, cross_ref, window_ref, low_ref,
-                   field_ref, proj_ref, field_sem, proj_sem):
-    field_copy = pltpu.make_async_copy(field_hbm, field_ref, field_sem)
-    cells = pl.ds(0, proj_ref.shape[2])
-    proj_copy = pltpu.make_async_copy(proj_hbm.at[:, :, cells], proj_ref, proj_sem)
-    field_copy.start()
-    proj_copy.start()
-    field_copy.wait()
-    window_ref[...] = field_ref[pl.ds(where_ref[FIRST_CHUNK + 6], REACH)]
-    write_halos(field_ref, where_ref[0], mate_ref, cross_ref)
-    proj_copy.wait()
-    pack_kernel(0, proj_ref, low_ref)
+    for ref in window_refs:
+        ref[...] = field_ref[pl.ds(where_ref[FIRST_CHUNK + 6], REACH)]
 
 
 def own_planes_kernel(corner_ref, where_ref, field_ref, window_ref, low_ref, high_ref,
@@ -266,31 +279,33 @@
     project(field_reader(window_ref), list(enumerate(chunks)), corner_ref, opposite_ref)
 
 
-def forward_kernel(above_ref, below_ref, above_out_ref, below_out_ref):
-    pass
-
-
-def beside_kernel(corner_ref, where_ref, field_ref, own_ref, returned_ref, *refs):
-    flat_ref = refs[-1]
+def forward_kernel(corner_ref, where_ref, field_ref, own_ref, returned_ref, above_ref, below_ref,
+                   flat_ref, above_out_ref, below_out_ref):
+    above_out_ref[...] = above_ref[...]
+    below_out_ref[...] = below_ref[...]
     flat_ref[...] = own_ref[...] + returned_ref[...]
-    chunks = [(where_ref[FIRST_CHUNK + 2 + i], ref) for i, ref in enumerate(refs[:-1])]
+    chunks = [(where_ref[FIRST_CHUNK + 3], above_ref), (where_ref[FIRST_CHUNK + 4], below_ref)]
     project(field_reader(field_ref), chunks, corner_ref, flat_ref, flat_ref)
 
 
-def table_kernel(atom_row_ref, energy_ref, *refs):
+def beside_kernel(corner_ref, where_ref, field_ref, start_ref, above_ref, below_ref, out_ref):
+    chunks = [(where_ref[FIRST_CHUNK + 2], above_ref), (where_ref[FIRST_CHUNK + 5], below_ref)]
+    project(field_reader(field_ref), chunks, corner_ref, out_ref, start_ref)
+
+
+def first_sums_kernel(member_ref, energy_ref, *refs):
     flat_refs, out_ref, flat_ref = refs[:-2], refs[-2], refs[-1]
     flat_ref[...] = total_of([ref[...] for ref in flat_refs])
-    energy = energy_ref[...]
-    sums = sum_atoms(flat_ref, atom_row_ref, energy.shape[1])
-    out_ref[...] = jnp.concatenate([to_rows(sums), to_rows(energy)], axis=0)
+    sums = sum_atoms(flat_ref, member_ref)
+    out_ref[...] = jnp.concatenate([to_rows(sums), to_rows(energy_ref[...])], axis=0)
 
 
 def whole_kernel(corner_ref, field_ref, whole_ref, out_ref):
     project(field_reader(field_ref), all_planes(whole_ref), corner_ref, out_ref)
 
 
-def step_kernel(index, chunk_count, corner_ref, where_ref, atom_row_ref, field_ref, potential_ref,
-                mate_ref, cross_ref, *refs):
+def step_kernel(index, chunk_count, corner_ref, where_ref, member_ref, along_z_ref, along_y_ref,
+                field_ref, potential_ref, mate_ref, cross_ref, *refs):
     factors = step_factors()
     is_first, is_last = index == 0, index + 1 == len(factors)
     refs = list(refs)
@@ -319,7 +334,7 @@
         energy_ref[...] = table[:, atoms:]
         table = table[:, :atoms]
     scaled = table * energy_ref[...]
-    deposit(scaled, chunks, corner_ref, atom_row_ref, flat_ref, box_ref, parts_ref)
+    deposit(scaled, chunks, corner_ref, member_ref, flat_ref, box_ref, parts_ref)
 
     cells = field_ref[...]
     padded_ref[REACH : REACH + extent] = cells
@@ -327,7 +342,7 @@
     cross_at = odd * (extent + REACH)
     padded_ref[pl.ds(mate_at, REACH)] = mate_ref[:HALO_ROWS].reshape(REACH, SY, LANES)
     padded_ref[pl.ds(cross_at, REACH)] = cross_ref[:HALO_ROWS].reshape(REACH, SY, LANES)
-    value = -0.5 * laplacian(padded_ref, extent) + (potential_ref[...] - CENTRE) * cells
+    value = -0.5 * laplacian(padded_ref, extent, along_z_ref, along_y_ref) + (potential_ref[...] - CENTRE) * cells
     for u in range(parts_ref.shape[0]):
         value = value + parts_ref[u]
     value = factors[index][0] * value
@@ -336,7 +351,7 @@
     next_ref[...] = value
     if not is_last:
         project(field_reader(next_ref), chunks, corner_ref, flat_ref)
-        sums = sum_atoms(flat_ref, atom_row_ref, scaled.shape[1])
+        sums = sum_atoms(flat_ref, member_ref)
         write_halos(next_ref, odd, next_mate_ref, next_cross_ref)
         next_mate_ref[HALO_ROWS:] = to_rows(sums)
         next_cross_ref[HALO_ROWS:] = to_rows(sums)
@@ -375,7 +390,7 @@
     def shaped(*shape):
         return jax.ShapeDtypeStruct(shape, jnp.float32)
 
-    def call(kernel, name, out_shape, scalars, operands, scratch, after=(), in_place={}):
+    def call(kernel, name, out_shape, scalars, operands, scratch, after=()):
         inputs = len(scalars) + len(operands)
 
         def body(*refs):
@@ -388,7 +403,6 @@
             out_specs=jax.tree.map(lambda _: VMEM, out_shape),
             scratch_shapes=[pltpu.VMEM(shape, jnp.float32) for shape in scratch],
             compiler_params=pltpu.CompilerParams(vmem_limit_bytes=16 * 2**20),
-            input_output_aliases=in_place,
             cost_estimate=pl.CostEstimate(flops=0, bytes_accessed=0, transcendentals=0),
             name=name,
         )(*scalars, *operands, *after)
@@ -409,6 +423,16 @@
             shaped(count, groups, ROWS, ROWS, LANES), [], [projectors], [], after,
         )
 
+    tables = call(
+        table_kernel, "tables",
+        [
+            jax.ShapeDtypeStruct(shape, jnp.bfloat16)
+            for shape in (
+                (atoms, slots * SZ), (3 * LANES, LANES), (planes * SY, 3 * planes * SY)
+            )
+        ],
+        [], [atom_row], [],
+    )
     odd = (place % 2).astype(jnp.int32)
     halos = [shaped(HALO_ROWS, LANES)] * 2
     if lax.axis_size("band") == 4 and tiles == 2 * HALVES:
@@ -416,24 +440,12 @@
         owners = [at, (at + 1) % 4, (at + 3) % 4, (at + 2) % 4]
         where = jnp.stack([odd] + [2 * part + h for part in owners for h in range(2)])
         window = shaped(REACH, SY, LANES)
-        packed_plane = shaped(HALVES, groups, ROWS, ROWS, LANES)
-        mate, cross, opposite, low = pl.pallas_call(
-            opening_kernel,
-            out_shape=halos + [window, packed_plane],
-            in_specs=[SMEM, ANY, ANY],
-            out_specs=[VMEM] * 4,
-            scratch_shapes=[
-                pltpu.VMEM(field.shape, jnp.float32),
-                pltpu.VMEM((slots, ROWS, HALVES * LANES), jnp.float32),
-                pltpu.SemaphoreType.DMA,
-                pltpu.SemaphoreType.DMA,
-            ],
-            compiler_params=pltpu.CompilerParams(vmem_limit_bytes=16 * 2**20),
-            cost_estimate=pl.CostEstimate(flops=0, bytes_accessed=0, transcendentals=0),
-            name="open",
-        )(where, field, projectors)
+        low = pack(0, HALVES)
+        below_low = turn(low, "band", 1)
+        mate, cross, opposite = call(
+            window_kernel, "cut_window", halos + [window], [where], [field], []
+        )
         opposite = turn(opposite, "band", 2)
-        below_low = turn(low, "band", 1)
         high = pack(HALVES, HALVES, [opposite])
         above_high = turn(high, "band", -1)
         below_high = turn(high, "band", 1)
@@ -443,31 +455,29 @@
             [field, opposite, low, high], [],
         )
         returned = turn(returned, "band", 2)
-        above_high, below_low = call(
-            forward_kernel, "forward", [packed_plane] * 2, [], [above_high, below_low], [],
-            [returned, above_low, below_high], {0: 0, 1: 1},
-        )
-        far_low = turn(below_low, "band", 1)
-        far_high = turn(above_high, "band", -1)
-        beside = [above_low, above_high, below_low, below_high]
-        flats = [
-            call(
-                beside_kernel, "project_beside", shaped(*flat), [slot_corner, where],
-                [field, own, returned, *beside], [],
-            )
-        ]
-        chunks = [low, high, *beside, far_low, far_high]
+        own, above_on, below_on = call(
+            forward_kernel, "project_and_forward", [shaped(*flat)] + [shaped(*low.shape)] * 2,
+            [slot_corner, where], [field, own, returned, above_high, below_low], [],
+        )
+        far_low = turn(below_on, "band", 1)
+        far_high = turn(above_on, "band", -1)
+        own = call(
+            beside_kernel, "project_beside", shaped(*flat), [slot_corner, where],
+            [field, own, above_low, below_high], [],
+        )
+        flats = [own]
+        chunks = [low, high, above_low, above_high, below_low, below_high, far_low, far_high]
     else:
         where = odd[None]
-        mate, cross = call(halo_kernel, "cut_halos", halos, [where], [field], [])
+        mate, cross = call(window_kernel, "cut_windows", halos, [where], [field], [])
         chunks = [lax.all_gather(pack(0, tiles), "band", axis=0, tiled=True)]
         flats = [
             call(whole_kernel, "project_first", shaped(*flat), [slot_corner], [field, *chunks], [])
         ]
     mate, cross = swap(mate, "dom", 0), swap(cross, "dom", 1)
     own = call(
-        table_kernel, "first_sums", shaped(2 * table_rows, LANES), [],
-        [atom_row, energy, *flats], [flat],
+        first_sums_kernel, "first_sums", shaped(2 * table_rows, LANES), [],
+        [tables[0], energy, *flats], [flat],
     )
     own = own + swap(own, "dom", 0)
     other = swap(own, "dom", 1)
@@ -480,7 +490,7 @@
             own = to_cross.at[HALO_ROWS:].add(mate[HALO_ROWS:])
             cross = swap(own, "dom", 1)
             far = swap(cross[HALO_ROWS:], "dom", 0)
-        operands = [atom_row, field, potential, mate, cross, own, far]
+        operands = [*tables, field, potential, mate, cross, own, far]
         if index == 0:
             operands.append(other)
         operands += chunks

time: 80.4 us -> 73.4 us (0.913)
  waiting for transfers between devices: 33.1 us -> 26.5 us
  starting transfers between devices: 27.5 us -> 31.6 us
  Pallas kernels: 16.3 us -> 12.3 us
    ppermute x11, starting transfers between devices: 15.6 us -> 21.8 us  [swap(): return lax.ppermute(values, axis, pairs)]
    ppermute x8, waiting for transfers between devices: 17.6 us -> 14.1 us  [turn(): lax.ppermute(values, axis, [(i, (i + step) % count) for i in range(count)])]
    ppermute x11, waiting for transfers between devices: 15.5 us -> 12.4 us  [swap(): return lax.ppermute(values, axis, pairs)]
    pallas_call x8 -> x11, Pallas kernels: 14.7 us -> 12.3 us  [call(): pl.pallas_call(body, out_shape=out_shape, in_specs=[SMEM] * len(scalars)...]
    ppermute x8, starting transfers between devices: 11.9 us -> 9.86 us  [turn(): lax.ppermute(values, axis, [(i, (i + step) % count) for i in range(count)])]
    pallas_call x1 -> x0, Pallas kernels: 1.61 us -> none  [on_device(): pl.pallas_call(opening_kernel, out_shape=halos + [window, packed_plane],...]
  transfers between devices with their start and end apart: 19 -> 19, of which waited for: 11 -> 11; matrix products, arithmetic and copies ran while one was open for 0% -> 0% of each run, Pallas kernels for 5% -> 7%
where the time goes in v2:
time: 73.4 us; the launch traced here: 72.8 us
  starting transfers between devices  31.6 us (43%)
  waiting for transfers between devices  26.5 us (36%)
  Pallas kernels  12.3 us (17%)
  local copies, waits for them, and re-layouts  2.19 us (3%)
    ppermute x11, starting transfers between devices, swap(): return lax.ppermute(values, axis, pairs)  21.8 us
    ppermute x8, waiting for transfers between devices, turn(): lax.ppermute(values, axis, [(i, (i + step) % count) for i in range(count)])  14.1 us
    ppermute x11, waiting for transfers between devices, swap(): return lax.ppermute(values, axis, pairs)  12.4 us
    pallas_call x11, Pallas kernels, call(): pl.pallas_call(body, out_shape=out_shape, in_specs=[SMEM] * len(scalars)...  12.3 us
    ppermute x8, starting transfers between devices, turn(): lax.ppermute(values, axis, [(i, (i + step) % count) for i in range(count)])  9.86 us
    unnamed x14, local copies, waits for them, and re-layouts  1.87 us
  transfers between devices with their start and end apart: 19, of which 11 were waited for; matrix products, arithmetic and copies ran while one was open for 0% of the time, Pallas kernels for 7%

profile of v2, /device:TPU:5, one launch (start us, length us, event | category | flops | bytes accessed | tf_op | source)
XLA Modules:
  0.0 72.8 jit_solution(8661333337607727652)
XLA Ops:
  1.5 2.4 %collective-permute-start.2 = (f32[6,16,128]{2,1,0:T(8,128)S(1)}, f32[6,16,128]{2,1,0:T(8,128)S(1)}, u32[]{:S(2)}, u32[]{:S(2)}) collective-permute-start(f32[6,16,128]{2,1,0:T(8,128)S(1)} %get-tuple-element.52), channel_id=1, source_target_pairs={{0,2},{1,3},{2,0},{3,1},{4,6},{5,7},{6,4},{7,5},{8,10},{9,11},{10,... | collective-permute-start | bytes 147464 | tf_op jit(solution)/shard_map/ppermute | solution.py:375
  3.8 1.0 %copy-done.1 = f32[32,8,512]{2,1,0:T(8,128)S(1)} copy-done((f32[32,8,512]{2,1,0:T(8,128)S(1)}, f32[32,8,512]{2,1,0:T(8,128)}, u32[]{:S(2)}) %copy-start.1) | copy-done | bytes 524312
  4.9 0.9 %pack_projectors.2.refs_4_.refs_12_.refs_11_ = f32[2,4,8,8,128]{4,3,2,1,0:T(8,128)S(1)} custom-call(f32[32,8,512]{2,1,0:T(8,128)S(1)} %copy-done.1), custom_call_target="tpu_custom_call" | custom-call | tf_op jit(solution)/shard_map/pack_projectors/pallas_call | solution.py:399
  5.8 1.3 %collective-permute-start.5 = (f32[2,4,8,8,128]{4,3,2,1,0:T(8,128)S(1)}, f32[2,4,8,8,128]{4,3,2,1,0:T(8,128)S(1)}, u32[]{:S(2)}, u32[]{:S(2)}) collective-permute-start(f32[2,4,8,8,128]{4,3,2,1,0:T(8,128)S(1)} %pack_projectors.2.refs_4_.refs_12_.refs_11_), channel_id=1, source_target_pairs={{0,1},{1,2},{2,3},{3,0},{4,5},{5,6},{6,7},{7,4},{8,9},{9,10},{10,1... | collective-permute-start | bytes 786440 | tf_op jit(solution)/shard_map/ppermute | solution.py:375
  7.1 0.9 %pack_projectors.3.refs_5_.refs_13_.refs_12_ = f32[2,4,8,8,128]{4,3,2,1,0:T(8,128)S(1)} custom-call(f32[32,8,512]{2,1,0:T(8,128)S(1)} %copy-done.2, f32[6,16,128]{2,1,0:T(8,128)S(1)} %collective-permute-done.2.refs_1_.refs_3_), custom_call_target="tpu_custom_call" | custom-call | tf_op jit(solution)/shard_map/pack_projectors/pallas_call | solution.py:399
  8.1 2.0 %collective-permute-start.4 = (f32[2,4,8,8,128]{4,3,2,1,0:T(8,128)S(1)}, f32[2,4,8,8,128]{4,3,2,1,0:T(8,128)S(1)}, u32[]{:S(2)}, u32[]{:S(2)}) collective-permute-start(f32[2,4,8,8,128]{4,3,2,1,0:T(8,128)S(1)} %pack_projectors.3.refs_5_.refs_13_.refs_12_), channel_id=1, source_target_pairs={{0,3},{1,0},{2,1},{3,2},{4,7},{5,4},{6,5},{7,6},{8,11},{9,8},{10,9... | collective-permute-start | bytes 786440 | tf_op jit(solution)/shard_map/ppermute | solution.py:375
  10.1 1.0 %project_own.1 = (f32[4,8,128]{2,1,0:T(8,128)S(1)}, f32[4,8,128]{2,1,0:T(8,128)S(1)}) custom-call(s32[3,32]{1,0:T(4,128)S(1)} %copy-done.4, s32[9]{0:T(128)S(1)} %stack.39.refs_0_.refs_1_, f32[12,16,128]{2,1,0:T(8,128)S(1)} %bitcast.13, f32[6,16,128]{2,1,0:T(8,128)S(1)} %collective-permute-done.2.refs_1_.refs_3_, ...), custom_call_target="tpu_custom_call" | custom-call | tf_op jit(solution)/shard_map/project_own/pallas_call | solution.py:399
  11.8 2.1 %collective-permute-start = (f32[96,128]{1,0:T(8,128)S(1)}, f32[96,128]{1,0:T(8,128)S(1)}, u32[]{:S(2)}, u32[]{:S(2)}) collective-permute-start(f32[96,128]{1,0:T(8,128)S(1)} %get-tuple-element.50), channel_id=1, source_target_pairs={{0,4},{4,0},{8,12},{12,8},{16,20},{20,16},{24,28},{28,24},{1,5},{5... | collective-permute-start | bytes 147464 | tf_op jit(solution)/shard_map/ppermute | solution.py:370
  13.9 13.9 %collective-permute-done.3.refs_4_ = f32[4,8,128]{2,1,0:T(8,128)S(1)} collective-permute-done((f32[4,8,128]{2,1,0:T(8,128)S(1)}, f32[4,8,128]{2,1,0:T(8,128)S(1)}, u32[]{:S(2)}, u32[]{:S(2)}) %collective-permute-start.3) | collective-permute-done | bytes 16416 | tf_op jit(solution)/shard_map/ppermute | solution.py:375
  27.8 0.8 %project_and_forward.1 = (f32[4,8,128]{2,1,0:T(8,128)S(1)}, f32[2,4,8,8,128]{4,3,2,1,0:T(8,128)S(1)}, f32[2,4,8,8,128]{4,3,2,1,0:T(8,128)S(1)}) custom-call(s32[3,32]{1,0:T(4,128)S(1)} %copy-done.4, s32[9]{0:T(128)S(1)} %stack.39.refs_0_.refs_1_, f32[12,16,128]{2,1,0:T(8,128)S(1)} %bitcast.14, f32[4,8,128]{2,1,0:T(8,128)S(1)} %get-tuple-element.53.refs_3_, ...), custom_call_target="tpu_custom_call" | custom-call | tf_op jit(solution)/shard_map/project_and_forward/pallas_call | solution.py:399
  28.8 3.3 %collective-permute-start.12 = (f32[2,4,8,8,128]{4,3,2,1,0:T(8,128)S(1)}, f32[2,4,8,8,128]{4,3,2,1,0:T(8,128)S(1)}, u32[]{:S(2)}, u32[]{:S(2)}) collective-permute-start(f32[2,4,8,8,128]{4,3,2,1,0:T(8,128)S(1)} %get-tuple-element.57), channel_id=1, source_target_pairs={{0,3},{1,0},{2,1},{3,2},{4,7},{5,4},{6,5},{7,6},{8,11},{9,8},{10,9... | collective-permute-start | bytes 786440 | tf_op jit(solution)/shard_map/ppermute | solution.py:375
  32.2 4.3 %collective-permute-start.1 = (f32[96,128]{1,0:T(8,128)S(1)}, f32[96,128]{1,0:T(8,128)S(1)}, u32[]{:S(2)}, u32[]{:S(2)}) collective-permute-start(f32[96,128]{1,0:T(8,128)S(1)} %get-tuple-element.51), channel_id=1, source_target_pairs={{4,8},{8,4},{12,16},{16,12},{20,24},{24,20},{5,9},{9,5},{13,17},{1... | collective-permute-start | bytes 147464 | tf_op jit(solution)/shard_map/ppermute | solution.py:370
  37.1 0.8 %project_beside.1.refs_2_ = f32[4,8,128]{2,1,0:T(8,128)S(1)} custom-call(s32[3,32]{1,0:T(4,128)S(1)} %copy-done.4, s32[9]{0:T(128)S(1)} %stack.39.refs_0_.refs_1_, f32[12,16,128]{2,1,0:T(8,128)S(1)} %bitcast.15, f32[4,8,128]{2,1,0:T(8,128)S(1)} %get-tuple-element.55.refs_3_, f32[2,4,8,8,128]{4,3,2,1,0:T(8,128)S(1)} %collective-permute-done.6.refs_4_.refs_14_.refs_13_, ...), custom_call_target="tpu_custom_call" | custom-call | tf_op jit(solution)/shard_map/project_beside/pallas_call | solution.py:399
  38.1 2.4 %collective-permute-start.8 = (f32[16,128]{1,0:T(8,128)S(1)}, f32[16,128]{1,0:T(8,128)S(1)}, u32[]{:S(2)}, u32[]{:S(2)}) collective-permute-start(f32[16,128]{1,0:T(8,128)S(1)} %first_sums.1), channel_id=1, source_target_pairs={{0,4},{4,0},{8,12},{12,8},{16,20},{20,16},{24,28},{28,24},{1,5},{5... | collective-permute-start | bytes 24584 | tf_op jit(solution)/shard_map/ppermute | solution.py:370
  40.5 0.8 %collective-permute-done.8 = f32[16,128]{1,0:T(8,128)S(1)} collective-permute-done((f32[16,128]{1,0:T(8,128)S(1)}, f32[16,128]{1,0:T(8,128)S(1)}, u32[]{:S(2)}, u32[]{:S(2)}) %collective-permute-start.8) | collective-permute-done | bytes 8224 | tf_op jit(solution)/shard_map/ppermute | solution.py:370
  41.3 3.3 %collective-permute-start.9 = (f32[16,128]{1,0:T(8,128)S(1)}, f32[16,128]{1,0:T(8,128)S(1)}, u32[]{:S(2)}, u32[]{:S(2)}) collective-permute-start(f32[16,128]{1,0:T(8,128)S(1)} %add.67.refs_9_), channel_id=1, source_target_pairs={{4,8},{8,4},{12,16},{16,12},{20,24},{24,20},{5,9},{9,5},{13,17},{1... | collective-permute-start | bytes 24584 | tf_op jit(solution)/shard_map/ppermute | solution.py:370
  44.6 1.9 %collective-permute-done.9.refs_11_ = f32[16,128]{1,0:T(8,128)S(1)} collective-permute-done((f32[16,128]{1,0:T(8,128)S(1)}, f32[16,128]{1,0:T(8,128)S(1)}, u32[]{:S(2)}, u32[]{:S(2)}) %collective-permute-start.9) | collective-permute-done | bytes 8224 | tf_op jit(solution)/shard_map/ppermute | solution.py:370
  46.6 0.9 %collective-permute-start.10 = (f32[16,128]{1,0:T(8,128)S(1)}, f32[16,128]{1,0:T(8,128)S(1)}, u32[]{:S(2)}, u32[]{:S(2)}) collective-permute-start(f32[16,128]{1,0:T(8,128)S(1)} %collective-permute-done.9.refs_11_), channel_id=1, source_target_pairs={{0,4},{4,0},{8,12},{12,8},{16,20},{20,16},{24,28},{28,24},{1,5},{5... | collective-permute-start | bytes 24584 | tf_op jit(solution)/shard_map/ppermute | solution.py:370
  47.5 0.8 %collective-permute-done.10.refs_10_ = f32[16,128]{1,0:T(8,128)S(1)} collective-permute-done((f32[16,128]{1,0:T(8,128)S(1)}, f32[16,128]{1,0:T(8,128)S(1)}, u32[]{:S(2)}, u32[]{:S(2)}) %collective-permute-start.10) | collective-permute-done | bytes 8224 | tf_op jit(solution)/shard_map/ppermute | solution.py:370
  48.3 2.4 %filter_step_1.1 = (f32[12,16,128]{2,1,0:T(8,128)S(1)}, f32[104,128]{1,0:T(8,128)S(1)}, f32[104,128]{1,0:T(8,128)S(1)}, f32[8,128]{1,0:T(8,128)S(1)}) custom-call(s32[3,32]{1,0:T(4,128)S(1)} %copy-done.4, s32[9]{0:T(128)S(1)} %stack.39.refs_0_.refs_1_, bf16[128,512]{1,0:T(8,128)(2,1)S(1)} %get-tuple-element.47.refs_0_.refs_2_, ...), custom_call_target="tpu_custom_call" | custom-call | tf_op jit(solution)/shard_map/filter_step_1/pallas_call | solution.py:399
  51.1 0.9 %collective-permute-done.13.refs_7_ = f32[104,128]{1,0:T(8,128)S(1)} collective-permute-done((f32[104,128]{1,0:T(8,128)S(1)}, f32[104,128]{1,0:T(8,128)S(1)}, u32[]{:S(2)}, u32[]{:S(2)}) %collective-permute-start.13) | collective-permute-done | bytes 53280 | tf_op jit(solution)/shard_map/ppermute | solution.py:370
  52.0 3.3 %collective-permute-start.14 = (f32[104,128]{1,0:T(8,128)S(1)}, f32[104,128]{1,0:T(8,128)S(1)}, u32[]{:S(2)}, u32[]{:S(2)}) collective-permute-start(f32[104,128]{1,0:T(8,128)S(1)} %fusion.1.refs_9_), channel_id=1, source_target_pairs={{4,8},{8,4},{12,16},{16,12},{20,24},{24,20},{5,9},{9,5},{13,17},{1... | collective-permute-start | bytes 159752 | tf_op jit(solution)/shard_map/ppermute | solution.py:370
  55.3 2.4 %collective-permute-done.14.refs_8_ = f32[104,128]{1,0:T(8,128)S(1)} collective-permute-done((f32[104,128]{1,0:T(8,128)S(1)}, f32[104,128]{1,0:T(8,128)S(1)}, u32[]{:S(2)}, u32[]{:S(2)}) %collective-permute-start.14) | collective-permute-done | bytes 53280 | tf_op jit(solution)/shard_map/ppermute | solution.py:370
  57.7 1.0 %collective-permute-start.15 = (f32[8,128]{1,0:T(8,128)S(1)}, f32[8,128]{1,0:T(8,128)S(1)}, u32[]{:S(2)}, u32[]{:S(2)}) collective-permute-start(f32[8,128]{1,0:T(8,128)S(1)} %slice.57), channel_id=1, source_target_pairs={{0,4},{4,0},{8,12},{12,8},{16,20},{20,16},{24,28},{28,24},{1,5},{5... | collective-permute-start | bytes 12296 | tf_op jit(solution)/shard_map/ppermute | solution.py:370
  58.7 0.8 %collective-permute-done.15.refs_10_ = f32[8,128]{1,0:T(8,128)S(1)} collective-permute-done((f32[8,128]{1,0:T(8,128)S(1)}, f32[8,128]{1,0:T(8,128)S(1)}, u32[]{:S(2)}, u32[]{:S(2)}) %collective-permute-start.15) | collective-permute-done | bytes 4128 | tf_op jit(solution)/shard_map/ppermute | solution.py:370
  59.5 2.3 %filter_step_2.1 = (f32[12,16,128]{2,1,0:T(8,128)S(1)}, f32[104,128]{1,0:T(8,128)S(1)}, f32[104,128]{1,0:T(8,128)S(1)}) custom-call(s32[3,32]{1,0:T(4,128)S(1)} %copy-done.4, s32[9]{0:T(128)S(1)} %stack.39.refs_0_.refs_1_, bf16[128,512]{1,0:T(8,128)(2,1)S(1)} %get-tuple-element.47.refs_0_.refs_2_, bf16[384,128]{1,0:T(8,128)(2,1)S(1)} %get-tuple-element.48.refs_3_, ...), custom_call_target="tpu_custom_call" | custom-call | tf_op jit(solution)/shard_map/filter_step_2/pallas_call | solution.py:399
  62.2 0.9 %collective-permute-done.16.refs_7_ = f32[104,128]{1,0:T(8,128)S(1)} collective-permute-done((f32[104,128]{1,0:T(8,128)S(1)}, f32[104,128]{1,0:T(8,128)S(1)}, u32[]{:S(2)}, u32[]{:S(2)}) %collective-permute-start.16) | collective-permute-done | bytes 53280 | tf_op jit(solution)/shard_map/ppermute | solution.py:370
  63.1 2.7 %collective-permute-start.17 = (f32[104,128]{1,0:T(8,128)S(1)}, f32[104,128]{1,0:T(8,128)S(1)}, u32[]{:S(2)}, u32[]{:S(2)}) collective-permute-start(f32[104,128]{1,0:T(8,128)S(1)} %fusion.refs_9_), channel_id=1, source_target_pairs={{4,8},{8,4},{12,16},{16,12},{20,24},{24,20},{5,9},{9,5},{13,17},{1... | collective-permute-start | bytes 159752 | tf_op jit(solution)/shard_map/ppermute | solution.py:370
  65.8 3.0 %collective-permute-done.17.refs_8_ = f32[104,128]{1,0:T(8,128)S(1)} collective-permute-done((f32[104,128]{1,0:T(8,128)S(1)}, f32[104,128]{1,0:T(8,128)S(1)}, u32[]{:S(2)}, u32[]{:S(2)}) %collective-permute-start.17) | collective-permute-done | bytes 53280 | tf_op jit(solution)/shard_map/ppermute | solution.py:370
  68.8 0.9 %collective-permute-start.18 = (f32[8,128]{1,0:T(8,128)S(1)}, f32[8,128]{1,0:T(8,128)S(1)}, u32[]{:S(2)}, u32[]{:S(2)}) collective-permute-start(f32[8,128]{1,0:T(8,128)S(1)} %slice.59), channel_id=1, source_target_pairs={{0,4},{4,0},{8,12},{12,8},{16,20},{20,16},{24,28},{28,24},{1,5},{5... | collective-permute-start | bytes 12296 | tf_op jit(solution)/shard_map/ppermute | solution.py:370
  69.8 0.8 %collective-permute-done.18.refs_10_ = f32[8,128]{1,0:T(8,128)S(1)} collective-permute-done((f32[8,128]{1,0:T(8,128)S(1)}, f32[8,128]{1,0:T(8,128)S(1)}, u32[]{:S(2)}, u32[]{:S(2)}) %collective-permute-start.18) | collective-permute-done | bytes 4128 | tf_op jit(solution)/shard_map/ppermute | solution.py:370
  70.6 2.2 %filter_step_3.1 = f32[12,16,128]{2,1,0:T(8,128)} custom-call(s32[3,32]{1,0:T(4,128)S(1)} %copy-done.4, s32[9]{0:T(128)S(1)} %stack.39.refs_0_.refs_1_, bf16[128,512]{1,0:T(8,128)(2,1)S(1)} %get-tuple-element.47.refs_0_.refs_2_, bf16[384,128]{1,0:T(8,128)(2,1)S(1)} %get-tuple-element.48.refs_3_, bf16[192,576]{1,0:T(8,128)(2,1)S(1)} %get-tuple-element.49.refs_4_, ...), custom_call_target="tpu_custom_call" | custom-call | tf_op jit(solution)/shard_map/filter_step_3/pallas_call | solution.py:399
  (43 shorter events, 3.8 us)
Async XLA Ops:
  0.0 0.9 %copy-start = (f32[1,12,16,128]{3,2,1,0:T(8,128)S(1)}, f32[1,12,16,128]{3,2,1,0:T(8,128)}, u32[]{:S(2)}) copy-start(f32[1,12,16,128]{3,2,1,0:T(8,128)} %param.10) | copy-start | bytes 294916
  1.5 5.7 %collective-permute-start.2 = (f32[6,16,128]{2,1,0:T(8,128)S(1)}, f32[6,16,128]{2,1,0:T(8,128)S(1)}, u32[]{:S(2)}, u32[]{:S(2)}) collective-permute-start(f32[6,16,128]{2,1,0:T(8,128)S(1)} %get-tuple-element.52), channel_id=1, source_target_pairs={{0,2},{1,3},{2,0},{3,1},{4,6},{5,7},{6,4},{7,5},{8,10},{9,11},{10,... | collective-permute-start | bytes 147464 | tf_op jit(solution)/shard_map/ppermute | solution.py:375
  3.8 1.0 %copy-start.1 = (f32[32,8,512]{2,1,0:T(8,128)S(1)}, f32[32,8,512]{2,1,0:T(8,128)}, u32[]{:S(2)}) copy-start(f32[32,8,512]{2,1,0:T(8,128)} %refs_0_.9) | copy-start | bytes 1572868
  4.9 2.3 %copy-start.2 = (f32[32,8,512]{2,1,0:T(8,128)S(1)}, f32[32,8,512]{2,1,0:T(8,128)}, u32[]{:S(2)}) copy-start(f32[32,8,512]{2,1,0:T(8,128)} %refs_0_.9) | copy-start | bytes 1572868
  5.8 4.4 %copy-start.4 = (s32[3,32]{1,0:T(4,128)S(1)}, s32[3,32]{1,0:T(4,128)}, u32[]{:S(2)}) copy-start(s32[3,32]{1,0:T(4,128)} %refs_0_.15) | copy-start | bytes 1156
  5.8 22.0 %collective-permute-start.5 = (f32[2,4,8,8,128]{4,3,2,1,0:T(8,128)S(1)}, f32[2,4,8,8,128]{4,3,2,1,0:T(8,128)S(1)}, u32[]{:S(2)}, u32[]{:S(2)}) collective-permute-start(f32[2,4,8,8,128]{4,3,2,1,0:T(8,128)S(1)} %pack_projectors.2.refs_4_.refs_12_.refs_11_), channel_id=1, source_target_pairs={{0,1},{1,2},{2,3},{3,0},{4,5},{5,6},{6,7},{7,4},{8,9},{9,10},{10,1... | collective-permute-start | bytes 786440 | tf_op jit(solution)/shard_map/ppermute | solution.py:375
  8.1 19.8 %collective-permute-start.4 = (f32[2,4,8,8,128]{4,3,2,1,0:T(8,128)S(1)}, f32[2,4,8,8,128]{4,3,2,1,0:T(8,128)S(1)}, u32[]{:S(2)}, u32[]{:S(2)}) collective-permute-start(f32[2,4,8,8,128]{4,3,2,1,0:T(8,128)S(1)} %pack_projectors.3.refs_5_.refs_13_.refs_12_), channel_id=1, source_target_pairs={{0,3},{1,0},{2,1},{3,2},{4,7},{5,4},{6,5},{7,6},{8,11},{9,8},{10,9... | collective-permute-start | bytes 786440 | tf_op jit(solution)/shard_map/ppermute | solution.py:375
  10.1 22.1 %collective-permute-start.6 = (f32[2,4,8,8,128]{4,3,2,1,0:T(8,128)S(1)}, f32[2,4,8,8,128]{4,3,2,1,0:T(8,128)S(1)}, u32[]{:S(2)}, u32[]{:S(2)}) collective-permute-start(f32[2,4,8,8,128]{4,3,2,1,0:T(8,128)S(1)} %pack_projectors.2.refs_4_.refs_12_.refs_11_), channel_id=1, source_target_pairs={{0,3},{1,0},{2,1},{3,2},{4,7},{5,4},{6,5},{7,6},{8,11},{9,8},{10,9... | collective-permute-start | bytes 786440 | tf_op jit(solution)/shard_map/ppermute | solution.py:375
  11.1 16.7 %collective-permute-start.3 = (f32[4,8,128]{2,1,0:T(8,128)S(1)}, f32[4,8,128]{2,1,0:T(8,128)S(1)}, u32[]{:S(2)}, u32[]{:S(2)}) collective-permute-start(f32[4,8,128]{2,1,0:T(8,128)S(1)} %get-tuple-element.54), channel_id=1, source_target_pairs={{0,2},{1,3},{2,0},{3,1},{4,6},{5,7},{6,4},{7,5},{8,10},{9,11},{10,... | collective-permute-start | bytes 49160 | tf_op jit(solution)/shard_map/ppermute | solution.py:375
  11.8 35.7 %collective-permute-start = (f32[96,128]{1,0:T(8,128)S(1)}, f32[96,128]{1,0:T(8,128)S(1)}, u32[]{:S(2)}, u32[]{:S(2)}) collective-permute-start(f32[96,128]{1,0:T(8,128)S(1)} %get-tuple-element.50), channel_id=1, source_target_pairs={{0,4},{4,0},{8,12},{12,8},{16,20},{20,16},{24,28},{28,24},{1,5},{5... | collective-permute-start | bytes 147464 | tf_op jit(solution)/shard_map/ppermute | solution.py:370
  27.8 9.3 %collective-permute-start.7 = (f32[2,4,8,8,128]{4,3,2,1,0:T(8,128)S(1)}, f32[2,4,8,8,128]{4,3,2,1,0:T(8,128)S(1)}, u32[]{:S(2)}, u32[]{:S(2)}) collective-permute-start(f32[2,4,8,8,128]{4,3,2,1,0:T(8,128)S(1)} %pack_projectors.3.refs_5_.refs_13_.refs_12_), channel_id=1, source_target_pairs={{0,1},{1,2},{2,3},{3,0},{4,5},{5,6},{6,7},{7,4},{8,9},{9,10},{10,1... | collective-permute-start | bytes 786440 | tf_op jit(solution)/shard_map/ppermute | solution.py:375
  28.7 3.4 %copy-start.5 = (f32[16,8]{0,1:T(8,128)S(1)}, f32[16,8]{0,1:T(8,128)}, u32[]{:S(2)}) copy-start(f32[16,8]{0,1:T(8,128)} %param.13) | copy-start | bytes 1540
  28.7 19.7 %collective-permute-start.11 = (f32[2,4,8,8,128]{4,3,2,1,0:T(8,128)S(1)}, f32[2,4,8,8,128]{4,3,2,1,0:T(8,128)S(1)}, u32[]{:S(2)}, u32[]{:S(2)}) collective-permute-start(f32[2,4,8,8,128]{4,3,2,1,0:T(8,128)S(1)} %get-tuple-element.56), channel_id=1, source_target_pairs={{0,1},{1,2},{2,3},{3,0},{4,5},{5,6},{6,7},{7,4},{8,9},{9,10},{10,1... | collective-permute-start | bytes 786440 | tf_op jit(solution)/shard_map/ppermute | solution.py:375
  28.8 19.6 %collective-permute-start.12 = (f32[2,4,8,8,128]{4,3,2,1,0:T(8,128)S(1)}, f32[2,4,8,8,128]{4,3,2,1,0:T(8,128)S(1)}, u32[]{:S(2)}, u32[]{:S(2)}) collective-permute-start(f32[2,4,8,8,128]{4,3,2,1,0:T(8,128)S(1)} %get-tuple-element.57), channel_id=1, source_target_pairs={{0,3},{1,0},{2,1},{3,2},{4,7},{5,4},{6,5},{7,6},{8,11},{9,8},{10,9... | collective-permute-start | bytes 786440 | tf_op jit(solution)/shard_map/ppermute | solution.py:375
  32.2 4.4 %copy-start.6 = (s32[32]{0:T(128)S(1)}, s32[32]{0:T(128)}, u32[]{:S(2)}) copy-start(s32[32]{0:T(128)} %param.14) | copy-start | bytes 388
  32.2 15.4 %collective-permute-start.1 = (f32[96,128]{1,0:T(8,128)S(1)}, f32[96,128]{1,0:T(8,128)S(1)}, u32[]{:S(2)}, u32[]{:S(2)}) collective-permute-start(f32[96,128]{1,0:T(8,128)S(1)} %get-tuple-element.51), channel_id=1, source_target_pairs={{4,8},{8,4},{12,16},{16,12},{20,24},{24,20},{5,9},{9,5},{13,17},{1... | collective-permute-start | bytes 147464 | tf_op jit(solution)/shard_map/ppermute | solution.py:370
  37.9 10.4 %copy-start.3 = (f32[12,16,128]{2,1,0:T(8,128)S(1)}, f32[12,16,128]{2,1,0:T(8,128)}, u32[]{:S(2)}) copy-start(f32[12,16,128]{2,1,0:T(8,128)} %refs_6_.5) | copy-start | bytes 294916
  38.1 3.2 %collective-permute-start.8 = (f32[16,128]{1,0:T(8,128)S(1)}, f32[16,128]{1,0:T(8,128)S(1)}, u32[]{:S(2)}, u32[]{:S(2)}) collective-permute-start(f32[16,128]{1,0:T(8,128)S(1)} %first_sums.1), channel_id=1, source_target_pairs={{0,4},{4,0},{8,12},{12,8},{16,20},{20,16},{24,28},{28,24},{1,5},{5... | collective-permute-start | bytes 24584 | tf_op jit(solution)/shard_map/ppermute | solution.py:370
  41.3 5.3 %collective-permute-start.9 = (f32[16,128]{1,0:T(8,128)S(1)}, f32[16,128]{1,0:T(8,128)S(1)}, u32[]{:S(2)}, u32[]{:S(2)}) collective-permute-start(f32[16,128]{1,0:T(8,128)S(1)} %add.67.refs_9_), channel_id=1, source_target_pairs={{4,8},{8,4},{12,16},{16,12},{20,24},{24,20},{5,9},{9,5},{13,17},{1... | collective-permute-start | bytes 24584 | tf_op jit(solution)/shard_map/ppermute | solution.py:370
  46.6 1.8 %collective-permute-start.10 = (f32[16,128]{1,0:T(8,128)S(1)}, f32[16,128]{1,0:T(8,128)S(1)}, u32[]{:S(2)}, u32[]{:S(2)}) collective-permute-start(f32[16,128]{1,0:T(8,128)S(1)} %collective-permute-done.9.refs_11_), channel_id=1, source_target_pairs={{0,4},{4,0},{8,12},{12,8},{16,20},{20,16},{24,28},{28,24},{1,5},{5... | collective-permute-start | bytes 24584 | tf_op jit(solution)/shard_map/ppermute | solution.py:370
  50.7 1.3 %collective-permute-start.13 = (f32[104,128]{1,0:T(8,128)S(1)}, f32[104,128]{1,0:T(8,128)S(1)}, u32[]{:S(2)}, u32[]{:S(2)}) collective-permute-start(f32[104,128]{1,0:T(8,128)S(1)} %get-tuple-element.59), channel_id=1, source_target_pairs={{0,4},{4,0},{8,12},{12,8},{16,20},{20,16},{24,28},{28,24},{1,5},{5... | collective-permute-start | bytes 159752 | tf_op jit(solution)/shard_map/ppermute | solution.py:370
  52.0 5.7 %collective-permute-start.14 = (f32[104,128]{1,0:T(8,128)S(1)}, f32[104,128]{1,0:T(8,128)S(1)}, u32[]{:S(2)}, u32[]{:S(2)}) collective-permute-start(f32[104,128]{1,0:T(8,128)S(1)} %fusion.1.refs_9_), channel_id=1, source_target_pairs={{4,8},{8,4},{12,16},{16,12},{20,24},{24,20},{5,9},{9,5},{13,17},{1... | collective-permute-start | bytes 159752 | tf_op jit(solution)/shard_map/ppermute | solution.py:370
  57.7 1.8 %collective-permute-start.15 = (f32[8,128]{1,0:T(8,128)S(1)}, f32[8,128]{1,0:T(8,128)S(1)}, u32[]{:S(2)}, u32[]{:S(2)}) collective-permute-start(f32[8,128]{1,0:T(8,128)S(1)} %slice.57), channel_id=1, source_target_pairs={{0,4},{4,0},{8,12},{12,8},{16,20},{20,16},{24,28},{28,24},{1,5},{5... | collective-permute-start | bytes 12296 | tf_op jit(solution)/shard_map/ppermute | solution.py:370
  61.9 1.2 %collective-permute-start.16 = (f32[104,128]{1,0:T(8,128)S(1)}, f32[104,128]{1,0:T(8,128)S(1)}, u32[]{:S(2)}, u32[]{:S(2)}) collective-permute-start(f32[104,128]{1,0:T(8,128)S(1)} %get-tuple-element.63), channel_id=1, source_target_pairs={{0,4},{4,0},{8,12},{12,8},{16,20},{20,16},{24,28},{28,24},{1,5},{5... | collective-permute-start | bytes 159752 | tf_op jit(solution)/shard_map/ppermute | solution.py:370
  63.1 5.7 %collective-permute-start.17 = (f32[104,128]{1,0:T(8,128)S(1)}, f32[104,128]{1,0:T(8,128)S(1)}, u32[]{:S(2)}, u32[]{:S(2)}) collective-permute-start(f32[104,128]{1,0:T(8,128)S(1)} %fusion.refs_9_), channel_id=1, source_target_pairs={{4,8},{8,4},{12,16},{16,12},{20,24},{24,20},{5,9},{9,5},{13,17},{1... | collective-permute-start | bytes 159752 | tf_op jit(solution)/shard_map/ppermute | solution.py:370
  68.8 1.8 %collective-permute-start.18 = (f32[8,128]{1,0:T(8,128)S(1)}, f32[8,128]{1,0:T(8,128)S(1)}, u32[]{:S(2)}, u32[]{:S(2)}) collective-permute-start(f32[8,128]{1,0:T(8,128)S(1)} %slice.59), channel_id=1, source_target_pairs={{0,4},{4,0},{8,12},{12,8},{16,20},{20,16},{24,28},{28,24},{1,5},{5... | collective-permute-start | bytes 12296 | tf_op jit(solution)/shard_map/ppermute | solution.py:370

commit v3 on v2

--- a/solution.py
+++ b/solution.py
@@ -70,8 +70,8 @@
     return result
 
 
-def pack_kernel(first_tile, proj_ref, out_ref):
-    tiles, groups = out_ref.shape[:2]
+def pack_plane(first_tile, tiles, proj_ref, out_ref):
+    groups = proj_ref.shape[0] // ROWS
     row = iota((ROWS, LANES), 0)
     block = iota((ROWS, LANES), 1) // SZ
     apart = (row - block + ROWS) % ROWS
@@ -92,7 +92,8 @@
             mixed = choose(apart_is, [by_lane[(d + e) % ROWS] for d in range(ROWS)])
             by_row.append(pltpu.roll(mixed, e, 0) if e else mixed)
         for p in range(ROWS):
-            out_ref[tile, group, p] = choose(row_is, [by_row[(j - p) % ROWS] for j in range(ROWS)])
+            at = pl.ds(pl.multiple_of((index * ROWS + p) * ROWS, ROWS), ROWS)
+            out_ref[at, :] = choose(row_is, [by_row[(j - p) % ROWS] for j in range(ROWS)])
         return carry
 
     lax.fori_loop(0, tiles * groups, one, 0)
@@ -132,6 +133,11 @@
     return products[0]
 
 
+def values_of(ref, base, groups, half, group, p):
+    at = base + ((half * groups + group) * ROWS + p) * ROWS
+    return ref[at : at + ROWS, :]
+
+
 def project(field, chunks, corner_ref, flat_ref, start_ref=None):
     groups = flat_ref.shape[0]
     lane_block = iota((ROWS, LANES), 1) // SZ
@@ -142,14 +148,14 @@
             lax.rem(LANES + u * SZ - corner_ref[2, group * ROWS + u], LANES) for u in range(ROWS)
         ]
         sums = [[] for _ in range(ROWS)]
-        for plane, ref in chunks:
+        for plane, ref, base in chunks:
             for half in range(HALVES):
                 box = None
                 for u in range(ROWS):
                     turned = pltpu.roll(field(corners[u] + plane, half), shifts[u], 1)
                     box = turned if u == 0 else jnp.where(lane_block == u, turned, box)
                 for p in range(ROWS):
-                    sums[p].append(ref[half, group, p] * box)
+                    sums[p].append(values_of(ref, base, groups, half, group, p) * box)
         flat = fold_rows([total_of(products) for products in sums])
         flat_ref[group] = flat if start_ref is None else flat + start_ref[group]
         return carry
@@ -169,7 +175,7 @@
 
 
 def deposit(scaled, chunks, corner_ref, member_ref, flat_ref, box_ref, parts_ref):
-    groups = chunks[0][1].shape[1]
+    groups = flat_ref.shape[0]
     copies = parts_ref.shape[0]
     lane_block = iota((ROWS, LANES), 1) // SZ
     flat = sum_thirds(
@@ -183,10 +189,13 @@
         factors = [
             jnp.broadcast_to(flat_ref[group, pl.ds(p, 1), :], (ROWS, LANES)) for p in range(ROWS)
         ]
-        for plane, ref in chunks:
+        for plane, ref, base in chunks:
             for half in range(HALVES):
                 box_ref[plane * HALVES + half] = total_of(
-                    [ref[half, group, p] * factors[p] for p in range(ROWS)]
+                    [
+                        values_of(ref, base, groups, half, group, p) * factors[p]
+                        for p in range(ROWS)
+                    ]
                 )
         for u in range(ROWS):
             slot = group * ROWS + u
@@ -258,50 +267,72 @@
 
 
 def all_planes(ref):
-    return [(x, ref.at[pl.ds(x * HALVES, HALVES)]) for x in range(SX)]
+    rows = ref.shape[0] // SX
+    return [(x, ref, x * rows) for x in range(SX)]
+
+
+def some_planes(where_ref, first, refs):
+    return [(where_ref[FIRST_CHUNK + first + i], ref, 0) for i, ref in enumerate(refs)]
 
 
 def field_reader(ref):
     return lambda x, half: ref[x, pl.ds(half * ROWS, ROWS), :]
 
 
-def window_kernel(where_ref, field_ref, mate_ref, cross_ref, *window_refs):
+def halo_kernel(where_ref, field_ref, mate_ref, cross_ref):
     write_halos(field_ref, where_ref[0], mate_ref, cross_ref)
-    for ref in window_refs:
-        ref[...] = field_ref[pl.ds(where_ref[FIRST_CHUNK + 6], REACH)]
-
-
-def own_planes_kernel(corner_ref, where_ref, field_ref, window_ref, low_ref, high_ref,
-                      own_ref, opposite_ref):
-    chunks = [low_ref, high_ref]
-    here = [(where_ref[FIRST_CHUNK + h], ref) for h, ref in enumerate(chunks)]
-    project(field_reader(field_ref), here, corner_ref, own_ref)
-    project(field_reader(window_ref), list(enumerate(chunks)), corner_ref, opposite_ref)
-
-
-def forward_kernel(corner_ref, where_ref, field_ref, own_ref, returned_ref, above_ref, below_ref,
-                   flat_ref, above_out_ref, below_out_ref):
-    above_out_ref[...] = above_ref[...]
-    below_out_ref[...] = below_ref[...]
-    flat_ref[...] = own_ref[...] + returned_ref[...]
-    chunks = [(where_ref[FIRST_CHUNK + 3], above_ref), (where_ref[FIRST_CHUNK + 4], below_ref)]
-    project(field_reader(field_ref), chunks, corner_ref, flat_ref, flat_ref)
-
-
-def beside_kernel(corner_ref, where_ref, field_ref, start_ref, above_ref, below_ref, out_ref):
-    chunks = [(where_ref[FIRST_CHUNK + 2], above_ref), (where_ref[FIRST_CHUNK + 5], below_ref)]
-    project(field_reader(field_ref), chunks, corner_ref, out_ref, start_ref)
-
-
-def first_sums_kernel(member_ref, energy_ref, *refs):
-    flat_refs, out_ref, flat_ref = refs[:-2], refs[-2], refs[-1]
-    flat_ref[...] = total_of([ref[...] for ref in flat_refs])
+
+
+def low_kernel(where_ref, field_ref, proj_ref, laden_ref, mate_ref, cross_ref):
+    window = field_ref[pl.ds(where_ref[FIRST_CHUNK + 2], REACH)]
+    laden_ref[laden_ref.shape[0] - HALO_ROWS :] = window.reshape(HALO_ROWS, LANES)
+    write_halos(field_ref, where_ref[0], mate_ref, cross_ref)
+    pack_plane(0, HALVES, proj_ref, laden_ref)
+
+
+def above_kernel(corner_ref, own_laden_ref, high_ref, laden_ref, flat_ref, on_ref):
+    rows = on_ref.shape[0]
+    on_ref[...] = laden_ref[:rows]
+
+    def field(x, half):
+        return laden_ref[pl.ds(pl.multiple_of(rows + x * SY + half * ROWS, ROWS), ROWS), :]
+
+    project(field, [(0, own_laden_ref, 0), (1, high_ref, 0)], corner_ref, flat_ref)
+
+
+def hand_on_kernel(given_ref, out_ref):
+    out_ref[...] = given_ref[...]
+
+
+def near_kernel(corner_ref, where_ref, field_ref, low_ref, high_ref, *refs):
+    chunks = some_planes(where_ref, 0, [low_ref, high_ref]) + some_planes(where_ref, 4, refs[:-1])
+    project(field_reader(field_ref), chunks, corner_ref, refs[-1])
+
+
+def write_table(flat_ref, member_ref, energy_ref, out_ref):
     sums = sum_atoms(flat_ref, member_ref)
     out_ref[...] = jnp.concatenate([to_rows(sums), to_rows(energy_ref[...])], axis=0)
 
 
-def whole_kernel(corner_ref, field_ref, whole_ref, out_ref):
-    project(field_reader(field_ref), all_planes(whole_ref), corner_ref, out_ref)
+def last_part_kernel(corner_ref, where_ref, member_ref, energy_ref, field_ref, near_ref,
+                     returned_ref, far_ref, out_ref, flat_ref):
+    flat_ref[...] = near_ref[...] + returned_ref[...]
+    chunks = some_planes(where_ref, 7, [far_ref])
+    project(field_reader(field_ref), chunks, corner_ref, flat_ref, flat_ref)
+    write_table(flat_ref, member_ref, energy_ref, out_ref)
+
+
+def whole_pack_kernel(proj_ref, out_ref):
+    pack_plane(0, proj_ref.shape[2] // LANES, proj_ref, out_ref)
+
+
+def high_kernel(proj_ref, out_ref):
+    pack_plane(HALVES, HALVES, proj_ref, out_ref)
+
+
+def whole_sums_kernel(corner_ref, member_ref, energy_ref, field_ref, whole_ref, out_ref, flat_ref):
+    project(field_reader(field_ref), all_planes(whole_ref), corner_ref, flat_ref)
+    write_table(flat_ref, member_ref, energy_ref, out_ref)
 
 
 def step_kernel(index, chunk_count, corner_ref, where_ref, member_ref, along_z_ref, along_y_ref,
@@ -316,7 +347,7 @@
     else:
         table = from_rows(own_ref[HALO_ROWS:] + cross_ref[HALO_ROWS:] + far_ref[...])
     if chunk_count > 1:
-        chunks = [(where_ref[FIRST_CHUNK + i], refs[i]) for i in range(chunk_count)]
+        chunks = some_planes(where_ref, 0, refs[:chunk_count])
     else:
         chunks = all_planes(refs[0])
     refs = refs[chunk_count:]
@@ -417,6 +448,13 @@
     table_rows = ROWS * atoms // LANES
     sends = [shaped(HALO_ROWS + table_rows, LANES)] * 2
 
+    flat = (groups, ROWS, LANES)
+    boxes = (TILES, ROWS, LANES)
+    parts = (COPIES, planes, SY, LANES)
+    padded = (planes + 2 * REACH, SY, LANES)
+    table_rows = ROWS * atoms // LANES
+    sends = [shaped(HALO_ROWS + table_rows, LANES)] * 2
+
     def pack(first_tile, count, after=()):
         return call(
             functools.partial(pack_kernel, first_tile), "pack_projectors",
@@ -439,46 +477,53 @@
         at = lax.axis_index("band").astype(jnp.int32)
         owners = [at, (at + 1) % 4, (at + 3) % 4, (at + 2) % 4]
         where = jnp.stack([odd] + [2 * part + h for part in owners for h in range(2)])
-        window = shaped(REACH, SY, LANES)
-        low = pack(0, HALVES)
+        rows = HALVES * groups * ROWS * ROWS
+        plane = shaped(rows, LANES)
+        low, mate, cross = call(
+            low_kernel, "pack_low", [shaped(rows + HALO_ROWS, LANES)] + halos,
+            [where], [field, projectors], [],
+        )
         below_low = turn(low, "band", 1)
-        mate, cross, opposite = call(
-            window_kernel, "cut_window", halos + [window], [where], [field], []
-        )
-        opposite = turn(opposite, "band", 2)
-        high = pack(HALVES, HALVES, [opposite])
-        above_high = turn(high, "band", -1)
+        high = call(high_kernel, "pack_high", plane, [], [projectors], [], [low])
         below_high = turn(high, "band", 1)
-        above_low = turn(low, "band", -1)
-        own, returned = call(
-            own_planes_kernel, "project_own", [shaped(*flat)] * 2, [slot_corner, where],
-            [field, opposite, low, high], [],
-        )
-        returned = turn(returned, "band", 2)
-        own, above_on, below_on = call(
-            forward_kernel, "project_and_forward", [shaped(*flat)] + [shaped(*low.shape)] * 2,
-            [slot_corner, where], [field, own, returned, above_high, below_low], [],
-        )
-        far_low = turn(below_on, "band", 1)
-        far_high = turn(above_on, "band", -1)
+        returned, on_low = call(
+            above_kernel, "project_above", [shaped(*flat), plane], [slot_corner],
+            [low, high, below_low], [],
+        )
+        returned = turn(returned, "band", -1)
+        far_low = turn(on_low, "band", 1)
+
+        def hand_on(values, *after):
+            return call(hand_on_kernel, "hand_on", plane, [], [values], [], after)
+
+        on_high = hand_on(below_high, on_low, returned)
+        far_high = turn(on_high, "band", 1)
+        on_far_low = hand_on(far_low, on_high)
+        above_low = turn(on_far_low, "band", 1)
+        near = call(
+            near_kernel, "project_near", shaped(*flat), [slot_corner, where],
+            [field, low, high, below_low, below_high, far_low], [],
+        )
+        on_far_high = hand_on(far_high, on_far_low, near, tables[0], energy)
+        above_high = turn(on_far_high, "band", 1)
         own = call(
-            beside_kernel, "project_beside", shaped(*flat), [slot_corner, where],
-            [field, own, above_low, below_high], [],
-        )
-        flats = [own]
+            last_part_kernel, "first_sums", shaped(2 * table_rows, LANES), [slot_corner, where],
+            [tables[0], energy, field, near, returned, far_high], [flat],
+        )
         chunks = [low, high, above_low, above_high, below_low, below_high, far_low, far_high]
     else:
         where = odd[None]
-        mate, cross = call(window_kernel, "cut_windows", halos, [where], [field], [])
-        chunks = [lax.all_gather(pack(0, tiles), "band", axis=0, tiled=True)]
-        flats = [
-            call(whole_kernel, "project_first", shaped(*flat), [slot_corner], [field, *chunks], [])
-        ]
+        mate, cross = call(halo_kernel, "cut_halos", halos, [where], [field], [])
+        packed = call(
+            whole_pack_kernel, "pack_projectors", shaped(tiles * groups * ROWS * ROWS, LANES),
+            [], [projectors], [],
+        )
+        chunks = [lax.all_gather(packed, "band", axis=0, tiled=True)]
+        own = call(
+            whole_sums_kernel, "first_sums", shaped(2 * table_rows, LANES), [slot_corner],
+            [tables[0], energy, field, *chunks], [flat],
+        )
     mate, cross = swap(mate, "dom", 0), swap(cross, "dom", 1)
-    own = call(
-        first_sums_kernel, "first_sums", shaped(2 * table_rows, LANES), [],
-        [tables[0], energy, *flats], [flat],
-    )
     own = own + swap(own, "dom", 0)
     other = swap(own, "dom", 1)
     far = swap(other, "dom", 0)

time: 73.4 us -> 72.1 us (0.982)
  starting transfers between devices: 31.6 us -> 22.9 us
  waiting for transfers between devices: 26.5 us -> 33.5 us
    ppermute x8 -> x7, starting transfers between devices: 9.86 us -> 4.78 us  [turn(): lax.ppermute(values, axis, [(i, (i + step) % count) for i in range(count)])]
    ppermute x8 -> x7, waiting for transfers between devices: 14.1 us -> 18.3 us  [turn(): lax.ppermute(values, axis, [(i, (i + step) % count) for i in range(count)])]
    ppermute x11, starting transfers between devices: 21.8 us -> 18.1 us  [swap(): return lax.ppermute(values, axis, pairs)]
    ppermute x11, waiting for transfers between devices: 12.4 us -> 15.3 us  [swap(): return lax.ppermute(values, axis, pairs)]
    unnamed x14 -> x12, local copies, waits for them, and re-layouts: 1.87 us -> 2.42 us
    pallas_call x11 -> x12, Pallas kernels: 12.3 us -> 12.3 us  [call(): pl.pallas_call(body, out_shape=out_shape, in_specs=[SMEM] * len(scalars)...]
  transfers between devices with their start and end apart: 19 -> 18, of which waited for: 11 -> 14; matrix products, arithmetic and copies ran while one was open for 0% -> 0% of each run, Pallas kernels for 7% -> 5%
where the time goes in v3:
time: 72.1 us; the launch traced here: 71.6 us
  waiting for transfers between devices  33.5 us (46%)
  starting transfers between devices  22.9 us (32%)
  Pallas kernels  12.3 us (17%)
  local copies, waits for them, and re-layouts  2.74 us (4%)
    ppermute x7, waiting for transfers between devices, turn(): lax.ppermute(values, axis, [(i, (i + step) % count) for i in range(count)])  18.3 us
    ppermute x11, starting transfers between devices, swap(): return lax.ppermute(values, axis, pairs)  18.1 us
    ppermute x11, waiting for transfers between devices, swap(): return lax.ppermute(values, axis, pairs)  15.3 us
    pallas_call x12, Pallas kernels, call(): pl.pallas_call(body, out_shape=out_shape, in_specs=[SMEM] * len(scalars)...  12.3 us
    ppermute x7, starting transfers between devices, turn(): lax.ppermute(values, axis, [(i, (i + step) % count) for i in range(count)])  4.78 us
    unnamed x12, local copies, waits for them, and re-layouts  2.42 us
  transfers between devices with their start and end apart: 18, of which 14 were waited for; matrix products, arithmetic and copies ran while one was open for 0% of the time, Pallas kernels for 5%

profile of v3, /device:TPU:5, one launch (start us, length us, event | category | flops | bytes accessed | tf_op | source)
XLA Modules:
  0.0 71.6 jit_solution(16157225067354495782)
XLA Ops:
  0.9 1.0 %copy-done.1 = f32[32,8,512]{2,1,0:T(8,128)S(1)} copy-done((f32[32,8,512]{2,1,0:T(8,128)S(1)}, f32[32,8,512]{2,1,0:T(8,128)}, u32[]{:S(2)}) %copy-start.1) | copy-done | bytes 524312
  1.9 1.4 %pack_low.1 = (f32[608,128]{1,0:T(8,128)S(1)}, f32[96,128]{1,0:T(8,128)S(1)}, f32[96,128]{1,0:T(8,128)S(1)}) custom-call(s32[9]{0:T(128)S(1)} %stack.39.refs_0_.refs_1_, f32[12,16,128]{2,1,0:T(8,128)S(1)} %bitcast.12, f32[32,8,512]{2,1,0:T(8,128)S(1)} %copy-done.1), custom_call_target="tpu_custom_call" | custom-call | tf_op jit(solution)/shard_map/pack_low/pallas_call | solution.py:430
  3.4 1.3 %collective-permute-start.2 = (f32[608,128]{1,0:T(8,128)S(1)}, f32[608,128]{1,0:T(8,128)S(1)}, u32[]{:S(2)}, u32[]{:S(2)}) collective-permute-start(f32[608,128]{1,0:T(8,128)S(1)} %get-tuple-element.49.refs_1_.refs_3_.refs_12_.refs_11_), channel_id=1, source_target_pairs={{0,1},{1,2},{2,3},{3,0},{4,5},{5,6},{6,7},{7,4},{8,9},{9,10},{10,1... | collective-permute-start | bytes 933896 | tf_op jit(solution)/shard_map/ppermute | solution.py:406
  4.7 0.9 %pack_high.1.refs_2_.refs_4_.refs_13_.refs_12_ = f32[512,128]{1,0:T(8,128)S(1)} custom-call(f32[32,8,512]{2,1,0:T(8,128)S(1)} %copy-done.1, f32[608,128]{1,0:T(8,128)S(1)} %get-tuple-element.49.refs_1_.refs_3_.refs_12_.refs_11_), custom_call_target="tpu_custom_call" | custom-call | tf_op jit(solution)/shard_map/pack_high/pallas_call | solution.py:430
  5.7 1.3 %collective-permute-start.3 = (f32[512,128]{1,0:T(8,128)S(1)}, f32[512,128]{1,0:T(8,128)S(1)}, u32[]{:S(2)}, u32[]{:S(2)}) collective-permute-start(f32[512,128]{1,0:T(8,128)S(1)} %pack_high.1.refs_2_.refs_4_.refs_13_.refs_12_), channel_id=1, source_target_pairs={{0,1},{1,2},{2,3},{3,0},{4,5},{5,6},{6,7},{7,4},{8,9},{9,10},{10,1... | collective-permute-start | bytes 786440 | tf_op jit(solution)/shard_map/ppermute | solution.py:406
  7.0 6.6 %collective-permute-done.2.refs_3_.refs_5_.refs_16_.refs_15_ = f32[608,128]{1,0:T(8,128)S(1)} collective-permute-done((f32[608,128]{1,0:T(8,128)S(1)}, f32[608,128]{1,0:T(8,128)S(1)}, u32[]{:S(2)}, u32[]{:S(2)}) %collective-permute-start.2) | collective-permute-done | bytes 311328 | tf_op jit(solution)/shard_map/ppermute | solution.py:406
  14.4 1.4 %collective-permute-start.5 = (f32[4,8,128]{2,1,0:T(8,128)S(1)}, f32[4,8,128]{2,1,0:T(8,128)S(1)}, u32[]{:S(2)}, u32[]{:S(2)}) collective-permute-start(f32[4,8,128]{2,1,0:T(8,128)S(1)} %get-tuple-element.51), channel_id=1, source_target_pairs={{0,3},{1,0},{2,1},{3,2},{4,7},{5,4},{6,5},{7,6},{8,11},{9,8},{10,9... | collective-permute-start | bytes 49160 | tf_op jit(solution)/shard_map/ppermute | solution.py:406
  15.9 3.3 %collective-permute-done.3.refs_6_.refs_0_.refs_17_.refs_16_ = f32[512,128]{1,0:T(8,128)S(1)} collective-permute-done((f32[512,128]{1,0:T(8,128)S(1)}, f32[512,128]{1,0:T(8,128)S(1)}, u32[]{:S(2)}, u32[]{:S(2)}) %collective-permute-start.3) | collective-permute-done | bytes 262176 | tf_op jit(solution)/shard_map/ppermute | solution.py:406
  21.2 2.1 %collective-permute-done.4.refs_7_.refs_0_.refs_18_.refs_17_ = f32[512,128]{1,0:T(8,128)S(1)} collective-permute-done((f32[512,128]{1,0:T(8,128)S(1)}, f32[512,128]{1,0:T(8,128)S(1)}, u32[]{:S(2)}, u32[]{:S(2)}) %collective-permute-start.4) | collective-permute-done | bytes 262176 | tf_op jit(solution)/shard_map/ppermute | solution.py:406
  23.7 1.0 %project_near.1.refs_5_.refs_2_ = f32[4,8,128]{2,1,0:T(8,128)S(1)} custom-call(s32[3,32]{1,0:T(4,128)S(1)} %copy-done.3, s32[9]{0:T(128)S(1)} %stack.39.refs_0_.refs_1_, f32[12,16,128]{2,1,0:T(8,128)S(1)} %bitcast.13, f32[608,128]{1,0:T(8,128)S(1)} %get-tuple-element.49.refs_1_.refs_3_.refs_12_.refs_11_, ...), custom_call_target="tpu_custom_call" | custom-call | tf_op jit(solution)/shard_map/project_near/pallas_call | solution.py:430
  24.8 5.5 %collective-permute-done.6.refs_7_.refs_0_.refs_19_.refs_18_ = f32[512,128]{1,0:T(8,128)S(1)} collective-permute-done((f32[512,128]{1,0:T(8,128)S(1)}, f32[512,128]{1,0:T(8,128)S(1)}, u32[]{:S(2)}, u32[]{:S(2)}) %collective-permute-start.6) | collective-permute-done | bytes 262176 | tf_op jit(solution)/shard_map/ppermute | solution.py:406
  30.3 4.4 %collective-permute-start = (f32[96,128]{1,0:T(8,128)S(1)}, f32[96,128]{1,0:T(8,128)S(1)}, u32[]{:S(2)}, u32[]{:S(2)}) collective-permute-start(f32[96,128]{1,0:T(8,128)S(1)} %get-tuple-element.47), channel_id=1, source_target_pairs={{0,4},{4,0},{8,12},{12,8},{16,20},{20,16},{24,28},{28,24},{1,5},{5... | collective-permute-start | bytes 147464 | tf_op jit(solution)/shard_map/ppermute | solution.py:401
  34.8 3.2 %collective-permute-start.1 = (f32[96,128]{1,0:T(8,128)S(1)}, f32[96,128]{1,0:T(8,128)S(1)}, u32[]{:S(2)}, u32[]{:S(2)}) collective-permute-start(f32[96,128]{1,0:T(8,128)S(1)} %get-tuple-element.48), channel_id=1, source_target_pairs={{4,8},{8,4},{12,16},{16,12},{20,24},{24,20},{5,9},{9,5},{13,17},{1... | collective-permute-start | bytes 147464 | tf_op jit(solution)/shard_map/ppermute | solution.py:401
  37.9 0.9 %first_sums.1 = f32[16,128]{1,0:T(8,128)S(1)} custom-call(s32[3,32]{1,0:T(4,128)S(1)} %copy-done.3, s32[9]{0:T(128)S(1)} %stack.39.refs_0_.refs_1_, bf16[128,512]{1,0:T(8,128)(2,1)S(1)} %get-tuple-element.44.refs_2_.refs_3_, f32[8,128]{1,0:T(8,128)S(1)} %broadcast_select_fusion.refs_3_.refs_4_, f32[12,16,128]{2,1,0:T(8,128)S(1)} %bitcast.14, ...), custom_call_target="tpu_custom_call" | custom-call | tf_op jit(solution)/shard_map/first_sums/pallas_call | solution.py:430
  39.3 0.8 %collective-permute-done.7 = f32[16,128]{1,0:T(8,128)S(1)} collective-permute-done((f32[16,128]{1,0:T(8,128)S(1)}, f32[16,128]{1,0:T(8,128)S(1)}, u32[]{:S(2)}, u32[]{:S(2)}) %collective-permute-start.7) | collective-permute-done | bytes 8224 | tf_op jit(solution)/shard_map/ppermute | solution.py:401
  40.1 2.4 %collective-permute-start.8 = (f32[16,128]{1,0:T(8,128)S(1)}, f32[16,128]{1,0:T(8,128)S(1)}, u32[]{:S(2)}, u32[]{:S(2)}) collective-permute-start(f32[16,128]{1,0:T(8,128)S(1)} %add.67.refs_9_), channel_id=1, source_target_pairs={{4,8},{8,4},{12,16},{16,12},{20,24},{24,20},{5,9},{9,5},{13,17},{1... | collective-permute-start | bytes 24584 | tf_op jit(solution)/shard_map/ppermute | solution.py:401
  42.6 2.5 %collective-permute-done.8.refs_11_ = f32[16,128]{1,0:T(8,128)S(1)} collective-permute-done((f32[16,128]{1,0:T(8,128)S(1)}, f32[16,128]{1,0:T(8,128)S(1)}, u32[]{:S(2)}, u32[]{:S(2)}) %collective-permute-start.8) | collective-permute-done | bytes 8224 | tf_op jit(solution)/shard_map/ppermute | solution.py:401
  45.1 1.2 %collective-permute-start.9 = (f32[16,128]{1,0:T(8,128)S(1)}, f32[16,128]{1,0:T(8,128)S(1)}, u32[]{:S(2)}, u32[]{:S(2)}) collective-permute-start(f32[16,128]{1,0:T(8,128)S(1)} %collective-permute-done.8.refs_11_), channel_id=1, source_target_pairs={{0,4},{4,0},{8,12},{12,8},{16,20},{20,16},{24,28},{28,24},{1,5},{5... | collective-permute-start | bytes 24584 | tf_op jit(solution)/shard_map/ppermute | solution.py:401
  46.3 0.8 %collective-permute-done.9.refs_10_ = f32[16,128]{1,0:T(8,128)S(1)} collective-permute-done((f32[16,128]{1,0:T(8,128)S(1)}, f32[16,128]{1,0:T(8,128)S(1)}, u32[]{:S(2)}, u32[]{:S(2)}) %collective-permute-start.9) | collective-permute-done | bytes 8224 | tf_op jit(solution)/shard_map/ppermute | solution.py:401
  47.2 2.4 %filter_step_1.1 = (f32[12,16,128]{2,1,0:T(8,128)S(1)}, f32[104,128]{1,0:T(8,128)S(1)}, f32[104,128]{1,0:T(8,128)S(1)}, f32[8,128]{1,0:T(8,128)S(1)}) custom-call(s32[3,32]{1,0:T(4,128)S(1)} %copy-done.3, s32[9]{0:T(128)S(1)} %stack.39.refs_0_.refs_1_, bf16[128,512]{1,0:T(8,128)(2,1)S(1)} %get-tuple-element.44.refs_2_.refs_3_, ...), custom_call_target="tpu_custom_call" | custom-call | tf_op jit(solution)/shard_map/filter_step_1/pallas_call | solution.py:430
  49.9 0.9 %collective-permute-done.12.refs_7_ = f32[104,128]{1,0:T(8,128)S(1)} collective-permute-done((f32[104,128]{1,0:T(8,128)S(1)}, f32[104,128]{1,0:T(8,128)S(1)}, u32[]{:S(2)}, u32[]{:S(2)}) %collective-permute-start.12) | collective-permute-done | bytes 53280 | tf_op jit(solution)/shard_map/ppermute | solution.py:401
  50.8 1.9 %collective-permute-start.13 = (f32[104,128]{1,0:T(8,128)S(1)}, f32[104,128]{1,0:T(8,128)S(1)}, u32[]{:S(2)}, u32[]{:S(2)}) collective-permute-start(f32[104,128]{1,0:T(8,128)S(1)} %fusion.1.refs_9_), channel_id=1, source_target_pairs={{4,8},{8,4},{12,16},{16,12},{20,24},{24,20},{5,9},{9,5},{13,17},{1... | collective-permute-start | bytes 159752 | tf_op jit(solution)/shard_map/ppermute | solution.py:401
  52.7 3.8 %collective-permute-done.13.refs_8_ = f32[104,128]{1,0:T(8,128)S(1)} collective-permute-done((f32[104,128]{1,0:T(8,128)S(1)}, f32[104,128]{1,0:T(8,128)S(1)}, u32[]{:S(2)}, u32[]{:S(2)}) %collective-permute-start.13) | collective-permute-done | bytes 53280 | tf_op jit(solution)/shard_map/ppermute | solution.py:401
  56.5 0.9 %collective-permute-start.14 = (f32[8,128]{1,0:T(8,128)S(1)}, f32[8,128]{1,0:T(8,128)S(1)}, u32[]{:S(2)}, u32[]{:S(2)}) collective-permute-start(f32[8,128]{1,0:T(8,128)S(1)} %slice.57), channel_id=1, source_target_pairs={{0,4},{4,0},{8,12},{12,8},{16,20},{20,16},{24,28},{28,24},{1,5},{5... | collective-permute-start | bytes 12296 | tf_op jit(solution)/shard_map/ppermute | solution.py:401
  57.5 0.8 %collective-permute-done.14.refs_10_ = f32[8,128]{1,0:T(8,128)S(1)} collective-permute-done((f32[8,128]{1,0:T(8,128)S(1)}, f32[8,128]{1,0:T(8,128)S(1)}, u32[]{:S(2)}, u32[]{:S(2)}) %collective-permute-start.14) | collective-permute-done | bytes 4128 | tf_op jit(solution)/shard_map/ppermute | solution.py:401
  58.3 2.4 %filter_step_2.1 = (f32[12,16,128]{2,1,0:T(8,128)S(1)}, f32[104,128]{1,0:T(8,128)S(1)}, f32[104,128]{1,0:T(8,128)S(1)}) custom-call(s32[3,32]{1,0:T(4,128)S(1)} %copy-done.3, s32[9]{0:T(128)S(1)} %stack.39.refs_0_.refs_1_, bf16[128,512]{1,0:T(8,128)(2,1)S(1)} %get-tuple-element.44.refs_2_.refs_3_, bf16[384,128]{1,0:T(8,128)(2,1)S(1)} %get-tuple-element.45.refs_3_, ...), custom_call_target="tpu_custom_call" | custom-call | tf_op jit(solution)/shard_map/filter_step_2/pallas_call | solution.py:430
  61.0 0.9 %collective-permute-done.15.refs_7_ = f32[104,128]{1,0:T(8,128)S(1)} collective-permute-done((f32[104,128]{1,0:T(8,128)S(1)}, f32[104,128]{1,0:T(8,128)S(1)}, u32[]{:S(2)}, u32[]{:S(2)}) %collective-permute-start.15) | collective-permute-done | bytes 53280 | tf_op jit(solution)/shard_map/ppermute | solution.py:401
  61.9 1.9 %collective-permute-start.16 = (f32[104,128]{1,0:T(8,128)S(1)}, f32[104,128]{1,0:T(8,128)S(1)}, u32[]{:S(2)}, u32[]{:S(2)}) collective-permute-start(f32[104,128]{1,0:T(8,128)S(1)} %fusion.refs_9_), channel_id=1, source_target_pairs={{4,8},{8,4},{12,16},{16,12},{20,24},{24,20},{5,9},{9,5},{13,17},{1... | collective-permute-start | bytes 159752 | tf_op jit(solution)/shard_map/ppermute | solution.py:401
  63.8 3.8 %collective-permute-done.16.refs_8_ = f32[104,128]{1,0:T(8,128)S(1)} collective-permute-done((f32[104,128]{1,0:T(8,128)S(1)}, f32[104,128]{1,0:T(8,128)S(1)}, u32[]{:S(2)}, u32[]{:S(2)}) %collective-permute-start.16) | collective-permute-done | bytes 53280 | tf_op jit(solution)/shard_map/ppermute | solution.py:401
  67.7 0.9 %collective-permute-start.17 = (f32[8,128]{1,0:T(8,128)S(1)}, f32[8,128]{1,0:T(8,128)S(1)}, u32[]{:S(2)}, u32[]{:S(2)}) collective-permute-start(f32[8,128]{1,0:T(8,128)S(1)} %slice.59), channel_id=1, source_target_pairs={{0,4},{4,0},{8,12},{12,8},{16,20},{20,16},{24,28},{28,24},{1,5},{5... | collective-permute-start | bytes 12296 | tf_op jit(solution)/shard_map/ppermute | solution.py:401
  68.6 0.8 %collective-permute-done.17.refs_10_ = f32[8,128]{1,0:T(8,128)S(1)} collective-permute-done((f32[8,128]{1,0:T(8,128)S(1)}, f32[8,128]{1,0:T(8,128)S(1)}, u32[]{:S(2)}, u32[]{:S(2)}) %collective-permute-start.17) | collective-permute-done | bytes 4128 | tf_op jit(solution)/shard_map/ppermute | solution.py:401
  69.4 2.2 %filter_step_3.1 = f32[12,16,128]{2,1,0:T(8,128)} custom-call(s32[3,32]{1,0:T(4,128)S(1)} %copy-done.3, s32[9]{0:T(128)S(1)} %stack.39.refs_0_.refs_1_, bf16[128,512]{1,0:T(8,128)(2,1)S(1)} %get-tuple-element.44.refs_2_.refs_3_, bf16[384,128]{1,0:T(8,128)(2,1)S(1)} %get-tuple-element.45.refs_3_, bf16[192,576]{1,0:T(8,128)(2,1)S(1)} %get-tuple-element.46.refs_4_, ...), custom_call_target="tpu_custom_call" | custom-call | tf_op jit(solution)/shard_map/filter_step_3/pallas_call | solution.py:430
  (40 shorter events, 5.4 us)
Async XLA Ops:
  0.0 0.9 %copy-start = (f32[1,12,16,128]{3,2,1,0:T(8,128)S(1)}, f32[1,12,16,128]{3,2,1,0:T(8,128)}, u32[]{:S(2)}) copy-start(f32[1,12,16,128]{3,2,1,0:T(8,128)} %param.10) | copy-start | bytes 294916
  0.9 1.0 %copy-start.1 = (f32[32,8,512]{2,1,0:T(8,128)S(1)}, f32[32,8,512]{2,1,0:T(8,128)}, u32[]{:S(2)}) copy-start(f32[32,8,512]{2,1,0:T(8,128)} %refs_0_.7) | copy-start | bytes 1572868
  3.4 10.2 %copy-start.3 = (s32[3,32]{1,0:T(4,128)S(1)}, s32[3,32]{1,0:T(4,128)}, u32[]{:S(2)}) copy-start(s32[3,32]{1,0:T(4,128)} %refs_0_.13) | copy-start | bytes 1156
  3.4 10.2 %collective-permute-start.2 = (f32[608,128]{1,0:T(8,128)S(1)}, f32[608,128]{1,0:T(8,128)S(1)}, u32[]{:S(2)}, u32[]{:S(2)}) collective-permute-start(f32[608,128]{1,0:T(8,128)S(1)} %get-tuple-element.49.refs_1_.refs_3_.refs_12_.refs_11_), channel_id=1, source_target_pairs={{0,1},{1,2},{2,3},{3,0},{4,5},{5,6},{6,7},{7,4},{8,9},{9,10},{10,1... | collective-permute-start | bytes 933896 | tf_op jit(solution)/shard_map/ppermute | solution.py:406
  5.7 13.6 %collective-permute-start.3 = (f32[512,128]{1,0:T(8,128)S(1)}, f32[512,128]{1,0:T(8,128)S(1)}, u32[]{:S(2)}, u32[]{:S(2)}) collective-permute-start(f32[512,128]{1,0:T(8,128)S(1)} %pack_high.1.refs_2_.refs_4_.refs_13_.refs_12_), channel_id=1, source_target_pairs={{0,1},{1,2},{2,3},{3,0},{4,5},{5,6},{6,7},{7,4},{8,9},{9,10},{10,1... | collective-permute-start | bytes 786440 | tf_op jit(solution)/shard_map/ppermute | solution.py:406
  14.4 5.6 %collective-permute-start.5 = (f32[4,8,128]{2,1,0:T(8,128)S(1)}, f32[4,8,128]{2,1,0:T(8,128)S(1)}, u32[]{:S(2)}, u32[]{:S(2)}) collective-permute-start(f32[4,8,128]{2,1,0:T(8,128)S(1)} %get-tuple-element.51), channel_id=1, source_target_pairs={{0,3},{1,0},{2,1},{3,2},{4,7},{5,4},{6,5},{7,6},{8,11},{9,8},{10,9... | collective-permute-start | bytes 49160 | tf_op jit(solution)/shard_map/ppermute | solution.py:406
  15.9 7.4 %collective-permute-start.4 = (f32[512,128]{1,0:T(8,128)S(1)}, f32[512,128]{1,0:T(8,128)S(1)}, u32[]{:S(2)}, u32[]{:S(2)}) collective-permute-start(f32[512,128]{1,0:T(8,128)S(1)} %get-tuple-element.50.refs_1_), channel_id=1, source_target_pairs={{0,1},{1,2},{2,3},{3,0},{4,5},{5,6},{6,7},{7,4},{8,9},{9,10},{10,1... | collective-permute-start | bytes 786440 | tf_op jit(solution)/shard_map/ppermute | solution.py:406
  20.1 0.7 copy-start.5
  20.1 10.2 %collective-permute-start.6 = (f32[512,128]{1,0:T(8,128)S(1)}, f32[512,128]{1,0:T(8,128)S(1)}, u32[]{:S(2)}, u32[]{:S(2)}) collective-permute-start(f32[512,128]{1,0:T(8,128)S(1)} %hand_on.3.refs_1_), channel_id=1, source_target_pairs={{0,1},{1,2},{2,3},{3,0},{4,5},{5,6},{6,7},{7,4},{8,9},{9,10},{10,1... | collective-permute-start | bytes 786440 | tf_op jit(solution)/shard_map/ppermute | solution.py:406
  20.2 0.7 %copy-start.4 = (f32[16,8]{0,1:T(8,128)S(1)}, f32[16,8]{0,1:T(8,128)}, u32[]{:S(2)}) copy-start(f32[16,8]{0,1:T(8,128)} %param.13) | copy-start | bytes 1540
  23.3 23.9 %collective-permute-start.10 = (f32[512,128]{1,0:T(8,128)S(1)}, f32[512,128]{1,0:T(8,128)S(1)}, u32[]{:S(2)}, u32[]{:S(2)}) collective-permute-start(f32[512,128]{1,0:T(8,128)S(1)} %hand_on.4.refs_1_), channel_id=1, source_target_pairs={{0,1},{1,2},{2,3},{3,0},{4,5},{5,6},{6,7},{7,4},{8,9},{9,10},{10,1... | collective-permute-start | bytes 786440 | tf_op jit(solution)/shard_map/ppermute | solution.py:406
  30.3 16.9 %collective-permute-start.11 = (f32[512,128]{1,0:T(8,128)S(1)}, f32[512,128]{1,0:T(8,128)S(1)}, u32[]{:S(2)}, u32[]{:S(2)}) collective-permute-start(f32[512,128]{1,0:T(8,128)S(1)} %hand_on.5), channel_id=1, source_target_pairs={{0,1},{1,2},{2,3},{3,0},{4,5},{5,6},{6,7},{7,4},{8,9},{9,10},{10,1... | collective-permute-start | bytes 786440 | tf_op jit(solution)/shard_map/ppermute | solution.py:406
  30.3 16.0 %collective-permute-start = (f32[96,128]{1,0:T(8,128)S(1)}, f32[96,128]{1,0:T(8,128)S(1)}, u32[]{:S(2)}, u32[]{:S(2)}) collective-permute-start(f32[96,128]{1,0:T(8,128)S(1)} %get-tuple-element.47), channel_id=1, source_target_pairs={{0,4},{4,0},{8,12},{12,8},{16,20},{20,16},{24,28},{28,24},{1,5},{5... | collective-permute-start | bytes 147464 | tf_op jit(solution)/shard_map/ppermute | solution.py:401
  34.8 12.4 %copy-start.2 = (f32[12,16,128]{2,1,0:T(8,128)S(1)}, f32[12,16,128]{2,1,0:T(8,128)}, u32[]{:S(2)}) copy-start(f32[12,16,128]{2,1,0:T(8,128)} %refs_6_.5) | copy-start | bytes 294916
  34.8 11.6 %collective-permute-start.1 = (f32[96,128]{1,0:T(8,128)S(1)}, f32[96,128]{1,0:T(8,128)S(1)}, u32[]{:S(2)}, u32[]{:S(2)}) collective-permute-start(f32[96,128]{1,0:T(8,128)S(1)} %get-tuple-element.48), channel_id=1, source_target_pairs={{4,8},{8,4},{12,16},{16,12},{20,24},{24,20},{5,9},{9,5},{13,17},{1... | collective-permute-start | bytes 147464 | tf_op jit(solution)/shard_map/ppermute | solution.py:401
  38.8 1.3 %collective-permute-start.7 = (f32[16,128]{1,0:T(8,128)S(1)}, f32[16,128]{1,0:T(8,128)S(1)}, u32[]{:S(2)}, u32[]{:S(2)}) collective-permute-start(f32[16,128]{1,0:T(8,128)S(1)} %first_sums.1), channel_id=1, source_target_pairs={{0,4},{4,0},{8,12},{12,8},{16,20},{20,16},{24,28},{28,24},{1,5},{5... | collective-permute-start | bytes 24584 | tf_op jit(solution)/shard_map/ppermute | solution.py:401
  40.1 5.0 %collective-permute-start.8 = (f32[16,128]{1,0:T(8,128)S(1)}, f32[16,128]{1,0:T(8,128)S(1)}, u32[]{:S(2)}, u32[]{:S(2)}) collective-permute-start(f32[16,128]{1,0:T(8,128)S(1)} %add.67.refs_9_), channel_id=1, source_target_pairs={{4,8},{8,4},{12,16},{16,12},{20,24},{24,20},{5,9},{9,5},{13,17},{1... | collective-permute-start | bytes 24584 | tf_op jit(solution)/shard_map/ppermute | solution.py:401
  45.1 2.1 %collective-permute-start.9 = (f32[16,128]{1,0:T(8,128)S(1)}, f32[16,128]{1,0:T(8,128)S(1)}, u32[]{:S(2)}, u32[]{:S(2)}) collective-permute-start(f32[16,128]{1,0:T(8,128)S(1)} %collective-permute-done.8.refs_11_), channel_id=1, source_target_pairs={{0,4},{4,0},{8,12},{12,8},{16,20},{20,16},{24,28},{28,24},{1,5},{5... | collective-permute-start | bytes 24584 | tf_op jit(solution)/shard_map/ppermute | solution.py:401
  49.6 1.2 %collective-permute-start.12 = (f32[104,128]{1,0:T(8,128)S(1)}, f32[104,128]{1,0:T(8,128)S(1)}, u32[]{:S(2)}, u32[]{:S(2)}) collective-permute-start(f32[104,128]{1,0:T(8,128)S(1)} %get-tuple-element.53), channel_id=1, source_target_pairs={{0,4},{4,0},{8,12},{12,8},{16,20},{20,16},{24,28},{28,24},{1,5},{5... | collective-permute-start | bytes 159752 | tf_op jit(solution)/shard_map/ppermute | solution.py:401
  50.8 5.7 %collective-permute-start.13 = (f32[104,128]{1,0:T(8,128)S(1)}, f32[104,128]{1,0:T(8,128)S(1)}, u32[]{:S(2)}, u32[]{:S(2)}) collective-permute-start(f32[104,128]{1,0:T(8,128)S(1)} %fusion.1.refs_9_), channel_id=1, source_target_pairs={{4,8},{8,4},{12,16},{16,12},{20,24},{24,20},{5,9},{9,5},{13,17},{1... | collective-permute-start | bytes 159752 | tf_op jit(solution)/shard_map/ppermute | solution.py:401
  56.5 1.8 %collective-permute-start.14 = (f32[8,128]{1,0:T(8,128)S(1)}, f32[8,128]{1,0:T(8,128)S(1)}, u32[]{:S(2)}, u32[]{:S(2)}) collective-permute-start(f32[8,128]{1,0:T(8,128)S(1)} %slice.57), channel_id=1, source_target_pairs={{0,4},{4,0},{8,12},{12,8},{16,20},{20,16},{24,28},{28,24},{1,5},{5... | collective-permute-start | bytes 12296 | tf_op jit(solution)/shard_map/ppermute | solution.py:401
  60.7 1.2 %collective-permute-start.15 = (f32[104,128]{1,0:T(8,128)S(1)}, f32[104,128]{1,0:T(8,128)S(1)}, u32[]{:S(2)}, u32[]{:S(2)}) collective-permute-start(f32[104,128]{1,0:T(8,128)S(1)} %get-tuple-element.57), channel_id=1, source_target_pairs={{0,4},{4,0},{8,12},{12,8},{16,20},{20,16},{24,28},{28,24},{1,5},{5... | collective-permute-start | bytes 159752 | tf_op jit(solution)/shard_map/ppermute | solution.py:401
  61.9 5.7 %collective-permute-start.16 = (f32[104,128]{1,0:T(8,128)S(1)}, f32[104,128]{1,0:T(8,128)S(1)}, u32[]{:S(2)}, u32[]{:S(2)}) collective-permute-start(f32[104,128]{1,0:T(8,128)S(1)} %fusion.refs_9_), channel_id=1, source_target_pairs={{4,8},{8,4},{12,16},{16,12},{20,24},{24,20},{5,9},{9,5},{13,17},{1... | collective-permute-start | bytes 159752 | tf_op jit(solution)/shard_map/ppermute | solution.py:401
  67.7 1.8 %collective-permute-start.17 = (f32[8,128]{1,0:T(8,128)S(1)}, f32[8,128]{1,0:T(8,128)S(1)}, u32[]{:S(2)}, u32[]{:S(2)}) collective-permute-start(f32[8,128]{1,0:T(8,128)S(1)} %slice.59), channel_id=1, source_target_pairs={{0,4},{4,0},{8,12},{12,8},{16,20},{20,16},{24,28},{28,24},{1,5},{5... | collective-permute-start | bytes 12296 | tf_op jit(solution)/shard_map/ppermute | solution.py:401

commit v4 on v3

--- a/solution.py
+++ b/solution.py
@@ -283,10 +283,18 @@
     write_halos(field_ref, where_ref[0], mate_ref, cross_ref)
 
 
-def low_kernel(where_ref, field_ref, proj_ref, laden_ref, mate_ref, cross_ref):
+def low_kernel(where_ref, field_hbm, proj_hbm, laden_ref, mate_ref, cross_ref,
+               field_ref, proj_ref, field_sem, proj_sem):
+    cells = pl.ds(0, proj_ref.shape[2])
+    proj_copy = pltpu.make_async_copy(proj_hbm.at[:, :, cells], proj_ref, proj_sem)
+    field_copy = pltpu.make_async_copy(field_hbm, field_ref, field_sem)
+    proj_copy.start()
+    field_copy.start()
+    field_copy.wait()
     window = field_ref[pl.ds(where_ref[FIRST_CHUNK + 2], REACH)]
     laden_ref[laden_ref.shape[0] - HALO_ROWS :] = window.reshape(HALO_ROWS, LANES)
     write_halos(field_ref, where_ref[0], mate_ref, cross_ref)
+    proj_copy.wait()
     pack_plane(0, HALVES, proj_ref, laden_ref)
 
 
@@ -391,6 +399,7 @@
 VMEM = pl.BlockSpec(memory_space=pltpu.VMEM)
 SMEM = pl.BlockSpec(memory_space=pltpu.SMEM)
 ANY = pl.BlockSpec(memory_space=pl.ANY)
+HBM = pl.BlockSpec(memory_space=pltpu.HBM)
 
 
 def swap(values, axis, first):
@@ -479,10 +488,22 @@
         where = jnp.stack([odd] + [2 * part + h for part in owners for h in range(2)])
         rows = HALVES * groups * ROWS * ROWS
         plane = shaped(rows, LANES)
-        low, mate, cross = call(
-            low_kernel, "pack_low", [shaped(rows + HALO_ROWS, LANES)] + halos,
-            [where], [field, projectors], [],
-        )
+        low, mate, cross = pl.pallas_call(
+            low_kernel,
+            out_shape=[shaped(rows + HALO_ROWS, LANES)] + halos,
+            in_specs=[SMEM, HBM, HBM],
+            out_specs=[VMEM] * 3,
+            scratch_shapes=[
+                pltpu.VMEM(field.shape, jnp.float32),
+                pltpu.VMEM((slots, ROWS, HALVES * LANES), jnp.float32),
+                pltpu.SemaphoreType.DMA,
+                pltpu.SemaphoreType.DMA,
+            ],
+            compiler_params=pltpu.CompilerParams(vmem_limit_bytes=62 * 2**20),
+            cost_estimate=pl.CostEstimate(flops=0, bytes_accessed=0, transcendentals=0),
+            name="pack_low",
+        )(where, field, projectors)
+        mate, cross = swap(mate, "dom", 0), swap(cross, "dom", 1)
         below_low = turn(low, "band", 1)
         high = call(high_kernel, "pack_high", plane, [], [projectors], [], [low])
         below_high = turn(high, "band", 1)
@@ -502,7 +523,7 @@
         above_low = turn(on_far_low, "band", 1)
         near = call(
             near_kernel, "project_near", shaped(*flat), [slot_corner, where],
-            [field, low, high, below_low, below_high, far_low], [],
+            [field, low, high, below_low, below_high, far_low], [], [mate, cross],
         )
         on_far_high = hand_on(far_high, on_far_low, near, tables[0], energy)
         above_high = turn(on_far_high, "band", 1)
@@ -510,6 +531,7 @@
             last_part_kernel, "first_sums", shaped(2 * table_rows, LANES), [slot_corner, where],
             [tables[0], energy, field, near, returned, far_high], [flat],
         )
+        own = own + swap(own, "dom", 0)
         chunks = [low, high, above_low, above_high, below_low, below_high, far_low, far_high]
     else:
         where = odd[None]
@@ -523,8 +545,8 @@
             whole_sums_kernel, "first_sums", shaped(2 * table_rows, LANES), [slot_corner],
             [tables[0], energy, field, *chunks], [flat],
         )
-    mate, cross = swap(mate, "dom", 0), swap(cross, "dom", 1)
-    own = own + swap(own, "dom", 0)
+        mate, cross = swap(mate, "dom", 0), swap(cross, "dom", 1)
+        own = own + swap(own, "dom", 0)
     other = swap(own, "dom", 1)
     far = swap(other, "dom", 0)
     before = None

time: 72.1 us -> 74.4 us (1.032)
  Pallas kernels: 12.3 us -> 14.1 us
    pallas_call x0 -> x1, Pallas kernels: none -> 3.27 us  [on_device(): pl.pallas_call(low_kernel, out_shape=[shaped(rows + HALO_ROWS, LANES)] +...]
    pallas_call x12 -> x11, Pallas kernels: 12.3 us -> 10.8 us  [call(): pl.pallas_call(body, out_shape=out_shape, in_specs=[SMEM] * len(scalars)...]
    ppermute x11, starting transfers between devices: 18.1 us -> 19 us  [swap(): return lax.ppermute(values, axis, pairs)]
    unnamed x12 -> x22, local copies, waits for them, and re-layouts: 2.42 us -> 2.26 us
  transfers between devices with their start and end apart: 18 -> 18, of which waited for: 14 -> 13; matrix products, arithmetic and copies ran while one was open for 0% -> 0% of each run, Pallas kernels for 5% -> 5%
where the time goes in v4:
time: 74.4 us; the launch traced here: 74.1 us
  waiting for transfers between devices  33.2 us (45%)
  starting transfers between devices  23.4 us (31%)
  Pallas kernels  14.1 us (19%)
  local copies, waits for them, and re-layouts  3.12 us (4%)
    ppermute x11, starting transfers between devices, swap(): return lax.ppermute(values, axis, pairs)  19 us
    ppermute x7, waiting for transfers between devices, turn(): lax.ppermute(values, axis, [(i, (i + step) % count) for i in range(count)])  17.8 us
    ppermute x11, waiting for transfers between devices, swap(): return lax.ppermute(values, axis, pairs)  15.5 us
    pallas_call x11, Pallas kernels, call(): pl.pallas_call(body, out_shape=out_shape, in_specs=[SMEM] * len(scalars)...  10.8 us
    ppermute x7, starting transfers between devices, turn(): lax.ppermute(values, axis, [(i, (i + step) % count) for i in range(count)])  4.37 us
    pallas_call x1, Pallas kernels, on_device(): pl.pallas_call(low_kernel, out_shape=[shaped(rows + HALO_ROWS, LANES)] +...  3.27 us
    unnamed x22, local copies, waits for them, and re-layouts  2.26 us
  transfers between devices with their start and end apart: 18, of which 13 were waited for; matrix products, arithmetic and copies ran while one was open for 0% of the time, Pallas kernels for 5%

profile of v4, /device:TPU:5, one launch (start us, length us, event | category | flops | bytes accessed | tf_op | source)
XLA Modules:
  0.0 74.1 jit_solution(16254626520002991937)
XLA Ops:
  0.6 3.3 %pack_low.1 = (f32[608,128]{1,0:T(8,128)}, f32[96,128]{1,0:T(8,128)}, f32[96,128]{1,0:T(8,128)}) custom-call(s32[9]{0:T(128)} %stack.39.where_ref.refs_1_, f32[12,16,128]{2,1,0:T(8,128)} %bitcast.12, f32[32,8,512]{2,1,0:T(8,128)} %refs_0_.7), custom_call_target="tpu_custom_call" | custom-call | tf_op jit(solution)/shard_map/pack_low/pallas_call | solution.py:491
  3.9 1.3 %collective-permute-start.2 = (f32[608,128]{1,0:T(8,128)}, f32[608,128]{1,0:T(8,128)S(1)}, u32[]{:S(2)}, u32[]{:S(2)}) collective-permute-start(f32[608,128]{1,0:T(8,128)} %get-tuple-element.49.refs_1_.refs_3_.refs_12_.refs_11_), channel_id=1, source_target_pairs={{0,1},{1,2},{2,3},{3,0},{4,5},{5,6},{6,7},{7,4},{8,9},{9,10},{10,1... | collective-permute-start | bytes 933896 | tf_op jit(solution)/shard_map/ppermute | solution.py:415
  5.3 1.0 %copy-done = f32[608,128]{1,0:T(8,128)S(1)} copy-done((f32[608,128]{1,0:T(8,128)S(1)}, f32[608,128]{1,0:T(8,128)}, u32[]{:S(2)}) %copy-start) | copy-done | bytes 311320
  6.3 0.9 %pack_high.1.refs_2_.refs_4_.refs_13_.refs_12_ = f32[512,128]{1,0:T(8,128)S(1)} custom-call(f32[32,8,512]{2,1,0:T(8,128)S(1)} %copy-done.3, f32[608,128]{1,0:T(8,128)S(1)} %copy-done), custom_call_target="tpu_custom_call" | custom-call | tf_op jit(solution)/shard_map/pack_high/pallas_call | solution.py:439
  7.2 1.3 %collective-permute-start.3 = (f32[512,128]{1,0:T(8,128)S(1)}, f32[512,128]{1,0:T(8,128)S(1)}, u32[]{:S(2)}, u32[]{:S(2)}) collective-permute-start(f32[512,128]{1,0:T(8,128)S(1)} %pack_high.1.refs_2_.refs_4_.refs_13_.refs_12_), channel_id=1, source_target_pairs={{0,1},{1,2},{2,3},{3,0},{4,5},{5,6},{6,7},{7,4},{8,9},{9,10},{10,1... | collective-permute-start | bytes 786440 | tf_op jit(solution)/shard_map/ppermute | solution.py:415
  8.5 5.8 %collective-permute-done.2.refs_3_.refs_5_.refs_16_.refs_15_ = f32[608,128]{1,0:T(8,128)S(1)} collective-permute-done((f32[608,128]{1,0:T(8,128)}, f32[608,128]{1,0:T(8,128)S(1)}, u32[]{:S(2)}, u32[]{:S(2)}) %collective-permute-start.2) | collective-permute-done | bytes 311328 | tf_op jit(solution)/shard_map/ppermute | solution.py:415
  15.2 1.4 %collective-permute-start.5 = (f32[4,8,128]{2,1,0:T(8,128)S(1)}, f32[4,8,128]{2,1,0:T(8,128)S(1)}, u32[]{:S(2)}, u32[]{:S(2)}) collective-permute-start(f32[4,8,128]{2,1,0:T(8,128)S(1)} %get-tuple-element.51), channel_id=1, source_target_pairs={{0,3},{1,0},{2,1},{3,2},{4,7},{5,4},{6,5},{7,6},{8,11},{9,8},{10,9... | collective-permute-start | bytes 49160 | tf_op jit(solution)/shard_map/ppermute | solution.py:415
  16.6 3.0 %collective-permute-start = (f32[96,128]{1,0:T(8,128)S(1)}, f32[96,128]{1,0:T(8,128)S(1)}, u32[]{:S(2)}, u32[]{:S(2)}) collective-permute-start(f32[96,128]{1,0:T(8,128)S(1)} %copy-done.10), channel_id=1, source_target_pairs={{0,4},{4,0},{8,12},{12,8},{16,20},{20,16},{24,28},{28,24},{1,5},{5... | collective-permute-start | bytes 147464 | tf_op jit(solution)/shard_map/ppermute | solution.py:410
  19.6 3.0 %collective-permute-start.1 = (f32[96,128]{1,0:T(8,128)S(1)}, f32[96,128]{1,0:T(8,128)S(1)}, u32[]{:S(2)}, u32[]{:S(2)}) collective-permute-start(f32[96,128]{1,0:T(8,128)S(1)} %copy-done.9), channel_id=1, source_target_pairs={{4,8},{8,4},{12,16},{16,12},{20,24},{24,20},{5,9},{9,5},{13,17},{1... | collective-permute-start | bytes 147464 | tf_op jit(solution)/shard_map/ppermute | solution.py:410
  24.5 7.4 %collective-permute-done.4.refs_7_.refs_0_.refs_18_.refs_17_ = f32[512,128]{1,0:T(8,128)S(1)} collective-permute-done((f32[512,128]{1,0:T(8,128)S(1)}, f32[512,128]{1,0:T(8,128)S(1)}, u32[]{:S(2)}, u32[]{:S(2)}) %collective-permute-start.4) | collective-permute-done | bytes 262176 | tf_op jit(solution)/shard_map/ppermute | solution.py:415
  32.0 1.0 %project_near.1.refs_5_.refs_2_ = f32[4,8,128]{2,1,0:T(8,128)S(1)} custom-call(s32[3,32]{1,0:T(4,128)S(1)} %copy-done.5, s32[9]{0:T(128)S(1)} %copy-done.6, f32[12,16,128]{2,1,0:T(8,128)S(1)} %bitcast.13, f32[608,128]{1,0:T(8,128)S(1)} %copy-done.1, f32[512,128]{1,0:T(8,128)S(1)} %pack_high.1.refs_2_.refs_4_.refs_13_.refs_12_, ...), custom_call_target="tpu_custom_call" | custom-call | tf_op jit(solution)/shard_map/project_near/pallas_call | solution.py:439
  33.1 4.4 %collective-permute-done.6.refs_7_.refs_0_.refs_19_.refs_18_ = f32[512,128]{1,0:T(8,128)S(1)} collective-permute-done((f32[512,128]{1,0:T(8,128)S(1)}, f32[512,128]{1,0:T(8,128)S(1)}, u32[]{:S(2)}, u32[]{:S(2)}) %collective-permute-start.6) | collective-permute-done | bytes 262176 | tf_op jit(solution)/shard_map/ppermute | solution.py:415
  37.6 0.9 %first_sums.1 = f32[16,128]{1,0:T(8,128)S(1)} custom-call(s32[3,32]{1,0:T(4,128)S(1)} %copy-done.5, s32[9]{0:T(128)S(1)} %copy-done.6, bf16[128,512]{1,0:T(8,128)(2,1)S(1)} %get-tuple-element.44.refs_2_.refs_3_, f32[8,128]{1,0:T(8,128)S(1)} %broadcast_select_fusion.refs_3_.refs_4_, f32[12,16,128]{2,1,0:T(8,128)S(1)} %bitcast.14, ...), custom_call_target="tpu_custom_call" | custom-call | tf_op jit(solution)/shard_map/first_sums/pallas_call | solution.py:439
  38.5 2.2 %collective-permute-start.7 = (f32[16,128]{1,0:T(8,128)S(1)}, f32[16,128]{1,0:T(8,128)S(1)}, u32[]{:S(2)}, u32[]{:S(2)}) collective-permute-start(f32[16,128]{1,0:T(8,128)S(1)} %first_sums.1), channel_id=1, source_target_pairs={{0,4},{4,0},{8,12},{12,8},{16,20},{20,16},{24,28},{28,24},{1,5},{5... | collective-permute-start | bytes 24584 | tf_op jit(solution)/shard_map/ppermute | solution.py:410
  40.7 0.8 %collective-permute-done.7 = f32[16,128]{1,0:T(8,128)S(1)} collective-permute-done((f32[16,128]{1,0:T(8,128)S(1)}, f32[16,128]{1,0:T(8,128)S(1)}, u32[]{:S(2)}, u32[]{:S(2)}) %collective-permute-start.7) | collective-permute-done | bytes 8224 | tf_op jit(solution)/shard_map/ppermute | solution.py:410
  41.5 2.5 %collective-permute-start.8 = (f32[16,128]{1,0:T(8,128)S(1)}, f32[16,128]{1,0:T(8,128)S(1)}, u32[]{:S(2)}, u32[]{:S(2)}) collective-permute-start(f32[16,128]{1,0:T(8,128)S(1)} %add.67.refs_9_), channel_id=1, source_target_pairs={{4,8},{8,4},{12,16},{16,12},{20,24},{24,20},{5,9},{9,5},{13,17},{1... | collective-permute-start | bytes 24584 | tf_op jit(solution)/shard_map/ppermute | solution.py:410
  44.1 2.7 %collective-permute-done.8.refs_11_ = f32[16,128]{1,0:T(8,128)S(1)} collective-permute-done((f32[16,128]{1,0:T(8,128)S(1)}, f32[16,128]{1,0:T(8,128)S(1)}, u32[]{:S(2)}, u32[]{:S(2)}) %collective-permute-start.8) | collective-permute-done | bytes 8224 | tf_op jit(solution)/shard_map/ppermute | solution.py:410
  46.8 0.9 %collective-permute-start.9 = (f32[16,128]{1,0:T(8,128)S(1)}, f32[16,128]{1,0:T(8,128)S(1)}, u32[]{:S(2)}, u32[]{:S(2)}) collective-permute-start(f32[16,128]{1,0:T(8,128)S(1)} %collective-permute-done.8.refs_11_), channel_id=1, source_target_pairs={{0,4},{4,0},{8,12},{12,8},{16,20},{20,16},{24,28},{28,24},{1,5},{5... | collective-permute-start | bytes 24584 | tf_op jit(solution)/shard_map/ppermute | solution.py:410
  47.7 0.8 %collective-permute-done.9.refs_10_ = f32[16,128]{1,0:T(8,128)S(1)} collective-permute-done((f32[16,128]{1,0:T(8,128)S(1)}, f32[16,128]{1,0:T(8,128)S(1)}, u32[]{:S(2)}, u32[]{:S(2)}) %collective-permute-start.9) | collective-permute-done | bytes 8224 | tf_op jit(solution)/shard_map/ppermute | solution.py:410
  48.7 2.4 %filter_step_1.1 = (f32[12,16,128]{2,1,0:T(8,128)S(1)}, f32[104,128]{1,0:T(8,128)S(1)}, f32[104,128]{1,0:T(8,128)S(1)}, f32[8,128]{1,0:T(8,128)S(1)}) custom-call(s32[3,32]{1,0:T(4,128)S(1)} %copy-done.5, s32[9]{0:T(128)S(1)} %copy-done.6, bf16[128,512]{1,0:T(8,128)(2,1)S(1)} %get-tuple-element.44.refs_2_.refs_3_, ...), custom_call_target="tpu_custom_call" | custom-call | tf_op jit(solution)/shard_map/filter_step_1/pallas_call | solution.py:439
  51.1 1.3 %collective-permute-start.12 = (f32[104,128]{1,0:T(8,128)S(1)}, f32[104,128]{1,0:T(8,128)S(1)}, u32[]{:S(2)}, u32[]{:S(2)}) collective-permute-start(f32[104,128]{1,0:T(8,128)S(1)} %get-tuple-element.53), channel_id=1, source_target_pairs={{0,4},{4,0},{8,12},{12,8},{16,20},{20,16},{24,28},{28,24},{1,5},{5... | collective-permute-start | bytes 159752 | tf_op jit(solution)/shard_map/ppermute | solution.py:410
  52.4 0.9 %collective-permute-done.12.refs_7_ = f32[104,128]{1,0:T(8,128)S(1)} collective-permute-done((f32[104,128]{1,0:T(8,128)S(1)}, f32[104,128]{1,0:T(8,128)S(1)}, u32[]{:S(2)}, u32[]{:S(2)}) %collective-permute-start.12) | collective-permute-done | bytes 53280 | tf_op jit(solution)/shard_map/ppermute | solution.py:410
  53.3 1.9 %collective-permute-start.13 = (f32[104,128]{1,0:T(8,128)S(1)}, f32[104,128]{1,0:T(8,128)S(1)}, u32[]{:S(2)}, u32[]{:S(2)}) collective-permute-start(f32[104,128]{1,0:T(8,128)S(1)} %fusion.1.refs_9_), channel_id=1, source_target_pairs={{4,8},{8,4},{12,16},{16,12},{20,24},{24,20},{5,9},{9,5},{13,17},{1... | collective-permute-start | bytes 159752 | tf_op jit(solution)/shard_map/ppermute | solution.py:410
  55.2 3.8 %collective-permute-done.13.refs_8_ = f32[104,128]{1,0:T(8,128)S(1)} collective-permute-done((f32[104,128]{1,0:T(8,128)S(1)}, f32[104,128]{1,0:T(8,128)S(1)}, u32[]{:S(2)}, u32[]{:S(2)}) %collective-permute-start.13) | collective-permute-done | bytes 53280 | tf_op jit(solution)/shard_map/ppermute | solution.py:410
  59.0 1.0 %collective-permute-start.14 = (f32[8,128]{1,0:T(8,128)S(1)}, f32[8,128]{1,0:T(8,128)S(1)}, u32[]{:S(2)}, u32[]{:S(2)}) collective-permute-start(f32[8,128]{1,0:T(8,128)S(1)} %slice.57), channel_id=1, source_target_pairs={{0,4},{4,0},{8,12},{12,8},{16,20},{20,16},{24,28},{28,24},{1,5},{5... | collective-permute-start | bytes 12296 | tf_op jit(solution)/shard_map/ppermute | solution.py:410
  60.0 0.8 %collective-permute-done.14.refs_10_ = f32[8,128]{1,0:T(8,128)S(1)} collective-permute-done((f32[8,128]{1,0:T(8,128)S(1)}, f32[8,128]{1,0:T(8,128)S(1)}, u32[]{:S(2)}, u32[]{:S(2)}) %collective-permute-start.14) | collective-permute-done | bytes 4128 | tf_op jit(solution)/shard_map/ppermute | solution.py:410
  60.8 2.4 %filter_step_2.1 = (f32[12,16,128]{2,1,0:T(8,128)S(1)}, f32[104,128]{1,0:T(8,128)S(1)}, f32[104,128]{1,0:T(8,128)S(1)}) custom-call(s32[3,32]{1,0:T(4,128)S(1)} %copy-done.5, s32[9]{0:T(128)S(1)} %copy-done.6, bf16[128,512]{1,0:T(8,128)(2,1)S(1)} %get-tuple-element.44.refs_2_.refs_3_, bf16[384,128]{1,0:T(8,128)(2,1)S(1)} %get-tuple-element.45.refs_3_, ...), custom_call_target="tpu_custom_call" | custom-call | tf_op jit(solution)/shard_map/filter_step_2/pallas_call | solution.py:439
  63.5 0.9 %collective-permute-done.15.refs_7_ = f32[104,128]{1,0:T(8,128)S(1)} collective-permute-done((f32[104,128]{1,0:T(8,128)S(1)}, f32[104,128]{1,0:T(8,128)S(1)}, u32[]{:S(2)}, u32[]{:S(2)}) %collective-permute-start.15) | collective-permute-done | bytes 53280 | tf_op jit(solution)/shard_map/ppermute | solution.py:410
  64.4 1.9 %collective-permute-start.16 = (f32[104,128]{1,0:T(8,128)S(1)}, f32[104,128]{1,0:T(8,128)S(1)}, u32[]{:S(2)}, u32[]{:S(2)}) collective-permute-start(f32[104,128]{1,0:T(8,128)S(1)} %fusion.refs_9_), channel_id=1, source_target_pairs={{4,8},{8,4},{12,16},{16,12},{20,24},{24,20},{5,9},{9,5},{13,17},{1... | collective-permute-start | bytes 159752 | tf_op jit(solution)/shard_map/ppermute | solution.py:410
  66.3 3.8 %collective-permute-done.16.refs_8_ = f32[104,128]{1,0:T(8,128)S(1)} collective-permute-done((f32[104,128]{1,0:T(8,128)S(1)}, f32[104,128]{1,0:T(8,128)S(1)}, u32[]{:S(2)}, u32[]{:S(2)}) %collective-permute-start.16) | collective-permute-done | bytes 53280 | tf_op jit(solution)/shard_map/ppermute | solution.py:410
  70.2 0.9 %collective-permute-start.17 = (f32[8,128]{1,0:T(8,128)S(1)}, f32[8,128]{1,0:T(8,128)S(1)}, u32[]{:S(2)}, u32[]{:S(2)}) collective-permute-start(f32[8,128]{1,0:T(8,128)S(1)} %slice.59), channel_id=1, source_target_pairs={{0,4},{4,0},{8,12},{12,8},{16,20},{20,16},{24,28},{28,24},{1,5},{5... | collective-permute-start | bytes 12296 | tf_op jit(solution)/shard_map/ppermute | solution.py:410
  71.9 2.2 %filter_step_3.1 = f32[12,16,128]{2,1,0:T(8,128)} custom-call(s32[3,32]{1,0:T(4,128)S(1)} %copy-done.5, s32[9]{0:T(128)S(1)} %copy-done.6, bf16[128,512]{1,0:T(8,128)(2,1)S(1)} %get-tuple-element.44.refs_2_.refs_3_, bf16[384,128]{1,0:T(8,128)(2,1)S(1)} %get-tuple-element.45.refs_3_, bf16[192,576]{1,0:T(8,128)(2,1)S(1)} %get-tuple-element.46.refs_4_, ...), custom_call_target="tpu_custom_call" | custom-call | tf_op jit(solution)/shard_map/filter_step_3/pallas_call | solution.py:439
  (50 shorter events, 4.8 us)
Async XLA Ops:
  0.0 5.3 %copy-start.3 = (f32[32,8,512]{2,1,0:T(8,128)S(1)}, f32[32,8,512]{2,1,0:T(8,128)}, u32[]{:S(2)}) copy-start(f32[32,8,512]{2,1,0:T(8,128)} %refs_0_.7) | copy-start | bytes 1572868
  3.9 10.4 %collective-permute-start.2 = (f32[608,128]{1,0:T(8,128)}, f32[608,128]{1,0:T(8,128)S(1)}, u32[]{:S(2)}, u32[]{:S(2)}) collective-permute-start(f32[608,128]{1,0:T(8,128)} %get-tuple-element.49.refs_1_.refs_3_.refs_12_.refs_11_), channel_id=1, source_target_pairs={{0,1},{1,2},{2,3},{3,0},{4,5},{5,6},{6,7},{7,4},{8,9},{9,10},{10,1... | collective-permute-start | bytes 933896 | tf_op jit(solution)/shard_map/ppermute | solution.py:415
  5.3 1.0 %copy-start = (f32[608,128]{1,0:T(8,128)S(1)}, f32[608,128]{1,0:T(8,128)}, u32[]{:S(2)}) copy-start(f32[608,128]{1,0:T(8,128)} %get-tuple-element.49.refs_1_.refs_3_.refs_12_.refs_11_) | copy-start | bytes 933892
  6.3 8.1 %copy-start.1 = (f32[608,128]{1,0:T(8,128)S(1)}, f32[608,128]{1,0:T(8,128)}, u32[]{:S(2)}) copy-start(f32[608,128]{1,0:T(8,128)} %get-tuple-element.49.refs_1_.refs_3_.refs_12_.refs_11_) | copy-start | bytes 933892
  6.3 8.1 %copy-start.5 = (s32[3,32]{1,0:T(4,128)S(1)}, s32[3,32]{1,0:T(4,128)}, u32[]{:S(2)}) copy-start(s32[3,32]{1,0:T(4,128)} %refs_0_.13) | copy-start | bytes 1156
  7.2 9.4 %copy-start.10 = (f32[96,128]{1,0:T(8,128)S(1)}, f32[96,128]{1,0:T(8,128)}, u32[]{:S(2)}) copy-start(f32[96,128]{1,0:T(8,128)} %get-tuple-element.47) | copy-start | bytes 147460
  7.2 12.4 %copy-start.9 = (f32[96,128]{1,0:T(8,128)S(1)}, f32[96,128]{1,0:T(8,128)}, u32[]{:S(2)}) copy-start(f32[96,128]{1,0:T(8,128)} %get-tuple-element.48) | copy-start | bytes 147460
  7.2 15.5 %collective-permute-start.3 = (f32[512,128]{1,0:T(8,128)S(1)}, f32[512,128]{1,0:T(8,128)S(1)}, u32[]{:S(2)}, u32[]{:S(2)}) collective-permute-start(f32[512,128]{1,0:T(8,128)S(1)} %pack_high.1.refs_2_.refs_4_.refs_13_.refs_12_), channel_id=1, source_target_pairs={{0,1},{1,2},{2,3},{3,0},{4,5},{5,6},{6,7},{7,4},{8,9},{9,10},{10,1... | collective-permute-start | bytes 786440 | tf_op jit(solution)/shard_map/ppermute | solution.py:415
  15.2 7.5 %collective-permute-start.5 = (f32[4,8,128]{2,1,0:T(8,128)S(1)}, f32[4,8,128]{2,1,0:T(8,128)S(1)}, u32[]{:S(2)}, u32[]{:S(2)}) collective-permute-start(f32[4,8,128]{2,1,0:T(8,128)S(1)} %get-tuple-element.51), channel_id=1, source_target_pairs={{0,3},{1,0},{2,1},{3,2},{4,7},{5,4},{6,5},{7,6},{8,11},{9,8},{10,9... | collective-permute-start | bytes 49160 | tf_op jit(solution)/shard_map/ppermute | solution.py:415
  16.6 15.4 %collective-permute-start = (f32[96,128]{1,0:T(8,128)S(1)}, f32[96,128]{1,0:T(8,128)S(1)}, u32[]{:S(2)}, u32[]{:S(2)}) collective-permute-start(f32[96,128]{1,0:T(8,128)S(1)} %copy-done.10), channel_id=1, source_target_pairs={{0,4},{4,0},{8,12},{12,8},{16,20},{20,16},{24,28},{28,24},{1,5},{5... | collective-permute-start | bytes 147464 | tf_op jit(solution)/shard_map/ppermute | solution.py:410
  19.6 12.4 %collective-permute-start.1 = (f32[96,128]{1,0:T(8,128)S(1)}, f32[96,128]{1,0:T(8,128)S(1)}, u32[]{:S(2)}, u32[]{:S(2)}) collective-permute-start(f32[96,128]{1,0:T(8,128)S(1)} %copy-done.9), channel_id=1, source_target_pairs={{4,8},{8,4},{12,16},{16,12},{20,24},{24,20},{5,9},{9,5},{13,17},{1... | collective-permute-start | bytes 147464 | tf_op jit(solution)/shard_map/ppermute | solution.py:410
  22.6 9.3 %collective-permute-start.4 = (f32[512,128]{1,0:T(8,128)S(1)}, f32[512,128]{1,0:T(8,128)S(1)}, u32[]{:S(2)}, u32[]{:S(2)}) collective-permute-start(f32[512,128]{1,0:T(8,128)S(1)} %get-tuple-element.50.refs_1_), channel_id=1, source_target_pairs={{0,1},{1,2},{2,3},{3,0},{4,5},{5,6},{6,7},{7,4},{8,9},{9,10},{10,1... | collective-permute-start | bytes 786440 | tf_op jit(solution)/shard_map/ppermute | solution.py:415
  22.7 0.7 copy-start.7
  22.7 14.8 %collective-permute-start.6 = (f32[512,128]{1,0:T(8,128)S(1)}, f32[512,128]{1,0:T(8,128)S(1)}, u32[]{:S(2)}, u32[]{:S(2)}) collective-permute-start(f32[512,128]{1,0:T(8,128)S(1)} %hand_on.3.refs_1_), channel_id=1, source_target_pairs={{0,1},{1,2},{2,3},{3,0},{4,5},{5,6},{6,7},{7,4},{8,9},{9,10},{10,1... | collective-permute-start | bytes 786440 | tf_op jit(solution)/shard_map/ppermute | solution.py:415
  23.4 0.7 copy-start.8
  24.5 7.5 %copy-start.2 = (f32[1,12,16,128]{3,2,1,0:T(8,128)S(1)}, f32[1,12,16,128]{3,2,1,0:T(8,128)}, u32[]{:S(2)}) copy-start(f32[1,12,16,128]{3,2,1,0:T(8,128)} %param.10) | copy-start | bytes 294916
  24.5 7.5 %copy-start.6 = (s32[9]{0:T(128)S(1)}, s32[9]{0:T(128)}, u32[]{:S(2)}) copy-start(s32[9]{0:T(128)} %stack.39.where_ref.refs_1_) | copy-start | bytes 112
  31.9 16.7 %collective-permute-start.10 = (f32[512,128]{1,0:T(8,128)S(1)}, f32[512,128]{1,0:T(8,128)S(1)}, u32[]{:S(2)}, u32[]{:S(2)}) collective-permute-start(f32[512,128]{1,0:T(8,128)S(1)} %hand_on.4.refs_1_), channel_id=1, source_target_pairs={{0,1},{1,2},{2,3},{3,0},{4,5},{5,6},{6,7},{7,4},{8,9},{9,10},{10,1... | collective-permute-start | bytes 786440 | tf_op jit(solution)/shard_map/ppermute | solution.py:415
  37.5 11.2 %copy-start.4 = (f32[12,16,128]{2,1,0:T(8,128)S(1)}, f32[12,16,128]{2,1,0:T(8,128)}, u32[]{:S(2)}) copy-start(f32[12,16,128]{2,1,0:T(8,128)} %refs_6_.5) | copy-start | bytes 294916
  37.5 11.2 %collective-permute-start.11 = (f32[512,128]{1,0:T(8,128)S(1)}, f32[512,128]{1,0:T(8,128)S(1)}, u32[]{:S(2)}, u32[]{:S(2)}) collective-permute-start(f32[512,128]{1,0:T(8,128)S(1)} %hand_on.5), channel_id=1, source_target_pairs={{0,1},{1,2},{2,3},{3,0},{4,5},{5,6},{6,7},{7,4},{8,9},{9,10},{10,1... | collective-permute-start | bytes 786440 | tf_op jit(solution)/shard_map/ppermute | solution.py:415
  38.5 3.0 %collective-permute-start.7 = (f32[16,128]{1,0:T(8,128)S(1)}, f32[16,128]{1,0:T(8,128)S(1)}, u32[]{:S(2)}, u32[]{:S(2)}) collective-permute-start(f32[16,128]{1,0:T(8,128)S(1)} %first_sums.1), channel_id=1, source_target_pairs={{0,4},{4,0},{8,12},{12,8},{16,20},{20,16},{24,28},{28,24},{1,5},{5... | collective-permute-start | bytes 24584 | tf_op jit(solution)/shard_map/ppermute | solution.py:410
  41.5 5.3 %collective-permute-start.8 = (f32[16,128]{1,0:T(8,128)S(1)}, f32[16,128]{1,0:T(8,128)S(1)}, u32[]{:S(2)}, u32[]{:S(2)}) collective-permute-start(f32[16,128]{1,0:T(8,128)S(1)} %add.67.refs_9_), channel_id=1, source_target_pairs={{4,8},{8,4},{12,16},{16,12},{20,24},{24,20},{5,9},{9,5},{13,17},{1... | collective-permute-start | bytes 24584 | tf_op jit(solution)/shard_map/ppermute | solution.py:410
  46.8 1.8 %collective-permute-start.9 = (f32[16,128]{1,0:T(8,128)S(1)}, f32[16,128]{1,0:T(8,128)S(1)}, u32[]{:S(2)}, u32[]{:S(2)}) collective-permute-start(f32[16,128]{1,0:T(8,128)S(1)} %collective-permute-done.8.refs_11_), channel_id=1, source_target_pairs={{0,4},{4,0},{8,12},{12,8},{16,20},{20,16},{24,28},{28,24},{1,5},{5... | collective-permute-start | bytes 24584 | tf_op jit(solution)/shard_map/ppermute | solution.py:410
  51.1 2.2 %collective-permute-start.12 = (f32[104,128]{1,0:T(8,128)S(1)}, f32[104,128]{1,0:T(8,128)S(1)}, u32[]{:S(2)}, u32[]{:S(2)}) collective-permute-start(f32[104,128]{1,0:T(8,128)S(1)} %get-tuple-element.53), channel_id=1, source_target_pairs={{0,4},{4,0},{8,12},{12,8},{16,20},{20,16},{24,28},{28,24},{1,5},{5... | collective-permute-start | bytes 159752 | tf_op jit(solution)/shard_map/ppermute | solution.py:410
  53.3 5.7 %collective-permute-start.13 = (f32[104,128]{1,0:T(8,128)S(1)}, f32[104,128]{1,0:T(8,128)S(1)}, u32[]{:S(2)}, u32[]{:S(2)}) collective-permute-start(f32[104,128]{1,0:T(8,128)S(1)} %fusion.1.refs_9_), channel_id=1, source_target_pairs={{4,8},{8,4},{12,16},{16,12},{20,24},{24,20},{5,9},{9,5},{13,17},{1... | collective-permute-start | bytes 159752 | tf_op jit(solution)/shard_map/ppermute | solution.py:410
  59.0 1.8 %collective-permute-start.14 = (f32[8,128]{1,0:T(8,128)S(1)}, f32[8,128]{1,0:T(8,128)S(1)}, u32[]{:S(2)}, u32[]{:S(2)}) collective-permute-start(f32[8,128]{1,0:T(8,128)S(1)} %slice.57), channel_id=1, source_target_pairs={{0,4},{4,0},{8,12},{12,8},{16,20},{20,16},{24,28},{28,24},{1,5},{5... | collective-permute-start | bytes 12296 | tf_op jit(solution)/shard_map/ppermute | solution.py:410
  63.2 1.2 %collective-permute-start.15 = (f32[104,128]{1,0:T(8,128)S(1)}, f32[104,128]{1,0:T(8,128)S(1)}, u32[]{:S(2)}, u32[]{:S(2)}) collective-permute-start(f32[104,128]{1,0:T(8,128)S(1)} %get-tuple-element.57), channel_id=1, source_target_pairs={{0,4},{4,0},{8,12},{12,8},{16,20},{20,16},{24,28},{28,24},{1,5},{5... | collective-permute-start | bytes 159752 | tf_op jit(solution)/shard_map/ppermute | solution.py:410
  64.4 5.7 %collective-permute-start.16 = (f32[104,128]{1,0:T(8,128)S(1)}, f32[104,128]{1,0:T(8,128)S(1)}, u32[]{:S(2)}, u32[]{:S(2)}) collective-permute-start(f32[104,128]{1,0:T(8,128)S(1)} %fusion.refs_9_), channel_id=1, source_target_pairs={{4,8},{8,4},{12,16},{16,12},{20,24},{24,20},{5,9},{9,5},{13,17},{1... | collective-permute-start | bytes 159752 | tf_op jit(solution)/shard_map/ppermute | solution.py:410
  70.2 1.8 %collective-permute-start.17 = (f32[8,128]{1,0:T(8,128)S(1)}, f32[8,128]{1,0:T(8,128)S(1)}, u32[]{:S(2)}, u32[]{:S(2)}) collective-permute-start(f32[8,128]{1,0:T(8,128)S(1)} %slice.59), channel_id=1, source_target_pairs={{0,4},{4,0},{8,12},{12,8},{16,20},{20,16},{24,28},{28,24},{1,5},{5... | collective-permute-start | bytes 12296 | tf_op jit(solution)/shard_map/ppermute | solution.py:410

commit v5 on v3

--- a/solution.py
+++ b/solution.py
@@ -483,6 +483,7 @@
             low_kernel, "pack_low", [shaped(rows + HALO_ROWS, LANES)] + halos,
             [where], [field, projectors], [],
         )
+        mate, cross = swap(mate, "dom", 0), swap(cross, "dom", 1)
         below_low = turn(low, "band", 1)
         high = call(high_kernel, "pack_high", plane, [], [projectors], [], [low])
         below_high = turn(high, "band", 1)
@@ -498,17 +499,21 @@
 
         on_high = hand_on(below_high, on_low, returned)
         far_high = turn(on_high, "band", 1)
-        on_far_low = hand_on(far_low, on_high)
+        on_far_low = hand_on(far_low, on_high, tables[0], energy)
         above_low = turn(on_far_low, "band", 1)
         near = call(
             near_kernel, "project_near", shaped(*flat), [slot_corner, where],
-            [field, low, high, below_low, below_high, far_low], [],
-        )
-        on_far_high = hand_on(far_high, on_far_low, near, tables[0], energy)
-        above_high = turn(on_far_high, "band", 1)
+            [field, low, high, below_low, below_high, far_low], [], [mate, cross],
+        )
         own = call(
             last_part_kernel, "first_sums", shaped(2 * table_rows, LANES), [slot_corner, where],
             [tables[0], energy, field, near, returned, far_high], [flat],
+        )
+        own = own + swap(own, "dom", 0)
+        on_far_high = hand_on(far_high, own)
+        above_high = turn(on_far_high, "band", 1)
+        own = call(
+            hand_on_kernel, "hold", shaped(*own.shape), [], [own], [], [above_low]
         )
         chunks = [low, high, above_low, above_high, below_low, below_high, far_low, far_high]
     else:
@@ -523,8 +528,8 @@
             whole_sums_kernel, "first_sums", shaped(2 * table_rows, LANES), [slot_corner],
             [tables[0], energy, field, *chunks], [flat],
         )
-    mate, cross = swap(mate, "dom", 0), swap(cross, "dom", 1)
-    own = own + swap(own, "dom", 0)
+        mate, cross = swap(mate, "dom", 0), swap(cross, "dom", 1)
+        own = own + swap(own, "dom", 0)
     other = swap(own, "dom", 1)
     far = swap(other, "dom", 0)
     before = None

time: 72.1 us -> 75.7 us (1.050)
  waiting for transfers between devices: 33.5 us -> 35.5 us
  starting transfers between devices: 22.9 us -> 24.1 us
    ppermute x7, waiting for transfers between devices: 18.3 us -> 20 us  [turn(): lax.ppermute(values, axis, [(i, (i + step) % count) for i in range(count)])]
    ppermute x11, starting transfers between devices: 18.1 us -> 19.7 us  [swap(): return lax.ppermute(values, axis, pairs)]
    pallas_call x12 -> x13, Pallas kernels: 12.3 us -> 12.3 us  [call(): pl.pallas_call(body, out_shape=out_shape, in_specs=[SMEM] * len(scalars)...]
  transfers between devices with their start and end apart: 18 -> 18, of which waited for: 14 -> 13; matrix products, arithmetic and copies ran while one was open for 0% -> 0% of each run, Pallas kernels for 5% -> 5%
where the time goes in v5:
time: 75.7 us; the launch traced here: 75.4 us
  waiting for transfers between devices  35.5 us (47%)
  starting transfers between devices  24.1 us (32%)
  Pallas kernels  12.3 us (16%)
  local copies, waits for them, and re-layouts  3.4 us (4%)
    ppermute x7, waiting for transfers between devices, turn(): lax.ppermute(values, axis, [(i, (i + step) % count) for i in range(count)])  20 us
    ppermute x11, starting transfers between devices, swap(): return lax.ppermute(values, axis, pairs)  19.7 us
    ppermute x11, waiting for transfers between devices, swap(): return lax.ppermute(values, axis, pairs)  15.4 us
    pallas_call x13, Pallas kernels, call(): pl.pallas_call(body, out_shape=out_shape, in_specs=[SMEM] * len(scalars)...  12.3 us
    ppermute x7, starting transfers between devices, turn(): lax.ppermute(values, axis, [(i, (i + step) % count) for i in range(count)])  4.37 us
    unnamed x12, local copies, waits for them, and re-layouts  3.08 us
  transfers between devices with their start and end apart: 18, of which 13 were waited for; matrix products, arithmetic and copies ran while one was open for 0% of the time, Pallas kernels for 5%

profile of v5, /device:TPU:5, one launch (start us, length us, event | category | flops | bytes accessed | tf_op | source)
XLA Modules:
  0.0 75.4 jit_solution(13552008943081297673)
XLA Ops:
  0.9 1.0 %copy-done.1 = f32[32,8,512]{2,1,0:T(8,128)S(1)} copy-done((f32[32,8,512]{2,1,0:T(8,128)S(1)}, f32[32,8,512]{2,1,0:T(8,128)}, u32[]{:S(2)}) %copy-start.1) | copy-done | bytes 524312
  1.9 1.4 %pack_low.1 = (f32[608,128]{1,0:T(8,128)S(1)}, f32[96,128]{1,0:T(8,128)S(1)}, f32[96,128]{1,0:T(8,128)S(1)}) custom-call(s32[9]{0:T(128)S(1)} %stack.39.refs_0_.refs_1_, f32[12,16,128]{2,1,0:T(8,128)S(1)} %bitcast.12, f32[32,8,512]{2,1,0:T(8,128)S(1)} %copy-done.1), custom_call_target="tpu_custom_call" | custom-call | tf_op jit(solution)/shard_map/pack_low/pallas_call | solution.py:430
  3.4 1.3 %collective-permute-start.2 = (f32[608,128]{1,0:T(8,128)S(1)}, f32[608,128]{1,0:T(8,128)S(1)}, u32[]{:S(2)}, u32[]{:S(2)}) collective-permute-start(f32[608,128]{1,0:T(8,128)S(1)} %get-tuple-element.49.refs_1_.refs_3_.refs_12_.refs_11_), channel_id=1, source_target_pairs={{0,1},{1,2},{2,3},{3,0},{4,5},{5,6},{6,7},{7,4},{8,9},{9,10},{10,1... | collective-permute-start | bytes 933896 | tf_op jit(solution)/shard_map/ppermute | solution.py:406
  4.7 0.9 %pack_high.1.refs_2_.refs_4_.refs_13_.refs_12_ = f32[512,128]{1,0:T(8,128)S(1)} custom-call(f32[32,8,512]{2,1,0:T(8,128)S(1)} %copy-done.1, f32[608,128]{1,0:T(8,128)S(1)} %get-tuple-element.49.refs_1_.refs_3_.refs_12_.refs_11_), custom_call_target="tpu_custom_call" | custom-call | tf_op jit(solution)/shard_map/pack_high/pallas_call | solution.py:430
  5.7 1.3 %collective-permute-start.3 = (f32[512,128]{1,0:T(8,128)S(1)}, f32[512,128]{1,0:T(8,128)S(1)}, u32[]{:S(2)}, u32[]{:S(2)}) collective-permute-start(f32[512,128]{1,0:T(8,128)S(1)} %pack_high.1.refs_2_.refs_4_.refs_13_.refs_12_), channel_id=1, source_target_pairs={{0,1},{1,2},{2,3},{3,0},{4,5},{5,6},{6,7},{7,4},{8,9},{9,10},{10,1... | collective-permute-start | bytes 786440 | tf_op jit(solution)/shard_map/ppermute | solution.py:406
  7.0 6.6 %collective-permute-done.2.refs_3_.refs_5_.refs_16_.refs_15_ = f32[608,128]{1,0:T(8,128)S(1)} collective-permute-done((f32[608,128]{1,0:T(8,128)S(1)}, f32[608,128]{1,0:T(8,128)S(1)}, u32[]{:S(2)}, u32[]{:S(2)}) %collective-permute-start.2) | collective-permute-done | bytes 311328 | tf_op jit(solution)/shard_map/ppermute | solution.py:406
  14.4 1.4 %collective-permute-start.5 = (f32[4,8,128]{2,1,0:T(8,128)S(1)}, f32[4,8,128]{2,1,0:T(8,128)S(1)}, u32[]{:S(2)}, u32[]{:S(2)}) collective-permute-start(f32[4,8,128]{2,1,0:T(8,128)S(1)} %get-tuple-element.51), channel_id=1, source_target_pairs={{0,3},{1,0},{2,1},{3,2},{4,7},{5,4},{6,5},{7,6},{8,11},{9,8},{10,9... | collective-permute-start | bytes 49160 | tf_op jit(solution)/shard_map/ppermute | solution.py:406
  15.9 3.0 %collective-permute-start = (f32[96,128]{1,0:T(8,128)S(1)}, f32[96,128]{1,0:T(8,128)S(1)}, u32[]{:S(2)}, u32[]{:S(2)}) collective-permute-start(f32[96,128]{1,0:T(8,128)S(1)} %get-tuple-element.47), channel_id=1, source_target_pairs={{0,4},{4,0},{8,12},{12,8},{16,20},{20,16},{24,28},{28,24},{1,5},{5... | collective-permute-start | bytes 147464 | tf_op jit(solution)/shard_map/ppermute | solution.py:401
  18.8 3.0 %collective-permute-start.1 = (f32[96,128]{1,0:T(8,128)S(1)}, f32[96,128]{1,0:T(8,128)S(1)}, u32[]{:S(2)}, u32[]{:S(2)}) collective-permute-start(f32[96,128]{1,0:T(8,128)S(1)} %get-tuple-element.48), channel_id=1, source_target_pairs={{4,8},{8,4},{12,16},{16,12},{20,24},{24,20},{5,9},{9,5},{13,17},{1... | collective-permute-start | bytes 147464 | tf_op jit(solution)/shard_map/ppermute | solution.py:401
  23.7 7.4 %collective-permute-done.4.refs_7_.refs_0_.refs_18_.refs_17_ = f32[512,128]{1,0:T(8,128)S(1)} collective-permute-done((f32[512,128]{1,0:T(8,128)S(1)}, f32[512,128]{1,0:T(8,128)S(1)}, u32[]{:S(2)}, u32[]{:S(2)}) %collective-permute-start.4) | collective-permute-done | bytes 262176 | tf_op jit(solution)/shard_map/ppermute | solution.py:406
  31.2 1.0 %project_near.1.refs_5_ = f32[4,8,128]{2,1,0:T(8,128)S(1)} custom-call(s32[3,32]{1,0:T(4,128)S(1)} %copy-done.3, s32[9]{0:T(128)S(1)} %stack.39.refs_0_.refs_1_, f32[12,16,128]{2,1,0:T(8,128)S(1)} %bitcast.13, f32[608,128]{1,0:T(8,128)S(1)} %get-tuple-element.49.refs_1_.refs_3_.refs_12_.refs_11_, f32[512,128]{1,0:T(8,128)S(1)} %pack_high.1.refs_2_.refs_4_.refs_13_.refs_12_, ...), custom_call_target="tpu_custom_call" | custom-call | tf_op jit(solution)/shard_map/project_near/pallas_call | solution.py:430
  32.3 4.5 %collective-permute-done.6.refs_7_.refs_0_.refs_19_.refs_18_ = f32[512,128]{1,0:T(8,128)S(1)} collective-permute-done((f32[512,128]{1,0:T(8,128)S(1)}, f32[512,128]{1,0:T(8,128)S(1)}, u32[]{:S(2)}, u32[]{:S(2)}) %collective-permute-start.6) | collective-permute-done | bytes 262176 | tf_op jit(solution)/shard_map/ppermute | solution.py:406
  36.7 0.9 %first_sums.1 = f32[16,128]{1,0:T(8,128)S(1)} custom-call(s32[3,32]{1,0:T(4,128)S(1)} %copy-done.3, s32[9]{0:T(128)S(1)} %stack.39.refs_0_.refs_1_, bf16[128,512]{1,0:T(8,128)(2,1)S(1)} %get-tuple-element.44.refs_2_, f32[8,128]{1,0:T(8,128)S(1)} %broadcast_select_fusion.refs_3_, f32[12,16,128]{2,1,0:T(8,128)S(1)} %bitcast.14, ...), custom_call_target="tpu_custom_call" | custom-call | tf_op jit(solution)/shard_map/first_sums/pallas_call | solution.py:430
  37.6 2.2 %collective-permute-start.7 = (f32[16,128]{1,0:T(8,128)S(1)}, f32[16,128]{1,0:T(8,128)S(1)}, u32[]{:S(2)}, u32[]{:S(2)}) collective-permute-start(f32[16,128]{1,0:T(8,128)S(1)} %first_sums.1), channel_id=1, source_target_pairs={{0,4},{4,0},{8,12},{12,8},{16,20},{20,16},{24,28},{28,24},{1,5},{5... | collective-permute-start | bytes 24584 | tf_op jit(solution)/shard_map/ppermute | solution.py:401
  39.9 0.8 %collective-permute-done.7 = f32[16,128]{1,0:T(8,128)S(1)} collective-permute-done((f32[16,128]{1,0:T(8,128)S(1)}, f32[16,128]{1,0:T(8,128)S(1)}, u32[]{:S(2)}, u32[]{:S(2)}) %collective-permute-start.7) | collective-permute-done | bytes 8224 | tf_op jit(solution)/shard_map/ppermute | solution.py:401
  40.8 1.6 %collective-permute-done.8.refs_1_.refs_14_.refs_13_ = f32[512,128]{1,0:T(8,128)S(1)} collective-permute-done((f32[512,128]{1,0:T(8,128)S(1)}, f32[512,128]{1,0:T(8,128)S(1)}, u32[]{:S(2)}, u32[]{:S(2)}) %collective-permute-start.8) | collective-permute-done | bytes 262176 | tf_op jit(solution)/shard_map/ppermute | solution.py:406
  42.4 1.9 %collective-permute-start.9 = (f32[16,128]{1,0:T(8,128)S(1)}, f32[16,128]{1,0:T(8,128)S(1)}, u32[]{:S(2)}, u32[]{:S(2)}) collective-permute-start(f32[16,128]{1,0:T(8,128)S(1)} %hold.1.refs_9_), channel_id=1, source_target_pairs={{4,8},{8,4},{12,16},{16,12},{20,24},{24,20},{5,9},{9,5},{13,17},{1... | collective-permute-start | bytes 24584 | tf_op jit(solution)/shard_map/ppermute | solution.py:401
  44.3 3.3 %collective-permute-done.9.refs_11_ = f32[16,128]{1,0:T(8,128)S(1)} collective-permute-done((f32[16,128]{1,0:T(8,128)S(1)}, f32[16,128]{1,0:T(8,128)S(1)}, u32[]{:S(2)}, u32[]{:S(2)}) %collective-permute-start.9) | collective-permute-done | bytes 8224 | tf_op jit(solution)/shard_map/ppermute | solution.py:401
  47.6 1.9 %collective-permute-start.10 = (f32[16,128]{1,0:T(8,128)S(1)}, f32[16,128]{1,0:T(8,128)S(1)}, u32[]{:S(2)}, u32[]{:S(2)}) collective-permute-start(f32[16,128]{1,0:T(8,128)S(1)} %collective-permute-done.9.refs_11_), channel_id=1, source_target_pairs={{0,4},{4,0},{8,12},{12,8},{16,20},{20,16},{24,28},{28,24},{1,5},{5... | collective-permute-start | bytes 24584 | tf_op jit(solution)/shard_map/ppermute | solution.py:401
  49.5 0.8 %collective-permute-done.10.refs_10_ = f32[16,128]{1,0:T(8,128)S(1)} collective-permute-done((f32[16,128]{1,0:T(8,128)S(1)}, f32[16,128]{1,0:T(8,128)S(1)}, u32[]{:S(2)}, u32[]{:S(2)}) %collective-permute-start.10) | collective-permute-done | bytes 8224 | tf_op jit(solution)/shard_map/ppermute | solution.py:401
  50.3 2.4 %filter_step_1.1 = (f32[12,16,128]{2,1,0:T(8,128)S(1)}, f32[104,128]{1,0:T(8,128)S(1)}, f32[104,128]{1,0:T(8,128)S(1)}, f32[8,128]{1,0:T(8,128)S(1)}) custom-call(s32[3,32]{1,0:T(4,128)S(1)} %copy-done.3, s32[9]{0:T(128)S(1)} %stack.39.refs_0_.refs_1_, bf16[128,512]{1,0:T(8,128)(2,1)S(1)} %get-tuple-element.44.refs_2_, ...), custom_call_target="tpu_custom_call" | custom-call | tf_op jit(solution)/shard_map/filter_step_1/pallas_call | solution.py:430
  52.7 1.0 %collective-permute-start.12 = (f32[104,128]{1,0:T(8,128)S(1)}, f32[104,128]{1,0:T(8,128)S(1)}, u32[]{:S(2)}, u32[]{:S(2)}) collective-permute-start(f32[104,128]{1,0:T(8,128)S(1)} %get-tuple-element.53), channel_id=1, source_target_pairs={{0,4},{4,0},{8,12},{12,8},{16,20},{20,16},{24,28},{28,24},{1,5},{5... | collective-permute-start | bytes 159752 | tf_op jit(solution)/shard_map/ppermute | solution.py:401
  53.7 0.9 %collective-permute-done.12.refs_7_ = f32[104,128]{1,0:T(8,128)S(1)} collective-permute-done((f32[104,128]{1,0:T(8,128)S(1)}, f32[104,128]{1,0:T(8,128)S(1)}, u32[]{:S(2)}, u32[]{:S(2)}) %collective-permute-start.12) | collective-permute-done | bytes 53280 | tf_op jit(solution)/shard_map/ppermute | solution.py:401
  54.6 2.5 %collective-permute-start.13 = (f32[104,128]{1,0:T(8,128)S(1)}, f32[104,128]{1,0:T(8,128)S(1)}, u32[]{:S(2)}, u32[]{:S(2)}) collective-permute-start(f32[104,128]{1,0:T(8,128)S(1)} %fusion.1.refs_9_), channel_id=1, source_target_pairs={{4,8},{8,4},{12,16},{16,12},{20,24},{24,20},{5,9},{9,5},{13,17},{1... | collective-permute-start | bytes 159752 | tf_op jit(solution)/shard_map/ppermute | solution.py:401
  57.1 3.2 %collective-permute-done.13.refs_8_ = f32[104,128]{1,0:T(8,128)S(1)} collective-permute-done((f32[104,128]{1,0:T(8,128)S(1)}, f32[104,128]{1,0:T(8,128)S(1)}, u32[]{:S(2)}, u32[]{:S(2)}) %collective-permute-start.13) | collective-permute-done | bytes 53280 | tf_op jit(solution)/shard_map/ppermute | solution.py:401
  60.3 1.0 %collective-permute-start.14 = (f32[8,128]{1,0:T(8,128)S(1)}, f32[8,128]{1,0:T(8,128)S(1)}, u32[]{:S(2)}, u32[]{:S(2)}) collective-permute-start(f32[8,128]{1,0:T(8,128)S(1)} %slice.57), channel_id=1, source_target_pairs={{0,4},{4,0},{8,12},{12,8},{16,20},{20,16},{24,28},{28,24},{1,5},{5... | collective-permute-start | bytes 12296 | tf_op jit(solution)/shard_map/ppermute | solution.py:401
  62.1 2.4 %filter_step_2.1 = (f32[12,16,128]{2,1,0:T(8,128)S(1)}, f32[104,128]{1,0:T(8,128)S(1)}, f32[104,128]{1,0:T(8,128)S(1)}) custom-call(s32[3,32]{1,0:T(4,128)S(1)} %copy-done.3, s32[9]{0:T(128)S(1)} %stack.39.refs_0_.refs_1_, bf16[128,512]{1,0:T(8,128)(2,1)S(1)} %get-tuple-element.44.refs_2_, bf16[384,128]{1,0:T(8,128)(2,1)S(1)} %get-tuple-element.45.refs_3_, ...), custom_call_target="tpu_custom_call" | custom-call | tf_op jit(solution)/shard_map/filter_step_2/pallas_call | solution.py:430
  64.8 0.9 %collective-permute-done.15.refs_7_ = f32[104,128]{1,0:T(8,128)S(1)} collective-permute-done((f32[104,128]{1,0:T(8,128)S(1)}, f32[104,128]{1,0:T(8,128)S(1)}, u32[]{:S(2)}, u32[]{:S(2)}) %collective-permute-start.15) | collective-permute-done | bytes 53280 | tf_op jit(solution)/shard_map/ppermute | solution.py:401
  65.7 1.9 %collective-permute-start.16 = (f32[104,128]{1,0:T(8,128)S(1)}, f32[104,128]{1,0:T(8,128)S(1)}, u32[]{:S(2)}, u32[]{:S(2)}) collective-permute-start(f32[104,128]{1,0:T(8,128)S(1)} %fusion.refs_9_), channel_id=1, source_target_pairs={{4,8},{8,4},{12,16},{16,12},{20,24},{24,20},{5,9},{9,5},{13,17},{1... | collective-permute-start | bytes 159752 | tf_op jit(solution)/shard_map/ppermute | solution.py:401
  67.6 3.8 %collective-permute-done.16.refs_8_ = f32[104,128]{1,0:T(8,128)S(1)} collective-permute-done((f32[104,128]{1,0:T(8,128)S(1)}, f32[104,128]{1,0:T(8,128)S(1)}, u32[]{:S(2)}, u32[]{:S(2)}) %collective-permute-start.16) | collective-permute-done | bytes 53280 | tf_op jit(solution)/shard_map/ppermute | solution.py:401
  71.4 0.9 %collective-permute-start.17 = (f32[8,128]{1,0:T(8,128)S(1)}, f32[8,128]{1,0:T(8,128)S(1)}, u32[]{:S(2)}, u32[]{:S(2)}) collective-permute-start(f32[8,128]{1,0:T(8,128)S(1)} %slice.59), channel_id=1, source_target_pairs={{0,4},{4,0},{8,12},{12,8},{16,20},{20,16},{24,28},{28,24},{1,5},{5... | collective-permute-start | bytes 12296 | tf_op jit(solution)/shard_map/ppermute | solution.py:401
  73.2 2.2 %filter_step_3.1 = f32[12,16,128]{2,1,0:T(8,128)} custom-call(s32[3,32]{1,0:T(4,128)S(1)} %copy-done.3, s32[9]{0:T(128)S(1)} %stack.39.refs_0_.refs_1_, bf16[128,512]{1,0:T(8,128)(2,1)S(1)} %get-tuple-element.44.refs_2_, bf16[384,128]{1,0:T(8,128)(2,1)S(1)} %get-tuple-element.45.refs_3_, bf16[192,576]{1,0:T(8,128)(2,1)S(1)} %get-tuple-element.46.refs_4_, ...), custom_call_target="tpu_custom_call" | custom-call | tf_op jit(solution)/shard_map/filter_step_3/pallas_call | solution.py:430
  (41 shorter events, 5.7 us)
Async XLA Ops:
  0.0 0.9 %copy-start = (f32[1,12,16,128]{3,2,1,0:T(8,128)S(1)}, f32[1,12,16,128]{3,2,1,0:T(8,128)}, u32[]{:S(2)}) copy-start(f32[1,12,16,128]{3,2,1,0:T(8,128)} %param.10) | copy-start | bytes 294916
  0.9 1.0 %copy-start.1 = (f32[32,8,512]{2,1,0:T(8,128)S(1)}, f32[32,8,512]{2,1,0:T(8,128)}, u32[]{:S(2)}) copy-start(f32[32,8,512]{2,1,0:T(8,128)} %refs_0_.7) | copy-start | bytes 1572868
  3.4 10.2 %copy-start.3 = (s32[3,32]{1,0:T(4,128)S(1)}, s32[3,32]{1,0:T(4,128)}, u32[]{:S(2)}) copy-start(s32[3,32]{1,0:T(4,128)} %refs_0_.13) | copy-start | bytes 1156
  3.4 10.2 %collective-permute-start.2 = (f32[608,128]{1,0:T(8,128)S(1)}, f32[608,128]{1,0:T(8,128)S(1)}, u32[]{:S(2)}, u32[]{:S(2)}) collective-permute-start(f32[608,128]{1,0:T(8,128)S(1)} %get-tuple-element.49.refs_1_.refs_3_.refs_12_.refs_11_), channel_id=1, source_target_pairs={{0,1},{1,2},{2,3},{3,0},{4,5},{5,6},{6,7},{7,4},{8,9},{9,10},{10,1... | collective-permute-start | bytes 933896 | tf_op jit(solution)/shard_map/ppermute | solution.py:406
  5.7 16.3 %collective-permute-start.3 = (f32[512,128]{1,0:T(8,128)S(1)}, f32[512,128]{1,0:T(8,128)S(1)}, u32[]{:S(2)}, u32[]{:S(2)}) collective-permute-start(f32[512,128]{1,0:T(8,128)S(1)} %pack_high.1.refs_2_.refs_4_.refs_13_.refs_12_), channel_id=1, source_target_pairs={{0,1},{1,2},{2,3},{3,0},{4,5},{5,6},{6,7},{7,4},{8,9},{9,10},{10,1... | collective-permute-start | bytes 786440 | tf_op jit(solution)/shard_map/ppermute | solution.py:406
  14.4 7.5 %collective-permute-start.5 = (f32[4,8,128]{2,1,0:T(8,128)S(1)}, f32[4,8,128]{2,1,0:T(8,128)S(1)}, u32[]{:S(2)}, u32[]{:S(2)}) collective-permute-start(f32[4,8,128]{2,1,0:T(8,128)S(1)} %get-tuple-element.51), channel_id=1, source_target_pairs={{0,3},{1,0},{2,1},{3,2},{4,7},{5,4},{6,5},{7,6},{8,11},{9,8},{10,9... | collective-permute-start | bytes 49160 | tf_op jit(solution)/shard_map/ppermute | solution.py:406
  15.9 15.4 %collective-permute-start = (f32[96,128]{1,0:T(8,128)S(1)}, f32[96,128]{1,0:T(8,128)S(1)}, u32[]{:S(2)}, u32[]{:S(2)}) collective-permute-start(f32[96,128]{1,0:T(8,128)S(1)} %get-tuple-element.47), channel_id=1, source_target_pairs={{0,4},{4,0},{8,12},{12,8},{16,20},{20,16},{24,28},{28,24},{1,5},{5... | collective-permute-start | bytes 147464 | tf_op jit(solution)/shard_map/ppermute | solution.py:401
  18.8 12.4 %collective-permute-start.1 = (f32[96,128]{1,0:T(8,128)S(1)}, f32[96,128]{1,0:T(8,128)S(1)}, u32[]{:S(2)}, u32[]{:S(2)}) collective-permute-start(f32[96,128]{1,0:T(8,128)S(1)} %get-tuple-element.48), channel_id=1, source_target_pairs={{4,8},{8,4},{12,16},{16,12},{20,24},{24,20},{5,9},{9,5},{13,17},{1... | collective-permute-start | bytes 147464 | tf_op jit(solution)/shard_map/ppermute | solution.py:401
  21.8 9.3 %collective-permute-start.4 = (f32[512,128]{1,0:T(8,128)S(1)}, f32[512,128]{1,0:T(8,128)S(1)}, u32[]{:S(2)}, u32[]{:S(2)}) collective-permute-start(f32[512,128]{1,0:T(8,128)S(1)} %get-tuple-element.50.refs_1_), channel_id=1, source_target_pairs={{0,1},{1,2},{2,3},{3,0},{4,5},{5,6},{6,7},{7,4},{8,9},{9,10},{10,1... | collective-permute-start | bytes 786440 | tf_op jit(solution)/shard_map/ppermute | solution.py:406
  21.9 0.7 copy-start.4
  22.0 14.8 %collective-permute-start.6 = (f32[512,128]{1,0:T(8,128)S(1)}, f32[512,128]{1,0:T(8,128)S(1)}, u32[]{:S(2)}, u32[]{:S(2)}) collective-permute-start(f32[512,128]{1,0:T(8,128)S(1)} %hand_on.3.refs_1_), channel_id=1, source_target_pairs={{0,1},{1,2},{2,3},{3,0},{4,5},{5,6},{6,7},{7,4},{8,9},{9,10},{10,1... | collective-permute-start | bytes 786440 | tf_op jit(solution)/shard_map/ppermute | solution.py:406
  22.7 0.7 copy-start.5
  31.2 11.2 %collective-permute-start.8 = (f32[512,128]{1,0:T(8,128)S(1)}, f32[512,128]{1,0:T(8,128)S(1)}, u32[]{:S(2)}, u32[]{:S(2)}) collective-permute-start(f32[512,128]{1,0:T(8,128)S(1)} %hand_on.4), channel_id=1, source_target_pairs={{0,1},{1,2},{2,3},{3,0},{4,5},{5,6},{6,7},{7,4},{8,9},{9,10},{10,1... | collective-permute-start | bytes 786440 | tf_op jit(solution)/shard_map/ppermute | solution.py:406
  37.6 3.1 %collective-permute-start.7 = (f32[16,128]{1,0:T(8,128)S(1)}, f32[16,128]{1,0:T(8,128)S(1)}, u32[]{:S(2)}, u32[]{:S(2)}) collective-permute-start(f32[16,128]{1,0:T(8,128)S(1)} %first_sums.1), channel_id=1, source_target_pairs={{0,4},{4,0},{8,12},{12,8},{16,20},{20,16},{24,28},{28,24},{1,5},{5... | collective-permute-start | bytes 24584 | tf_op jit(solution)/shard_map/ppermute | solution.py:401
  40.7 9.6 %copy-start.2 = (f32[12,16,128]{2,1,0:T(8,128)S(1)}, f32[12,16,128]{2,1,0:T(8,128)}, u32[]{:S(2)}) copy-start(f32[12,16,128]{2,1,0:T(8,128)} %refs_6_.5) | copy-start | bytes 294916
  40.7 9.6 %collective-permute-start.11 = (f32[512,128]{1,0:T(8,128)S(1)}, f32[512,128]{1,0:T(8,128)S(1)}, u32[]{:S(2)}, u32[]{:S(2)}) collective-permute-start(f32[512,128]{1,0:T(8,128)S(1)} %hand_on.5), channel_id=1, source_target_pairs={{0,1},{1,2},{2,3},{3,0},{4,5},{5,6},{6,7},{7,4},{8,9},{9,10},{10,1... | collective-permute-start | bytes 786440 | tf_op jit(solution)/shard_map/ppermute | solution.py:406
  42.4 5.3 %collective-permute-start.9 = (f32[16,128]{1,0:T(8,128)S(1)}, f32[16,128]{1,0:T(8,128)S(1)}, u32[]{:S(2)}, u32[]{:S(2)}) collective-permute-start(f32[16,128]{1,0:T(8,128)S(1)} %hold.1.refs_9_), channel_id=1, source_target_pairs={{4,8},{8,4},{12,16},{16,12},{20,24},{24,20},{5,9},{9,5},{13,17},{1... | collective-permute-start | bytes 24584 | tf_op jit(solution)/shard_map/ppermute | solution.py:401
  47.6 2.7 %collective-permute-start.10 = (f32[16,128]{1,0:T(8,128)S(1)}, f32[16,128]{1,0:T(8,128)S(1)}, u32[]{:S(2)}, u32[]{:S(2)}) collective-permute-start(f32[16,128]{1,0:T(8,128)S(1)} %collective-permute-done.9.refs_11_), channel_id=1, source_target_pairs={{0,4},{4,0},{8,12},{12,8},{16,20},{20,16},{24,28},{28,24},{1,5},{5... | collective-permute-start | bytes 24584 | tf_op jit(solution)/shard_map/ppermute | solution.py:401
  52.7 1.9 %collective-permute-start.12 = (f32[104,128]{1,0:T(8,128)S(1)}, f32[104,128]{1,0:T(8,128)S(1)}, u32[]{:S(2)}, u32[]{:S(2)}) collective-permute-start(f32[104,128]{1,0:T(8,128)S(1)} %get-tuple-element.53), channel_id=1, source_target_pairs={{0,4},{4,0},{8,12},{12,8},{16,20},{20,16},{24,28},{28,24},{1,5},{5... | collective-permute-start | bytes 159752 | tf_op jit(solution)/shard_map/ppermute | solution.py:401
  54.6 5.7 %collective-permute-start.13 = (f32[104,128]{1,0:T(8,128)S(1)}, f32[104,128]{1,0:T(8,128)S(1)}, u32[]{:S(2)}, u32[]{:S(2)}) collective-permute-start(f32[104,128]{1,0:T(8,128)S(1)} %fusion.1.refs_9_), channel_id=1, source_target_pairs={{4,8},{8,4},{12,16},{16,12},{20,24},{24,20},{5,9},{9,5},{13,17},{1... | collective-permute-start | bytes 159752 | tf_op jit(solution)/shard_map/ppermute | solution.py:401
  60.3 1.8 %collective-permute-start.14 = (f32[8,128]{1,0:T(8,128)S(1)}, f32[8,128]{1,0:T(8,128)S(1)}, u32[]{:S(2)}, u32[]{:S(2)}) collective-permute-start(f32[8,128]{1,0:T(8,128)S(1)} %slice.57), channel_id=1, source_target_pairs={{0,4},{4,0},{8,12},{12,8},{16,20},{20,16},{24,28},{28,24},{1,5},{5... | collective-permute-start | bytes 12296 | tf_op jit(solution)/shard_map/ppermute | solution.py:401
  64.5 1.2 %collective-permute-start.15 = (f32[104,128]{1,0:T(8,128)S(1)}, f32[104,128]{1,0:T(8,128)S(1)}, u32[]{:S(2)}, u32[]{:S(2)}) collective-permute-start(f32[104,128]{1,0:T(8,128)S(1)} %get-tuple-element.57), channel_id=1, source_target_pairs={{0,4},{4,0},{8,12},{12,8},{16,20},{20,16},{24,28},{28,24},{1,5},{5... | collective-permute-start | bytes 159752 | tf_op jit(solution)/shard_map/ppermute | solution.py:401
  65.7 5.7 %collective-permute-start.16 = (f32[104,128]{1,0:T(8,128)S(1)}, f32[104,128]{1,0:T(8,128)S(1)}, u32[]{:S(2)}, u32[]{:S(2)}) collective-permute-start(f32[104,128]{1,0:T(8,128)S(1)} %fusion.refs_9_), channel_id=1, source_target_pairs={{4,8},{8,4},{12,16},{16,12},{20,24},{24,20},{5,9},{9,5},{13,17},{1... | collective-permute-start | bytes 159752 | tf_op jit(solution)/shard_map/ppermute | solution.py:401
  71.4 1.8 %collective-permute-start.17 = (f32[8,128]{1,0:T(8,128)S(1)}, f32[8,128]{1,0:T(8,128)S(1)}, u32[]{:S(2)}, u32[]{:S(2)}) collective-permute-start(f32[8,128]{1,0:T(8,128)S(1)} %slice.59), channel_id=1, source_target_pairs={{0,4},{4,0},{8,12},{12,8},{16,20},{20,16},{24,28},{28,24},{1,5},{5... | collective-permute-start | bytes 12296 | tf_op jit(solution)/shard_map/ppermute | solution.py:401

commit v6 on v3

--- a/solution.py
+++ b/solution.py
@@ -283,11 +283,13 @@
     write_halos(field_ref, where_ref[0], mate_ref, cross_ref)
 
 
-def low_kernel(where_ref, field_ref, proj_ref, laden_ref, mate_ref, cross_ref):
+def low_kernel(proj_ref, laden_ref):
+    pack_plane(0, HALVES, proj_ref, laden_ref)
+
+
+def window_kernel(where_ref, field_ref, laden_ref, out_ref):
     window = field_ref[pl.ds(where_ref[FIRST_CHUNK + 2], REACH)]
-    laden_ref[laden_ref.shape[0] - HALO_ROWS :] = window.reshape(HALO_ROWS, LANES)
-    write_halos(field_ref, where_ref[0], mate_ref, cross_ref)
-    pack_plane(0, HALVES, proj_ref, laden_ref)
+    out_ref[out_ref.shape[0] - HALO_ROWS :] = window.reshape(HALO_ROWS, LANES)
 
 
 def above_kernel(corner_ref, own_laden_ref, high_ref, laden_ref, flat_ref, on_ref):
@@ -421,7 +423,7 @@
     def shaped(*shape):
         return jax.ShapeDtypeStruct(shape, jnp.float32)
 
-    def call(kernel, name, out_shape, scalars, operands, scratch, after=()):
+    def call(kernel, name, out_shape, scalars, operands, scratch, after=(), in_place={}):
         inputs = len(scalars) + len(operands)
 
         def body(*refs):
@@ -434,6 +436,7 @@
             out_specs=jax.tree.map(lambda _: VMEM, out_shape),
             scratch_shapes=[pltpu.VMEM(shape, jnp.float32) for shape in scratch],
             compiler_params=pltpu.CompilerParams(vmem_limit_bytes=16 * 2**20),
+            input_output_aliases=in_place,
             cost_estimate=pl.CostEstimate(flops=0, bytes_accessed=0, transcendentals=0),
             name=name,
         )(*scalars, *operands, *after)
@@ -479,9 +482,10 @@
         where = jnp.stack([odd] + [2 * part + h for part in owners for h in range(2)])
         rows = HALVES * groups * ROWS * ROWS
         plane = shaped(rows, LANES)
-        low, mate, cross = call(
-            low_kernel, "pack_low", [shaped(rows + HALO_ROWS, LANES)] + halos,
-            [where], [field, projectors], [],
+        laden = shaped(rows + HALO_ROWS, LANES)
+        low = call(low_kernel, "pack_low", laden, [], [projectors], [])
+        low = call(
+            window_kernel, "add_window", laden, [where], [field, low], [], (), {2: 0}
         )
         below_low = turn(low, "band", 1)
         high = call(high_kernel, "pack_high", plane, [], [projectors], [], [low])
@@ -498,13 +502,17 @@
 
         on_high = hand_on(below_high, on_low, returned)
         far_high = turn(on_high, "band", 1)
-        on_far_low = hand_on(far_low, on_high)
+        on_far_low = hand_on(far_low, on_high, tables[0], energy)
         above_low = turn(on_far_low, "band", 1)
+        mate, cross = call(
+            halo_kernel, "cut_halos", halos, [where], [field], [], [on_far_low]
+        )
+        mate, cross = swap(mate, "dom", 0), swap(cross, "dom", 1)
         near = call(
             near_kernel, "project_near", shaped(*flat), [slot_corner, where],
             [field, low, high, below_low, below_high, far_low], [],
         )
-        on_far_high = hand_on(far_high, on_far_low, near, tables[0], energy)
+        on_far_high = hand_on(far_high, near, tables[0], energy, mate, cross)
         above_high = turn(on_far_high, "band", 1)
         own = call(
             last_part_kernel, "first_sums", shaped(2 * table_rows, LANES), [slot_corner, where],
@@ -523,7 +531,7 @@
             whole_sums_kernel, "first_sums", shaped(2 * table_rows, LANES), [slot_corner],
             [tables[0], energy, field, *chunks], [flat],
         )
-    mate, cross = swap(mate, "dom", 0), swap(cross, "dom", 1)
+        mate, cross = swap(mate, "dom", 0), swap(cross, "dom", 1)
     own = own + swap(own, "dom", 0)
     other = swap(own, "dom", 1)
     far = swap(other, "dom", 0)

time: 72.1 us -> 72.5 us (level)
  starting transfers between devices: 22.9 us -> 24.6 us
  local copies, waits for them, and re-layouts: 2.74 us -> 1.84 us
  waiting for transfers between devices: 33.5 us -> 32.7 us
    ppermute x7, waiting for transfers between devices: 18.3 us -> 15.6 us  [turn(): lax.ppermute(values, axis, [(i, (i + step) % count) for i in range(count)])]
    ppermute x11, starting transfers between devices: 18.1 us -> 20.2 us  [swap(): return lax.ppermute(values, axis, pairs)]
    ppermute x11, waiting for transfers between devices: 15.3 us -> 17.1 us  [swap(): return lax.ppermute(values, axis, pairs)]
    unnamed x12 -> x14, local copies, waits for them, and re-layouts: 2.42 us -> 1.51 us
    pallas_call x12 -> x14, Pallas kernels: 12.3 us -> 12.8 us  [call(): pl.pallas_call(body, out_shape=out_shape, in_specs=[SMEM] * len(scalars)...]
  transfers between devices with their start and end apart: 18 -> 18, of which waited for: 14 -> 15; matrix products, arithmetic and copies ran while one was open for 0% -> 0% of each run, Pallas kernels for 5% -> 6%
where the time goes in v6:
time: 72.5 us; the launch traced here: 72.2 us
  waiting for transfers between devices  32.7 us (45%)
  starting transfers between devices  24.6 us (34%)
  Pallas kernels  12.8 us (18%)
  local copies, waits for them, and re-layouts  1.84 us (3%)
    ppermute x11, starting transfers between devices, swap(): return lax.ppermute(values, axis, pairs)  20.2 us
    ppermute x11, waiting for transfers between devices, swap(): return lax.ppermute(values, axis, pairs)  17.1 us
    ppermute x7, waiting for transfers between devices, turn(): lax.ppermute(values, axis, [(i, (i + step) % count) for i in range(count)])  15.6 us
    pallas_call x14, Pallas kernels, call(): pl.pallas_call(body, out_shape=out_shape, in_specs=[SMEM] * len(scalars)...  12.8 us
    ppermute x7, starting transfers between devices, turn(): lax.ppermute(values, axis, [(i, (i + step) % count) for i in range(count)])  4.39 us
    unnamed x14, local copies, waits for them, and re-layouts  1.51 us
  transfers between devices with their start and end apart: 18, of which 15 were waited for; matrix products, arithmetic and copies ran while one was open for 0% of the time, Pallas kernels for 6%

profile of v6, /device:TPU:5, one launch (start us, length us, event | category | flops | bytes accessed | tf_op | source)
XLA Modules:
  0.0 72.2 jit_solution(13081548588499160912)
XLA Ops:
  0.0 1.0 %copy-done.1 = f32[32,8,512]{2,1,0:T(8,128)S(1)} copy-done((f32[32,8,512]{2,1,0:T(8,128)S(1)}, f32[32,8,512]{2,1,0:T(8,128)}, u32[]{:S(2)}) %copy-start.1) | copy-done | bytes 524312
  1.0 0.9 %pack_low.1.refs_2_ = f32[608,128]{1,0:T(8,128)S(1)} custom-call(f32[32,8,512]{2,1,0:T(8,128)S(1)} %copy-done.1), custom_call_target="tpu_custom_call" | custom-call | tf_op jit(solution)/shard_map/pack_low/pallas_call | solution.py:432
  2.6 1.3 %collective-permute-start = (f32[608,128]{1,0:T(8,128)S(1)}, f32[608,128]{1,0:T(8,128)S(1)}, u32[]{:S(2)}, u32[]{:S(2)}) collective-permute-start(f32[608,128]{1,0:T(8,128)S(1)} %add_window.1.refs_1_.refs_3_.refs_12_.refs_11_), channel_id=1, source_target_pairs={{0,1},{1,2},{2,3},{3,0},{4,5},{5,6},{6,7},{7,4},{8,9},{9,10},{10,1... | collective-permute-start | bytes 933896 | tf_op jit(solution)/shard_map/ppermute | solution.py:408
  4.0 0.9 %pack_high.1.refs_2_.refs_4_.refs_13_.refs_12_ = f32[512,128]{1,0:T(8,128)S(1)} custom-call(f32[32,8,512]{2,1,0:T(8,128)S(1)} %copy-done.2, f32[608,128]{1,0:T(8,128)S(1)} %add_window.1.refs_1_.refs_3_.refs_12_.refs_11_), custom_call_target="tpu_custom_call" | custom-call | tf_op jit(solution)/shard_map/pack_high/pallas_call | solution.py:432
  4.9 1.3 %collective-permute-start.2 = (f32[512,128]{1,0:T(8,128)S(1)}, f32[512,128]{1,0:T(8,128)S(1)}, u32[]{:S(2)}, u32[]{:S(2)}) collective-permute-start(f32[512,128]{1,0:T(8,128)S(1)} %pack_high.1.refs_2_.refs_4_.refs_13_.refs_12_), channel_id=1, source_target_pairs={{0,1},{1,2},{2,3},{3,0},{4,5},{5,6},{6,7},{7,4},{8,9},{9,10},{10,1... | collective-permute-start | bytes 786440 | tf_op jit(solution)/shard_map/ppermute | solution.py:408
  6.2 6.6 %collective-permute-done.refs_3_.refs_5_.refs_16_.refs_15_ = f32[608,128]{1,0:T(8,128)S(1)} collective-permute-done((f32[608,128]{1,0:T(8,128)S(1)}, f32[608,128]{1,0:T(8,128)S(1)}, u32[]{:S(2)}, u32[]{:S(2)}) %collective-permute-start) | collective-permute-done | bytes 311328 | tf_op jit(solution)/shard_map/ppermute | solution.py:408
  13.7 1.4 %collective-permute-start.3 = (f32[4,8,128]{2,1,0:T(8,128)S(1)}, f32[4,8,128]{2,1,0:T(8,128)S(1)}, u32[]{:S(2)}, u32[]{:S(2)}) collective-permute-start(f32[4,8,128]{2,1,0:T(8,128)S(1)} %get-tuple-element.47), channel_id=1, source_target_pairs={{0,3},{1,0},{2,1},{3,2},{4,7},{5,4},{6,5},{7,6},{8,11},{9,8},{10,9... | collective-permute-start | bytes 49160 | tf_op jit(solution)/shard_map/ppermute | solution.py:408
  16.1 2.4 %collective-permute-done.2.refs_0_.refs_6_.refs_17_.refs_16_ = f32[512,128]{1,0:T(8,128)S(1)} collective-permute-done((f32[512,128]{1,0:T(8,128)S(1)}, f32[512,128]{1,0:T(8,128)S(1)}, u32[]{:S(2)}, u32[]{:S(2)}) %collective-permute-start.2) | collective-permute-done | bytes 262176 | tf_op jit(solution)/shard_map/ppermute | solution.py:408
  19.4 3.1 %collective-permute-done.1.refs_0_.refs_7_.refs_18_.refs_17_ = f32[512,128]{1,0:T(8,128)S(1)} collective-permute-done((f32[512,128]{1,0:T(8,128)S(1)}, f32[512,128]{1,0:T(8,128)S(1)}, u32[]{:S(2)}, u32[]{:S(2)}) %collective-permute-start.1) | collective-permute-done | bytes 262176 | tf_op jit(solution)/shard_map/ppermute | solution.py:408
  23.1 5.8 %collective-permute-start.4 = (f32[96,128]{1,0:T(8,128)S(1)}, f32[96,128]{1,0:T(8,128)S(1)}, u32[]{:S(2)}, u32[]{:S(2)}) collective-permute-start(f32[96,128]{1,0:T(8,128)S(1)} %get-tuple-element.48), channel_id=1, source_target_pairs={{0,4},{4,0},{8,12},{12,8},{16,20},{20,16},{24,28},{28,24},{1,5},{5... | collective-permute-start | bytes 147464 | tf_op jit(solution)/shard_map/ppermute | solution.py:403
  28.9 3.0 %collective-permute-start.5 = (f32[96,128]{1,0:T(8,128)S(1)}, f32[96,128]{1,0:T(8,128)S(1)}, u32[]{:S(2)}, u32[]{:S(2)}) collective-permute-start(f32[96,128]{1,0:T(8,128)S(1)} %get-tuple-element.49), channel_id=1, source_target_pairs={{4,8},{8,4},{12,16},{16,12},{20,24},{24,20},{5,9},{9,5},{13,17},{1... | collective-permute-start | bytes 147464 | tf_op jit(solution)/shard_map/ppermute | solution.py:403
  32.0 1.0 %project_near.1.refs_5_.refs_1_ = f32[4,8,128]{2,1,0:T(8,128)S(1)} custom-call(s32[3,32]{1,0:T(4,128)S(1)} %copy-done.4, s32[9]{0:T(128)S(1)} %stack.39.refs_0_.refs_1_, f32[12,16,128]{2,1,0:T(8,128)S(1)} %bitcast.14, f32[608,128]{1,0:T(8,128)S(1)} %add_window.1.refs_1_.refs_3_.refs_12_.refs_11_, f32[512,128]{1,0:T(8,128)S(1)} %pack_high.1.refs_2_.refs_4_.refs_13_.refs_12_, ...), custom_call_target="tpu_custom_call" | custom-call | tf_op jit(solution)/shard_map/project_near/pallas_call | solution.py:432
  33.1 1.5 %collective-permute-done.5.refs_5_.refs_8_ = f32[96,128]{1,0:T(8,128)S(1)} collective-permute-done((f32[96,128]{1,0:T(8,128)S(1)}, f32[96,128]{1,0:T(8,128)S(1)}, u32[]{:S(2)}, u32[]{:S(2)}) %collective-permute-start.5) | collective-permute-done | bytes 49184 | tf_op jit(solution)/shard_map/ppermute | solution.py:403
  34.7 0.9 %first_sums.1 = f32[16,128]{1,0:T(8,128)S(1)} custom-call(s32[3,32]{1,0:T(4,128)S(1)} %copy-done.4, s32[9]{0:T(128)S(1)} %stack.39.refs_0_.refs_1_, bf16[128,512]{1,0:T(8,128)(2,1)S(1)} %get-tuple-element.43.refs_2_, f32[8,128]{1,0:T(8,128)S(1)} %broadcast_select_fusion.refs_3_, f32[12,16,128]{2,1,0:T(8,128)S(1)} %bitcast.15, ...), custom_call_target="tpu_custom_call" | custom-call | tf_op jit(solution)/shard_map/first_sums/pallas_call | solution.py:432
  36.3 0.8 %collective-permute-done.7 = f32[16,128]{1,0:T(8,128)S(1)} collective-permute-done((f32[16,128]{1,0:T(8,128)S(1)}, f32[16,128]{1,0:T(8,128)S(1)}, u32[]{:S(2)}, u32[]{:S(2)}) %collective-permute-start.7) | collective-permute-done | bytes 8224 | tf_op jit(solution)/shard_map/ppermute | solution.py:403
  37.1 2.4 %collective-permute-start.8 = (f32[16,128]{1,0:T(8,128)S(1)}, f32[16,128]{1,0:T(8,128)S(1)}, u32[]{:S(2)}, u32[]{:S(2)}) collective-permute-start(f32[16,128]{1,0:T(8,128)S(1)} %add.67.refs_9_), channel_id=1, source_target_pairs={{4,8},{8,4},{12,16},{16,12},{20,24},{24,20},{5,9},{9,5},{13,17},{1... | collective-permute-start | bytes 24584 | tf_op jit(solution)/shard_map/ppermute | solution.py:403
  39.6 2.8 %collective-permute-done.8.refs_11_ = f32[16,128]{1,0:T(8,128)S(1)} collective-permute-done((f32[16,128]{1,0:T(8,128)S(1)}, f32[16,128]{1,0:T(8,128)S(1)}, u32[]{:S(2)}, u32[]{:S(2)}) %collective-permute-start.8) | collective-permute-done | bytes 8224 | tf_op jit(solution)/shard_map/ppermute | solution.py:403
  42.4 0.9 %collective-permute-start.9 = (f32[16,128]{1,0:T(8,128)S(1)}, f32[16,128]{1,0:T(8,128)S(1)}, u32[]{:S(2)}, u32[]{:S(2)}) collective-permute-start(f32[16,128]{1,0:T(8,128)S(1)} %collective-permute-done.8.refs_11_), channel_id=1, source_target_pairs={{0,4},{4,0},{8,12},{12,8},{16,20},{20,16},{24,28},{28,24},{1,5},{5... | collective-permute-start | bytes 24584 | tf_op jit(solution)/shard_map/ppermute | solution.py:403
  43.3 0.8 %collective-permute-done.9.refs_10_ = f32[16,128]{1,0:T(8,128)S(1)} collective-permute-done((f32[16,128]{1,0:T(8,128)S(1)}, f32[16,128]{1,0:T(8,128)S(1)}, u32[]{:S(2)}, u32[]{:S(2)}) %collective-permute-start.9) | collective-permute-done | bytes 8224 | tf_op jit(solution)/shard_map/ppermute | solution.py:403
  44.1 2.7 %collective-permute-done.11.refs_15_.refs_14_ = f32[512,128]{1,0:T(8,128)S(1)} collective-permute-done((f32[512,128]{1,0:T(8,128)S(1)}, f32[512,128]{1,0:T(8,128)S(1)}, u32[]{:S(2)}, u32[]{:S(2)}) %collective-permute-start.11) | collective-permute-done | bytes 262176 | tf_op jit(solution)/shard_map/ppermute | solution.py:408
  46.9 2.4 %filter_step_1.1 = (f32[12,16,128]{2,1,0:T(8,128)S(1)}, f32[104,128]{1,0:T(8,128)S(1)}, f32[104,128]{1,0:T(8,128)S(1)}, f32[8,128]{1,0:T(8,128)S(1)}) custom-call(s32[3,32]{1,0:T(4,128)S(1)} %copy-done.4, s32[9]{0:T(128)S(1)} %stack.39.refs_0_.refs_1_, bf16[128,512]{1,0:T(8,128)(2,1)S(1)} %get-tuple-element.43.refs_2_, ...), custom_call_target="tpu_custom_call" | custom-call | tf_op jit(solution)/shard_map/filter_step_1/pallas_call | solution.py:432
  49.2 1.3 %collective-permute-start.12 = (f32[104,128]{1,0:T(8,128)S(1)}, f32[104,128]{1,0:T(8,128)S(1)}, u32[]{:S(2)}, u32[]{:S(2)}) collective-permute-start(f32[104,128]{1,0:T(8,128)S(1)} %get-tuple-element.51), channel_id=1, source_target_pairs={{0,4},{4,0},{8,12},{12,8},{16,20},{20,16},{24,28},{28,24},{1,5},{5... | collective-permute-start | bytes 159752 | tf_op jit(solution)/shard_map/ppermute | solution.py:403
  50.5 0.9 %collective-permute-done.12.refs_7_ = f32[104,128]{1,0:T(8,128)S(1)} collective-permute-done((f32[104,128]{1,0:T(8,128)S(1)}, f32[104,128]{1,0:T(8,128)S(1)}, u32[]{:S(2)}, u32[]{:S(2)}) %collective-permute-start.12) | collective-permute-done | bytes 53280 | tf_op jit(solution)/shard_map/ppermute | solution.py:403
  51.4 1.9 %collective-permute-start.13 = (f32[104,128]{1,0:T(8,128)S(1)}, f32[104,128]{1,0:T(8,128)S(1)}, u32[]{:S(2)}, u32[]{:S(2)}) collective-permute-start(f32[104,128]{1,0:T(8,128)S(1)} %fusion.1.refs_9_), channel_id=1, source_target_pairs={{4,8},{8,4},{12,16},{16,12},{20,24},{24,20},{5,9},{9,5},{13,17},{1... | collective-permute-start | bytes 159752 | tf_op jit(solution)/shard_map/ppermute | solution.py:403
  53.3 3.8 %collective-permute-done.13.refs_8_ = f32[104,128]{1,0:T(8,128)S(1)} collective-permute-done((f32[104,128]{1,0:T(8,128)S(1)}, f32[104,128]{1,0:T(8,128)S(1)}, u32[]{:S(2)}, u32[]{:S(2)}) %collective-permute-start.13) | collective-permute-done | bytes 53280 | tf_op jit(solution)/shard_map/ppermute | solution.py:403
  57.1 1.0 %collective-permute-start.14 = (f32[8,128]{1,0:T(8,128)S(1)}, f32[8,128]{1,0:T(8,128)S(1)}, u32[]{:S(2)}, u32[]{:S(2)}) collective-permute-start(f32[8,128]{1,0:T(8,128)S(1)} %slice.57), channel_id=1, source_target_pairs={{0,4},{4,0},{8,12},{12,8},{16,20},{20,16},{24,28},{28,24},{1,5},{5... | collective-permute-start | bytes 12296 | tf_op jit(solution)/shard_map/ppermute | solution.py:403
  58.9 2.4 %filter_step_2.1 = (f32[12,16,128]{2,1,0:T(8,128)S(1)}, f32[104,128]{1,0:T(8,128)S(1)}, f32[104,128]{1,0:T(8,128)S(1)}) custom-call(s32[3,32]{1,0:T(4,128)S(1)} %copy-done.4, s32[9]{0:T(128)S(1)} %stack.39.refs_0_.refs_1_, bf16[128,512]{1,0:T(8,128)(2,1)S(1)} %get-tuple-element.43.refs_2_, bf16[384,128]{1,0:T(8,128)(2,1)S(1)} %get-tuple-element.44.refs_3_, ...), custom_call_target="tpu_custom_call" | custom-call | tf_op jit(solution)/shard_map/filter_step_2/pallas_call | solution.py:432
  61.6 0.9 %collective-permute-done.15.refs_7_ = f32[104,128]{1,0:T(8,128)S(1)} collective-permute-done((f32[104,128]{1,0:T(8,128)S(1)}, f32[104,128]{1,0:T(8,128)S(1)}, u32[]{:S(2)}, u32[]{:S(2)}) %collective-permute-start.15) | collective-permute-done | bytes 53280 | tf_op jit(solution)/shard_map/ppermute | solution.py:403
  62.5 1.9 %collective-permute-start.16 = (f32[104,128]{1,0:T(8,128)S(1)}, f32[104,128]{1,0:T(8,128)S(1)}, u32[]{:S(2)}, u32[]{:S(2)}) collective-permute-start(f32[104,128]{1,0:T(8,128)S(1)} %fusion.refs_9_), channel_id=1, source_target_pairs={{4,8},{8,4},{12,16},{16,12},{20,24},{24,20},{5,9},{9,5},{13,17},{1... | collective-permute-start | bytes 159752 | tf_op jit(solution)/shard_map/ppermute | solution.py:403
  64.4 3.8 %collective-permute-done.16.refs_8_ = f32[104,128]{1,0:T(8,128)S(1)} collective-permute-done((f32[104,128]{1,0:T(8,128)S(1)}, f32[104,128]{1,0:T(8,128)S(1)}, u32[]{:S(2)}, u32[]{:S(2)}) %collective-permute-start.16) | collective-permute-done | bytes 53280 | tf_op jit(solution)/shard_map/ppermute | solution.py:403
  68.3 0.9 %collective-permute-start.17 = (f32[8,128]{1,0:T(8,128)S(1)}, f32[8,128]{1,0:T(8,128)S(1)}, u32[]{:S(2)}, u32[]{:S(2)}) collective-permute-start(f32[8,128]{1,0:T(8,128)S(1)} %slice.59), channel_id=1, source_target_pairs={{0,4},{4,0},{8,12},{12,8},{16,20},{20,16},{24,28},{28,24},{1,5},{5... | collective-permute-start | bytes 12296 | tf_op jit(solution)/shard_map/ppermute | solution.py:403
  70.0 2.2 %filter_step_3.1 = f32[12,16,128]{2,1,0:T(8,128)} custom-call(s32[3,32]{1,0:T(4,128)S(1)} %copy-done.4, s32[9]{0:T(128)S(1)} %stack.39.refs_0_.refs_1_, bf16[128,512]{1,0:T(8,128)(2,1)S(1)} %get-tuple-element.43.refs_2_, bf16[384,128]{1,0:T(8,128)(2,1)S(1)} %get-tuple-element.44.refs_3_, bf16[192,576]{1,0:T(8,128)(2,1)S(1)} %get-tuple-element.45.refs_4_, ...), custom_call_target="tpu_custom_call" | custom-call | tf_op jit(solution)/shard_map/filter_step_3/pallas_call | solution.py:432
  (44 shorter events, 6.7 us)
Async XLA Ops:
  0.0 1.0 %copy-start.1 = (f32[32,8,512]{2,1,0:T(8,128)S(1)}, f32[32,8,512]{2,1,0:T(8,128)}, u32[]{:S(2)}) copy-start(f32[32,8,512]{2,1,0:T(8,128)} %refs_0_.9) | copy-start | bytes 1572868
  1.0 1.0 %copy-start = (f32[1,12,16,128]{3,2,1,0:T(8,128)S(1)}, f32[1,12,16,128]{3,2,1,0:T(8,128)}, u32[]{:S(2)}) copy-start(f32[1,12,16,128]{3,2,1,0:T(8,128)} %param.10) | copy-start | bytes 294916
  1.9 2.0 %copy-start.2 = (f32[32,8,512]{2,1,0:T(8,128)S(1)}, f32[32,8,512]{2,1,0:T(8,128)}, u32[]{:S(2)}) copy-start(f32[32,8,512]{2,1,0:T(8,128)} %refs_0_.9) | copy-start | bytes 1572868
  2.6 10.2 %copy-start.4 = (s32[3,32]{1,0:T(4,128)S(1)}, s32[3,32]{1,0:T(4,128)}, u32[]{:S(2)}) copy-start(s32[3,32]{1,0:T(4,128)} %refs_0_.15) | copy-start | bytes 1156
  2.6 10.2 %collective-permute-start = (f32[608,128]{1,0:T(8,128)S(1)}, f32[608,128]{1,0:T(8,128)S(1)}, u32[]{:S(2)}, u32[]{:S(2)}) collective-permute-start(f32[608,128]{1,0:T(8,128)S(1)} %add_window.1.refs_1_.refs_3_.refs_12_.refs_11_), channel_id=1, source_target_pairs={{0,1},{1,2},{2,3},{3,0},{4,5},{5,6},{6,7},{7,4},{8,9},{9,10},{10,1... | collective-permute-start | bytes 933896 | tf_op jit(solution)/shard_map/ppermute | solution.py:408
  4.9 13.6 %collective-permute-start.2 = (f32[512,128]{1,0:T(8,128)S(1)}, f32[512,128]{1,0:T(8,128)S(1)}, u32[]{:S(2)}, u32[]{:S(2)}) collective-permute-start(f32[512,128]{1,0:T(8,128)S(1)} %pack_high.1.refs_2_.refs_4_.refs_13_.refs_12_), channel_id=1, source_target_pairs={{0,1},{1,2},{2,3},{3,0},{4,5},{5,6},{6,7},{7,4},{8,9},{9,10},{10,1... | collective-permute-start | bytes 786440 | tf_op jit(solution)/shard_map/ppermute | solution.py:408
  12.8 2.3 %copy-start.6 = (s32[32]{0:T(128)S(1)}, s32[32]{0:T(128)}, u32[]{:S(2)}) copy-start(s32[32]{0:T(128)} %param.14) | copy-start | bytes 388
  13.7 5.6 %collective-permute-start.3 = (f32[4,8,128]{2,1,0:T(8,128)S(1)}, f32[4,8,128]{2,1,0:T(8,128)S(1)}, u32[]{:S(2)}, u32[]{:S(2)}) collective-permute-start(f32[4,8,128]{2,1,0:T(8,128)S(1)} %get-tuple-element.47), channel_id=1, source_target_pairs={{0,3},{1,0},{2,1},{3,2},{4,7},{5,4},{6,5},{7,6},{8,11},{9,8},{10,9... | collective-permute-start | bytes 49160 | tf_op jit(solution)/shard_map/ppermute | solution.py:408
  15.1 0.7 copy-start.5
  15.1 7.4 %collective-permute-start.1 = (f32[512,128]{1,0:T(8,128)S(1)}, f32[512,128]{1,0:T(8,128)S(1)}, u32[]{:S(2)}, u32[]{:S(2)}) collective-permute-start(f32[512,128]{1,0:T(8,128)S(1)} %get-tuple-element.46.refs_1_), channel_id=1, source_target_pairs={{0,1},{1,2},{2,3},{3,0},{4,5},{5,6},{6,7},{7,4},{8,9},{9,10},{10,1... | collective-permute-start | bytes 786440 | tf_op jit(solution)/shard_map/ppermute | solution.py:408
  19.3 13.7 %collective-permute-start.6 = (f32[512,128]{1,0:T(8,128)S(1)}, f32[512,128]{1,0:T(8,128)S(1)}, u32[]{:S(2)}, u32[]{:S(2)}) collective-permute-start(f32[512,128]{1,0:T(8,128)S(1)} %hand_on.3.refs_1_), channel_id=1, source_target_pairs={{0,1},{1,2},{2,3},{3,0},{4,5},{5,6},{6,7},{7,4},{8,9},{9,10},{10,1... | collective-permute-start | bytes 786440 | tf_op jit(solution)/shard_map/ppermute | solution.py:408
  23.1 10.0 %collective-permute-start.4 = (f32[96,128]{1,0:T(8,128)S(1)}, f32[96,128]{1,0:T(8,128)S(1)}, u32[]{:S(2)}, u32[]{:S(2)}) collective-permute-start(f32[96,128]{1,0:T(8,128)S(1)} %get-tuple-element.48), channel_id=1, source_target_pairs={{0,4},{4,0},{8,12},{12,8},{16,20},{20,16},{24,28},{28,24},{1,5},{5... | collective-permute-start | bytes 147464 | tf_op jit(solution)/shard_map/ppermute | solution.py:403
  28.9 5.7 %collective-permute-start.5 = (f32[96,128]{1,0:T(8,128)S(1)}, f32[96,128]{1,0:T(8,128)S(1)}, u32[]{:S(2)}, u32[]{:S(2)}) collective-permute-start(f32[96,128]{1,0:T(8,128)S(1)} %get-tuple-element.49), channel_id=1, source_target_pairs={{4,8},{8,4},{12,16},{16,12},{20,24},{24,20},{5,9},{9,5},{13,17},{1... | collective-permute-start | bytes 147464 | tf_op jit(solution)/shard_map/ppermute | solution.py:403
  31.9 12.2 %collective-permute-start.10 = (f32[512,128]{1,0:T(8,128)S(1)}, f32[512,128]{1,0:T(8,128)S(1)}, u32[]{:S(2)}, u32[]{:S(2)}) collective-permute-start(f32[512,128]{1,0:T(8,128)S(1)} %hand_on.4.refs_2_), channel_id=1, source_target_pairs={{0,1},{1,2},{2,3},{3,0},{4,5},{5,6},{6,7},{7,4},{8,9},{9,10},{10,1... | collective-permute-start | bytes 786440 | tf_op jit(solution)/shard_map/ppermute | solution.py:408
  34.6 12.2 %copy-start.3 = (f32[12,16,128]{2,1,0:T(8,128)S(1)}, f32[12,16,128]{2,1,0:T(8,128)}, u32[]{:S(2)}) copy-start(f32[12,16,128]{2,1,0:T(8,128)} %refs_6_.5) | copy-start | bytes 294916
  34.6 12.2 %collective-permute-start.11 = (f32[512,128]{1,0:T(8,128)S(1)}, f32[512,128]{1,0:T(8,128)S(1)}, u32[]{:S(2)}, u32[]{:S(2)}) collective-permute-start(f32[512,128]{1,0:T(8,128)S(1)} %hand_on.5), channel_id=1, source_target_pairs={{0,1},{1,2},{2,3},{3,0},{4,5},{5,6},{6,7},{7,4},{8,9},{9,10},{10,1... | collective-permute-start | bytes 786440 | tf_op jit(solution)/shard_map/ppermute | solution.py:408
  35.6 1.5 %collective-permute-start.7 = (f32[16,128]{1,0:T(8,128)S(1)}, f32[16,128]{1,0:T(8,128)S(1)}, u32[]{:S(2)}, u32[]{:S(2)}) collective-permute-start(f32[16,128]{1,0:T(8,128)S(1)} %first_sums.1), channel_id=1, source_target_pairs={{0,4},{4,0},{8,12},{12,8},{16,20},{20,16},{24,28},{28,24},{1,5},{5... | collective-permute-start | bytes 24584 | tf_op jit(solution)/shard_map/ppermute | solution.py:403
  37.1 5.3 %collective-permute-start.8 = (f32[16,128]{1,0:T(8,128)S(1)}, f32[16,128]{1,0:T(8,128)S(1)}, u32[]{:S(2)}, u32[]{:S(2)}) collective-permute-start(f32[16,128]{1,0:T(8,128)S(1)} %add.67.refs_9_), channel_id=1, source_target_pairs={{4,8},{8,4},{12,16},{16,12},{20,24},{24,20},{5,9},{9,5},{13,17},{1... | collective-permute-start | bytes 24584 | tf_op jit(solution)/shard_map/ppermute | solution.py:403
  42.4 1.8 %collective-permute-start.9 = (f32[16,128]{1,0:T(8,128)S(1)}, f32[16,128]{1,0:T(8,128)S(1)}, u32[]{:S(2)}, u32[]{:S(2)}) collective-permute-start(f32[16,128]{1,0:T(8,128)S(1)} %collective-permute-done.8.refs_11_), channel_id=1, source_target_pairs={{0,4},{4,0},{8,12},{12,8},{16,20},{20,16},{24,28},{28,24},{1,5},{5... | collective-permute-start | bytes 24584 | tf_op jit(solution)/shard_map/ppermute | solution.py:403
  49.2 2.2 %collective-permute-start.12 = (f32[104,128]{1,0:T(8,128)S(1)}, f32[104,128]{1,0:T(8,128)S(1)}, u32[]{:S(2)}, u32[]{:S(2)}) collective-permute-start(f32[104,128]{1,0:T(8,128)S(1)} %get-tuple-element.51), channel_id=1, source_target_pairs={{0,4},{4,0},{8,12},{12,8},{16,20},{20,16},{24,28},{28,24},{1,5},{5... | collective-permute-start | bytes 159752 | tf_op jit(solution)/shard_map/ppermute | solution.py:403
  51.4 5.7 %collective-permute-start.13 = (f32[104,128]{1,0:T(8,128)S(1)}, f32[104,128]{1,0:T(8,128)S(1)}, u32[]{:S(2)}, u32[]{:S(2)}) collective-permute-start(f32[104,128]{1,0:T(8,128)S(1)} %fusion.1.refs_9_), channel_id=1, source_target_pairs={{4,8},{8,4},{12,16},{16,12},{20,24},{24,20},{5,9},{9,5},{13,17},{1... | collective-permute-start | bytes 159752 | tf_op jit(solution)/shard_map/ppermute | solution.py:403
  57.1 1.8 %collective-permute-start.14 = (f32[8,128]{1,0:T(8,128)S(1)}, f32[8,128]{1,0:T(8,128)S(1)}, u32[]{:S(2)}, u32[]{:S(2)}) collective-permute-start(f32[8,128]{1,0:T(8,128)S(1)} %slice.57), channel_id=1, source_target_pairs={{0,4},{4,0},{8,12},{12,8},{16,20},{20,16},{24,28},{28,24},{1,5},{5... | collective-permute-start | bytes 12296 | tf_op jit(solution)/shard_map/ppermute | solution.py:403
  61.3 1.2 %collective-permute-start.15 = (f32[104,128]{1,0:T(8,128)S(1)}, f32[104,128]{1,0:T(8,128)S(1)}, u32[]{:S(2)}, u32[]{:S(2)}) collective-permute-start(f32[104,128]{1,0:T(8,128)S(1)} %get-tuple-element.55), channel_id=1, source_target_pairs={{0,4},{4,0},{8,12},{12,8},{16,20},{20,16},{24,28},{28,24},{1,5},{5... | collective-permute-start | bytes 159752 | tf_op jit(solution)/shard_map/ppermute | solution.py:403
  62.5 5.7 %collective-permute-start.16 = (f32[104,128]{1,0:T(8,128)S(1)}, f32[104,128]{1,0:T(8,128)S(1)}, u32[]{:S(2)}, u32[]{:S(2)}) collective-permute-start(f32[104,128]{1,0:T(8,128)S(1)} %fusion.refs_9_), channel_id=1, source_target_pairs={{4,8},{8,4},{12,16},{16,12},{20,24},{24,20},{5,9},{9,5},{13,17},{1... | collective-permute-start | bytes 159752 | tf_op jit(solution)/shard_map/ppermute | solution.py:403
  68.3 1.8 %collective-permute-start.17 = (f32[8,128]{1,0:T(8,128)S(1)}, f32[8,128]{1,0:T(8,128)S(1)}, u32[]{:S(2)}, u32[]{:S(2)}) collective-permute-start(f32[8,128]{1,0:T(8,128)S(1)} %slice.59), channel_id=1, source_target_pairs={{0,4},{4,0},{8,12},{12,8},{16,20},{20,16},{24,28},{28,24},{1,5},{5... | collective-permute-start | bytes 12296 | tf_op jit(solution)/shard_map/ppermute | solution.py:403

commit v7 on v6

--- a/solution.py
+++ b/solution.py
@@ -33,7 +33,7 @@
 CENTRE = (UPPER_EDGE + LOWER_EDGE) / 2.0
 SIGMA_FIRST = HALF_WIDTH / (ANCHOR_POINT - CENTRE)
 COPIES = 4
-FIRST_CHUNK = 1
+PARTS_FROM = (0, 1, 3, 2)
 
 
 def step_factors():
@@ -44,6 +44,15 @@
         factors.append((2.0 * sigma_next / HALF_WIDTH, sigma_now * sigma_next))
         sigma_now = sigma_next
     return factors
+
+
+def odd_here():
+    return lax.rem(lax.axis_index("dom"), 2)
+
+
+def plane_here(index):
+    owner = lax.rem(lax.axis_index("band") + PARTS_FROM[index // 2], 4)
+    return owner * 2 + index % 2
 
 
 def iota(shape, dim):
@@ -174,29 +183,31 @@
     )
 
 
-def deposit(scaled, chunks, corner_ref, member_ref, flat_ref, box_ref, parts_ref):
+def box_values(scaled, chunks, member_ref, flat_ref, box_ref):
     groups = flat_ref.shape[0]
-    copies = parts_ref.shape[0]
-    lane_block = iota((ROWS, LANES), 1) // SZ
     flat = sum_thirds(
         jnp.dot(thirds_of(scaled), member_ref[...], preferred_element_type=jnp.float32)
     )
     for g in range(groups):
         flat_ref[g] = flat[:, g * LANES : (g + 1) * LANES]
-    parts_ref[...] = jnp.zeros(parts_ref.shape, jnp.float32)
-
-    def one(group, carry):
+    for group in range(groups):
         factors = [
             jnp.broadcast_to(flat_ref[group, pl.ds(p, 1), :], (ROWS, LANES)) for p in range(ROWS)
         ]
         for plane, ref, base in chunks:
             for half in range(HALVES):
-                box_ref[plane * HALVES + half] = total_of(
+                box_ref[group, plane * HALVES + half] = total_of(
                     [
                         values_of(ref, base, groups, half, group, p) * factors[p]
                         for p in range(ROWS)
                     ]
                 )
+
+
+def deposit(corner_ref, box_ref, parts_ref):
+    copies = parts_ref.shape[0]
+    lane_block = iota((ROWS, LANES), 1) // SZ
+    for group in range(box_ref.shape[0]):
         for u in range(ROWS):
             slot = group * ROWS + u
             planes = pl.ds(corner_ref[0, slot], SX)
@@ -205,15 +216,11 @@
                 at = (u % copies, planes, pl.ds(half * ROWS, ROWS), slice(None))
                 added = [
                     pltpu.roll(
-                        jnp.where(lane_block == u, box_ref[x * HALVES + half], 0.0), shift, 1
+                        jnp.where(lane_block == u, box_ref[group, x * HALVES + half], 0.0), shift, 1
                     )
                     for x in range(SX)
                 ]
                 parts_ref[at] = parts_ref[at] + jnp.stack(added)
-        return carry
-
-    for group in range(groups):
-        one(group, 0)
 
 
 def band_matrix(size, block, centre):
@@ -271,24 +278,24 @@
     return [(x, ref, x * rows) for x in range(SX)]
 
 
-def some_planes(where_ref, first, refs):
-    return [(where_ref[FIRST_CHUNK + first + i], ref, 0) for i, ref in enumerate(refs)]
+def some_planes(first, refs):
+    return [(plane_here(first + i), ref, 0) for i, ref in enumerate(refs)]
 
 
 def field_reader(ref):
     return lambda x, half: ref[x, pl.ds(half * ROWS, ROWS), :]
 
 
-def halo_kernel(where_ref, field_ref, mate_ref, cross_ref):
-    write_halos(field_ref, where_ref[0], mate_ref, cross_ref)
+def halo_kernel(field_ref, mate_ref, cross_ref):
+    write_halos(field_ref, odd_here(), mate_ref, cross_ref)
 
 
 def low_kernel(proj_ref, laden_ref):
     pack_plane(0, HALVES, proj_ref, laden_ref)
 
 
-def window_kernel(where_ref, field_ref, laden_ref, out_ref):
-    window = field_ref[pl.ds(where_ref[FIRST_CHUNK + 2], REACH)]
+def window_kernel(field_ref, laden_ref, out_ref):
+    window = field_ref[pl.ds(plane_here(2), REACH)]
     out_ref[out_ref.shape[0] - HALO_ROWS :] = window.reshape(HALO_ROWS, LANES)
 
 
@@ -306,8 +313,8 @@
     out_ref[...] = given_ref[...]
 
 
-def near_kernel(corner_ref, where_ref, field_ref, low_ref, high_ref, *refs):
-    chunks = some_planes(where_ref, 0, [low_ref, high_ref]) + some_planes(where_ref, 4, refs[:-1])
+def near_kernel(corner_ref, field_ref, low_ref, high_ref, *refs):
+    chunks = some_planes(0, [low_ref, high_ref]) + some_planes(4, refs[:-1])
     project(field_reader(field_ref), chunks, corner_ref, refs[-1])
 
 
@@ -316,10 +323,10 @@
     out_ref[...] = jnp.concatenate([to_rows(sums), to_rows(energy_ref[...])], axis=0)
 
 
-def last_part_kernel(corner_ref, where_ref, member_ref, energy_ref, field_ref, near_ref,
+def last_part_kernel(corner_ref, member_ref, energy_ref, field_ref, near_ref,
                      returned_ref, far_ref, out_ref, flat_ref):
     flat_ref[...] = near_ref[...] + returned_ref[...]
-    chunks = some_planes(where_ref, 7, [far_ref])
+    chunks = some_planes(7, [far_ref])
     project(field_reader(field_ref), chunks, corner_ref, flat_ref, flat_ref)
     write_table(flat_ref, member_ref, energy_ref, out_ref)
 
@@ -337,37 +344,40 @@
     write_table(flat_ref, member_ref, energy_ref, out_ref)
 
 
-def step_kernel(index, chunk_count, corner_ref, where_ref, member_ref, along_z_ref, along_y_ref,
-                field_ref, potential_ref, mate_ref, cross_ref, *refs):
+def step_kernel(index, chunk_count, member_ref, along_z_ref, along_y_ref, field_ref, potential_ref,
+                mate_ref, cross_ref, *refs):
     factors = step_factors()
     is_first, is_last = index == 0, index + 1 == len(factors)
     refs = list(refs)
-    odd = where_ref[0]
+    odd = odd_here()
     own_ref, far_ref = refs.pop(0), refs.pop(0)
     if is_first:
         table = from_rows(own_ref[...] + refs.pop(0)[...] + far_ref[...])
     else:
         table = from_rows(own_ref[HALO_ROWS:] + cross_ref[HALO_ROWS:] + far_ref[...])
     if chunk_count > 1:
-        chunks = some_planes(where_ref, 0, refs[:chunk_count])
+        chunks = some_planes(0, refs[:chunk_count])
     else:
         chunks = all_planes(refs[0])
     refs = refs[chunk_count:]
     energy_ref = None if is_first else refs.pop(0)
     before_ref = None if is_first else refs.pop(0)
+    corner_hbm = refs.pop(0)
     next_ref = refs.pop(0)
     if not is_last:
         next_mate_ref, next_cross_ref = refs.pop(0), refs.pop(0)
     if is_first:
         energy_ref = refs.pop(0)
-    flat_ref, box_ref, parts_ref, padded_ref = refs
+    flat_ref, box_ref, parts_ref, padded_ref, corner_ref, corner_sem = refs
+    corner_copy = pltpu.make_async_copy(corner_hbm, corner_ref, corner_sem)
+    corner_copy.start()
     extent = field_ref.shape[0]
     if is_first:
         atoms = table.shape[1] // 2
         energy_ref[...] = table[:, atoms:]
         table = table[:, :atoms]
     scaled = table * energy_ref[...]
-    deposit(scaled, chunks, corner_ref, member_ref, flat_ref, box_ref, parts_ref)
+    box_values(scaled, chunks, member_ref, flat_ref, box_ref)
 
     cells = field_ref[...]
     padded_ref[REACH : REACH + extent] = cells
@@ -376,8 +386,11 @@
     padded_ref[pl.ds(mate_at, REACH)] = mate_ref[:HALO_ROWS].reshape(REACH, SY, LANES)
     padded_ref[pl.ds(cross_at, REACH)] = cross_ref[:HALO_ROWS].reshape(REACH, SY, LANES)
     value = -0.5 * laplacian(padded_ref, extent, along_z_ref, along_y_ref) + (potential_ref[...] - CENTRE) * cells
-    for u in range(parts_ref.shape[0]):
-        value = value + parts_ref[u]
+    parts_ref[0] = value
+    parts_ref[1:] = jnp.zeros((COPIES - 1,) + value.shape, jnp.float32)
+    corner_copy.wait()
+    deposit(corner_ref, box_ref, parts_ref)
+    value = total_of([parts_ref[u] for u in range(COPIES)])
     value = factors[index][0] * value
     if not is_first:
         value = value - factors[index][1] * before_ref[...]
@@ -423,8 +436,8 @@
     def shaped(*shape):
         return jax.ShapeDtypeStruct(shape, jnp.float32)
 
-    def call(kernel, name, out_shape, scalars, operands, scratch, after=(), in_place={}):
-        inputs = len(scalars) + len(operands)
+    def call(kernel, name, out_shape, scalars, operands, scratch, after=(), in_place={}, late=()):
+        inputs = len(scalars) + len(operands) + len(late)
 
         def body(*refs):
             kernel(*refs[:inputs], *refs[inputs + len(after) :])
@@ -432,27 +445,31 @@
         return pl.pallas_call(
             body,
             out_shape=out_shape,
-            in_specs=[SMEM] * len(scalars) + [VMEM] * len(operands) + [ANY] * len(after),
+            in_specs=[SMEM] * len(scalars) + [VMEM] * len(operands)
+            + [ANY] * (len(late) + len(after)),
             out_specs=jax.tree.map(lambda _: VMEM, out_shape),
-            scratch_shapes=[pltpu.VMEM(shape, jnp.float32) for shape in scratch],
+            scratch_shapes=[
+                pltpu.VMEM(shape, jnp.float32) if isinstance(shape, tuple) else shape
+                for shape in scratch
+            ],
             compiler_params=pltpu.CompilerParams(vmem_limit_bytes=16 * 2**20),
             input_output_aliases=in_place,
             cost_estimate=pl.CostEstimate(flops=0, bytes_accessed=0, transcendentals=0),
             name=name,
-        )(*scalars, *operands, *after)
+        )(*scalars, *operands, *late, *after)
 
     atom_row = jnp.repeat(slot_atom, SZ)[None, :]
     own_atoms = (jnp.arange(atoms) // atom_own) == place
     energy = jnp.where(own_atoms[None, :], jnp.tile(kb_energy.T, (1, atoms // atom_own)), 0.0)
     flat = (groups, ROWS, LANES)
-    boxes = (TILES, ROWS, LANES)
+    boxes = (groups, TILES, ROWS, LANES)
     parts = (COPIES, planes, SY, LANES)
     padded = (planes + 2 * REACH, SY, LANES)
     table_rows = ROWS * atoms // LANES
     sends = [shaped(HALO_ROWS + table_rows, LANES)] * 2
 
     flat = (groups, ROWS, LANES)
-    boxes = (TILES, ROWS, LANES)
+    boxes = (groups, TILES, ROWS, LANES)
     parts = (COPIES, planes, SY, LANES)
     padded = (planes + 2 * REACH, SY, LANES)
     table_rows = ROWS * atoms // LANES
@@ -474,18 +491,14 @@
         ],
         [], [atom_row], [],
     )
-    odd = (place % 2).astype(jnp.int32)
     halos = [shaped(HALO_ROWS, LANES)] * 2
     if lax.axis_size("band") == 4 and tiles == 2 * HALVES:
-        at = lax.axis_index("band").astype(jnp.int32)
-        owners = [at, (at + 1) % 4, (at + 3) % 4, (at + 2) % 4]
-        where = jnp.stack([odd] + [2 * part + h for part in owners for h in range(2)])
         rows = HALVES * groups * ROWS * ROWS
         plane = shaped(rows, LANES)
         laden = shaped(rows + HALO_ROWS, LANES)
         low = call(low_kernel, "pack_low", laden, [], [projectors], [])
         low = call(
-            window_kernel, "add_window", laden, [where], [field, low], [], (), {2: 0}
+            window_kernel, "add_window", laden, [], [field, low], [], (), {1: 0}
         )
         below_low = turn(low, "band", 1)
         high = call(high_kernel, "pack_high", plane, [], [projectors], [], [low])
@@ -505,23 +518,22 @@
         on_far_low = hand_on(far_low, on_high, tables[0], energy)
         above_low = turn(on_far_low, "band", 1)
         mate, cross = call(
-            halo_kernel, "cut_halos", halos, [where], [field], [], [on_far_low]
+            halo_kernel, "cut_halos", halos, [], [field], [], [on_far_low]
         )
         mate, cross = swap(mate, "dom", 0), swap(cross, "dom", 1)
         near = call(
-            near_kernel, "project_near", shaped(*flat), [slot_corner, where],
+            near_kernel, "project_near", shaped(*flat), [slot_corner],
             [field, low, high, below_low, below_high, far_low], [],
         )
         on_far_high = hand_on(far_high, near, tables[0], energy, mate, cross)
         above_high = turn(on_far_high, "band", 1)
         own = call(
-            last_part_kernel, "first_sums", shaped(2 * table_rows, LANES), [slot_corner, where],
+            last_part_kernel, "first_sums", shaped(2 * table_rows, LANES), [slot_corner],
             [tables[0], energy, field, near, returned, far_high], [flat],
         )
         chunks = [low, high, above_low, above_high, below_low, below_high, far_low, far_high]
     else:
-        where = odd[None]
-        mate, cross = call(halo_kernel, "cut_halos", halos, [where], [field], [])
+        mate, cross = call(halo_kernel, "cut_halos", halos, [], [field], [])
         packed = call(
             whole_pack_kernel, "pack_projectors", shaped(tiles * groups * ROWS * ROWS, LANES),
             [], [projectors], [],
@@ -556,7 +568,12 @@
             out_shape += [shaped(ROWS, atoms)]
         result = call(
             functools.partial(step_kernel, index, len(chunks)), f"filter_step_{index + 1}",
-            out_shape, [slot_corner, where], operands, [flat, boxes, parts, padded],
+            out_shape, [], operands,
+            [
+                flat, boxes, parts, padded,
+                pltpu.SMEM(slot_corner.shape, jnp.int32), pltpu.SemaphoreType.DMA,
+            ],
+            late=[slot_corner],
         )
         before, field = field, result[0]
         sent = result[1:3]

time: 72.5 us -> 71.1 us (0.981)
  Pallas kernels: 12.8 us -> 11.4 us
    pallas_call x14, Pallas kernels: 12.8 us -> 11.4 us  [call(): pl.pallas_call(body, out_shape=out_shape, in_specs=[SMEM] * len(scalars)...]
where the time goes in v7:
time: 71.1 us; the launch traced here: 70.8 us
  waiting for transfers between devices  32.7 us (46%)
  starting transfers between devices  24.7 us (35%)
  Pallas kernels  11.4 us (16%)
  local copies, waits for them, and re-layouts  1.9 us (3%)
    ppermute x11, starting transfers between devices, swap(): return lax.ppermute(values, axis, pairs)  20.3 us
    ppermute x11, waiting for transfers between devices, swap(): return lax.ppermute(values, axis, pairs)  17.1 us
    ppermute x7, waiting for transfers between devices, turn(): lax.ppermute(values, axis, [(i, (i + step) % count) for i in range(count)])  15.6 us
    pallas_call x14, Pallas kernels, call(): pl.pallas_call(body, out_shape=out_shape, in_specs=[SMEM] * len(scalars)...  11.4 us
    ppermute x7, starting transfers between devices, turn(): lax.ppermute(values, axis, [(i, (i + step) % count) for i in range(count)])  4.39 us
    unnamed x14, local copies, waits for them, and re-layouts  1.67 us
  transfers between devices with their start and end apart: 18, of which 15 were waited for; matrix products, arithmetic and copies ran while one was open for 0% of the time, Pallas kernels for 6%

profile of v7, /device:TPU:5, one launch (start us, length us, event | category | flops | bytes accessed | tf_op | source)
XLA Modules:
  0.0 70.8 jit_solution(6846648494869851374)
XLA Ops:
  0.0 1.1 %copy-done.1 = f32[32,8,512]{2,1,0:T(8,128)S(1)} copy-done((f32[32,8,512]{2,1,0:T(8,128)S(1)}, f32[32,8,512]{2,1,0:T(8,128)}, u32[]{:S(2)}) %copy-start.1) | copy-done | bytes 524312
  1.1 0.9 %pack_low.1.refs_1_ = f32[608,128]{1,0:T(8,128)S(1)} custom-call(f32[32,8,512]{2,1,0:T(8,128)S(1)} %copy-done.1), custom_call_target="tpu_custom_call" | custom-call | tf_op jit(solution)/shard_map/pack_low/pallas_call | solution.py:445
  2.0 1.3 %collective-permute-start = (f32[608,128]{1,0:T(8,128)S(1)}, f32[608,128]{1,0:T(8,128)S(1)}, u32[]{:S(2)}, u32[]{:S(2)}) collective-permute-start(f32[608,128]{1,0:T(8,128)S(1)} %add_window.1.refs_1_.refs_2_.refs_10_.refs_9_), channel_id=1, source_target_pairs={{0,1},{1,2},{2,3},{3,0},{4,5},{5,6},{6,7},{7,4},{8,9},{9,10},{10,1... | collective-permute-start | bytes 933896 | tf_op jit(solution)/shard_map/ppermute | solution.py:421
  3.4 0.9 %pack_high.1.refs_2_.refs_3_.refs_11_.refs_10_ = f32[512,128]{1,0:T(8,128)S(1)} custom-call(f32[32,8,512]{2,1,0:T(8,128)S(1)} %copy-done.2, f32[608,128]{1,0:T(8,128)S(1)} %add_window.1.refs_1_.refs_2_.refs_10_.refs_9_), custom_call_target="tpu_custom_call" | custom-call | tf_op jit(solution)/shard_map/pack_high/pallas_call | solution.py:445
  4.3 1.3 %collective-permute-start.2 = (f32[512,128]{1,0:T(8,128)S(1)}, f32[512,128]{1,0:T(8,128)S(1)}, u32[]{:S(2)}, u32[]{:S(2)}) collective-permute-start(f32[512,128]{1,0:T(8,128)S(1)} %pack_high.1.refs_2_.refs_3_.refs_11_.refs_10_), channel_id=1, source_target_pairs={{0,1},{1,2},{2,3},{3,0},{4,5},{5,6},{6,7},{7,4},{8,9},{9,10},{10,1... | collective-permute-start | bytes 786440 | tf_op jit(solution)/shard_map/ppermute | solution.py:421
  5.6 6.6 %collective-permute-done.refs_3_.refs_4_.refs_14_.refs_13_ = f32[608,128]{1,0:T(8,128)S(1)} collective-permute-done((f32[608,128]{1,0:T(8,128)S(1)}, f32[608,128]{1,0:T(8,128)S(1)}, u32[]{:S(2)}, u32[]{:S(2)}) %collective-permute-start) | collective-permute-done | bytes 311328 | tf_op jit(solution)/shard_map/ppermute | solution.py:421
  13.1 1.4 %collective-permute-start.3 = (f32[4,8,128]{2,1,0:T(8,128)S(1)}, f32[4,8,128]{2,1,0:T(8,128)S(1)}, u32[]{:S(2)}, u32[]{:S(2)}) collective-permute-start(f32[4,8,128]{2,1,0:T(8,128)S(1)} %get-tuple-element.47), channel_id=1, source_target_pairs={{0,3},{1,0},{2,1},{3,2},{4,7},{5,4},{6,5},{7,6},{8,11},{9,8},{10,9... | collective-permute-start | bytes 49160 | tf_op jit(solution)/shard_map/ppermute | solution.py:421
  15.6 2.3 %collective-permute-done.2.refs_0_.refs_5_.refs_15_.refs_14_ = f32[512,128]{1,0:T(8,128)S(1)} collective-permute-done((f32[512,128]{1,0:T(8,128)S(1)}, f32[512,128]{1,0:T(8,128)S(1)}, u32[]{:S(2)}, u32[]{:S(2)}) %collective-permute-start.2) | collective-permute-done | bytes 262176 | tf_op jit(solution)/shard_map/ppermute | solution.py:421
  18.8 3.1 %collective-permute-done.1.refs_0_.refs_6_.refs_16_.refs_15_ = f32[512,128]{1,0:T(8,128)S(1)} collective-permute-done((f32[512,128]{1,0:T(8,128)S(1)}, f32[512,128]{1,0:T(8,128)S(1)}, u32[]{:S(2)}, u32[]{:S(2)}) %collective-permute-start.1) | collective-permute-done | bytes 262176 | tf_op jit(solution)/shard_map/ppermute | solution.py:421
  22.0 5.8 %collective-permute-start.4 = (f32[96,128]{1,0:T(8,128)S(1)}, f32[96,128]{1,0:T(8,128)S(1)}, u32[]{:S(2)}, u32[]{:S(2)}) collective-permute-start(f32[96,128]{1,0:T(8,128)S(1)} %get-tuple-element.48), channel_id=1, source_target_pairs={{0,4},{4,0},{8,12},{12,8},{16,20},{20,16},{24,28},{28,24},{1,5},{5... | collective-permute-start | bytes 147464 | tf_op jit(solution)/shard_map/ppermute | solution.py:416
  27.8 3.0 %collective-permute-start.5 = (f32[96,128]{1,0:T(8,128)S(1)}, f32[96,128]{1,0:T(8,128)S(1)}, u32[]{:S(2)}, u32[]{:S(2)}) collective-permute-start(f32[96,128]{1,0:T(8,128)S(1)} %get-tuple-element.49), channel_id=1, source_target_pairs={{4,8},{8,4},{12,16},{16,12},{20,24},{24,20},{5,9},{9,5},{13,17},{1... | collective-permute-start | bytes 147464 | tf_op jit(solution)/shard_map/ppermute | solution.py:416
  30.9 1.0 %project_near.1.refs_4_.refs_1_ = f32[4,8,128]{2,1,0:T(8,128)S(1)} custom-call(s32[3,32]{1,0:T(4,128)S(1)} %copy-done.4, f32[12,16,128]{2,1,0:T(8,128)S(1)} %bitcast.5, f32[608,128]{1,0:T(8,128)S(1)} %add_window.1.refs_1_.refs_2_.refs_10_.refs_9_, f32[512,128]{1,0:T(8,128)S(1)} %pack_high.1.refs_2_.refs_3_.refs_11_.refs_10_, ...), custom_call_target="tpu_custom_call" | custom-call | tf_op jit(solution)/shard_map/project_near/pallas_call | solution.py:445
  31.9 1.5 %collective-permute-done.5.refs_5_.refs_6_ = f32[96,128]{1,0:T(8,128)S(1)} collective-permute-done((f32[96,128]{1,0:T(8,128)S(1)}, f32[96,128]{1,0:T(8,128)S(1)}, u32[]{:S(2)}, u32[]{:S(2)}) %collective-permute-start.5) | collective-permute-done | bytes 49184 | tf_op jit(solution)/shard_map/ppermute | solution.py:416
  33.6 0.9 %first_sums.1 = f32[16,128]{1,0:T(8,128)S(1)} custom-call(s32[3,32]{1,0:T(4,128)S(1)} %copy-done.4, bf16[128,512]{1,0:T(8,128)(2,1)S(1)} %get-tuple-element.43.refs_2_.refs_1_.refs_0_, f32[8,128]{1,0:T(8,128)S(1)} %broadcast_select_fusion.refs_3_.refs_2_, f32[12,16,128]{2,1,0:T(8,128)S(1)} %bitcast.6, f32[4,8,128]{2,1,0:T(8,128)S(1)} %project_near.1.refs_4_.refs_1_, ...), custom_call_target="tpu_custom_call" | custom-call | tf_op jit(solution)/shard_map/first_sums/pallas_call | solution.py:445
  35.1 0.8 %collective-permute-done.7 = f32[16,128]{1,0:T(8,128)S(1)} collective-permute-done((f32[16,128]{1,0:T(8,128)S(1)}, f32[16,128]{1,0:T(8,128)S(1)}, u32[]{:S(2)}, u32[]{:S(2)}) %collective-permute-start.7) | collective-permute-done | bytes 8224 | tf_op jit(solution)/shard_map/ppermute | solution.py:416
  35.9 2.4 %collective-permute-start.8 = (f32[16,128]{1,0:T(8,128)S(1)}, f32[16,128]{1,0:T(8,128)S(1)}, u32[]{:S(2)}, u32[]{:S(2)}) collective-permute-start(f32[16,128]{1,0:T(8,128)S(1)} %add.22.refs_7_), channel_id=1, source_target_pairs={{4,8},{8,4},{12,16},{16,12},{20,24},{24,20},{5,9},{9,5},{13,17},{1... | collective-permute-start | bytes 24584 | tf_op jit(solution)/shard_map/ppermute | solution.py:416
  38.4 2.8 %collective-permute-done.8.refs_9_ = f32[16,128]{1,0:T(8,128)S(1)} collective-permute-done((f32[16,128]{1,0:T(8,128)S(1)}, f32[16,128]{1,0:T(8,128)S(1)}, u32[]{:S(2)}, u32[]{:S(2)}) %collective-permute-start.8) | collective-permute-done | bytes 8224 | tf_op jit(solution)/shard_map/ppermute | solution.py:416
  41.2 0.9 %collective-permute-start.9 = (f32[16,128]{1,0:T(8,128)S(1)}, f32[16,128]{1,0:T(8,128)S(1)}, u32[]{:S(2)}, u32[]{:S(2)}) collective-permute-start(f32[16,128]{1,0:T(8,128)S(1)} %collective-permute-done.8.refs_9_), channel_id=1, source_target_pairs={{0,4},{4,0},{8,12},{12,8},{16,20},{20,16},{24,28},{28,24},{1,5},{5... | collective-permute-start | bytes 24584 | tf_op jit(solution)/shard_map/ppermute | solution.py:416
  42.1 0.8 %collective-permute-done.9.refs_8_ = f32[16,128]{1,0:T(8,128)S(1)} collective-permute-done((f32[16,128]{1,0:T(8,128)S(1)}, f32[16,128]{1,0:T(8,128)S(1)}, u32[]{:S(2)}, u32[]{:S(2)}) %collective-permute-start.9) | collective-permute-done | bytes 8224 | tf_op jit(solution)/shard_map/ppermute | solution.py:416
  43.0 2.8 %collective-permute-done.11.refs_13_.refs_12_ = f32[512,128]{1,0:T(8,128)S(1)} collective-permute-done((f32[512,128]{1,0:T(8,128)S(1)}, f32[512,128]{1,0:T(8,128)S(1)}, u32[]{:S(2)}, u32[]{:S(2)}) %collective-permute-start.11) | collective-permute-done | bytes 262176 | tf_op jit(solution)/shard_map/ppermute | solution.py:421
  45.7 2.2 %filter_step_1.1 = (f32[12,16,128]{2,1,0:T(8,128)S(1)}, f32[104,128]{1,0:T(8,128)S(1)}, f32[104,128]{1,0:T(8,128)S(1)}, f32[8,128]{1,0:T(8,128)S(1)}) custom-call(bf16[128,512]{1,0:T(8,128)(2,1)S(1)} %get-tuple-element.43.refs_2_.refs_1_.refs_0_, bf16[384,128]{1,0:T(8,128)(2,1)S(1)} %get-tuple-element.44.refs_1_, ...), custom_call_target="tpu_custom_call" | custom-call | tf_op jit(solution)/shard_map/filter_step_1/pallas_call | solution.py:445
  47.9 1.3 %collective-permute-start.12 = (f32[104,128]{1,0:T(8,128)S(1)}, f32[104,128]{1,0:T(8,128)S(1)}, u32[]{:S(2)}, u32[]{:S(2)}) collective-permute-start(f32[104,128]{1,0:T(8,128)S(1)} %get-tuple-element.51), channel_id=1, source_target_pairs={{0,4},{4,0},{8,12},{12,8},{16,20},{20,16},{24,28},{28,24},{1,5},{5... | collective-permute-start | bytes 159752 | tf_op jit(solution)/shard_map/ppermute | solution.py:416
  49.2 0.9 %collective-permute-done.12.refs_5_ = f32[104,128]{1,0:T(8,128)S(1)} collective-permute-done((f32[104,128]{1,0:T(8,128)S(1)}, f32[104,128]{1,0:T(8,128)S(1)}, u32[]{:S(2)}, u32[]{:S(2)}) %collective-permute-start.12) | collective-permute-done | bytes 53280 | tf_op jit(solution)/shard_map/ppermute | solution.py:416
  50.1 1.9 %collective-permute-start.13 = (f32[104,128]{1,0:T(8,128)S(1)}, f32[104,128]{1,0:T(8,128)S(1)}, u32[]{:S(2)}, u32[]{:S(2)}) collective-permute-start(f32[104,128]{1,0:T(8,128)S(1)} %fusion.1.refs_7_), channel_id=1, source_target_pairs={{4,8},{8,4},{12,16},{16,12},{20,24},{24,20},{5,9},{9,5},{13,17},{1... | collective-permute-start | bytes 159752 | tf_op jit(solution)/shard_map/ppermute | solution.py:416
  52.0 3.8 %collective-permute-done.13.refs_6_ = f32[104,128]{1,0:T(8,128)S(1)} collective-permute-done((f32[104,128]{1,0:T(8,128)S(1)}, f32[104,128]{1,0:T(8,128)S(1)}, u32[]{:S(2)}, u32[]{:S(2)}) %collective-permute-start.13) | collective-permute-done | bytes 53280 | tf_op jit(solution)/shard_map/ppermute | solution.py:416
  55.9 1.0 %collective-permute-start.14 = (f32[8,128]{1,0:T(8,128)S(1)}, f32[8,128]{1,0:T(8,128)S(1)}, u32[]{:S(2)}, u32[]{:S(2)}) collective-permute-start(f32[8,128]{1,0:T(8,128)S(1)} %slice.57), channel_id=1, source_target_pairs={{0,4},{4,0},{8,12},{12,8},{16,20},{20,16},{24,28},{28,24},{1,5},{5... | collective-permute-start | bytes 12296 | tf_op jit(solution)/shard_map/ppermute | solution.py:416
  57.6 2.2 %filter_step_2.1 = (f32[12,16,128]{2,1,0:T(8,128)S(1)}, f32[104,128]{1,0:T(8,128)S(1)}, f32[104,128]{1,0:T(8,128)S(1)}) custom-call(bf16[128,512]{1,0:T(8,128)(2,1)S(1)} %get-tuple-element.43.refs_2_.refs_1_.refs_0_, bf16[384,128]{1,0:T(8,128)(2,1)S(1)} %get-tuple-element.44.refs_1_, bf16[192,576]{1,0:T(8,128)(2,1)S(1)} %get-tuple-element.45.refs_2_, ...), custom_call_target="tpu_custom_call" | custom-call | tf_op jit(solution)/shard_map/filter_step_2/pallas_call | solution.py:445
  60.2 0.9 %collective-permute-done.15.refs_5_ = f32[104,128]{1,0:T(8,128)S(1)} collective-permute-done((f32[104,128]{1,0:T(8,128)S(1)}, f32[104,128]{1,0:T(8,128)S(1)}, u32[]{:S(2)}, u32[]{:S(2)}) %collective-permute-start.15) | collective-permute-done | bytes 53280 | tf_op jit(solution)/shard_map/ppermute | solution.py:416
  61.1 1.9 %collective-permute-start.16 = (f32[104,128]{1,0:T(8,128)S(1)}, f32[104,128]{1,0:T(8,128)S(1)}, u32[]{:S(2)}, u32[]{:S(2)}) collective-permute-start(f32[104,128]{1,0:T(8,128)S(1)} %fusion.refs_7_), channel_id=1, source_target_pairs={{4,8},{8,4},{12,16},{16,12},{20,24},{24,20},{5,9},{9,5},{13,17},{1... | collective-permute-start | bytes 159752 | tf_op jit(solution)/shard_map/ppermute | solution.py:416
  63.0 3.8 %collective-permute-done.16.refs_6_ = f32[104,128]{1,0:T(8,128)S(1)} collective-permute-done((f32[104,128]{1,0:T(8,128)S(1)}, f32[104,128]{1,0:T(8,128)S(1)}, u32[]{:S(2)}, u32[]{:S(2)}) %collective-permute-start.16) | collective-permute-done | bytes 53280 | tf_op jit(solution)/shard_map/ppermute | solution.py:416
  66.9 0.9 %collective-permute-start.17 = (f32[8,128]{1,0:T(8,128)S(1)}, f32[8,128]{1,0:T(8,128)S(1)}, u32[]{:S(2)}, u32[]{:S(2)}) collective-permute-start(f32[8,128]{1,0:T(8,128)S(1)} %slice.59), channel_id=1, source_target_pairs={{0,4},{4,0},{8,12},{12,8},{16,20},{20,16},{24,28},{28,24},{1,5},{5... | collective-permute-start | bytes 12296 | tf_op jit(solution)/shard_map/ppermute | solution.py:416
  68.6 2.2 %filter_step_3.1 = f32[12,16,128]{2,1,0:T(8,128)} custom-call(bf16[128,512]{1,0:T(8,128)(2,1)S(1)} %get-tuple-element.43.refs_2_.refs_1_.refs_0_, bf16[384,128]{1,0:T(8,128)(2,1)S(1)} %get-tuple-element.44.refs_1_, bf16[192,576]{1,0:T(8,128)(2,1)S(1)} %get-tuple-element.45.refs_2_, f32[12,16,128]{2,1,0:T(8,128)S(1)} %get-tuple-element.54.refs_3_, ...), custom_call_target="tpu_custom_call" | custom-call | tf_op jit(solution)/shard_map/filter_step_3/pallas_call | solution.py:445
  (43 shorter events, 5.7 us)
Async XLA Ops:
  0.0 2.0 %copy-start = (f32[1,12,16,128]{3,2,1,0:T(8,128)S(1)}, f32[1,12,16,128]{3,2,1,0:T(8,128)}, u32[]{:S(2)}) copy-start(f32[1,12,16,128]{3,2,1,0:T(8,128)} %param.10) | copy-start | bytes 294916
  0.0 1.1 %copy-start.1 = (f32[32,8,512]{2,1,0:T(8,128)S(1)}, f32[32,8,512]{2,1,0:T(8,128)}, u32[]{:S(2)}) copy-start(f32[32,8,512]{2,1,0:T(8,128)} %refs_0_.6) | copy-start | bytes 1572868
  2.0 1.4 %copy-start.2 = (f32[32,8,512]{2,1,0:T(8,128)S(1)}, f32[32,8,512]{2,1,0:T(8,128)}, u32[]{:S(2)}) copy-start(f32[32,8,512]{2,1,0:T(8,128)} %refs_0_.6) | copy-start | bytes 1572868
  2.0 10.2 %collective-permute-start = (f32[608,128]{1,0:T(8,128)S(1)}, f32[608,128]{1,0:T(8,128)S(1)}, u32[]{:S(2)}, u32[]{:S(2)}) collective-permute-start(f32[608,128]{1,0:T(8,128)S(1)} %add_window.1.refs_1_.refs_2_.refs_10_.refs_9_), channel_id=1, source_target_pairs={{0,1},{1,2},{2,3},{3,0},{4,5},{5,6},{6,7},{7,4},{8,9},{9,10},{10,1... | collective-permute-start | bytes 933896 | tf_op jit(solution)/shard_map/ppermute | solution.py:421
  4.3 13.6 %collective-permute-start.2 = (f32[512,128]{1,0:T(8,128)S(1)}, f32[512,128]{1,0:T(8,128)S(1)}, u32[]{:S(2)}, u32[]{:S(2)}) collective-permute-start(f32[512,128]{1,0:T(8,128)S(1)} %pack_high.1.refs_2_.refs_3_.refs_11_.refs_10_), channel_id=1, source_target_pairs={{0,1},{1,2},{2,3},{3,0},{4,5},{5,6},{6,7},{7,4},{8,9},{9,10},{10,1... | collective-permute-start | bytes 786440 | tf_op jit(solution)/shard_map/ppermute | solution.py:421
  5.6 6.6 %copy-start.4 = (s32[3,32]{1,0:T(4,128)S(1)}, s32[3,32]{1,0:T(4,128)}, u32[]{:S(2)}) copy-start(s32[3,32]{1,0:T(4,128)} %refs_19_.3) | copy-start | bytes 1156
  13.1 5.6 %collective-permute-start.3 = (f32[4,8,128]{2,1,0:T(8,128)S(1)}, f32[4,8,128]{2,1,0:T(8,128)S(1)}, u32[]{:S(2)}, u32[]{:S(2)}) collective-permute-start(f32[4,8,128]{2,1,0:T(8,128)S(1)} %get-tuple-element.47), channel_id=1, source_target_pairs={{0,3},{1,0},{2,1},{3,2},{4,7},{5,4},{6,5},{7,6},{8,11},{9,8},{10,9... | collective-permute-start | bytes 49160 | tf_op jit(solution)/shard_map/ppermute | solution.py:421
  14.5 0.7 copy-start.6
  14.5 7.4 %collective-permute-start.1 = (f32[512,128]{1,0:T(8,128)S(1)}, f32[512,128]{1,0:T(8,128)S(1)}, u32[]{:S(2)}, u32[]{:S(2)}) collective-permute-start(f32[512,128]{1,0:T(8,128)S(1)} %get-tuple-element.46.refs_1_), channel_id=1, source_target_pairs={{0,1},{1,2},{2,3},{3,0},{4,5},{5,6},{6,7},{7,4},{8,9},{9,10},{10,1... | collective-permute-start | bytes 786440 | tf_op jit(solution)/shard_map/ppermute | solution.py:421
  14.6 0.7 %copy-start.5 = (f32[16,8]{0,1:T(8,128)S(1)}, f32[16,8]{0,1:T(8,128)}, u32[]{:S(2)}) copy-start(f32[16,8]{0,1:T(8,128)} %param.13) | copy-start | bytes 1540
  18.7 13.2 %collective-permute-start.6 = (f32[512,128]{1,0:T(8,128)S(1)}, f32[512,128]{1,0:T(8,128)S(1)}, u32[]{:S(2)}, u32[]{:S(2)}) collective-permute-start(f32[512,128]{1,0:T(8,128)S(1)} %hand_on.3.refs_1_), channel_id=1, source_target_pairs={{0,1},{1,2},{2,3},{3,0},{4,5},{5,6},{6,7},{7,4},{8,9},{9,10},{10,1... | collective-permute-start | bytes 786440 | tf_op jit(solution)/shard_map/ppermute | solution.py:421
  22.0 10.0 %collective-permute-start.4 = (f32[96,128]{1,0:T(8,128)S(1)}, f32[96,128]{1,0:T(8,128)S(1)}, u32[]{:S(2)}, u32[]{:S(2)}) collective-permute-start(f32[96,128]{1,0:T(8,128)S(1)} %get-tuple-element.48), channel_id=1, source_target_pairs={{0,4},{4,0},{8,12},{12,8},{16,20},{20,16},{24,28},{28,24},{1,5},{5... | collective-permute-start | bytes 147464 | tf_op jit(solution)/shard_map/ppermute | solution.py:416
  27.8 5.7 %collective-permute-start.5 = (f32[96,128]{1,0:T(8,128)S(1)}, f32[96,128]{1,0:T(8,128)S(1)}, u32[]{:S(2)}, u32[]{:S(2)}) collective-permute-start(f32[96,128]{1,0:T(8,128)S(1)} %get-tuple-element.49), channel_id=1, source_target_pairs={{4,8},{8,4},{12,16},{16,12},{20,24},{24,20},{5,9},{9,5},{13,17},{1... | collective-permute-start | bytes 147464 | tf_op jit(solution)/shard_map/ppermute | solution.py:416
  30.8 12.2 %collective-permute-start.10 = (f32[512,128]{1,0:T(8,128)S(1)}, f32[512,128]{1,0:T(8,128)S(1)}, u32[]{:S(2)}, u32[]{:S(2)}) collective-permute-start(f32[512,128]{1,0:T(8,128)S(1)} %hand_on.4.refs_1_), channel_id=1, source_target_pairs={{0,1},{1,2},{2,3},{3,0},{4,5},{5,6},{6,7},{7,4},{8,9},{9,10},{10,1... | collective-permute-start | bytes 786440 | tf_op jit(solution)/shard_map/ppermute | solution.py:421
  33.5 12.2 %copy-start.3 = (f32[12,16,128]{2,1,0:T(8,128)S(1)}, f32[12,16,128]{2,1,0:T(8,128)}, u32[]{:S(2)}) copy-start(f32[12,16,128]{2,1,0:T(8,128)} %refs_4_.5) | copy-start | bytes 294916
  33.5 12.2 %collective-permute-start.11 = (f32[512,128]{1,0:T(8,128)S(1)}, f32[512,128]{1,0:T(8,128)S(1)}, u32[]{:S(2)}, u32[]{:S(2)}) collective-permute-start(f32[512,128]{1,0:T(8,128)S(1)} %hand_on.5), channel_id=1, source_target_pairs={{0,1},{1,2},{2,3},{3,0},{4,5},{5,6},{6,7},{7,4},{8,9},{9,10},{10,1... | collective-permute-start | bytes 786440 | tf_op jit(solution)/shard_map/ppermute | solution.py:421
  34.5 1.5 %collective-permute-start.7 = (f32[16,128]{1,0:T(8,128)S(1)}, f32[16,128]{1,0:T(8,128)S(1)}, u32[]{:S(2)}, u32[]{:S(2)}) collective-permute-start(f32[16,128]{1,0:T(8,128)S(1)} %first_sums.1), channel_id=1, source_target_pairs={{0,4},{4,0},{8,12},{12,8},{16,20},{20,16},{24,28},{28,24},{1,5},{5... | collective-permute-start | bytes 24584 | tf_op jit(solution)/shard_map/ppermute | solution.py:416
  35.9 5.3 %collective-permute-start.8 = (f32[16,128]{1,0:T(8,128)S(1)}, f32[16,128]{1,0:T(8,128)S(1)}, u32[]{:S(2)}, u32[]{:S(2)}) collective-permute-start(f32[16,128]{1,0:T(8,128)S(1)} %add.22.refs_7_), channel_id=1, source_target_pairs={{4,8},{8,4},{12,16},{16,12},{20,24},{24,20},{5,9},{9,5},{13,17},{1... | collective-permute-start | bytes 24584 | tf_op jit(solution)/shard_map/ppermute | solution.py:416
  41.2 1.8 %collective-permute-start.9 = (f32[16,128]{1,0:T(8,128)S(1)}, f32[16,128]{1,0:T(8,128)S(1)}, u32[]{:S(2)}, u32[]{:S(2)}) collective-permute-start(f32[16,128]{1,0:T(8,128)S(1)} %collective-permute-done.8.refs_9_), channel_id=1, source_target_pairs={{0,4},{4,0},{8,12},{12,8},{16,20},{20,16},{24,28},{28,24},{1,5},{5... | collective-permute-start | bytes 24584 | tf_op jit(solution)/shard_map/ppermute | solution.py:416
  47.9 2.2 %collective-permute-start.12 = (f32[104,128]{1,0:T(8,128)S(1)}, f32[104,128]{1,0:T(8,128)S(1)}, u32[]{:S(2)}, u32[]{:S(2)}) collective-permute-start(f32[104,128]{1,0:T(8,128)S(1)} %get-tuple-element.51), channel_id=1, source_target_pairs={{0,4},{4,0},{8,12},{12,8},{16,20},{20,16},{24,28},{28,24},{1,5},{5... | collective-permute-start | bytes 159752 | tf_op jit(solution)/shard_map/ppermute | solution.py:416
  50.1 5.7 %collective-permute-start.13 = (f32[104,128]{1,0:T(8,128)S(1)}, f32[104,128]{1,0:T(8,128)S(1)}, u32[]{:S(2)}, u32[]{:S(2)}) collective-permute-start(f32[104,128]{1,0:T(8,128)S(1)} %fusion.1.refs_7_), channel_id=1, source_target_pairs={{4,8},{8,4},{12,16},{16,12},{20,24},{24,20},{5,9},{9,5},{13,17},{1... | collective-permute-start | bytes 159752 | tf_op jit(solution)/shard_map/ppermute | solution.py:416
  55.9 1.8 %collective-permute-start.14 = (f32[8,128]{1,0:T(8,128)S(1)}, f32[8,128]{1,0:T(8,128)S(1)}, u32[]{:S(2)}, u32[]{:S(2)}) collective-permute-start(f32[8,128]{1,0:T(8,128)S(1)} %slice.57), channel_id=1, source_target_pairs={{0,4},{4,0},{8,12},{12,8},{16,20},{20,16},{24,28},{28,24},{1,5},{5... | collective-permute-start | bytes 12296 | tf_op jit(solution)/shard_map/ppermute | solution.py:416
  59.8 1.3 %collective-permute-start.15 = (f32[104,128]{1,0:T(8,128)S(1)}, f32[104,128]{1,0:T(8,128)S(1)}, u32[]{:S(2)}, u32[]{:S(2)}) collective-permute-start(f32[104,128]{1,0:T(8,128)S(1)} %get-tuple-element.55), channel_id=1, source_target_pairs={{0,4},{4,0},{8,12},{12,8},{16,20},{20,16},{24,28},{28,24},{1,5},{5... | collective-permute-start | bytes 159752 | tf_op jit(solution)/shard_map/ppermute | solution.py:416
  61.1 5.7 %collective-permute-start.16 = (f32[104,128]{1,0:T(8,128)S(1)}, f32[104,128]{1,0:T(8,128)S(1)}, u32[]{:S(2)}, u32[]{:S(2)}) collective-permute-start(f32[104,128]{1,0:T(8,128)S(1)} %fusion.refs_7_), channel_id=1, source_target_pairs={{4,8},{8,4},{12,16},{16,12},{20,24},{24,20},{5,9},{9,5},{13,17},{1... | collective-permute-start | bytes 159752 | tf_op jit(solution)/shard_map/ppermute | solution.py:416
  66.9 1.8 %collective-permute-start.17 = (f32[8,128]{1,0:T(8,128)S(1)}, f32[8,128]{1,0:T(8,128)S(1)}, u32[]{:S(2)}, u32[]{:S(2)}) collective-permute-start(f32[8,128]{1,0:T(8,128)S(1)} %slice.59), channel_id=1, source_target_pairs={{0,4},{4,0},{8,12},{12,8},{16,20},{20,16},{24,28},{28,24},{1,5},{5... | collective-permute-start | bytes 12296 | tf_op jit(solution)/shard_map/ppermute | solution.py:416

commit v8 on v7

--- a/solution.py
+++ b/solution.py
@@ -233,9 +233,112 @@
     return jnp.where(row // block == column // block, table, 0.0)
 
 
-def laplacian(padded_ref, extent, along_z_ref, along_y_ref):
-    inner = padded_ref[REACH : REACH + extent]
-    high, low = halves_of(inner.reshape(extent * SY, LANES))
+HALO_ROWS = REACH * SY
+
+
+def to_rows(table):
+    blocks = [table[:, at : at + LANES] for at in range(0, table.shape[1], LANES)]
+    return jnp.concatenate(blocks, axis=0)
+
+
+def from_rows(rows):
+    blocks = [rows[at : at + ROWS] for at in range(0, rows.shape[0], ROWS)]
+    return jnp.concatenate(blocks, axis=1)
+
+
+def write_halos(field_ref, odd, mate_ref, cross_ref):
+    extent = field_ref.shape[0]
+    mate_start = (1 - odd) * (extent - REACH)
+    cross_start = odd * (extent - REACH)
+    for start, ref in ((mate_start, mate_ref), (cross_start, cross_ref)):
+        ref[:HALO_ROWS] = field_ref[pl.ds(start, REACH)].reshape(HALO_ROWS, LANES)
+
+
+def all_planes(ref):
+    rows = ref.shape[0] // SX
+    return [(x, ref, x * rows) for x in range(SX)]
+
+
+def some_planes(first, refs):
+    return [(plane_here(first + i), ref, 0) for i, ref in enumerate(refs)]
+
+
+def field_reader(ref):
+    return lambda x, half: ref[x, pl.ds(half * ROWS, ROWS), :]
+
+
+def halo_kernel(field_ref, mate_ref, cross_ref):
+    write_halos(field_ref, odd_here(), mate_ref, cross_ref)
+
+
+def low_kernel(proj_ref, laden_ref):
+    pack_plane(0, HALVES, proj_ref, laden_ref)
+
+
+def window_kernel(field_ref, laden_ref, out_ref):
+    window = field_ref[pl.ds(plane_here(2), REACH)]
+    out_ref[out_ref.shape[0] - HALO_ROWS :] = window.reshape(HALO_ROWS, LANES)
+
+
+def above_kernel(corner_ref, own_laden_ref, high_ref, laden_ref, flat_ref, on_ref):
+    rows = on_ref.shape[0]
+    on_ref[...] = laden_ref[:rows]
+
+    def field(x, half):
+        return laden_ref[pl.ds(pl.multiple_of(rows + x * SY + half * ROWS, ROWS), ROWS), :]
+
+    project(field, [(0, own_laden_ref, 0), (1, high_ref, 0)], corner_ref, flat_ref)
+
+
+def hand_on_kernel(given_ref, out_ref):
+    out_ref[...] = given_ref[...]
+
+
+def near_kernel(corner_ref, field_ref, low_ref, high_ref, *refs):
+    chunks = some_planes(0, [low_ref, high_ref]) + some_planes(4, refs[:-1])
+    project(field_reader(field_ref), chunks, corner_ref, refs[-1])
+
+
+def write_table(flat_ref, member_ref, energy_ref, out_ref):
+    sums = sum_atoms(flat_ref, member_ref)
+    out_ref[...] = jnp.concatenate([to_rows(sums), to_rows(energy_ref[...])], axis=0)
+
+
+def last_part_kernel(corner_ref, member_ref, energy_ref, field_ref, near_ref,
+                     returned_ref, far_ref, out_ref, flat_ref):
+    flat_ref[...] = near_ref[...] + returned_ref[...]
+    chunks = some_planes(7, [far_ref])
+    project(field_reader(field_ref), chunks, corner_ref, flat_ref, flat_ref)
+    write_table(flat_ref, member_ref, energy_ref, out_ref)
+
+
+def whole_pack_kernel(proj_ref, out_ref):
+    pack_plane(0, proj_ref.shape[2] // LANES, proj_ref, out_ref)
+
+
+def high_kernel(proj_ref, out_ref):
+    pack_plane(HALVES, HALVES, proj_ref, out_ref)
+
+
+def whole_sums_kernel(corner_ref, member_ref, energy_ref, field_ref, whole_ref, out_ref, flat_ref):
+    project(field_reader(field_ref), all_planes(whole_ref), corner_ref, flat_ref)
+    write_table(flat_ref, member_ref, energy_ref, out_ref)
+
+
+def local_kernel(index, along_z_ref, along_y_ref, field_ref, potential_ref, mate_ref, *refs):
+    refs = list(refs)
+    before_ref = refs.pop(0) if index > 0 else None
+    out_ref, padded_ref = refs
+    first, second = step_factors()[index]
+    extent = field_ref.shape[0]
+    odd = odd_here()
+    cells = field_ref[...]
+    padded_ref[REACH : REACH + extent] = cells
+    mate_at = (1 - odd) * (extent + REACH)
+    cross_at = odd * (extent + REACH)
+    padded_ref[pl.ds(mate_at, REACH)] = mate_ref[:HALO_ROWS].reshape(REACH, SY, LANES)
+    padded_ref[pl.ds(cross_at, REACH)] = jnp.zeros((REACH, SY, LANES), jnp.float32)
+    high, low = halves_of(cells.reshape(extent * SY, LANES))
     along_z = jnp.dot(
         jnp.concatenate([high, high, low], axis=1), along_z_ref[...],
         preferred_element_type=jnp.float32,
@@ -244,112 +347,34 @@
         along_y_ref[...], jnp.concatenate([high, low, high], axis=0),
         preferred_element_type=jnp.float32,
     )
-    total = (along_z + along_y).reshape(inner.shape)
+    total = (along_z + along_y).reshape(cells.shape)
     for k in range(1, REACH + 1):
         total = total + STENCIL_WEIGHTS[k] * (
             padded_ref[REACH + k : REACH + k + extent] + padded_ref[REACH - k : REACH - k + extent]
         )
-    return total
-
-
-HALO_ROWS = REACH * SY
-
-
-def to_rows(table):
-    blocks = [table[:, at : at + LANES] for at in range(0, table.shape[1], LANES)]
-    return jnp.concatenate(blocks, axis=0)
-
-
-def from_rows(rows):
-    blocks = [rows[at : at + ROWS] for at in range(0, rows.shape[0], ROWS)]
-    return jnp.concatenate(blocks, axis=1)
-
-
-def write_halos(field_ref, odd, mate_ref, cross_ref):
-    extent = field_ref.shape[0]
-    mate_start = (1 - odd) * (extent - REACH)
-    cross_start = odd * (extent - REACH)
-    for start, ref in ((mate_start, mate_ref), (cross_start, cross_ref)):
-        ref[:HALO_ROWS] = field_ref[pl.ds(start, REACH)].reshape(HALO_ROWS, LANES)
-
-
-def all_planes(ref):
-    rows = ref.shape[0] // SX
-    return [(x, ref, x * rows) for x in range(SX)]
-
-
-def some_planes(first, refs):
-    return [(plane_here(first + i), ref, 0) for i, ref in enumerate(refs)]
-
-
-def field_reader(ref):
-    return lambda x, half: ref[x, pl.ds(half * ROWS, ROWS), :]
-
-
-def halo_kernel(field_ref, mate_ref, cross_ref):
-    write_halos(field_ref, odd_here(), mate_ref, cross_ref)
-
-
-def low_kernel(proj_ref, laden_ref):
-    pack_plane(0, HALVES, proj_ref, laden_ref)
-
-
-def window_kernel(field_ref, laden_ref, out_ref):
-    window = field_ref[pl.ds(plane_here(2), REACH)]
-    out_ref[out_ref.shape[0] - HALO_ROWS :] = window.reshape(HALO_ROWS, LANES)
-
-
-def above_kernel(corner_ref, own_laden_ref, high_ref, laden_ref, flat_ref, on_ref):
-    rows = on_ref.shape[0]
-    on_ref[...] = laden_ref[:rows]
-
-    def field(x, half):
-        return laden_ref[pl.ds(pl.multiple_of(rows + x * SY + half * ROWS, ROWS), ROWS), :]
-
-    project(field, [(0, own_laden_ref, 0), (1, high_ref, 0)], corner_ref, flat_ref)
-
-
-def hand_on_kernel(given_ref, out_ref):
-    out_ref[...] = given_ref[...]
-
-
-def near_kernel(corner_ref, field_ref, low_ref, high_ref, *refs):
-    chunks = some_planes(0, [low_ref, high_ref]) + some_planes(4, refs[:-1])
-    project(field_reader(field_ref), chunks, corner_ref, refs[-1])
-
-
-def write_table(flat_ref, member_ref, energy_ref, out_ref):
-    sums = sum_atoms(flat_ref, member_ref)
-    out_ref[...] = jnp.concatenate([to_rows(sums), to_rows(energy_ref[...])], axis=0)
-
-
-def last_part_kernel(corner_ref, member_ref, energy_ref, field_ref, near_ref,
-                     returned_ref, far_ref, out_ref, flat_ref):
-    flat_ref[...] = near_ref[...] + returned_ref[...]
-    chunks = some_planes(7, [far_ref])
-    project(field_reader(field_ref), chunks, corner_ref, flat_ref, flat_ref)
-    write_table(flat_ref, member_ref, energy_ref, out_ref)
-
-
-def whole_pack_kernel(proj_ref, out_ref):
-    pack_plane(0, proj_ref.shape[2] // LANES, proj_ref, out_ref)
-
-
-def high_kernel(proj_ref, out_ref):
-    pack_plane(HALVES, HALVES, proj_ref, out_ref)
-
-
-def whole_sums_kernel(corner_ref, member_ref, energy_ref, field_ref, whole_ref, out_ref, flat_ref):
-    project(field_reader(field_ref), all_planes(whole_ref), corner_ref, flat_ref)
-    write_table(flat_ref, member_ref, energy_ref, out_ref)
-
-
-def step_kernel(index, chunk_count, member_ref, along_z_ref, along_y_ref, field_ref, potential_ref,
-                mate_ref, cross_ref, *refs):
-    factors = step_factors()
-    is_first, is_last = index == 0, index + 1 == len(factors)
+    total = -0.5 * total + (potential_ref[...] - CENTRE) * cells
+    if index > 0:
+        total = total - (second / first) * before_ref[...]
+    out_ref[...] = total
+
+
+def add_cross_halo(cross_ref, parts_ref, extent):
+    odd = odd_here()
+    for near in range(REACH):
+        total = None
+        for k in range(near + 1, REACH + 1):
+            plane = odd * (k - 1 - near) + (1 - odd) * (REACH + near - k)
+            cells = cross_ref[pl.ds(pl.multiple_of(plane * SY, SY), SY), :]
+            term = (-0.5 * STENCIL_WEIGHTS[k]) * cells
+            total = term if total is None else total + term
+        at = (0, odd * (extent - 1 - near) + (1 - odd) * near)
+        parts_ref[at] = parts_ref[at] + total
+
+
+def step_kernel(index, chunk_count, member_ref, local_ref, cross_ref, *refs):
+    first, _ = step_factors()[index]
+    is_first, is_last = index == 0, index + 1 == DEGREE
     refs = list(refs)
-    odd = odd_here()
     own_ref, far_ref = refs.pop(0), refs.pop(0)
     if is_first:
         table = from_rows(own_ref[...] + refs.pop(0)[...] + far_ref[...])
@@ -361,44 +386,31 @@
         chunks = all_planes(refs[0])
     refs = refs[chunk_count:]
     energy_ref = None if is_first else refs.pop(0)
-    before_ref = None if is_first else refs.pop(0)
     corner_hbm = refs.pop(0)
     next_ref = refs.pop(0)
     if not is_last:
         next_mate_ref, next_cross_ref = refs.pop(0), refs.pop(0)
     if is_first:
         energy_ref = refs.pop(0)
-    flat_ref, box_ref, parts_ref, padded_ref, corner_ref, corner_sem = refs
+    flat_ref, box_ref, parts_ref, corner_ref, corner_sem = refs
     corner_copy = pltpu.make_async_copy(corner_hbm, corner_ref, corner_sem)
     corner_copy.start()
-    extent = field_ref.shape[0]
     if is_first:
         atoms = table.shape[1] // 2
         energy_ref[...] = table[:, atoms:]
         table = table[:, :atoms]
     scaled = table * energy_ref[...]
     box_values(scaled, chunks, member_ref, flat_ref, box_ref)
-
-    cells = field_ref[...]
-    padded_ref[REACH : REACH + extent] = cells
-    mate_at = (1 - odd) * (extent + REACH)
-    cross_at = odd * (extent + REACH)
-    padded_ref[pl.ds(mate_at, REACH)] = mate_ref[:HALO_ROWS].reshape(REACH, SY, LANES)
-    padded_ref[pl.ds(cross_at, REACH)] = cross_ref[:HALO_ROWS].reshape(REACH, SY, LANES)
-    value = -0.5 * laplacian(padded_ref, extent, along_z_ref, along_y_ref) + (potential_ref[...] - CENTRE) * cells
-    parts_ref[0] = value
-    parts_ref[1:] = jnp.zeros((COPIES - 1,) + value.shape, jnp.float32)
+    parts_ref[0] = local_ref[...]
+    parts_ref[1:] = jnp.zeros((COPIES - 1,) + local_ref.shape, jnp.float32)
+    add_cross_halo(cross_ref, parts_ref, local_ref.shape[0])
     corner_copy.wait()
     deposit(corner_ref, box_ref, parts_ref)
-    value = total_of([parts_ref[u] for u in range(COPIES)])
-    value = factors[index][0] * value
-    if not is_first:
-        value = value - factors[index][1] * before_ref[...]
-    next_ref[...] = value
+    next_ref[...] = first * total_of([parts_ref[u] for u in range(COPIES)])
     if not is_last:
         project(field_reader(next_ref), chunks, corner_ref, flat_ref)
         sums = sum_atoms(flat_ref, member_ref)
-        write_halos(next_ref, odd, next_mate_ref, next_cross_ref)
+        write_halos(next_ref, odd_here(), next_mate_ref, next_cross_ref)
         next_mate_ref[HALO_ROWS:] = to_rows(sums)
         next_cross_ref[HALO_ROWS:] = to_rows(sums)
 
@@ -406,6 +418,8 @@
 VMEM = pl.BlockSpec(memory_space=pltpu.VMEM)
 SMEM = pl.BlockSpec(memory_space=pltpu.SMEM)
 ANY = pl.BlockSpec(memory_space=pl.ANY)
+NO_COST = pl.CostEstimate(flops=0, bytes_accessed=0, transcendentals=0)
+LOCAL_COST = pl.CostEstimate(flops=5 * 10**7, bytes_accessed=10**6, transcendentals=0)
 
 
 def swap(values, axis, first):
@@ -436,7 +450,8 @@
     def shaped(*shape):
         return jax.ShapeDtypeStruct(shape, jnp.float32)
 
-    def call(kernel, name, out_shape, scalars, operands, scratch, after=(), in_place={}, late=()):
+    def call(kernel, name, out_shape, scalars, operands, scratch, after=(), in_place={}, late=(),
+             cost=NO_COST):
         inputs = len(scalars) + len(operands) + len(late)
 
         def body(*refs):
@@ -454,7 +469,7 @@
             ],
             compiler_params=pltpu.CompilerParams(vmem_limit_bytes=16 * 2**20),
             input_output_aliases=in_place,
-            cost_estimate=pl.CostEstimate(flops=0, bytes_accessed=0, transcendentals=0),
+            cost_estimate=cost,
             name=name,
         )(*scalars, *operands, *late, *after)
 
@@ -555,13 +570,19 @@
             own = to_cross.at[HALO_ROWS:].add(mate[HALO_ROWS:])
             cross = swap(own, "dom", 1)
             far = swap(cross[HALO_ROWS:], "dom", 0)
-        operands = [*tables, field, potential, mate, cross, own, far]
+        local = call(
+            functools.partial(local_kernel, index), f"local_{index + 1}",
+            shaped(planes, SY, LANES), [],
+            [*tables[1:], field, potential, mate] + ([before] if index > 0 else []), [padded],
+            cost=LOCAL_COST,
+        )
+        operands = [tables[0], local, cross, own, far]
         if index == 0:
             operands.append(other)
         operands += chunks
         out_shape = [shaped(planes, SY, LANES)]
         if index > 0:
-            operands += [energy, before]
+            operands.append(energy)
         if index + 1 < DEGREE:
             out_shape += sends
         if index == 0:
@@ -570,7 +591,7 @@
             functools.partial(step_kernel, index, len(chunks)), f"filter_step_{index + 1}",
             out_shape, [], operands,
             [
-                flat, boxes, parts, padded,
+                flat, boxes, parts,
                 pltpu.SMEM(slot_corner.shape, jnp.int32), pltpu.SemaphoreType.DMA,
             ],
             late=[slot_corner],

time: 71.1 us -> 70.6 us (level)
  waiting for transfers between devices: 32.7 us -> 31.7 us
    ppermute x11, waiting for transfers between devices: 17.1 us -> 16.1 us  [swap(): return lax.ppermute(values, axis, pairs)]
    pallas_call x14 -> x17, Pallas kernels: 11.4 us -> 11.8 us  [call(): pl.pallas_call(body, out_shape=out_shape, in_specs=[SMEM] * len(scalars)...]
  transfers between devices with their start and end apart: 18 -> 18, of which waited for: 15 -> 15; matrix products, arithmetic and copies ran while one was open for 0% -> 0% of each run, Pallas kernels for 6% -> 7%
where the time goes in v8:
time: 70.6 us; the launch traced here: 70.4 us
  waiting for transfers between devices  31.7 us (45%)
  starting transfers between devices  24.7 us (35%)
  Pallas kernels  11.8 us (17%)
  local copies, waits for them, and re-layouts  1.9 us (3%)
    ppermute x11, starting transfers between devices, swap(): return lax.ppermute(values, axis, pairs)  20.3 us
    ppermute x11, waiting for transfers between devices, swap(): return lax.ppermute(values, axis, pairs)  16.1 us
    ppermute x7, waiting for transfers between devices, turn(): lax.ppermute(values, axis, [(i, (i + step) % count) for i in range(count)])  15.6 us
    pallas_call x17, Pallas kernels, call(): pl.pallas_call(body, out_shape=out_shape, in_specs=[SMEM] * len(scalars)...  11.8 us
    ppermute x7, starting transfers between devices, turn(): lax.ppermute(values, axis, [(i, (i + step) % count) for i in range(count)])  4.39 us
    unnamed x14, local copies, waits for them, and re-layouts  1.67 us
  transfers between devices with their start and end apart: 18, of which 15 were waited for; matrix products, arithmetic and copies ran while one was open for 0% of the time, Pallas kernels for 7%

profile of v8, /device:TPU:5, one launch (start us, length us, event | category | flops | bytes accessed | tf_op | source)
XLA Modules:
  0.0 70.4 jit_solution(10094535378364348376)
XLA Ops:
  0.0 1.1 %copy-done.1 = f32[32,8,512]{2,1,0:T(8,128)S(1)} copy-done((f32[32,8,512]{2,1,0:T(8,128)S(1)}, f32[32,8,512]{2,1,0:T(8,128)}, u32[]{:S(2)}) %copy-start.1) | copy-done | bytes 524312
  1.1 0.9 %pack_low.1.refs_1_ = f32[608,128]{1,0:T(8,128)S(1)} custom-call(f32[32,8,512]{2,1,0:T(8,128)S(1)} %copy-done.1), custom_call_target="tpu_custom_call" | custom-call | tf_op jit(solution)/shard_map/pack_low/pallas_call | solution.py:460
  2.0 1.3 %collective-permute-start = (f32[608,128]{1,0:T(8,128)S(1)}, f32[608,128]{1,0:T(8,128)S(1)}, u32[]{:S(2)}, u32[]{:S(2)}) collective-permute-start(f32[608,128]{1,0:T(8,128)S(1)} %add_window.1.refs_1_.refs_2_.refs_6_.refs_5_), channel_id=1, source_target_pairs={{0,1},{1,2},{2,3},{3,0},{4,5},{5,6},{6,7},{7,4},{8,9},{9,10},{10,1... | collective-permute-start | bytes 933896 | tf_op jit(solution)/shard_map/ppermute | solution.py:435
  3.4 0.9 %pack_high.1.refs_2_.refs_3_.refs_7_.refs_6_ = f32[512,128]{1,0:T(8,128)S(1)} custom-call(f32[32,8,512]{2,1,0:T(8,128)S(1)} %copy-done.2, f32[608,128]{1,0:T(8,128)S(1)} %add_window.1.refs_1_.refs_2_.refs_6_.refs_5_), custom_call_target="tpu_custom_call" | custom-call | tf_op jit(solution)/shard_map/pack_high/pallas_call | solution.py:460
  4.3 1.3 %collective-permute-start.2 = (f32[512,128]{1,0:T(8,128)S(1)}, f32[512,128]{1,0:T(8,128)S(1)}, u32[]{:S(2)}, u32[]{:S(2)}) collective-permute-start(f32[512,128]{1,0:T(8,128)S(1)} %pack_high.1.refs_2_.refs_3_.refs_7_.refs_6_), channel_id=1, source_target_pairs={{0,1},{1,2},{2,3},{3,0},{4,5},{5,6},{6,7},{7,4},{8,9},{9,10},{10,1... | collective-permute-start | bytes 786440 | tf_op jit(solution)/shard_map/ppermute | solution.py:435
  5.6 6.6 %collective-permute-done.refs_3_.refs_4_.refs_10_.refs_9_ = f32[608,128]{1,0:T(8,128)S(1)} collective-permute-done((f32[608,128]{1,0:T(8,128)S(1)}, f32[608,128]{1,0:T(8,128)S(1)}, u32[]{:S(2)}, u32[]{:S(2)}) %collective-permute-start) | collective-permute-done | bytes 311328 | tf_op jit(solution)/shard_map/ppermute | solution.py:435
  12.2 0.8 %project_above.1 = (f32[4,8,128]{2,1,0:T(8,128)S(1)}, f32[512,128]{1,0:T(8,128)S(1)}) custom-call(s32[3,32]{1,0:T(4,128)S(1)} %copy-done.4, f32[608,128]{1,0:T(8,128)S(1)} %add_window.1.refs_1_.refs_2_.refs_6_.refs_5_, f32[512,128]{1,0:T(8,128)S(1)} %pack_high.1.refs_2_.refs_3_.refs_7_.refs_6_, ...), custom_call_target="tpu_custom_call" | custom-call | tf_op jit(solution)/shard_map/project_above/pallas_call | solution.py:460
  13.1 1.4 %collective-permute-start.3 = (f32[4,8,128]{2,1,0:T(8,128)S(1)}, f32[4,8,128]{2,1,0:T(8,128)S(1)}, u32[]{:S(2)}, u32[]{:S(2)}) collective-permute-start(f32[4,8,128]{2,1,0:T(8,128)S(1)} %get-tuple-element.47), channel_id=1, source_target_pairs={{0,3},{1,0},{2,1},{3,2},{4,7},{5,4},{6,5},{7,6},{8,11},{9,8},{10,9... | collective-permute-start | bytes 49160 | tf_op jit(solution)/shard_map/ppermute | solution.py:435
  15.6 2.3 %collective-permute-done.2.refs_0_.refs_5_.refs_11_.refs_10_ = f32[512,128]{1,0:T(8,128)S(1)} collective-permute-done((f32[512,128]{1,0:T(8,128)S(1)}, f32[512,128]{1,0:T(8,128)S(1)}, u32[]{:S(2)}, u32[]{:S(2)}) %collective-permute-start.2) | collective-permute-done | bytes 262176 | tf_op jit(solution)/shard_map/ppermute | solution.py:435
  18.8 3.1 %collective-permute-done.1.refs_0_.refs_6_.refs_12_.refs_11_ = f32[512,128]{1,0:T(8,128)S(1)} collective-permute-done((f32[512,128]{1,0:T(8,128)S(1)}, f32[512,128]{1,0:T(8,128)S(1)}, u32[]{:S(2)}, u32[]{:S(2)}) %collective-permute-start.1) | collective-permute-done | bytes 262176 | tf_op jit(solution)/shard_map/ppermute | solution.py:435
  22.0 5.8 %collective-permute-start.4 = (f32[96,128]{1,0:T(8,128)S(1)}, f32[96,128]{1,0:T(8,128)S(1)}, u32[]{:S(2)}, u32[]{:S(2)}) collective-permute-start(f32[96,128]{1,0:T(8,128)S(1)} %get-tuple-element.48), channel_id=1, source_target_pairs={{0,4},{4,0},{8,12},{12,8},{16,20},{20,16},{24,28},{28,24},{1,5},{5... | collective-permute-start | bytes 147464 | tf_op jit(solution)/shard_map/ppermute | solution.py:430
  27.8 3.0 %collective-permute-start.5 = (f32[96,128]{1,0:T(8,128)S(1)}, f32[96,128]{1,0:T(8,128)S(1)}, u32[]{:S(2)}, u32[]{:S(2)}) collective-permute-start(f32[96,128]{1,0:T(8,128)S(1)} %get-tuple-element.49), channel_id=1, source_target_pairs={{4,8},{8,4},{12,16},{16,12},{20,24},{24,20},{5,9},{9,5},{13,17},{1... | collective-permute-start | bytes 147464 | tf_op jit(solution)/shard_map/ppermute | solution.py:430
  30.9 1.0 %project_near.1.refs_4_.refs_1_ = f32[4,8,128]{2,1,0:T(8,128)S(1)} custom-call(s32[3,32]{1,0:T(4,128)S(1)} %copy-done.4, f32[12,16,128]{2,1,0:T(8,128)S(1)} %bitcast.5, f32[608,128]{1,0:T(8,128)S(1)} %add_window.1.refs_1_.refs_2_.refs_6_.refs_5_, f32[512,128]{1,0:T(8,128)S(1)} %pack_high.1.refs_2_.refs_3_.refs_7_.refs_6_, ...), custom_call_target="tpu_custom_call" | custom-call | tf_op jit(solution)/shard_map/project_near/pallas_call | solution.py:460
  31.9 1.5 %collective-permute-done.5.refs_5_.refs_2_ = f32[96,128]{1,0:T(8,128)S(1)} collective-permute-done((f32[96,128]{1,0:T(8,128)S(1)}, f32[96,128]{1,0:T(8,128)S(1)}, u32[]{:S(2)}, u32[]{:S(2)}) %collective-permute-start.5) | collective-permute-done | bytes 49184 | tf_op jit(solution)/shard_map/ppermute | solution.py:430
  33.6 0.9 %first_sums.1 = f32[16,128]{1,0:T(8,128)S(1)} custom-call(s32[3,32]{1,0:T(4,128)S(1)} %copy-done.4, bf16[128,512]{1,0:T(8,128)(2,1)S(1)} %get-tuple-element.43.refs_2_.refs_1_.refs_0_, f32[8,128]{1,0:T(8,128)S(1)} %broadcast_select_fusion.refs_3_.refs_2_, f32[12,16,128]{2,1,0:T(8,128)S(1)} %bitcast.6, f32[4,8,128]{2,1,0:T(8,128)S(1)} %project_near.1.refs_4_.refs_1_, ...), custom_call_target="tpu_custom_call" | custom-call | tf_op jit(solution)/shard_map/first_sums/pallas_call | solution.py:460
  35.1 0.8 %collective-permute-done.7 = f32[16,128]{1,0:T(8,128)S(1)} collective-permute-done((f32[16,128]{1,0:T(8,128)S(1)}, f32[16,128]{1,0:T(8,128)S(1)}, u32[]{:S(2)}, u32[]{:S(2)}) %collective-permute-start.7) | collective-permute-done | bytes 8224 | tf_op jit(solution)/shard_map/ppermute | solution.py:430
  35.9 2.4 %collective-permute-start.8 = (f32[16,128]{1,0:T(8,128)S(1)}, f32[16,128]{1,0:T(8,128)S(1)}, u32[]{:S(2)}, u32[]{:S(2)}) collective-permute-start(f32[16,128]{1,0:T(8,128)S(1)} %add.22.refs_3_), channel_id=1, source_target_pairs={{4,8},{8,4},{12,16},{16,12},{20,24},{24,20},{5,9},{9,5},{13,17},{1... | collective-permute-start | bytes 24584 | tf_op jit(solution)/shard_map/ppermute | solution.py:430
  38.4 2.8 %collective-permute-done.8.refs_5_ = f32[16,128]{1,0:T(8,128)S(1)} collective-permute-done((f32[16,128]{1,0:T(8,128)S(1)}, f32[16,128]{1,0:T(8,128)S(1)}, u32[]{:S(2)}, u32[]{:S(2)}) %collective-permute-start.8) | collective-permute-done | bytes 8224 | tf_op jit(solution)/shard_map/ppermute | solution.py:430
  41.2 0.9 %collective-permute-start.9 = (f32[16,128]{1,0:T(8,128)S(1)}, f32[16,128]{1,0:T(8,128)S(1)}, u32[]{:S(2)}, u32[]{:S(2)}) collective-permute-start(f32[16,128]{1,0:T(8,128)S(1)} %collective-permute-done.8.refs_5_), channel_id=1, source_target_pairs={{0,4},{4,0},{8,12},{12,8},{16,20},{20,16},{24,28},{28,24},{1,5},{5... | collective-permute-start | bytes 24584 | tf_op jit(solution)/shard_map/ppermute | solution.py:430
  43.0 2.8 %collective-permute-done.11.refs_9_.refs_8_ = f32[512,128]{1,0:T(8,128)S(1)} collective-permute-done((f32[512,128]{1,0:T(8,128)S(1)}, f32[512,128]{1,0:T(8,128)S(1)}, u32[]{:S(2)}, u32[]{:S(2)}) %collective-permute-start.11) | collective-permute-done | bytes 262176 | tf_op jit(solution)/shard_map/ppermute | solution.py:435
  45.7 2.1 %filter_step_1.1 = (f32[12,16,128]{2,1,0:T(8,128)S(1)}, f32[104,128]{1,0:T(8,128)S(1)}, f32[104,128]{1,0:T(8,128)S(1)}, f32[8,128]{1,0:T(8,128)S(1)}) custom-call(bf16[128,512]{1,0:T(8,128)(2,1)S(1)} %get-tuple-element.43.refs_2_.refs_1_.refs_0_, f32[12,16,128]{2,1,0:T(8,128)S(1)} %local_1.1.refs_1_, f32[96,128]{1,0:T(8,128)S(1)} %collective-permute-done.5.refs_5_.refs_2_, ...), custom_call_target="tpu_custom_call" | custom-call | tf_op jit(solution)/shard_map/filter_step_1/pallas_call | solution.py:460
  47.8 1.3 %collective-permute-start.12 = (f32[104,128]{1,0:T(8,128)S(1)}, f32[104,128]{1,0:T(8,128)S(1)}, u32[]{:S(2)}, u32[]{:S(2)}) collective-permute-start(f32[104,128]{1,0:T(8,128)S(1)} %get-tuple-element.51), channel_id=1, source_target_pairs={{0,4},{4,0},{8,12},{12,8},{16,20},{20,16},{24,28},{28,24},{1,5},{5... | collective-permute-start | bytes 159752 | tf_op jit(solution)/shard_map/ppermute | solution.py:430
  49.1 0.9 %collective-permute-done.12.refs_4_ = f32[104,128]{1,0:T(8,128)S(1)} collective-permute-done((f32[104,128]{1,0:T(8,128)S(1)}, f32[104,128]{1,0:T(8,128)S(1)}, u32[]{:S(2)}, u32[]{:S(2)}) %collective-permute-start.12) | collective-permute-done | bytes 53280 | tf_op jit(solution)/shard_map/ppermute | solution.py:430
  50.0 1.9 %collective-permute-start.13 = (f32[104,128]{1,0:T(8,128)S(1)}, f32[104,128]{1,0:T(8,128)S(1)}, u32[]{:S(2)}, u32[]{:S(2)}) collective-permute-start(f32[104,128]{1,0:T(8,128)S(1)} %fusion.1.refs_3_), channel_id=1, source_target_pairs={{4,8},{8,4},{12,16},{16,12},{20,24},{24,20},{5,9},{9,5},{13,17},{1... | collective-permute-start | bytes 159752 | tf_op jit(solution)/shard_map/ppermute | solution.py:430
  52.0 3.8 %collective-permute-done.13.refs_2_ = f32[104,128]{1,0:T(8,128)S(1)} collective-permute-done((f32[104,128]{1,0:T(8,128)S(1)}, f32[104,128]{1,0:T(8,128)S(1)}, u32[]{:S(2)}, u32[]{:S(2)}) %collective-permute-start.13) | collective-permute-done | bytes 53280 | tf_op jit(solution)/shard_map/ppermute | solution.py:430
  55.8 1.0 %collective-permute-start.14 = (f32[8,128]{1,0:T(8,128)S(1)}, f32[8,128]{1,0:T(8,128)S(1)}, u32[]{:S(2)}, u32[]{:S(2)}) collective-permute-start(f32[8,128]{1,0:T(8,128)S(1)} %slice.57), channel_id=1, source_target_pairs={{0,4},{4,0},{8,12},{12,8},{16,20},{20,16},{24,28},{28,24},{1,5},{5... | collective-permute-start | bytes 12296 | tf_op jit(solution)/shard_map/ppermute | solution.py:430
  57.6 2.1 %filter_step_2.1 = (f32[12,16,128]{2,1,0:T(8,128)S(1)}, f32[104,128]{1,0:T(8,128)S(1)}, f32[104,128]{1,0:T(8,128)S(1)}) custom-call(bf16[128,512]{1,0:T(8,128)(2,1)S(1)} %get-tuple-element.43.refs_2_.refs_1_.refs_0_, f32[12,16,128]{2,1,0:T(8,128)S(1)} %local_2.1.refs_1_, f32[104,128]{1,0:T(8,128)S(1)} %collective-permute-done.13.refs_2_, ...), custom_call_target="tpu_custom_call" | custom-call | tf_op jit(solution)/shard_map/filter_step_2/pallas_call | solution.py:460
  60.1 0.9 %collective-permute-done.15.refs_4_ = f32[104,128]{1,0:T(8,128)S(1)} collective-permute-done((f32[104,128]{1,0:T(8,128)S(1)}, f32[104,128]{1,0:T(8,128)S(1)}, u32[]{:S(2)}, u32[]{:S(2)}) %collective-permute-start.15) | collective-permute-done | bytes 53280 | tf_op jit(solution)/shard_map/ppermute | solution.py:430
  61.0 1.9 %collective-permute-start.16 = (f32[104,128]{1,0:T(8,128)S(1)}, f32[104,128]{1,0:T(8,128)S(1)}, u32[]{:S(2)}, u32[]{:S(2)}) collective-permute-start(f32[104,128]{1,0:T(8,128)S(1)} %fusion.refs_3_), channel_id=1, source_target_pairs={{4,8},{8,4},{12,16},{16,12},{20,24},{24,20},{5,9},{9,5},{13,17},{1... | collective-permute-start | bytes 159752 | tf_op jit(solution)/shard_map/ppermute | solution.py:430
  62.9 3.8 %collective-permute-done.16.refs_2_ = f32[104,128]{1,0:T(8,128)S(1)} collective-permute-done((f32[104,128]{1,0:T(8,128)S(1)}, f32[104,128]{1,0:T(8,128)S(1)}, u32[]{:S(2)}, u32[]{:S(2)}) %collective-permute-start.16) | collective-permute-done | bytes 53280 | tf_op jit(solution)/shard_map/ppermute | solution.py:430
  66.7 0.9 %collective-permute-start.17 = (f32[8,128]{1,0:T(8,128)S(1)}, f32[8,128]{1,0:T(8,128)S(1)}, u32[]{:S(2)}, u32[]{:S(2)}) collective-permute-start(f32[8,128]{1,0:T(8,128)S(1)} %slice.59), channel_id=1, source_target_pairs={{0,4},{4,0},{8,12},{12,8},{16,20},{20,16},{24,28},{28,24},{1,5},{5... | collective-permute-start | bytes 12296 | tf_op jit(solution)/shard_map/ppermute | solution.py:430
  68.5 1.9 %filter_step_3.1 = f32[12,16,128]{2,1,0:T(8,128)} custom-call(bf16[128,512]{1,0:T(8,128)(2,1)S(1)} %get-tuple-element.43.refs_2_.refs_1_.refs_0_, f32[12,16,128]{2,1,0:T(8,128)S(1)} %local_3.1.refs_1_, f32[104,128]{1,0:T(8,128)S(1)} %collective-permute-done.16.refs_2_, f32[104,128]{1,0:T(8,128)S(1)} %fusion.refs_3_, ...), custom_call_target="tpu_custom_call" | custom-call | tf_op jit(solution)/shard_map/filter_step_3/pallas_call | solution.py:460
  (46 shorter events, 5.7 us)
Async XLA Ops:
  0.0 2.0 %copy-start = (f32[1,12,16,128]{3,2,1,0:T(8,128)S(1)}, f32[1,12,16,128]{3,2,1,0:T(8,128)}, u32[]{:S(2)}) copy-start(f32[1,12,16,128]{3,2,1,0:T(8,128)} %param.10) | copy-start | bytes 294916
  0.0 1.1 %copy-start.1 = (f32[32,8,512]{2,1,0:T(8,128)S(1)}, f32[32,8,512]{2,1,0:T(8,128)}, u32[]{:S(2)}) copy-start(f32[32,8,512]{2,1,0:T(8,128)} %refs_0_.6) | copy-start | bytes 1572868
  2.0 1.4 %copy-start.2 = (f32[32,8,512]{2,1,0:T(8,128)S(1)}, f32[32,8,512]{2,1,0:T(8,128)}, u32[]{:S(2)}) copy-start(f32[32,8,512]{2,1,0:T(8,128)} %refs_0_.6) | copy-start | bytes 1572868
  2.0 10.2 %collective-permute-start = (f32[608,128]{1,0:T(8,128)S(1)}, f32[608,128]{1,0:T(8,128)S(1)}, u32[]{:S(2)}, u32[]{:S(2)}) collective-permute-start(f32[608,128]{1,0:T(8,128)S(1)} %add_window.1.refs_1_.refs_2_.refs_6_.refs_5_), channel_id=1, source_target_pairs={{0,1},{1,2},{2,3},{3,0},{4,5},{5,6},{6,7},{7,4},{8,9},{9,10},{10,1... | collective-permute-start | bytes 933896 | tf_op jit(solution)/shard_map/ppermute | solution.py:435
  4.3 13.6 %collective-permute-start.2 = (f32[512,128]{1,0:T(8,128)S(1)}, f32[512,128]{1,0:T(8,128)S(1)}, u32[]{:S(2)}, u32[]{:S(2)}) collective-permute-start(f32[512,128]{1,0:T(8,128)S(1)} %pack_high.1.refs_2_.refs_3_.refs_7_.refs_6_), channel_id=1, source_target_pairs={{0,1},{1,2},{2,3},{3,0},{4,5},{5,6},{6,7},{7,4},{8,9},{9,10},{10,1... | collective-permute-start | bytes 786440 | tf_op jit(solution)/shard_map/ppermute | solution.py:435
  5.6 6.6 %copy-start.4 = (s32[3,32]{1,0:T(4,128)S(1)}, s32[3,32]{1,0:T(4,128)}, u32[]{:S(2)}) copy-start(s32[3,32]{1,0:T(4,128)} %refs_14_.5) | copy-start | bytes 1156
  13.1 5.6 %collective-permute-start.3 = (f32[4,8,128]{2,1,0:T(8,128)S(1)}, f32[4,8,128]{2,1,0:T(8,128)S(1)}, u32[]{:S(2)}, u32[]{:S(2)}) collective-permute-start(f32[4,8,128]{2,1,0:T(8,128)S(1)} %get-tuple-element.47), channel_id=1, source_target_pairs={{0,3},{1,0},{2,1},{3,2},{4,7},{5,4},{6,5},{7,6},{8,11},{9,8},{10,9... | collective-permute-start | bytes 49160 | tf_op jit(solution)/shard_map/ppermute | solution.py:435
  14.5 0.7 copy-start.6
  14.5 7.4 %collective-permute-start.1 = (f32[512,128]{1,0:T(8,128)S(1)}, f32[512,128]{1,0:T(8,128)S(1)}, u32[]{:S(2)}, u32[]{:S(2)}) collective-permute-start(f32[512,128]{1,0:T(8,128)S(1)} %get-tuple-element.46.refs_1_), channel_id=1, source_target_pairs={{0,1},{1,2},{2,3},{3,0},{4,5},{5,6},{6,7},{7,4},{8,9},{9,10},{10,1... | collective-permute-start | bytes 786440 | tf_op jit(solution)/shard_map/ppermute | solution.py:435
  14.6 0.7 %copy-start.5 = (f32[16,8]{0,1:T(8,128)S(1)}, f32[16,8]{0,1:T(8,128)}, u32[]{:S(2)}) copy-start(f32[16,8]{0,1:T(8,128)} %param.13) | copy-start | bytes 1540
  18.7 13.2 %collective-permute-start.6 = (f32[512,128]{1,0:T(8,128)S(1)}, f32[512,128]{1,0:T(8,128)S(1)}, u32[]{:S(2)}, u32[]{:S(2)}) collective-permute-start(f32[512,128]{1,0:T(8,128)S(1)} %hand_on.3.refs_1_), channel_id=1, source_target_pairs={{0,1},{1,2},{2,3},{3,0},{4,5},{5,6},{6,7},{7,4},{8,9},{9,10},{10,1... | collective-permute-start | bytes 786440 | tf_op jit(solution)/shard_map/ppermute | solution.py:435
  22.0 10.0 %collective-permute-start.4 = (f32[96,128]{1,0:T(8,128)S(1)}, f32[96,128]{1,0:T(8,128)S(1)}, u32[]{:S(2)}, u32[]{:S(2)}) collective-permute-start(f32[96,128]{1,0:T(8,128)S(1)} %get-tuple-element.48), channel_id=1, source_target_pairs={{0,4},{4,0},{8,12},{12,8},{16,20},{20,16},{24,28},{28,24},{1,5},{5... | collective-permute-start | bytes 147464 | tf_op jit(solution)/shard_map/ppermute | solution.py:430
  27.8 5.7 %collective-permute-start.5 = (f32[96,128]{1,0:T(8,128)S(1)}, f32[96,128]{1,0:T(8,128)S(1)}, u32[]{:S(2)}, u32[]{:S(2)}) collective-permute-start(f32[96,128]{1,0:T(8,128)S(1)} %get-tuple-element.49), channel_id=1, source_target_pairs={{4,8},{8,4},{12,16},{16,12},{20,24},{24,20},{5,9},{9,5},{13,17},{1... | collective-permute-start | bytes 147464 | tf_op jit(solution)/shard_map/ppermute | solution.py:430
  30.8 12.2 %collective-permute-start.10 = (f32[512,128]{1,0:T(8,128)S(1)}, f32[512,128]{1,0:T(8,128)S(1)}, u32[]{:S(2)}, u32[]{:S(2)}) collective-permute-start(f32[512,128]{1,0:T(8,128)S(1)} %hand_on.4.refs_1_), channel_id=1, source_target_pairs={{0,1},{1,2},{2,3},{3,0},{4,5},{5,6},{6,7},{7,4},{8,9},{9,10},{10,1... | collective-permute-start | bytes 786440 | tf_op jit(solution)/shard_map/ppermute | solution.py:435
  33.5 8.6 %copy-start.3 = (f32[12,16,128]{2,1,0:T(8,128)S(1)}, f32[12,16,128]{2,1,0:T(8,128)}, u32[]{:S(2)}) copy-start(f32[12,16,128]{2,1,0:T(8,128)} %refs_3_.5) | copy-start | bytes 294916
  33.5 12.2 %collective-permute-start.11 = (f32[512,128]{1,0:T(8,128)S(1)}, f32[512,128]{1,0:T(8,128)S(1)}, u32[]{:S(2)}, u32[]{:S(2)}) collective-permute-start(f32[512,128]{1,0:T(8,128)S(1)} %hand_on.5), channel_id=1, source_target_pairs={{0,1},{1,2},{2,3},{3,0},{4,5},{5,6},{6,7},{7,4},{8,9},{9,10},{10,1... | collective-permute-start | bytes 786440 | tf_op jit(solution)/shard_map/ppermute | solution.py:435
  34.4 1.5 %collective-permute-start.7 = (f32[16,128]{1,0:T(8,128)S(1)}, f32[16,128]{1,0:T(8,128)S(1)}, u32[]{:S(2)}, u32[]{:S(2)}) collective-permute-start(f32[16,128]{1,0:T(8,128)S(1)} %first_sums.1), channel_id=1, source_target_pairs={{0,4},{4,0},{8,12},{12,8},{16,20},{20,16},{24,28},{28,24},{1,5},{5... | collective-permute-start | bytes 24584 | tf_op jit(solution)/shard_map/ppermute | solution.py:430
  35.9 5.3 %collective-permute-start.8 = (f32[16,128]{1,0:T(8,128)S(1)}, f32[16,128]{1,0:T(8,128)S(1)}, u32[]{:S(2)}, u32[]{:S(2)}) collective-permute-start(f32[16,128]{1,0:T(8,128)S(1)} %add.22.refs_3_), channel_id=1, source_target_pairs={{4,8},{8,4},{12,16},{16,12},{20,24},{24,20},{5,9},{9,5},{13,17},{1... | collective-permute-start | bytes 24584 | tf_op jit(solution)/shard_map/ppermute | solution.py:430
  41.2 1.8 %collective-permute-start.9 = (f32[16,128]{1,0:T(8,128)S(1)}, f32[16,128]{1,0:T(8,128)S(1)}, u32[]{:S(2)}, u32[]{:S(2)}) collective-permute-start(f32[16,128]{1,0:T(8,128)S(1)} %collective-permute-done.8.refs_5_), channel_id=1, source_target_pairs={{0,4},{4,0},{8,12},{12,8},{16,20},{20,16},{24,28},{28,24},{1,5},{5... | collective-permute-start | bytes 24584 | tf_op jit(solution)/shard_map/ppermute | solution.py:430
  47.8 2.2 %collective-permute-start.12 = (f32[104,128]{1,0:T(8,128)S(1)}, f32[104,128]{1,0:T(8,128)S(1)}, u32[]{:S(2)}, u32[]{:S(2)}) collective-permute-start(f32[104,128]{1,0:T(8,128)S(1)} %get-tuple-element.51), channel_id=1, source_target_pairs={{0,4},{4,0},{8,12},{12,8},{16,20},{20,16},{24,28},{28,24},{1,5},{5... | collective-permute-start | bytes 159752 | tf_op jit(solution)/shard_map/ppermute | solution.py:430
  50.0 5.7 %collective-permute-start.13 = (f32[104,128]{1,0:T(8,128)S(1)}, f32[104,128]{1,0:T(8,128)S(1)}, u32[]{:S(2)}, u32[]{:S(2)}) collective-permute-start(f32[104,128]{1,0:T(8,128)S(1)} %fusion.1.refs_3_), channel_id=1, source_target_pairs={{4,8},{8,4},{12,16},{16,12},{20,24},{24,20},{5,9},{9,5},{13,17},{1... | collective-permute-start | bytes 159752 | tf_op jit(solution)/shard_map/ppermute | solution.py:430
  55.8 1.8 %collective-permute-start.14 = (f32[8,128]{1,0:T(8,128)S(1)}, f32[8,128]{1,0:T(8,128)S(1)}, u32[]{:S(2)}, u32[]{:S(2)}) collective-permute-start(f32[8,128]{1,0:T(8,128)S(1)} %slice.57), channel_id=1, source_target_pairs={{0,4},{4,0},{8,12},{12,8},{16,20},{20,16},{24,28},{28,24},{1,5},{5... | collective-permute-start | bytes 12296 | tf_op jit(solution)/shard_map/ppermute | solution.py:430
  59.6 1.3 %collective-permute-start.15 = (f32[104,128]{1,0:T(8,128)S(1)}, f32[104,128]{1,0:T(8,128)S(1)}, u32[]{:S(2)}, u32[]{:S(2)}) collective-permute-start(f32[104,128]{1,0:T(8,128)S(1)} %get-tuple-element.55), channel_id=1, source_target_pairs={{0,4},{4,0},{8,12},{12,8},{16,20},{20,16},{24,28},{28,24},{1,5},{5... | collective-permute-start | bytes 159752 | tf_op jit(solution)/shard_map/ppermute | solution.py:430
  61.0 5.7 %collective-permute-start.16 = (f32[104,128]{1,0:T(8,128)S(1)}, f32[104,128]{1,0:T(8,128)S(1)}, u32[]{:S(2)}, u32[]{:S(2)}) collective-permute-start(f32[104,128]{1,0:T(8,128)S(1)} %fusion.refs_3_), channel_id=1, source_target_pairs={{4,8},{8,4},{12,16},{16,12},{20,24},{24,20},{5,9},{9,5},{13,17},{1... | collective-permute-start | bytes 159752 | tf_op jit(solution)/shard_map/ppermute | solution.py:430
  66.7 1.8 %collective-permute-start.17 = (f32[8,128]{1,0:T(8,128)S(1)}, f32[8,128]{1,0:T(8,128)S(1)}, u32[]{:S(2)}, u32[]{:S(2)}) collective-permute-start(f32[8,128]{1,0:T(8,128)S(1)} %slice.59), channel_id=1, source_target_pairs={{0,4},{4,0},{8,12},{12,8},{16,20},{20,16},{24,28},{28,24},{1,5},{5... | collective-permute-start | bytes 12296 | tf_op jit(solution)/shard_map/ppermute | solution.py:430

commit v9 on v8

--- a/solution.py
+++ b/solution.py
@@ -204,23 +204,22 @@
                 )
 
 
-def deposit(corner_ref, box_ref, parts_ref):
-    copies = parts_ref.shape[0]
+def deposit(corner_ref, box_ref, parts_refs):
     lane_block = iota((ROWS, LANES), 1) // SZ
     for group in range(box_ref.shape[0]):
         for u in range(ROWS):
             slot = group * ROWS + u
+            part_ref = parts_refs[u % len(parts_refs)]
             planes = pl.ds(corner_ref[0, slot], SX)
             shift = lax.rem(LANES + corner_ref[2, slot] - u * SZ, LANES)
-            for half in range(HALVES):
-                at = (u % copies, planes, pl.ds(half * ROWS, ROWS), slice(None))
-                added = [
-                    pltpu.roll(
-                        jnp.where(lane_block == u, box_ref[group, x * HALVES + half], 0.0), shift, 1
-                    )
-                    for x in range(SX)
-                ]
-                parts_ref[at] = parts_ref[at] + jnp.stack(added)
+            turned = [
+                pltpu.roll(jnp.where(lane_block == u, box_ref[group, tile], 0.0), shift, 1)
+                for tile in range(TILES)
+            ]
+            added = [
+                jnp.concatenate(turned[x * HALVES : (x + 1) * HALVES], axis=0) for x in range(SX)
+            ]
+            part_ref[planes] = part_ref[planes] + jnp.stack(added)
 
 
 def band_matrix(size, block, centre):
@@ -358,7 +357,7 @@
     out_ref[...] = total
 
 
-def add_cross_halo(cross_ref, parts_ref, extent):
+def add_cross_halo(cross_ref, part_ref, extent):
     odd = odd_here()
     for near in range(REACH):
         total = None
@@ -367,8 +366,8 @@
             cells = cross_ref[pl.ds(pl.multiple_of(plane * SY, SY), SY), :]
             term = (-0.5 * STENCIL_WEIGHTS[k]) * cells
             total = term if total is None else total + term
-        at = (0, odd * (extent - 1 - near) + (1 - odd) * near)
-        parts_ref[at] = parts_ref[at] + total
+        at = odd * (extent - 1 - near) + (1 - odd) * near
+        part_ref[at] = part_ref[at] + total
 
 
 def step_kernel(index, chunk_count, member_ref, local_ref, cross_ref, *refs):
@@ -392,7 +391,7 @@
         next_mate_ref, next_cross_ref = refs.pop(0), refs.pop(0)
     if is_first:
         energy_ref = refs.pop(0)
-    flat_ref, box_ref, parts_ref, corner_ref, corner_sem = refs
+    flat_ref, box_ref, corner_ref, corner_sem, *parts_refs = refs
     corner_copy = pltpu.make_async_copy(corner_hbm, corner_ref, corner_sem)
     corner_copy.start()
     if is_first:
@@ -401,12 +400,13 @@
         table = table[:, :atoms]
     scaled = table * energy_ref[...]
     box_values(scaled, chunks, member_ref, flat_ref, box_ref)
-    parts_ref[0] = local_ref[...]
-    parts_ref[1:] = jnp.zeros((COPIES - 1,) + local_ref.shape, jnp.float32)
-    add_cross_halo(cross_ref, parts_ref, local_ref.shape[0])
+    parts_refs[0][...] = local_ref[...]
+    for part_ref in parts_refs[1:]:
+        part_ref[...] = jnp.zeros(part_ref.shape, jnp.float32)
+    add_cross_halo(cross_ref, parts_refs[0], local_ref.shape[0])
     corner_copy.wait()
-    deposit(corner_ref, box_ref, parts_ref)
-    next_ref[...] = first * total_of([parts_ref[u] for u in range(COPIES)])
+    deposit(corner_ref, box_ref, parts_refs)
+    next_ref[...] = first * total_of([part_ref[...] for part_ref in parts_refs])
     if not is_last:
         project(field_reader(next_ref), chunks, corner_ref, flat_ref)
         sums = sum_atoms(flat_ref, member_ref)
@@ -478,14 +478,14 @@
     energy = jnp.where(own_atoms[None, :], jnp.tile(kb_energy.T, (1, atoms // atom_own)), 0.0)
     flat = (groups, ROWS, LANES)
     boxes = (groups, TILES, ROWS, LANES)
-    parts = (COPIES, planes, SY, LANES)
+    parts = (planes, SY, LANES)
     padded = (planes + 2 * REACH, SY, LANES)
     table_rows = ROWS * atoms // LANES
     sends = [shaped(HALO_ROWS + table_rows, LANES)] * 2
 
     flat = (groups, ROWS, LANES)
     boxes = (groups, TILES, ROWS, LANES)
-    parts = (COPIES, planes, SY, LANES)
+    parts = (planes, SY, LANES)
     padded = (planes + 2 * REACH, SY, LANES)
     table_rows = ROWS * atoms // LANES
     sends = [shaped(HALO_ROWS + table_rows, LANES)] * 2
@@ -591,8 +591,9 @@
             functools.partial(step_kernel, index, len(chunks)), f"filter_step_{index + 1}",
             out_shape, [], operands,
             [
-                flat, boxes, parts,
+                flat, boxes,
                 pltpu.SMEM(slot_corner.shape, jnp.int32), pltpu.SemaphoreType.DMA,
+                *[parts] * COPIES,
             ],
             late=[slot_corner],
         )

time: 70.6 us -> 70.6 us (level)
  no operation moved by 1% of the time
where the time goes in v9:
time: 70.6 us; the launch traced here: 70.3 us
  waiting for transfers between devices  31.7 us (45%)
  starting transfers between devices  24.7 us (35%)
  Pallas kernels  11.7 us (17%)
  local copies, waits for them, and re-layouts  1.9 us (3%)
    ppermute x11, starting transfers between devices, swap(): return lax.ppermute(values, axis, pairs)  20.3 us
    ppermute x11, waiting for transfers between devices, swap(): return lax.ppermute(values, axis, pairs)  16.1 us
    ppermute x7, waiting for transfers between devices, turn(): lax.ppermute(values, axis, [(i, (i + step) % count) for i in range(count)])  15.6 us
    pallas_call x17, Pallas kernels, call(): pl.pallas_call(body, out_shape=out_shape, in_specs=[SMEM] * len(scalars)...  11.7 us
    ppermute x7, starting transfers between devices, turn(): lax.ppermute(values, axis, [(i, (i + step) % count) for i in range(count)])  4.39 us
    unnamed x14, local copies, waits for them, and re-layouts  1.67 us
  transfers between devices with their start and end apart: 18, of which 15 were waited for; matrix products, arithmetic and copies ran while one was open for 0% of the time, Pallas kernels for 7%

profile of v9, /device:TPU:5, one launch (start us, length us, event | category | flops | bytes accessed | tf_op | source)
XLA Modules:
  0.0 70.3 jit_solution(17658484667332554666)
XLA Ops:
  0.0 1.1 %copy-done.1 = f32[32,8,512]{2,1,0:T(8,128)S(1)} copy-done((f32[32,8,512]{2,1,0:T(8,128)S(1)}, f32[32,8,512]{2,1,0:T(8,128)}, u32[]{:S(2)}) %copy-start.1) | copy-done | bytes 524312
  1.1 0.9 %pack_low.1.refs_1_ = f32[608,128]{1,0:T(8,128)S(1)} custom-call(f32[32,8,512]{2,1,0:T(8,128)S(1)} %copy-done.1), custom_call_target="tpu_custom_call" | custom-call | tf_op jit(solution)/shard_map/pack_low/pallas_call | solution.py:460
  2.0 1.3 %collective-permute-start = (f32[608,128]{1,0:T(8,128)S(1)}, f32[608,128]{1,0:T(8,128)S(1)}, u32[]{:S(2)}, u32[]{:S(2)}) collective-permute-start(f32[608,128]{1,0:T(8,128)S(1)} %add_window.1.refs_1_.refs_2_.refs_6_.refs_5_), channel_id=1, source_target_pairs={{0,1},{1,2},{2,3},{3,0},{4,5},{5,6},{6,7},{7,4},{8,9},{9,10},{10,1... | collective-permute-start | bytes 933896 | tf_op jit(solution)/shard_map/ppermute | solution.py:435
  3.4 0.9 %pack_high.1.refs_2_.refs_3_.refs_7_.refs_6_ = f32[512,128]{1,0:T(8,128)S(1)} custom-call(f32[32,8,512]{2,1,0:T(8,128)S(1)} %copy-done.2, f32[608,128]{1,0:T(8,128)S(1)} %add_window.1.refs_1_.refs_2_.refs_6_.refs_5_), custom_call_target="tpu_custom_call" | custom-call | tf_op jit(solution)/shard_map/pack_high/pallas_call | solution.py:460
  4.3 1.3 %collective-permute-start.2 = (f32[512,128]{1,0:T(8,128)S(1)}, f32[512,128]{1,0:T(8,128)S(1)}, u32[]{:S(2)}, u32[]{:S(2)}) collective-permute-start(f32[512,128]{1,0:T(8,128)S(1)} %pack_high.1.refs_2_.refs_3_.refs_7_.refs_6_), channel_id=1, source_target_pairs={{0,1},{1,2},{2,3},{3,0},{4,5},{5,6},{6,7},{7,4},{8,9},{9,10},{10,1... | collective-permute-start | bytes 786440 | tf_op jit(solution)/shard_map/ppermute | solution.py:435
  5.6 6.6 %collective-permute-done.refs_3_.refs_4_.refs_10_.refs_9_ = f32[608,128]{1,0:T(8,128)S(1)} collective-permute-done((f32[608,128]{1,0:T(8,128)S(1)}, f32[608,128]{1,0:T(8,128)S(1)}, u32[]{:S(2)}, u32[]{:S(2)}) %collective-permute-start) | collective-permute-done | bytes 311328 | tf_op jit(solution)/shard_map/ppermute | solution.py:435
  12.2 0.8 %project_above.1 = (f32[4,8,128]{2,1,0:T(8,128)S(1)}, f32[512,128]{1,0:T(8,128)S(1)}) custom-call(s32[3,32]{1,0:T(4,128)S(1)} %copy-done.4, f32[608,128]{1,0:T(8,128)S(1)} %add_window.1.refs_1_.refs_2_.refs_6_.refs_5_, f32[512,128]{1,0:T(8,128)S(1)} %pack_high.1.refs_2_.refs_3_.refs_7_.refs_6_, ...), custom_call_target="tpu_custom_call" | custom-call | tf_op jit(solution)/shard_map/project_above/pallas_call | solution.py:460
  13.1 1.4 %collective-permute-start.3 = (f32[4,8,128]{2,1,0:T(8,128)S(1)}, f32[4,8,128]{2,1,0:T(8,128)S(1)}, u32[]{:S(2)}, u32[]{:S(2)}) collective-permute-start(f32[4,8,128]{2,1,0:T(8,128)S(1)} %get-tuple-element.47), channel_id=1, source_target_pairs={{0,3},{1,0},{2,1},{3,2},{4,7},{5,4},{6,5},{7,6},{8,11},{9,8},{10,9... | collective-permute-start | bytes 49160 | tf_op jit(solution)/shard_map/ppermute | solution.py:435
  15.6 2.3 %collective-permute-done.2.refs_0_.refs_5_.refs_11_.refs_10_ = f32[512,128]{1,0:T(8,128)S(1)} collective-permute-done((f32[512,128]{1,0:T(8,128)S(1)}, f32[512,128]{1,0:T(8,128)S(1)}, u32[]{:S(2)}, u32[]{:S(2)}) %collective-permute-start.2) | collective-permute-done | bytes 262176 | tf_op jit(solution)/shard_map/ppermute | solution.py:435
  18.8 3.1 %collective-permute-done.1.refs_0_.refs_6_.refs_12_.refs_11_ = f32[512,128]{1,0:T(8,128)S(1)} collective-permute-done((f32[512,128]{1,0:T(8,128)S(1)}, f32[512,128]{1,0:T(8,128)S(1)}, u32[]{:S(2)}, u32[]{:S(2)}) %collective-permute-start.1) | collective-permute-done | bytes 262176 | tf_op jit(solution)/shard_map/ppermute | solution.py:435
  22.0 5.8 %collective-permute-start.4 = (f32[96,128]{1,0:T(8,128)S(1)}, f32[96,128]{1,0:T(8,128)S(1)}, u32[]{:S(2)}, u32[]{:S(2)}) collective-permute-start(f32[96,128]{1,0:T(8,128)S(1)} %get-tuple-element.48), channel_id=1, source_target_pairs={{0,4},{4,0},{8,12},{12,8},{16,20},{20,16},{24,28},{28,24},{1,5},{5... | collective-permute-start | bytes 147464 | tf_op jit(solution)/shard_map/ppermute | solution.py:430
  27.8 3.0 %collective-permute-start.5 = (f32[96,128]{1,0:T(8,128)S(1)}, f32[96,128]{1,0:T(8,128)S(1)}, u32[]{:S(2)}, u32[]{:S(2)}) collective-permute-start(f32[96,128]{1,0:T(8,128)S(1)} %get-tuple-element.49), channel_id=1, source_target_pairs={{4,8},{8,4},{12,16},{16,12},{20,24},{24,20},{5,9},{9,5},{13,17},{1... | collective-permute-start | bytes 147464 | tf_op jit(solution)/shard_map/ppermute | solution.py:430
  30.9 1.0 %project_near.1.refs_4_.refs_1_ = f32[4,8,128]{2,1,0:T(8,128)S(1)} custom-call(s32[3,32]{1,0:T(4,128)S(1)} %copy-done.4, f32[12,16,128]{2,1,0:T(8,128)S(1)} %bitcast.5, f32[608,128]{1,0:T(8,128)S(1)} %add_window.1.refs_1_.refs_2_.refs_6_.refs_5_, f32[512,128]{1,0:T(8,128)S(1)} %pack_high.1.refs_2_.refs_3_.refs_7_.refs_6_, ...), custom_call_target="tpu_custom_call" | custom-call | tf_op jit(solution)/shard_map/project_near/pallas_call | solution.py:460
  31.9 1.5 %collective-permute-done.5.refs_5_.refs_2_ = f32[96,128]{1,0:T(8,128)S(1)} collective-permute-done((f32[96,128]{1,0:T(8,128)S(1)}, f32[96,128]{1,0:T(8,128)S(1)}, u32[]{:S(2)}, u32[]{:S(2)}) %collective-permute-start.5) | collective-permute-done | bytes 49184 | tf_op jit(solution)/shard_map/ppermute | solution.py:430
  33.6 0.9 %first_sums.1 = f32[16,128]{1,0:T(8,128)S(1)} custom-call(s32[3,32]{1,0:T(4,128)S(1)} %copy-done.4, bf16[128,512]{1,0:T(8,128)(2,1)S(1)} %get-tuple-element.43.refs_2_.refs_1_.refs_0_, f32[8,128]{1,0:T(8,128)S(1)} %broadcast_select_fusion.refs_3_.refs_2_, f32[12,16,128]{2,1,0:T(8,128)S(1)} %bitcast.6, f32[4,8,128]{2,1,0:T(8,128)S(1)} %project_near.1.refs_4_.refs_1_, ...), custom_call_target="tpu_custom_call" | custom-call | tf_op jit(solution)/shard_map/first_sums/pallas_call | solution.py:460
  35.1 0.8 %collective-permute-done.7 = f32[16,128]{1,0:T(8,128)S(1)} collective-permute-done((f32[16,128]{1,0:T(8,128)S(1)}, f32[16,128]{1,0:T(8,128)S(1)}, u32[]{:S(2)}, u32[]{:S(2)}) %collective-permute-start.7) | collective-permute-done | bytes 8224 | tf_op jit(solution)/shard_map/ppermute | solution.py:430
  35.9 2.4 %collective-permute-start.8 = (f32[16,128]{1,0:T(8,128)S(1)}, f32[16,128]{1,0:T(8,128)S(1)}, u32[]{:S(2)}, u32[]{:S(2)}) collective-permute-start(f32[16,128]{1,0:T(8,128)S(1)} %add.22.refs_3_), channel_id=1, source_target_pairs={{4,8},{8,4},{12,16},{16,12},{20,24},{24,20},{5,9},{9,5},{13,17},{1... | collective-permute-start | bytes 24584 | tf_op jit(solution)/shard_map/ppermute | solution.py:430
  38.4 2.8 %collective-permute-done.8.refs_5_ = f32[16,128]{1,0:T(8,128)S(1)} collective-permute-done((f32[16,128]{1,0:T(8,128)S(1)}, f32[16,128]{1,0:T(8,128)S(1)}, u32[]{:S(2)}, u32[]{:S(2)}) %collective-permute-start.8) | collective-permute-done | bytes 8224 | tf_op jit(solution)/shard_map/ppermute | solution.py:430
  41.2 0.9 %collective-permute-start.9 = (f32[16,128]{1,0:T(8,128)S(1)}, f32[16,128]{1,0:T(8,128)S(1)}, u32[]{:S(2)}, u32[]{:S(2)}) collective-permute-start(f32[16,128]{1,0:T(8,128)S(1)} %collective-permute-done.8.refs_5_), channel_id=1, source_target_pairs={{0,4},{4,0},{8,12},{12,8},{16,20},{20,16},{24,28},{28,24},{1,5},{5... | collective-permute-start | bytes 24584 | tf_op jit(solution)/shard_map/ppermute | solution.py:430
  43.0 2.8 %collective-permute-done.11.refs_9_.refs_8_ = f32[512,128]{1,0:T(8,128)S(1)} collective-permute-done((f32[512,128]{1,0:T(8,128)S(1)}, f32[512,128]{1,0:T(8,128)S(1)}, u32[]{:S(2)}, u32[]{:S(2)}) %collective-permute-start.11) | collective-permute-done | bytes 262176 | tf_op jit(solution)/shard_map/ppermute | solution.py:435
  45.7 2.1 %filter_step_1.1 = (f32[12,16,128]{2,1,0:T(8,128)S(1)}, f32[104,128]{1,0:T(8,128)S(1)}, f32[104,128]{1,0:T(8,128)S(1)}, f32[8,128]{1,0:T(8,128)S(1)}) custom-call(bf16[128,512]{1,0:T(8,128)(2,1)S(1)} %get-tuple-element.43.refs_2_.refs_1_.refs_0_, f32[12,16,128]{2,1,0:T(8,128)S(1)} %local_1.1.refs_1_, f32[96,128]{1,0:T(8,128)S(1)} %collective-permute-done.5.refs_5_.refs_2_, ...), custom_call_target="tpu_custom_call" | custom-call | tf_op jit(solution)/shard_map/filter_step_1/pallas_call | solution.py:460
  47.8 1.3 %collective-permute-start.12 = (f32[104,128]{1,0:T(8,128)S(1)}, f32[104,128]{1,0:T(8,128)S(1)}, u32[]{:S(2)}, u32[]{:S(2)}) collective-permute-start(f32[104,128]{1,0:T(8,128)S(1)} %get-tuple-element.51), channel_id=1, source_target_pairs={{0,4},{4,0},{8,12},{12,8},{16,20},{20,16},{24,28},{28,24},{1,5},{5... | collective-permute-start | bytes 159752 | tf_op jit(solution)/shard_map/ppermute | solution.py:430
  49.1 0.9 %collective-permute-done.12.refs_4_ = f32[104,128]{1,0:T(8,128)S(1)} collective-permute-done((f32[104,128]{1,0:T(8,128)S(1)}, f32[104,128]{1,0:T(8,128)S(1)}, u32[]{:S(2)}, u32[]{:S(2)}) %collective-permute-start.12) | collective-permute-done | bytes 53280 | tf_op jit(solution)/shard_map/ppermute | solution.py:430
  50.0 1.9 %collective-permute-start.13 = (f32[104,128]{1,0:T(8,128)S(1)}, f32[104,128]{1,0:T(8,128)S(1)}, u32[]{:S(2)}, u32[]{:S(2)}) collective-permute-start(f32[104,128]{1,0:T(8,128)S(1)} %fusion.1.refs_3_), channel_id=1, source_target_pairs={{4,8},{8,4},{12,16},{16,12},{20,24},{24,20},{5,9},{9,5},{13,17},{1... | collective-permute-start | bytes 159752 | tf_op jit(solution)/shard_map/ppermute | solution.py:430
  51.9 3.8 %collective-permute-done.13.refs_2_ = f32[104,128]{1,0:T(8,128)S(1)} collective-permute-done((f32[104,128]{1,0:T(8,128)S(1)}, f32[104,128]{1,0:T(8,128)S(1)}, u32[]{:S(2)}, u32[]{:S(2)}) %collective-permute-start.13) | collective-permute-done | bytes 53280 | tf_op jit(solution)/shard_map/ppermute | solution.py:430
  55.8 1.0 %collective-permute-start.14 = (f32[8,128]{1,0:T(8,128)S(1)}, f32[8,128]{1,0:T(8,128)S(1)}, u32[]{:S(2)}, u32[]{:S(2)}) collective-permute-start(f32[8,128]{1,0:T(8,128)S(1)} %slice.57), channel_id=1, source_target_pairs={{0,4},{4,0},{8,12},{12,8},{16,20},{20,16},{24,28},{28,24},{1,5},{5... | collective-permute-start | bytes 12296 | tf_op jit(solution)/shard_map/ppermute | solution.py:430
  57.5 2.1 %filter_step_2.1 = (f32[12,16,128]{2,1,0:T(8,128)S(1)}, f32[104,128]{1,0:T(8,128)S(1)}, f32[104,128]{1,0:T(8,128)S(1)}) custom-call(bf16[128,512]{1,0:T(8,128)(2,1)S(1)} %get-tuple-element.43.refs_2_.refs_1_.refs_0_, f32[12,16,128]{2,1,0:T(8,128)S(1)} %local_2.1.refs_1_, f32[104,128]{1,0:T(8,128)S(1)} %collective-permute-done.13.refs_2_, ...), custom_call_target="tpu_custom_call" | custom-call | tf_op jit(solution)/shard_map/filter_step_2/pallas_call | solution.py:460
  60.0 0.9 %collective-permute-done.15.refs_4_ = f32[104,128]{1,0:T(8,128)S(1)} collective-permute-done((f32[104,128]{1,0:T(8,128)S(1)}, f32[104,128]{1,0:T(8,128)S(1)}, u32[]{:S(2)}, u32[]{:S(2)}) %collective-permute-start.15) | collective-permute-done | bytes 53280 | tf_op jit(solution)/shard_map/ppermute | solution.py:430
  60.9 1.9 %collective-permute-start.16 = (f32[104,128]{1,0:T(8,128)S(1)}, f32[104,128]{1,0:T(8,128)S(1)}, u32[]{:S(2)}, u32[]{:S(2)}) collective-permute-start(f32[104,128]{1,0:T(8,128)S(1)} %fusion.refs_3_), channel_id=1, source_target_pairs={{4,8},{8,4},{12,16},{16,12},{20,24},{24,20},{5,9},{9,5},{13,17},{1... | collective-permute-start | bytes 159752 | tf_op jit(solution)/shard_map/ppermute | solution.py:430
  62.8 3.8 %collective-permute-done.16.refs_2_ = f32[104,128]{1,0:T(8,128)S(1)} collective-permute-done((f32[104,128]{1,0:T(8,128)S(1)}, f32[104,128]{1,0:T(8,128)S(1)}, u32[]{:S(2)}, u32[]{:S(2)}) %collective-permute-start.16) | collective-permute-done | bytes 53280 | tf_op jit(solution)/shard_map/ppermute | solution.py:430
  66.7 1.0 %collective-permute-start.17 = (f32[8,128]{1,0:T(8,128)S(1)}, f32[8,128]{1,0:T(8,128)S(1)}, u32[]{:S(2)}, u32[]{:S(2)}) collective-permute-start(f32[8,128]{1,0:T(8,128)S(1)} %slice.59), channel_id=1, source_target_pairs={{0,4},{4,0},{8,12},{12,8},{16,20},{20,16},{24,28},{28,24},{1,5},{5... | collective-permute-start | bytes 12296 | tf_op jit(solution)/shard_map/ppermute | solution.py:430
  68.4 1.9 %filter_step_3.1 = f32[12,16,128]{2,1,0:T(8,128)} custom-call(bf16[128,512]{1,0:T(8,128)(2,1)S(1)} %get-tuple-element.43.refs_2_.refs_1_.refs_0_, f32[12,16,128]{2,1,0:T(8,128)S(1)} %local_3.1.refs_1_, f32[104,128]{1,0:T(8,128)S(1)} %collective-permute-done.16.refs_2_, f32[104,128]{1,0:T(8,128)S(1)} %fusion.refs_3_, ...), custom_call_target="tpu_custom_call" | custom-call | tf_op jit(solution)/shard_map/filter_step_3/pallas_call | solution.py:460
  (46 shorter events, 5.7 us)
Async XLA Ops:
  0.0 2.0 %copy-start = (f32[1,12,16,128]{3,2,1,0:T(8,128)S(1)}, f32[1,12,16,128]{3,2,1,0:T(8,128)}, u32[]{:S(2)}) copy-start(f32[1,12,16,128]{3,2,1,0:T(8,128)} %param.10) | copy-start | bytes 294916
  0.0 1.1 %copy-start.1 = (f32[32,8,512]{2,1,0:T(8,128)S(1)}, f32[32,8,512]{2,1,0:T(8,128)}, u32[]{:S(2)}) copy-start(f32[32,8,512]{2,1,0:T(8,128)} %refs_0_.6) | copy-start | bytes 1572868
  2.0 1.4 %copy-start.2 = (f32[32,8,512]{2,1,0:T(8,128)S(1)}, f32[32,8,512]{2,1,0:T(8,128)}, u32[]{:S(2)}) copy-start(f32[32,8,512]{2,1,0:T(8,128)} %refs_0_.6) | copy-start | bytes 1572868
  2.0 10.2 %collective-permute-start = (f32[608,128]{1,0:T(8,128)S(1)}, f32[608,128]{1,0:T(8,128)S(1)}, u32[]{:S(2)}, u32[]{:S(2)}) collective-permute-start(f32[608,128]{1,0:T(8,128)S(1)} %add_window.1.refs_1_.refs_2_.refs_6_.refs_5_), channel_id=1, source_target_pairs={{0,1},{1,2},{2,3},{3,0},{4,5},{5,6},{6,7},{7,4},{8,9},{9,10},{10,1... | collective-permute-start | bytes 933896 | tf_op jit(solution)/shard_map/ppermute | solution.py:435
  4.3 13.6 %collective-permute-start.2 = (f32[512,128]{1,0:T(8,128)S(1)}, f32[512,128]{1,0:T(8,128)S(1)}, u32[]{:S(2)}, u32[]{:S(2)}) collective-permute-start(f32[512,128]{1,0:T(8,128)S(1)} %pack_high.1.refs_2_.refs_3_.refs_7_.refs_6_), channel_id=1, source_target_pairs={{0,1},{1,2},{2,3},{3,0},{4,5},{5,6},{6,7},{7,4},{8,9},{9,10},{10,1... | collective-permute-start | bytes 786440 | tf_op jit(solution)/shard_map/ppermute | solution.py:435
  5.6 6.6 %copy-start.4 = (s32[3,32]{1,0:T(4,128)S(1)}, s32[3,32]{1,0:T(4,128)}, u32[]{:S(2)}) copy-start(s32[3,32]{1,0:T(4,128)} %refs_14_.5) | copy-start | bytes 1156
  13.1 5.6 %collective-permute-start.3 = (f32[4,8,128]{2,1,0:T(8,128)S(1)}, f32[4,8,128]{2,1,0:T(8,128)S(1)}, u32[]{:S(2)}, u32[]{:S(2)}) collective-permute-start(f32[4,8,128]{2,1,0:T(8,128)S(1)} %get-tuple-element.47), channel_id=1, source_target_pairs={{0,3},{1,0},{2,1},{3,2},{4,7},{5,4},{6,5},{7,6},{8,11},{9,8},{10,9... | collective-permute-start | bytes 49160 | tf_op jit(solution)/shard_map/ppermute | solution.py:435
  14.5 0.7 copy-start.6
  14.5 7.4 %collective-permute-start.1 = (f32[512,128]{1,0:T(8,128)S(1)}, f32[512,128]{1,0:T(8,128)S(1)}, u32[]{:S(2)}, u32[]{:S(2)}) collective-permute-start(f32[512,128]{1,0:T(8,128)S(1)} %get-tuple-element.46.refs_1_), channel_id=1, source_target_pairs={{0,1},{1,2},{2,3},{3,0},{4,5},{5,6},{6,7},{7,4},{8,9},{9,10},{10,1... | collective-permute-start | bytes 786440 | tf_op jit(solution)/shard_map/ppermute | solution.py:435
  14.6 0.7 %copy-start.5 = (f32[16,8]{0,1:T(8,128)S(1)}, f32[16,8]{0,1:T(8,128)}, u32[]{:S(2)}) copy-start(f32[16,8]{0,1:T(8,128)} %param.13) | copy-start | bytes 1540
  18.7 13.2 %collective-permute-start.6 = (f32[512,128]{1,0:T(8,128)S(1)}, f32[512,128]{1,0:T(8,128)S(1)}, u32[]{:S(2)}, u32[]{:S(2)}) collective-permute-start(f32[512,128]{1,0:T(8,128)S(1)} %hand_on.3.refs_1_), channel_id=1, source_target_pairs={{0,1},{1,2},{2,3},{3,0},{4,5},{5,6},{6,7},{7,4},{8,9},{9,10},{10,1... | collective-permute-start | bytes 786440 | tf_op jit(solution)/shard_map/ppermute | solution.py:435
  22.0 9.9 %collective-permute-start.4 = (f32[96,128]{1,0:T(8,128)S(1)}, f32[96,128]{1,0:T(8,128)S(1)}, u32[]{:S(2)}, u32[]{:S(2)}) collective-permute-start(f32[96,128]{1,0:T(8,128)S(1)} %get-tuple-element.48), channel_id=1, source_target_pairs={{0,4},{4,0},{8,12},{12,8},{16,20},{20,16},{24,28},{28,24},{1,5},{5... | collective-permute-start | bytes 147464 | tf_op jit(solution)/shard_map/ppermute | solution.py:430
  27.8 5.7 %collective-permute-start.5 = (f32[96,128]{1,0:T(8,128)S(1)}, f32[96,128]{1,0:T(8,128)S(1)}, u32[]{:S(2)}, u32[]{:S(2)}) collective-permute-start(f32[96,128]{1,0:T(8,128)S(1)} %get-tuple-element.49), channel_id=1, source_target_pairs={{4,8},{8,4},{12,16},{16,12},{20,24},{24,20},{5,9},{9,5},{13,17},{1... | collective-permute-start | bytes 147464 | tf_op jit(solution)/shard_map/ppermute | solution.py:430
  30.8 12.2 %collective-permute-start.10 = (f32[512,128]{1,0:T(8,128)S(1)}, f32[512,128]{1,0:T(8,128)S(1)}, u32[]{:S(2)}, u32[]{:S(2)}) collective-permute-start(f32[512,128]{1,0:T(8,128)S(1)} %hand_on.4.refs_1_), channel_id=1, source_target_pairs={{0,1},{1,2},{2,3},{3,0},{4,5},{5,6},{6,7},{7,4},{8,9},{9,10},{10,1... | collective-permute-start | bytes 786440 | tf_op jit(solution)/shard_map/ppermute | solution.py:435
  33.5 8.6 %copy-start.3 = (f32[12,16,128]{2,1,0:T(8,128)S(1)}, f32[12,16,128]{2,1,0:T(8,128)}, u32[]{:S(2)}) copy-start(f32[12,16,128]{2,1,0:T(8,128)} %refs_3_.5) | copy-start | bytes 294916
  33.5 12.2 %collective-permute-start.11 = (f32[512,128]{1,0:T(8,128)S(1)}, f32[512,128]{1,0:T(8,128)S(1)}, u32[]{:S(2)}, u32[]{:S(2)}) collective-permute-start(f32[512,128]{1,0:T(8,128)S(1)} %hand_on.5), channel_id=1, source_target_pairs={{0,1},{1,2},{2,3},{3,0},{4,5},{5,6},{6,7},{7,4},{8,9},{9,10},{10,1... | collective-permute-start | bytes 786440 | tf_op jit(solution)/shard_map/ppermute | solution.py:435
  34.5 1.5 %collective-permute-start.7 = (f32[16,128]{1,0:T(8,128)S(1)}, f32[16,128]{1,0:T(8,128)S(1)}, u32[]{:S(2)}, u32[]{:S(2)}) collective-permute-start(f32[16,128]{1,0:T(8,128)S(1)} %first_sums.1), channel_id=1, source_target_pairs={{0,4},{4,0},{8,12},{12,8},{16,20},{20,16},{24,28},{28,24},{1,5},{5... | collective-permute-start | bytes 24584 | tf_op jit(solution)/shard_map/ppermute | solution.py:430
  35.9 5.3 %collective-permute-start.8 = (f32[16,128]{1,0:T(8,128)S(1)}, f32[16,128]{1,0:T(8,128)S(1)}, u32[]{:S(2)}, u32[]{:S(2)}) collective-permute-start(f32[16,128]{1,0:T(8,128)S(1)} %add.22.refs_3_), channel_id=1, source_target_pairs={{4,8},{8,4},{12,16},{16,12},{20,24},{24,20},{5,9},{9,5},{13,17},{1... | collective-permute-start | bytes 24584 | tf_op jit(solution)/shard_map/ppermute | solution.py:430
  41.2 1.8 %collective-permute-start.9 = (f32[16,128]{1,0:T(8,128)S(1)}, f32[16,128]{1,0:T(8,128)S(1)}, u32[]{:S(2)}, u32[]{:S(2)}) collective-permute-start(f32[16,128]{1,0:T(8,128)S(1)} %collective-permute-done.8.refs_5_), channel_id=1, source_target_pairs={{0,4},{4,0},{8,12},{12,8},{16,20},{20,16},{24,28},{28,24},{1,5},{5... | collective-permute-start | bytes 24584 | tf_op jit(solution)/shard_map/ppermute | solution.py:430
  47.8 2.2 %collective-permute-start.12 = (f32[104,128]{1,0:T(8,128)S(1)}, f32[104,128]{1,0:T(8,128)S(1)}, u32[]{:S(2)}, u32[]{:S(2)}) collective-permute-start(f32[104,128]{1,0:T(8,128)S(1)} %get-tuple-element.51), channel_id=1, source_target_pairs={{0,4},{4,0},{8,12},{12,8},{16,20},{20,16},{24,28},{28,24},{1,5},{5... | collective-permute-start | bytes 159752 | tf_op jit(solution)/shard_map/ppermute | solution.py:430
  50.0 5.7 %collective-permute-start.13 = (f32[104,128]{1,0:T(8,128)S(1)}, f32[104,128]{1,0:T(8,128)S(1)}, u32[]{:S(2)}, u32[]{:S(2)}) collective-permute-start(f32[104,128]{1,0:T(8,128)S(1)} %fusion.1.refs_3_), channel_id=1, source_target_pairs={{4,8},{8,4},{12,16},{16,12},{20,24},{24,20},{5,9},{9,5},{13,17},{1... | collective-permute-start | bytes 159752 | tf_op jit(solution)/shard_map/ppermute | solution.py:430
  55.8 1.8 %collective-permute-start.14 = (f32[8,128]{1,0:T(8,128)S(1)}, f32[8,128]{1,0:T(8,128)S(1)}, u32[]{:S(2)}, u32[]{:S(2)}) collective-permute-start(f32[8,128]{1,0:T(8,128)S(1)} %slice.57), channel_id=1, source_target_pairs={{0,4},{4,0},{8,12},{12,8},{16,20},{20,16},{24,28},{28,24},{1,5},{5... | collective-permute-start | bytes 12296 | tf_op jit(solution)/shard_map/ppermute | solution.py:430
  59.6 1.3 %collective-permute-start.15 = (f32[104,128]{1,0:T(8,128)S(1)}, f32[104,128]{1,0:T(8,128)S(1)}, u32[]{:S(2)}, u32[]{:S(2)}) collective-permute-start(f32[104,128]{1,0:T(8,128)S(1)} %get-tuple-element.55), channel_id=1, source_target_pairs={{0,4},{4,0},{8,12},{12,8},{16,20},{20,16},{24,28},{28,24},{1,5},{5... | collective-permute-start | bytes 159752 | tf_op jit(solution)/shard_map/ppermute | solution.py:430
  60.9 5.7 %collective-permute-start.16 = (f32[104,128]{1,0:T(8,128)S(1)}, f32[104,128]{1,0:T(8,128)S(1)}, u32[]{:S(2)}, u32[]{:S(2)}) collective-permute-start(f32[104,128]{1,0:T(8,128)S(1)} %fusion.refs_3_), channel_id=1, source_target_pairs={{4,8},{8,4},{12,16},{16,12},{20,24},{24,20},{5,9},{9,5},{13,17},{1... | collective-permute-start | bytes 159752 | tf_op jit(solution)/shard_map/ppermute | solution.py:430
  66.7 1.8 %collective-permute-start.17 = (f32[8,128]{1,0:T(8,128)S(1)}, f32[8,128]{1,0:T(8,128)S(1)}, u32[]{:S(2)}, u32[]{:S(2)}) collective-permute-start(f32[8,128]{1,0:T(8,128)S(1)} %slice.59), channel_id=1, source_target_pairs={{0,4},{4,0},{8,12},{12,8},{16,20},{20,16},{24,28},{28,24},{1,5},{5... | collective-permute-start | bytes 12296 | tf_op jit(solution)/shard_map/ppermute | solution.py:430

commit v10 on v9

--- a/solution.py
+++ b/solution.py
@@ -32,7 +32,6 @@
 HALF_WIDTH = (UPPER_EDGE - LOWER_EDGE) / 2.0
 CENTRE = (UPPER_EDGE + LOWER_EDGE) / 2.0
 SIGMA_FIRST = HALF_WIDTH / (ANCHOR_POINT - CENTRE)
-COPIES = 4
 PARTS_FROM = (0, 1, 3, 2)
 
 
@@ -126,7 +125,9 @@
     return value[:ROWS] + value[ROWS : 2 * ROWS] + value[2 * ROWS :]
 
 
-def table_kernel(atom_row_ref, member_ref, along_z_ref, along_y_ref):
+def table_kernel(atom_row_ref, cell_row_ref, member_ref, along_z_ref, along_y_ref, select_ref):
+    cells = iota(select_ref.shape, 0)
+    select_ref[...] = (cells == cell_row_ref[...]).astype(jnp.float32).astype(jnp.bfloat16)
     atoms = iota(member_ref.shape, 0)
     member_ref[...] = (atoms == atom_row_ref[...]).astype(jnp.float32).astype(jnp.bfloat16)
     high, low = halves_of(band_matrix(LANES, LANES, 3.0 * STENCIL_WEIGHTS[0]))
@@ -183,20 +184,59 @@
     )
 
 
+def stacked_halves(value):
+    return jnp.concatenate(halves_of(value), axis=0)
+
+
+def sum_halves(value):
+    rows = value.shape[0] // 2
+    return value[:rows] + value[rows:]
+
+
+def group_lanes(group):
+    return pl.ds(group * LANES, LANES)
+
+
+def project_slab(field, chunks, corner_ref, select_ref, lanes_ref, flat_ref):
+    groups = flat_ref.shape[0]
+    lane_block = iota((ROWS, LANES), 1) // SZ
+    windows = jnp.dot(
+        stacked_halves(field.reshape(-1, LANES)), select_ref[...], preferred_element_type=jnp.float32
+    )
+    lanes_ref[...] = sum_halves(windows).reshape(lanes_ref.shape)
+    for group in range(groups):
+        corners = [corner_ref[0, group * ROWS + u] for u in range(ROWS)]
+        sums = [[] for _ in range(ROWS)]
+        for plane, ref, base in chunks:
+            for half in range(HALVES):
+                rows = pl.ds(half * ROWS, ROWS)
+                box = None
+                for u in range(ROWS):
+                    cells = lanes_ref[corners[u] + plane, rows, group_lanes(group)]
+                    box = cells if u == 0 else jnp.where(lane_block == u, cells, box)
+                for p in range(ROWS):
+                    sums[p].append(values_of(ref, base, groups, half, group, p) * box)
+        flat_ref[group] = fold_rows([total_of(products) for products in sums])
+
+
 def box_values(scaled, chunks, member_ref, flat_ref, box_ref):
     groups = flat_ref.shape[0]
+    margin = (box_ref.shape[1] - SX) // 2
     flat = sum_thirds(
         jnp.dot(thirds_of(scaled), member_ref[...], preferred_element_type=jnp.float32)
     )
     for g in range(groups):
         flat_ref[g] = flat[:, g * LANES : (g + 1) * LANES]
+    empty = jnp.zeros((groups, margin) + box_ref.shape[2:], jnp.float32)
+    box_ref[:, :margin] = empty
+    box_ref[:, margin + SX :] = empty
     for group in range(groups):
         factors = [
             jnp.broadcast_to(flat_ref[group, pl.ds(p, 1), :], (ROWS, LANES)) for p in range(ROWS)
         ]
         for plane, ref, base in chunks:
             for half in range(HALVES):
-                box_ref[group, plane * HALVES + half] = total_of(
+                box_ref[group, margin + plane, half] = total_of(
                     [
                         values_of(ref, base, groups, half, group, p) * factors[p]
                         for p in range(ROWS)
@@ -204,22 +244,26 @@
                 )
 
 
-def deposit(corner_ref, box_ref, parts_refs):
+def deposit(corner_ref, box_ref, select_ref, lanes_ref):
+    extent = lanes_ref.shape[0]
+    groups = box_ref.shape[0]
+    margin = (box_ref.shape[1] - SX) // 2
     lane_block = iota((ROWS, LANES), 1) // SZ
-    for group in range(box_ref.shape[0]):
-        for u in range(ROWS):
-            slot = group * ROWS + u
-            part_ref = parts_refs[u % len(parts_refs)]
-            planes = pl.ds(corner_ref[0, slot], SX)
-            shift = lax.rem(LANES + corner_ref[2, slot] - u * SZ, LANES)
-            turned = [
-                pltpu.roll(jnp.where(lane_block == u, box_ref[group, tile], 0.0), shift, 1)
-                for tile in range(TILES)
-            ]
-            added = [
-                jnp.concatenate(turned[x * HALVES : (x + 1) * HALVES], axis=0) for x in range(SX)
-            ]
-            part_ref[planes] = part_ref[planes] + jnp.stack(added)
+    for group in range(groups):
+        corners = [corner_ref[0, group * ROWS + u] for u in range(ROWS)]
+        for x in range(extent):
+            for half in range(HALVES):
+                value = None
+                for u in range(ROWS):
+                    cells = box_ref[group, margin + x - corners[u], half]
+                    value = cells if u == 0 else jnp.where(lane_block == u, cells, value)
+                lanes_ref[x, pl.ds(half * ROWS, ROWS), group_lanes(group)] = value
+    spread = lanes_ref[...].reshape(extent * SY, groups * LANES)
+    placed = lax.dot_general(
+        stacked_halves(spread), select_ref[...], (((1,), (1,)), ((), ())),
+        preferred_element_type=jnp.float32,
+    )
+    return sum_halves(placed).reshape(extent, SY, LANES)
 
 
 def band_matrix(size, block, centre):
@@ -370,7 +414,7 @@
         part_ref[at] = part_ref[at] + total
 
 
-def step_kernel(index, chunk_count, member_ref, local_ref, cross_ref, *refs):
+def step_kernel(index, chunk_count, member_ref, select_ref, local_ref, cross_ref, *refs):
     first, _ = step_factors()[index]
     is_first, is_last = index == 0, index + 1 == DEGREE
     refs = list(refs)
@@ -391,7 +435,7 @@
         next_mate_ref, next_cross_ref = refs.pop(0), refs.pop(0)
     if is_first:
         energy_ref = refs.pop(0)
-    flat_ref, box_ref, corner_ref, corner_sem, *parts_refs = refs
+    flat_ref, box_ref, lanes_ref, corner_ref, corner_sem = refs
     corner_copy = pltpu.make_async_copy(corner_hbm, corner_ref, corner_sem)
     corner_copy.start()
     if is_first:
@@ -400,15 +444,13 @@
         table = table[:, :atoms]
     scaled = table * energy_ref[...]
     box_values(scaled, chunks, member_ref, flat_ref, box_ref)
-    parts_refs[0][...] = local_ref[...]
-    for part_ref in parts_refs[1:]:
-        part_ref[...] = jnp.zeros(part_ref.shape, jnp.float32)
-    add_cross_halo(cross_ref, parts_refs[0], local_ref.shape[0])
+    next_ref[...] = local_ref[...]
+    add_cross_halo(cross_ref, next_ref, local_ref.shape[0])
     corner_copy.wait()
-    deposit(corner_ref, box_ref, parts_refs)
-    next_ref[...] = first * total_of([part_ref[...] for part_ref in parts_refs])
+    value = first * (next_ref[...] + deposit(corner_ref, box_ref, select_ref, lanes_ref))
+    next_ref[...] = value
     if not is_last:
-        project(field_reader(next_ref), chunks, corner_ref, flat_ref)
+        project_slab(value, chunks, corner_ref, select_ref, lanes_ref, flat_ref)
         sums = sum_atoms(flat_ref, member_ref)
         write_halos(next_ref, odd_here(), next_mate_ref, next_cross_ref)
         next_mate_ref[HALO_ROWS:] = to_rows(sums)
@@ -474,18 +516,17 @@
         )(*scalars, *operands, *late, *after)
 
     atom_row = jnp.repeat(slot_atom, SZ)[None, :]
+    cell_row = (slot_corner[2][:, None] + jnp.arange(SZ, dtype=jnp.int32)[None, :]).reshape(1, -1)
     own_atoms = (jnp.arange(atoms) // atom_own) == place
     energy = jnp.where(own_atoms[None, :], jnp.tile(kb_energy.T, (1, atoms // atom_own)), 0.0)
     flat = (groups, ROWS, LANES)
-    boxes = (groups, TILES, ROWS, LANES)
-    parts = (planes, SY, LANES)
+    boxes = (groups, 2 * planes - SX, HALVES, ROWS, LANES)
     padded = (planes + 2 * REACH, SY, LANES)
     table_rows = ROWS * atoms // LANES
     sends = [shaped(HALO_ROWS + table_rows, LANES)] * 2
 
     flat = (groups, ROWS, LANES)
-    boxes = (groups, TILES, ROWS, LANES)
-    parts = (planes, SY, LANES)
+    boxes = (groups, 2 * planes - SX, HALVES, ROWS, LANES)
     padded = (planes + 2 * REACH, SY, LANES)
     table_rows = ROWS * atoms // LANES
     sends = [shaped(HALO_ROWS + table_rows, LANES)] * 2
@@ -501,10 +542,11 @@
         [
             jax.ShapeDtypeStruct(shape, jnp.bfloat16)
             for shape in (
-                (atoms, slots * SZ), (3 * LANES, LANES), (planes * SY, 3 * planes * SY)
+                (atoms, slots * SZ), (3 * LANES, LANES), (planes * SY, 3 * planes * SY),
+                (LANES, slots * SZ),
             )
         ],
-        [], [atom_row], [],
+        [], [atom_row, cell_row], [],
     )
     halos = [shaped(HALO_ROWS, LANES)] * 2
     if lax.axis_size("band") == 4 and tiles == 2 * HALVES:
@@ -573,10 +615,10 @@
         local = call(
             functools.partial(local_kernel, index), f"local_{index + 1}",
             shaped(planes, SY, LANES), [],
-            [*tables[1:], field, potential, mate] + ([before] if index > 0 else []), [padded],
+            [*tables[1:3], field, potential, mate] + ([before] if index > 0 else []), [padded],
             cost=LOCAL_COST,
         )
-        operands = [tables[0], local, cross, own, far]
+        operands = [tables[0], tables[3], local, cross, own, far]
         if index == 0:
             operands.append(other)
         operands += chunks
@@ -591,9 +633,8 @@
             functools.partial(step_kernel, index, len(chunks)), f"filter_step_{index + 1}",
             out_shape, [], operands,
             [
-                flat, boxes,
+                flat, boxes, (planes, SY, slots * SZ),
                 pltpu.SMEM(slot_corner.shape, jnp.int32), pltpu.SemaphoreType.DMA,
-                *[parts] * COPIES,
             ],
             late=[slot_corner],
         )

time: 70.6 us -> 70.6 us (level)
  transfers between devices with their start and end apart: 18 -> 18, of which waited for: 15 -> 15; matrix products, arithmetic and copies ran while one was open for 0% -> 1% of each run, Pallas kernels for 7% -> 7%
where the time goes in v10:
time: 70.6 us; the launch traced here: 70.3 us
  waiting for transfers between devices  31.5 us (45%)
  starting transfers between devices  24.7 us (35%)
  Pallas kernels  11.8 us (17%)
  local copies, waits for them, and re-layouts  1.99 us (3%)
    ppermute x11, starting transfers between devices, swap(): return lax.ppermute(values, axis, pairs)  20.3 us
    ppermute x11, waiting for transfers between devices, swap(): return lax.ppermute(values, axis, pairs)  16.2 us
    ppermute x7, waiting for transfers between devices, turn(): lax.ppermute(values, axis, [(i, (i + step) % count) for i in range(count)])  15.4 us
    pallas_call x17, Pallas kernels, call(): pl.pallas_call(body, out_shape=out_shape, in_specs=[SMEM] * len(scalars)...  11.8 us
    ppermute x7, starting transfers between devices, turn(): lax.ppermute(values, axis, [(i, (i + step) % count) for i in range(count)])  4.39 us
    unnamed x14, local copies, waits for them, and re-layouts  1.67 us
  transfers between devices with their start and end apart: 18, of which 15 were waited for; matrix products, arithmetic and copies ran while one was open for 1% of the time, Pallas kernels for 7%

profile of v10, /device:TPU:5, one launch (start us, length us, event | category | flops | bytes accessed | tf_op | source)
XLA Modules:
  0.0 70.3 jit_solution(403132326226657461)
XLA Ops:
  0.0 1.1 %copy-done.1 = f32[32,8,512]{2,1,0:T(8,128)S(1)} copy-done((f32[32,8,512]{2,1,0:T(8,128)S(1)}, f32[32,8,512]{2,1,0:T(8,128)}, u32[]{:S(2)}) %copy-start.1) | copy-done | bytes 524312
  1.1 0.9 %pack_low.1.refs_1_ = f32[608,128]{1,0:T(8,128)S(1)} custom-call(f32[32,8,512]{2,1,0:T(8,128)S(1)} %copy-done.1), custom_call_target="tpu_custom_call" | custom-call | tf_op jit(solution)/shard_map/pack_low/pallas_call | solution.py:502
  2.0 1.3 %collective-permute-start = (f32[608,128]{1,0:T(8,128)S(1)}, f32[608,128]{1,0:T(8,128)S(1)}, u32[]{:S(2)}, u32[]{:S(2)}) collective-permute-start(f32[608,128]{1,0:T(8,128)S(1)} %add_window.1.refs_1_.refs_2_.refs_7_.refs_6_), channel_id=1, source_target_pairs={{0,1},{1,2},{2,3},{3,0},{4,5},{5,6},{6,7},{7,4},{8,9},{9,10},{10,1... | collective-permute-start | bytes 933896 | tf_op jit(solution)/shard_map/ppermute | solution.py:477
  3.4 0.9 %pack_high.1.refs_2_.refs_3_.refs_8_.refs_7_ = f32[512,128]{1,0:T(8,128)S(1)} custom-call(f32[32,8,512]{2,1,0:T(8,128)S(1)} %copy-done.2, f32[608,128]{1,0:T(8,128)S(1)} %add_window.1.refs_1_.refs_2_.refs_7_.refs_6_), custom_call_target="tpu_custom_call" | custom-call | tf_op jit(solution)/shard_map/pack_high/pallas_call | solution.py:502
  4.3 1.3 %collective-permute-start.2 = (f32[512,128]{1,0:T(8,128)S(1)}, f32[512,128]{1,0:T(8,128)S(1)}, u32[]{:S(2)}, u32[]{:S(2)}) collective-permute-start(f32[512,128]{1,0:T(8,128)S(1)} %pack_high.1.refs_2_.refs_3_.refs_8_.refs_7_), channel_id=1, source_target_pairs={{0,1},{1,2},{2,3},{3,0},{4,5},{5,6},{6,7},{7,4},{8,9},{9,10},{10,1... | collective-permute-start | bytes 786440 | tf_op jit(solution)/shard_map/ppermute | solution.py:477
  5.7 6.5 %collective-permute-done.refs_3_.refs_4_.refs_11_.refs_10_ = f32[608,128]{1,0:T(8,128)S(1)} collective-permute-done((f32[608,128]{1,0:T(8,128)S(1)}, f32[608,128]{1,0:T(8,128)S(1)}, u32[]{:S(2)}, u32[]{:S(2)}) %collective-permute-start) | collective-permute-done | bytes 311328 | tf_op jit(solution)/shard_map/ppermute | solution.py:477
  12.3 0.8 %project_above.1 = (f32[4,8,128]{2,1,0:T(8,128)S(1)}, f32[512,128]{1,0:T(8,128)S(1)}) custom-call(s32[3,32]{1,0:T(4,128)S(1)} %copy-done.4, f32[608,128]{1,0:T(8,128)S(1)} %add_window.1.refs_1_.refs_2_.refs_7_.refs_6_, f32[512,128]{1,0:T(8,128)S(1)} %pack_high.1.refs_2_.refs_3_.refs_8_.refs_7_, ...), custom_call_target="tpu_custom_call" | custom-call | tf_op jit(solution)/shard_map/project_above/pallas_call | solution.py:502
  13.1 1.4 %collective-permute-start.3 = (f32[4,8,128]{2,1,0:T(8,128)S(1)}, f32[4,8,128]{2,1,0:T(8,128)S(1)}, u32[]{:S(2)}, u32[]{:S(2)}) collective-permute-start(f32[4,8,128]{2,1,0:T(8,128)S(1)} %get-tuple-element.49), channel_id=1, source_target_pairs={{0,3},{1,0},{2,1},{3,2},{4,7},{5,4},{6,5},{7,6},{8,11},{9,8},{10,9... | collective-permute-start | bytes 49160 | tf_op jit(solution)/shard_map/ppermute | solution.py:477
  15.7 2.2 %collective-permute-done.2.refs_0_.refs_5_.refs_12_.refs_11_ = f32[512,128]{1,0:T(8,128)S(1)} collective-permute-done((f32[512,128]{1,0:T(8,128)S(1)}, f32[512,128]{1,0:T(8,128)S(1)}, u32[]{:S(2)}, u32[]{:S(2)}) %collective-permute-start.2) | collective-permute-done | bytes 262176 | tf_op jit(solution)/shard_map/ppermute | solution.py:477
  18.8 3.1 %collective-permute-done.1.refs_0_.refs_6_.refs_13_.refs_12_ = f32[512,128]{1,0:T(8,128)S(1)} collective-permute-done((f32[512,128]{1,0:T(8,128)S(1)}, f32[512,128]{1,0:T(8,128)S(1)}, u32[]{:S(2)}, u32[]{:S(2)}) %collective-permute-start.1) | collective-permute-done | bytes 262176 | tf_op jit(solution)/shard_map/ppermute | solution.py:477
  22.0 5.8 %collective-permute-start.4 = (f32[96,128]{1,0:T(8,128)S(1)}, f32[96,128]{1,0:T(8,128)S(1)}, u32[]{:S(2)}, u32[]{:S(2)}) collective-permute-start(f32[96,128]{1,0:T(8,128)S(1)} %get-tuple-element.50), channel_id=1, source_target_pairs={{0,4},{4,0},{8,12},{12,8},{16,20},{20,16},{24,28},{28,24},{1,5},{5... | collective-permute-start | bytes 147464 | tf_op jit(solution)/shard_map/ppermute | solution.py:472
  27.8 3.0 %collective-permute-start.5 = (f32[96,128]{1,0:T(8,128)S(1)}, f32[96,128]{1,0:T(8,128)S(1)}, u32[]{:S(2)}, u32[]{:S(2)}) collective-permute-start(f32[96,128]{1,0:T(8,128)S(1)} %get-tuple-element.51), channel_id=1, source_target_pairs={{4,8},{8,4},{12,16},{16,12},{20,24},{24,20},{5,9},{9,5},{13,17},{1... | collective-permute-start | bytes 147464 | tf_op jit(solution)/shard_map/ppermute | solution.py:472
  30.9 1.0 %project_near.1.refs_4_.refs_1_ = f32[4,8,128]{2,1,0:T(8,128)S(1)} custom-call(s32[3,32]{1,0:T(4,128)S(1)} %copy-done.4, f32[12,16,128]{2,1,0:T(8,128)S(1)} %bitcast.7, f32[608,128]{1,0:T(8,128)S(1)} %add_window.1.refs_1_.refs_2_.refs_7_.refs_6_, f32[512,128]{1,0:T(8,128)S(1)} %pack_high.1.refs_2_.refs_3_.refs_8_.refs_7_, ...), custom_call_target="tpu_custom_call" | custom-call | tf_op jit(solution)/shard_map/project_near/pallas_call | solution.py:502
  31.9 1.5 %collective-permute-done.5.refs_5_.refs_3_ = f32[96,128]{1,0:T(8,128)S(1)} collective-permute-done((f32[96,128]{1,0:T(8,128)S(1)}, f32[96,128]{1,0:T(8,128)S(1)}, u32[]{:S(2)}, u32[]{:S(2)}) %collective-permute-start.5) | collective-permute-done | bytes 49184 | tf_op jit(solution)/shard_map/ppermute | solution.py:472
  33.5 0.9 %first_sums.1 = f32[16,128]{1,0:T(8,128)S(1)} custom-call(s32[3,32]{1,0:T(4,128)S(1)} %copy-done.4, bf16[128,512]{1,0:T(8,128)(2,1)S(1)} %get-tuple-element.44.refs_2_.refs_1_.refs_0_, f32[8,128]{1,0:T(8,128)S(1)} %broadcast_select_fusion.refs_3_.refs_2_, f32[12,16,128]{2,1,0:T(8,128)S(1)} %bitcast.8, f32[4,8,128]{2,1,0:T(8,128)S(1)} %project_near.1.refs_4_.refs_1_, ...), custom_call_target="tpu_custom_call" | custom-call | tf_op jit(solution)/shard_map/first_sums/pallas_call | solution.py:502
  35.1 0.8 %collective-permute-done.7 = f32[16,128]{1,0:T(8,128)S(1)} collective-permute-done((f32[16,128]{1,0:T(8,128)S(1)}, f32[16,128]{1,0:T(8,128)S(1)}, u32[]{:S(2)}, u32[]{:S(2)}) %collective-permute-start.7) | collective-permute-done | bytes 8224 | tf_op jit(solution)/shard_map/ppermute | solution.py:472
  35.9 2.4 %collective-permute-start.8 = (f32[16,128]{1,0:T(8,128)S(1)}, f32[16,128]{1,0:T(8,128)S(1)}, u32[]{:S(2)}, u32[]{:S(2)}) collective-permute-start(f32[16,128]{1,0:T(8,128)S(1)} %add.52.refs_4_), channel_id=1, source_target_pairs={{4,8},{8,4},{12,16},{16,12},{20,24},{24,20},{5,9},{9,5},{13,17},{1... | collective-permute-start | bytes 24584 | tf_op jit(solution)/shard_map/ppermute | solution.py:472
  38.4 2.8 %collective-permute-done.8.refs_6_ = f32[16,128]{1,0:T(8,128)S(1)} collective-permute-done((f32[16,128]{1,0:T(8,128)S(1)}, f32[16,128]{1,0:T(8,128)S(1)}, u32[]{:S(2)}, u32[]{:S(2)}) %collective-permute-start.8) | collective-permute-done | bytes 8224 | tf_op jit(solution)/shard_map/ppermute | solution.py:472
  41.2 0.9 %collective-permute-start.9 = (f32[16,128]{1,0:T(8,128)S(1)}, f32[16,128]{1,0:T(8,128)S(1)}, u32[]{:S(2)}, u32[]{:S(2)}) collective-permute-start(f32[16,128]{1,0:T(8,128)S(1)} %collective-permute-done.8.refs_6_), channel_id=1, source_target_pairs={{0,4},{4,0},{8,12},{12,8},{16,20},{20,16},{24,28},{28,24},{1,5},{5... | collective-permute-start | bytes 24584 | tf_op jit(solution)/shard_map/ppermute | solution.py:472
  42.9 2.8 %collective-permute-done.11.refs_10_.refs_9_ = f32[512,128]{1,0:T(8,128)S(1)} collective-permute-done((f32[512,128]{1,0:T(8,128)S(1)}, f32[512,128]{1,0:T(8,128)S(1)}, u32[]{:S(2)}, u32[]{:S(2)}) %collective-permute-start.11) | collective-permute-done | bytes 262176 | tf_op jit(solution)/shard_map/ppermute | solution.py:477
  45.7 2.1 %filter_step_1.1 = (f32[12,16,128]{2,1,0:T(8,128)S(1)}, f32[104,128]{1,0:T(8,128)S(1)}, f32[104,128]{1,0:T(8,128)S(1)}, f32[8,128]{1,0:T(8,128)S(1)}) custom-call(bf16[128,512]{1,0:T(8,128)(2,1)S(1)} %get-tuple-element.44.refs_2_.refs_1_.refs_0_, bf16[128,512]{1,0:T(8,128)(2,1)S(1)} %get-tuple-element.45.refs_1_, f32[12,16,128]{2,1,0:T(8,128)S(1)} %local_1.1.refs_2_, ...), custom_call_target="tpu_custom_call" | custom-call | tf_op jit(solution)/shard_map/filter_step_1/pallas_call | solution.py:502
  47.8 1.3 %collective-permute-start.12 = (f32[104,128]{1,0:T(8,128)S(1)}, f32[104,128]{1,0:T(8,128)S(1)}, u32[]{:S(2)}, u32[]{:S(2)}) collective-permute-start(f32[104,128]{1,0:T(8,128)S(1)} %get-tuple-element.53), channel_id=1, source_target_pairs={{0,4},{4,0},{8,12},{12,8},{16,20},{20,16},{24,28},{28,24},{1,5},{5... | collective-permute-start | bytes 159752 | tf_op jit(solution)/shard_map/ppermute | solution.py:472
  49.1 0.9 %collective-permute-done.12.refs_4_ = f32[104,128]{1,0:T(8,128)S(1)} collective-permute-done((f32[104,128]{1,0:T(8,128)S(1)}, f32[104,128]{1,0:T(8,128)S(1)}, u32[]{:S(2)}, u32[]{:S(2)}) %collective-permute-start.12) | collective-permute-done | bytes 53280 | tf_op jit(solution)/shard_map/ppermute | solution.py:472
  50.0 1.9 %collective-permute-start.13 = (f32[104,128]{1,0:T(8,128)S(1)}, f32[104,128]{1,0:T(8,128)S(1)}, u32[]{:S(2)}, u32[]{:S(2)}) collective-permute-start(f32[104,128]{1,0:T(8,128)S(1)} %fusion.1.refs_4_), channel_id=1, source_target_pairs={{4,8},{8,4},{12,16},{16,12},{20,24},{24,20},{5,9},{9,5},{13,17},{1... | collective-permute-start | bytes 159752 | tf_op jit(solution)/shard_map/ppermute | solution.py:472
  51.9 3.8 %collective-permute-done.13.refs_3_ = f32[104,128]{1,0:T(8,128)S(1)} collective-permute-done((f32[104,128]{1,0:T(8,128)S(1)}, f32[104,128]{1,0:T(8,128)S(1)}, u32[]{:S(2)}, u32[]{:S(2)}) %collective-permute-start.13) | collective-permute-done | bytes 53280 | tf_op jit(solution)/shard_map/ppermute | solution.py:472
  55.8 1.0 %collective-permute-start.14 = (f32[8,128]{1,0:T(8,128)S(1)}, f32[8,128]{1,0:T(8,128)S(1)}, u32[]{:S(2)}, u32[]{:S(2)}) collective-permute-start(f32[8,128]{1,0:T(8,128)S(1)} %slice.61), channel_id=1, source_target_pairs={{0,4},{4,0},{8,12},{12,8},{16,20},{20,16},{24,28},{28,24},{1,5},{5... | collective-permute-start | bytes 12296 | tf_op jit(solution)/shard_map/ppermute | solution.py:472
  57.5 2.1 %filter_step_2.1 = (f32[12,16,128]{2,1,0:T(8,128)S(1)}, f32[104,128]{1,0:T(8,128)S(1)}, f32[104,128]{1,0:T(8,128)S(1)}) custom-call(bf16[128,512]{1,0:T(8,128)(2,1)S(1)} %get-tuple-element.44.refs_2_.refs_1_.refs_0_, bf16[128,512]{1,0:T(8,128)(2,1)S(1)} %get-tuple-element.45.refs_1_, f32[12,16,128]{2,1,0:T(8,128)S(1)} %local_2.1.refs_2_, ...), custom_call_target="tpu_custom_call" | custom-call | tf_op jit(solution)/shard_map/filter_step_2/pallas_call | solution.py:502
  60.1 0.9 %collective-permute-done.15.refs_4_ = f32[104,128]{1,0:T(8,128)S(1)} collective-permute-done((f32[104,128]{1,0:T(8,128)S(1)}, f32[104,128]{1,0:T(8,128)S(1)}, u32[]{:S(2)}, u32[]{:S(2)}) %collective-permute-start.15) | collective-permute-done | bytes 53280 | tf_op jit(solution)/shard_map/ppermute | solution.py:472
  60.9 1.9 %collective-permute-start.16 = (f32[104,128]{1,0:T(8,128)S(1)}, f32[104,128]{1,0:T(8,128)S(1)}, u32[]{:S(2)}, u32[]{:S(2)}) collective-permute-start(f32[104,128]{1,0:T(8,128)S(1)} %fusion.refs_4_), channel_id=1, source_target_pairs={{4,8},{8,4},{12,16},{16,12},{20,24},{24,20},{5,9},{9,5},{13,17},{1... | collective-permute-start | bytes 159752 | tf_op jit(solution)/shard_map/ppermute | solution.py:472
  62.9 3.8 %collective-permute-done.16.refs_3_ = f32[104,128]{1,0:T(8,128)S(1)} collective-permute-done((f32[104,128]{1,0:T(8,128)S(1)}, f32[104,128]{1,0:T(8,128)S(1)}, u32[]{:S(2)}, u32[]{:S(2)}) %collective-permute-start.16) | collective-permute-done | bytes 53280 | tf_op jit(solution)/shard_map/ppermute | solution.py:472
  66.7 0.9 %collective-permute-start.17 = (f32[8,128]{1,0:T(8,128)S(1)}, f32[8,128]{1,0:T(8,128)S(1)}, u32[]{:S(2)}, u32[]{:S(2)}) collective-permute-start(f32[8,128]{1,0:T(8,128)S(1)} %slice.63), channel_id=1, source_target_pairs={{0,4},{4,0},{8,12},{12,8},{16,20},{20,16},{24,28},{28,24},{1,5},{5... | collective-permute-start | bytes 12296 | tf_op jit(solution)/shard_map/ppermute | solution.py:472
  68.5 1.9 %filter_step_3.1 = f32[12,16,128]{2,1,0:T(8,128)} custom-call(bf16[128,512]{1,0:T(8,128)(2,1)S(1)} %get-tuple-element.44.refs_2_.refs_1_.refs_0_, bf16[128,512]{1,0:T(8,128)(2,1)S(1)} %get-tuple-element.45.refs_1_, f32[12,16,128]{2,1,0:T(8,128)S(1)} %local_3.1.refs_2_, f32[104,128]{1,0:T(8,128)S(1)} %collective-permute-done.16.refs_3_, ...), custom_call_target="tpu_custom_call" | custom-call | tf_op jit(solution)/shard_map/filter_step_3/pallas_call | solution.py:502
  (49 shorter events, 5.9 us)
Async XLA Ops:
  0.0 2.0 %copy-start = (f32[1,12,16,128]{3,2,1,0:T(8,128)S(1)}, f32[1,12,16,128]{3,2,1,0:T(8,128)}, u32[]{:S(2)}) copy-start(f32[1,12,16,128]{3,2,1,0:T(8,128)} %param.10) | copy-start | bytes 294916
  0.0 1.1 %copy-start.1 = (f32[32,8,512]{2,1,0:T(8,128)S(1)}, f32[32,8,512]{2,1,0:T(8,128)}, u32[]{:S(2)}) copy-start(f32[32,8,512]{2,1,0:T(8,128)} %refs_0_.6) | copy-start | bytes 1572868
  2.0 1.4 %copy-start.2 = (f32[32,8,512]{2,1,0:T(8,128)S(1)}, f32[32,8,512]{2,1,0:T(8,128)}, u32[]{:S(2)}) copy-start(f32[32,8,512]{2,1,0:T(8,128)} %refs_0_.6) | copy-start | bytes 1572868
  2.0 3.6 %copy-start.4 = (s32[3,32]{1,0:T(4,128)S(1)}, s32[3,32]{1,0:T(4,128)}, u32[]{:S(2)}) copy-start(s32[3,32]{1,0:T(4,128)} %refs_15_.5) | copy-start | bytes 1156
  2.0 10.2 %collective-permute-start = (f32[608,128]{1,0:T(8,128)S(1)}, f32[608,128]{1,0:T(8,128)S(1)}, u32[]{:S(2)}, u32[]{:S(2)}) collective-permute-start(f32[608,128]{1,0:T(8,128)S(1)} %add_window.1.refs_1_.refs_2_.refs_7_.refs_6_), channel_id=1, source_target_pairs={{0,1},{1,2},{2,3},{3,0},{4,5},{5,6},{6,7},{7,4},{8,9},{9,10},{10,1... | collective-permute-start | bytes 933896 | tf_op jit(solution)/shard_map/ppermute | solution.py:477
  4.3 13.6 %collective-permute-start.2 = (f32[512,128]{1,0:T(8,128)S(1)}, f32[512,128]{1,0:T(8,128)S(1)}, u32[]{:S(2)}, u32[]{:S(2)}) collective-permute-start(f32[512,128]{1,0:T(8,128)S(1)} %pack_high.1.refs_2_.refs_3_.refs_8_.refs_7_), channel_id=1, source_target_pairs={{0,1},{1,2},{2,3},{3,0},{4,5},{5,6},{6,7},{7,4},{8,9},{9,10},{10,1... | collective-permute-start | bytes 786440 | tf_op jit(solution)/shard_map/ppermute | solution.py:477
  13.1 5.6 %collective-permute-start.3 = (f32[4,8,128]{2,1,0:T(8,128)S(1)}, f32[4,8,128]{2,1,0:T(8,128)S(1)}, u32[]{:S(2)}, u32[]{:S(2)}) collective-permute-start(f32[4,8,128]{2,1,0:T(8,128)S(1)} %get-tuple-element.49), channel_id=1, source_target_pairs={{0,3},{1,0},{2,1},{3,2},{4,7},{5,4},{6,5},{7,6},{8,11},{9,8},{10,9... | collective-permute-start | bytes 49160 | tf_op jit(solution)/shard_map/ppermute | solution.py:477
  14.5 7.4 %collective-permute-start.1 = (f32[512,128]{1,0:T(8,128)S(1)}, f32[512,128]{1,0:T(8,128)S(1)}, u32[]{:S(2)}, u32[]{:S(2)}) collective-permute-start(f32[512,128]{1,0:T(8,128)S(1)} %get-tuple-element.48.refs_1_), channel_id=1, source_target_pairs={{0,1},{1,2},{2,3},{3,0},{4,5},{5,6},{6,7},{7,4},{8,9},{9,10},{10,1... | collective-permute-start | bytes 786440 | tf_op jit(solution)/shard_map/ppermute | solution.py:477
  14.6 0.7 copy-start.6
  14.6 0.8 %copy-start.5 = (f32[16,8]{0,1:T(8,128)S(1)}, f32[16,8]{0,1:T(8,128)}, u32[]{:S(2)}) copy-start(f32[16,8]{0,1:T(8,128)} %param.13) | copy-start | bytes 1540
  18.7 13.2 %collective-permute-start.6 = (f32[512,128]{1,0:T(8,128)S(1)}, f32[512,128]{1,0:T(8,128)S(1)}, u32[]{:S(2)}, u32[]{:S(2)}) collective-permute-start(f32[512,128]{1,0:T(8,128)S(1)} %hand_on.3.refs_1_), channel_id=1, source_target_pairs={{0,1},{1,2},{2,3},{3,0},{4,5},{5,6},{6,7},{7,4},{8,9},{9,10},{10,1... | collective-permute-start | bytes 786440 | tf_op jit(solution)/shard_map/ppermute | solution.py:477
  22.0 9.9 %collective-permute-start.4 = (f32[96,128]{1,0:T(8,128)S(1)}, f32[96,128]{1,0:T(8,128)S(1)}, u32[]{:S(2)}, u32[]{:S(2)}) collective-permute-start(f32[96,128]{1,0:T(8,128)S(1)} %get-tuple-element.50), channel_id=1, source_target_pairs={{0,4},{4,0},{8,12},{12,8},{16,20},{20,16},{24,28},{28,24},{1,5},{5... | collective-permute-start | bytes 147464 | tf_op jit(solution)/shard_map/ppermute | solution.py:472
  27.8 5.7 %collective-permute-start.5 = (f32[96,128]{1,0:T(8,128)S(1)}, f32[96,128]{1,0:T(8,128)S(1)}, u32[]{:S(2)}, u32[]{:S(2)}) collective-permute-start(f32[96,128]{1,0:T(8,128)S(1)} %get-tuple-element.51), channel_id=1, source_target_pairs={{4,8},{8,4},{12,16},{16,12},{20,24},{24,20},{5,9},{9,5},{13,17},{1... | collective-permute-start | bytes 147464 | tf_op jit(solution)/shard_map/ppermute | solution.py:472
  30.8 12.2 %collective-permute-start.10 = (f32[512,128]{1,0:T(8,128)S(1)}, f32[512,128]{1,0:T(8,128)S(1)}, u32[]{:S(2)}, u32[]{:S(2)}) collective-permute-start(f32[512,128]{1,0:T(8,128)S(1)} %hand_on.4.refs_1_), channel_id=1, source_target_pairs={{0,1},{1,2},{2,3},{3,0},{4,5},{5,6},{6,7},{7,4},{8,9},{9,10},{10,1... | collective-permute-start | bytes 786440 | tf_op jit(solution)/shard_map/ppermute | solution.py:477
  33.5 8.6 %copy-start.3 = (f32[12,16,128]{2,1,0:T(8,128)S(1)}, f32[12,16,128]{2,1,0:T(8,128)}, u32[]{:S(2)}) copy-start(f32[12,16,128]{2,1,0:T(8,128)} %refs_3_.5) | copy-start | bytes 294916
  33.5 12.2 %collective-permute-start.11 = (f32[512,128]{1,0:T(8,128)S(1)}, f32[512,128]{1,0:T(8,128)S(1)}, u32[]{:S(2)}, u32[]{:S(2)}) collective-permute-start(f32[512,128]{1,0:T(8,128)S(1)} %hand_on.5), channel_id=1, source_target_pairs={{0,1},{1,2},{2,3},{3,0},{4,5},{5,6},{6,7},{7,4},{8,9},{9,10},{10,1... | collective-permute-start | bytes 786440 | tf_op jit(solution)/shard_map/ppermute | solution.py:477
  34.4 1.5 %collective-permute-start.7 = (f32[16,128]{1,0:T(8,128)S(1)}, f32[16,128]{1,0:T(8,128)S(1)}, u32[]{:S(2)}, u32[]{:S(2)}) collective-permute-start(f32[16,128]{1,0:T(8,128)S(1)} %first_sums.1), channel_id=1, source_target_pairs={{0,4},{4,0},{8,12},{12,8},{16,20},{20,16},{24,28},{28,24},{1,5},{5... | collective-permute-start | bytes 24584 | tf_op jit(solution)/shard_map/ppermute | solution.py:472
  35.9 5.3 %collective-permute-start.8 = (f32[16,128]{1,0:T(8,128)S(1)}, f32[16,128]{1,0:T(8,128)S(1)}, u32[]{:S(2)}, u32[]{:S(2)}) collective-permute-start(f32[16,128]{1,0:T(8,128)S(1)} %add.52.refs_4_), channel_id=1, source_target_pairs={{4,8},{8,4},{12,16},{16,12},{20,24},{24,20},{5,9},{9,5},{13,17},{1... | collective-permute-start | bytes 24584 | tf_op jit(solution)/shard_map/ppermute | solution.py:472
  41.2 1.8 %collective-permute-start.9 = (f32[16,128]{1,0:T(8,128)S(1)}, f32[16,128]{1,0:T(8,128)S(1)}, u32[]{:S(2)}, u32[]{:S(2)}) collective-permute-start(f32[16,128]{1,0:T(8,128)S(1)} %collective-permute-done.8.refs_6_), channel_id=1, source_target_pairs={{0,4},{4,0},{8,12},{12,8},{16,20},{20,16},{24,28},{28,24},{1,5},{5... | collective-permute-start | bytes 24584 | tf_op jit(solution)/shard_map/ppermute | solution.py:472
  47.8 2.2 %collective-permute-start.12 = (f32[104,128]{1,0:T(8,128)S(1)}, f32[104,128]{1,0:T(8,128)S(1)}, u32[]{:S(2)}, u32[]{:S(2)}) collective-permute-start(f32[104,128]{1,0:T(8,128)S(1)} %get-tuple-element.53), channel_id=1, source_target_pairs={{0,4},{4,0},{8,12},{12,8},{16,20},{20,16},{24,28},{28,24},{1,5},{5... | collective-permute-start | bytes 159752 | tf_op jit(solution)/shard_map/ppermute | solution.py:472
  50.0 5.7 %collective-permute-start.13 = (f32[104,128]{1,0:T(8,128)S(1)}, f32[104,128]{1,0:T(8,128)S(1)}, u32[]{:S(2)}, u32[]{:S(2)}) collective-permute-start(f32[104,128]{1,0:T(8,128)S(1)} %fusion.1.refs_4_), channel_id=1, source_target_pairs={{4,8},{8,4},{12,16},{16,12},{20,24},{24,20},{5,9},{9,5},{13,17},{1... | collective-permute-start | bytes 159752 | tf_op jit(solution)/shard_map/ppermute | solution.py:472
  55.8 1.8 %collective-permute-start.14 = (f32[8,128]{1,0:T(8,128)S(1)}, f32[8,128]{1,0:T(8,128)S(1)}, u32[]{:S(2)}, u32[]{:S(2)}) collective-permute-start(f32[8,128]{1,0:T(8,128)S(1)} %slice.61), channel_id=1, source_target_pairs={{0,4},{4,0},{8,12},{12,8},{16,20},{20,16},{24,28},{28,24},{1,5},{5... | collective-permute-start | bytes 12296 | tf_op jit(solution)/shard_map/ppermute | solution.py:472
  59.6 1.3 %collective-permute-start.15 = (f32[104,128]{1,0:T(8,128)S(1)}, f32[104,128]{1,0:T(8,128)S(1)}, u32[]{:S(2)}, u32[]{:S(2)}) collective-permute-start(f32[104,128]{1,0:T(8,128)S(1)} %get-tuple-element.57), channel_id=1, source_target_pairs={{0,4},{4,0},{8,12},{12,8},{16,20},{20,16},{24,28},{28,24},{1,5},{5... | collective-permute-start | bytes 159752 | tf_op jit(solution)/shard_map/ppermute | solution.py:472
  60.9 5.7 %collective-permute-start.16 = (f32[104,128]{1,0:T(8,128)S(1)}, f32[104,128]{1,0:T(8,128)S(1)}, u32[]{:S(2)}, u32[]{:S(2)}) collective-permute-start(f32[104,128]{1,0:T(8,128)S(1)} %fusion.refs_4_), channel_id=1, source_target_pairs={{4,8},{8,4},{12,16},{16,12},{20,24},{24,20},{5,9},{9,5},{13,17},{1... | collective-permute-start | bytes 159752 | tf_op jit(solution)/shard_map/ppermute | solution.py:472
  66.7 1.8 %collective-permute-start.17 = (f32[8,128]{1,0:T(8,128)S(1)}, f32[8,128]{1,0:T(8,128)S(1)}, u32[]{:S(2)}, u32[]{:S(2)}) collective-permute-start(f32[8,128]{1,0:T(8,128)S(1)} %slice.63), channel_id=1, source_target_pairs={{0,4},{4,0},{8,12},{12,8},{16,20},{20,16},{24,28},{28,24},{1,5},{5... | collective-permute-start | bytes 12296 | tf_op jit(solution)/shard_map/ppermute | solution.py:472

commit v11 on v10

--- a/solution.py
+++ b/solution.py
@@ -574,14 +574,14 @@
         far_high = turn(on_high, "band", 1)
         on_far_low = hand_on(far_low, on_high, tables[0], energy)
         above_low = turn(on_far_low, "band", 1)
-        mate, cross = call(
-            halo_kernel, "cut_halos", halos, [], [field], [], [on_far_low]
-        )
-        mate, cross = swap(mate, "dom", 0), swap(cross, "dom", 1)
         near = call(
             near_kernel, "project_near", shaped(*flat), [slot_corner],
             [field, low, high, below_low, below_high, far_low], [],
         )
+        mate, cross = call(
+            halo_kernel, "cut_halos", halos, [], [field], [], [on_far_low, near]
+        )
+        mate, cross = swap(mate, "dom", 0), swap(cross, "dom", 1)
         on_far_high = hand_on(far_high, near, tables[0], energy, mate, cross)
         above_high = turn(on_far_high, "band", 1)
         own = call(

time: 70.6 us -> 71.6 us (1.014)
  waiting for transfers between devices: 31.5 us -> 32.6 us
    ppermute x11, waiting for transfers between devices: 16.2 us -> 17.2 us  [swap(): return lax.ppermute(values, axis, pairs)]
where the time goes in v11:
time: 71.6 us; the launch traced here: 71.4 us
  waiting for transfers between devices  32.6 us (46%)
  starting transfers between devices  24.7 us (34%)
  Pallas kernels  11.8 us (16%)
  local copies, waits for them, and re-layouts  1.99 us (3%)
    ppermute x11, starting transfers between devices, swap(): return lax.ppermute(values, axis, pairs)  20.3 us
    ppermute x11, waiting for transfers between devices, swap(): return lax.ppermute(values, axis, pairs)  17.2 us
    ppermute x7, waiting for transfers between devices, turn(): lax.ppermute(values, axis, [(i, (i + step) % count) for i in range(count)])  15.4 us
    pallas_call x17, Pallas kernels, call(): pl.pallas_call(body, out_shape=out_shape, in_specs=[SMEM] * len(scalars)...  11.8 us
    ppermute x7, starting transfers between devices, turn(): lax.ppermute(values, axis, [(i, (i + step) % count) for i in range(count)])  4.39 us
    unnamed x14, local copies, waits for them, and re-layouts  1.67 us
  transfers between devices with their start and end apart: 18, of which 15 were waited for; matrix products, arithmetic and copies ran while one was open for 1% of the time, Pallas kernels for 7%

profile of v11, /device:TPU:5, one launch (start us, length us, event | category | flops | bytes accessed | tf_op | source)
XLA Modules:
  0.0 71.4 jit_solution(10899079392295377711)
XLA Ops:
  0.0 1.1 %copy-done.1 = f32[32,8,512]{2,1,0:T(8,128)S(1)} copy-done((f32[32,8,512]{2,1,0:T(8,128)S(1)}, f32[32,8,512]{2,1,0:T(8,128)}, u32[]{:S(2)}) %copy-start.1) | copy-done | bytes 524312
  1.1 0.9 %pack_low.1.refs_1_ = f32[608,128]{1,0:T(8,128)S(1)} custom-call(f32[32,8,512]{2,1,0:T(8,128)S(1)} %copy-done.1), custom_call_target="tpu_custom_call" | custom-call | tf_op jit(solution)/shard_map/pack_low/pallas_call | solution.py:502
  2.0 1.3 %collective-permute-start = (f32[608,128]{1,0:T(8,128)S(1)}, f32[608,128]{1,0:T(8,128)S(1)}, u32[]{:S(2)}, u32[]{:S(2)}) collective-permute-start(f32[608,128]{1,0:T(8,128)S(1)} %add_window.1.refs_1_.refs_2_.refs_7_.refs_6_), channel_id=1, source_target_pairs={{0,1},{1,2},{2,3},{3,0},{4,5},{5,6},{6,7},{7,4},{8,9},{9,10},{10,1... | collective-permute-start | bytes 933896 | tf_op jit(solution)/shard_map/ppermute | solution.py:477
  3.4 0.9 %pack_high.1.refs_2_.refs_3_.refs_8_.refs_7_ = f32[512,128]{1,0:T(8,128)S(1)} custom-call(f32[32,8,512]{2,1,0:T(8,128)S(1)} %copy-done.2, f32[608,128]{1,0:T(8,128)S(1)} %add_window.1.refs_1_.refs_2_.refs_7_.refs_6_), custom_call_target="tpu_custom_call" | custom-call | tf_op jit(solution)/shard_map/pack_high/pallas_call | solution.py:502
  4.3 1.3 %collective-permute-start.2 = (f32[512,128]{1,0:T(8,128)S(1)}, f32[512,128]{1,0:T(8,128)S(1)}, u32[]{:S(2)}, u32[]{:S(2)}) collective-permute-start(f32[512,128]{1,0:T(8,128)S(1)} %pack_high.1.refs_2_.refs_3_.refs_8_.refs_7_), channel_id=1, source_target_pairs={{0,1},{1,2},{2,3},{3,0},{4,5},{5,6},{6,7},{7,4},{8,9},{9,10},{10,1... | collective-permute-start | bytes 786440 | tf_op jit(solution)/shard_map/ppermute | solution.py:477
  5.7 6.5 %collective-permute-done.refs_3_.refs_4_.refs_11_.refs_10_ = f32[608,128]{1,0:T(8,128)S(1)} collective-permute-done((f32[608,128]{1,0:T(8,128)S(1)}, f32[608,128]{1,0:T(8,128)S(1)}, u32[]{:S(2)}, u32[]{:S(2)}) %collective-permute-start) | collective-permute-done | bytes 311328 | tf_op jit(solution)/shard_map/ppermute | solution.py:477
  12.3 0.8 %project_above.1 = (f32[4,8,128]{2,1,0:T(8,128)S(1)}, f32[512,128]{1,0:T(8,128)S(1)}) custom-call(s32[3,32]{1,0:T(4,128)S(1)} %copy-done.4, f32[608,128]{1,0:T(8,128)S(1)} %add_window.1.refs_1_.refs_2_.refs_7_.refs_6_, f32[512,128]{1,0:T(8,128)S(1)} %pack_high.1.refs_2_.refs_3_.refs_8_.refs_7_, ...), custom_call_target="tpu_custom_call" | custom-call | tf_op jit(solution)/shard_map/project_above/pallas_call | solution.py:502
  13.1 1.4 %collective-permute-start.3 = (f32[4,8,128]{2,1,0:T(8,128)S(1)}, f32[4,8,128]{2,1,0:T(8,128)S(1)}, u32[]{:S(2)}, u32[]{:S(2)}) collective-permute-start(f32[4,8,128]{2,1,0:T(8,128)S(1)} %get-tuple-element.49), channel_id=1, source_target_pairs={{0,3},{1,0},{2,1},{3,2},{4,7},{5,4},{6,5},{7,6},{8,11},{9,8},{10,9... | collective-permute-start | bytes 49160 | tf_op jit(solution)/shard_map/ppermute | solution.py:477
  15.7 2.2 %collective-permute-done.2.refs_0_.refs_5_.refs_12_.refs_11_ = f32[512,128]{1,0:T(8,128)S(1)} collective-permute-done((f32[512,128]{1,0:T(8,128)S(1)}, f32[512,128]{1,0:T(8,128)S(1)}, u32[]{:S(2)}, u32[]{:S(2)}) %collective-permute-start.2) | collective-permute-done | bytes 262176 | tf_op jit(solution)/shard_map/ppermute | solution.py:477
  18.8 3.1 %collective-permute-done.1.refs_0_.refs_6_.refs_13_.refs_12_ = f32[512,128]{1,0:T(8,128)S(1)} collective-permute-done((f32[512,128]{1,0:T(8,128)S(1)}, f32[512,128]{1,0:T(8,128)S(1)}, u32[]{:S(2)}, u32[]{:S(2)}) %collective-permute-start.1) | collective-permute-done | bytes 262176 | tf_op jit(solution)/shard_map/ppermute | solution.py:477
  21.9 1.0 %project_near.1.refs_2_.refs_4_.refs_1_ = f32[4,8,128]{2,1,0:T(8,128)S(1)} custom-call(s32[3,32]{1,0:T(4,128)S(1)} %copy-done.4, f32[12,16,128]{2,1,0:T(8,128)S(1)} %bitcast.6, f32[608,128]{1,0:T(8,128)S(1)} %add_window.1.refs_1_.refs_2_.refs_7_.refs_6_, f32[512,128]{1,0:T(8,128)S(1)} %pack_high.1.refs_2_.refs_3_.refs_8_.refs_7_, ...), custom_call_target="tpu_custom_call" | custom-call | tf_op jit(solution)/shard_map/project_near/pallas_call | solution.py:502
  23.0 5.8 %collective-permute-start.4 = (f32[96,128]{1,0:T(8,128)S(1)}, f32[96,128]{1,0:T(8,128)S(1)}, u32[]{:S(2)}, u32[]{:S(2)}) collective-permute-start(f32[96,128]{1,0:T(8,128)S(1)} %get-tuple-element.50), channel_id=1, source_target_pairs={{0,4},{4,0},{8,12},{12,8},{16,20},{20,16},{24,28},{28,24},{1,5},{5... | collective-permute-start | bytes 147464 | tf_op jit(solution)/shard_map/ppermute | solution.py:472
  28.8 3.0 %collective-permute-start.5 = (f32[96,128]{1,0:T(8,128)S(1)}, f32[96,128]{1,0:T(8,128)S(1)}, u32[]{:S(2)}, u32[]{:S(2)}) collective-permute-start(f32[96,128]{1,0:T(8,128)S(1)} %get-tuple-element.51), channel_id=1, source_target_pairs={{4,8},{8,4},{12,16},{16,12},{20,24},{24,20},{5,9},{9,5},{13,17},{1... | collective-permute-start | bytes 147464 | tf_op jit(solution)/shard_map/ppermute | solution.py:472
  31.9 2.6 %collective-permute-done.5.refs_5_.refs_3_ = f32[96,128]{1,0:T(8,128)S(1)} collective-permute-done((f32[96,128]{1,0:T(8,128)S(1)}, f32[96,128]{1,0:T(8,128)S(1)}, u32[]{:S(2)}, u32[]{:S(2)}) %collective-permute-start.5) | collective-permute-done | bytes 49184 | tf_op jit(solution)/shard_map/ppermute | solution.py:472
  34.6 0.9 %first_sums.1 = f32[16,128]{1,0:T(8,128)S(1)} custom-call(s32[3,32]{1,0:T(4,128)S(1)} %copy-done.4, bf16[128,512]{1,0:T(8,128)(2,1)S(1)} %get-tuple-element.44.refs_2_.refs_1_.refs_0_, f32[8,128]{1,0:T(8,128)S(1)} %broadcast_select_fusion.refs_3_.refs_2_, f32[12,16,128]{2,1,0:T(8,128)S(1)} %bitcast.8, f32[4,8,128]{2,1,0:T(8,128)S(1)} %project_near.1.refs_2_.refs_4_.refs_1_, ...), custom_call_target="tpu_custom_call" | custom-call | tf_op jit(solution)/shard_map/first_sums/pallas_call | solution.py:502
  36.1 0.8 %collective-permute-done.7 = f32[16,128]{1,0:T(8,128)S(1)} collective-permute-done((f32[16,128]{1,0:T(8,128)S(1)}, f32[16,128]{1,0:T(8,128)S(1)}, u32[]{:S(2)}, u32[]{:S(2)}) %collective-permute-start.7) | collective-permute-done | bytes 8224 | tf_op jit(solution)/shard_map/ppermute | solution.py:472
  37.0 2.4 %collective-permute-start.8 = (f32[16,128]{1,0:T(8,128)S(1)}, f32[16,128]{1,0:T(8,128)S(1)}, u32[]{:S(2)}, u32[]{:S(2)}) collective-permute-start(f32[16,128]{1,0:T(8,128)S(1)} %add.52.refs_4_), channel_id=1, source_target_pairs={{4,8},{8,4},{12,16},{16,12},{20,24},{24,20},{5,9},{9,5},{13,17},{1... | collective-permute-start | bytes 24584 | tf_op jit(solution)/shard_map/ppermute | solution.py:472
  39.4 2.8 %collective-permute-done.8.refs_6_ = f32[16,128]{1,0:T(8,128)S(1)} collective-permute-done((f32[16,128]{1,0:T(8,128)S(1)}, f32[16,128]{1,0:T(8,128)S(1)}, u32[]{:S(2)}, u32[]{:S(2)}) %collective-permute-start.8) | collective-permute-done | bytes 8224 | tf_op jit(solution)/shard_map/ppermute | solution.py:472
  42.2 0.9 %collective-permute-start.9 = (f32[16,128]{1,0:T(8,128)S(1)}, f32[16,128]{1,0:T(8,128)S(1)}, u32[]{:S(2)}, u32[]{:S(2)}) collective-permute-start(f32[16,128]{1,0:T(8,128)S(1)} %collective-permute-done.8.refs_6_), channel_id=1, source_target_pairs={{0,4},{4,0},{8,12},{12,8},{16,20},{20,16},{24,28},{28,24},{1,5},{5... | collective-permute-start | bytes 24584 | tf_op jit(solution)/shard_map/ppermute | solution.py:472
  44.0 2.7 %collective-permute-done.11.refs_10_.refs_9_ = f32[512,128]{1,0:T(8,128)S(1)} collective-permute-done((f32[512,128]{1,0:T(8,128)S(1)}, f32[512,128]{1,0:T(8,128)S(1)}, u32[]{:S(2)}, u32[]{:S(2)}) %collective-permute-start.11) | collective-permute-done | bytes 262176 | tf_op jit(solution)/shard_map/ppermute | solution.py:477
  46.7 2.1 %filter_step_1.1 = (f32[12,16,128]{2,1,0:T(8,128)S(1)}, f32[104,128]{1,0:T(8,128)S(1)}, f32[104,128]{1,0:T(8,128)S(1)}, f32[8,128]{1,0:T(8,128)S(1)}) custom-call(bf16[128,512]{1,0:T(8,128)(2,1)S(1)} %get-tuple-element.44.refs_2_.refs_1_.refs_0_, bf16[128,512]{1,0:T(8,128)(2,1)S(1)} %get-tuple-element.45.refs_1_, f32[12,16,128]{2,1,0:T(8,128)S(1)} %local_1.1.refs_2_, ...), custom_call_target="tpu_custom_call" | custom-call | tf_op jit(solution)/shard_map/filter_step_1/pallas_call | solution.py:502
  48.8 1.3 %collective-permute-start.12 = (f32[104,128]{1,0:T(8,128)S(1)}, f32[104,128]{1,0:T(8,128)S(1)}, u32[]{:S(2)}, u32[]{:S(2)}) collective-permute-start(f32[104,128]{1,0:T(8,128)S(1)} %get-tuple-element.53), channel_id=1, source_target_pairs={{0,4},{4,0},{8,12},{12,8},{16,20},{20,16},{24,28},{28,24},{1,5},{5... | collective-permute-start | bytes 159752 | tf_op jit(solution)/shard_map/ppermute | solution.py:472
  50.2 0.9 %collective-permute-done.12.refs_4_ = f32[104,128]{1,0:T(8,128)S(1)} collective-permute-done((f32[104,128]{1,0:T(8,128)S(1)}, f32[104,128]{1,0:T(8,128)S(1)}, u32[]{:S(2)}, u32[]{:S(2)}) %collective-permute-start.12) | collective-permute-done | bytes 53280 | tf_op jit(solution)/shard_map/ppermute | solution.py:472
  51.1 1.9 %collective-permute-start.13 = (f32[104,128]{1,0:T(8,128)S(1)}, f32[104,128]{1,0:T(8,128)S(1)}, u32[]{:S(2)}, u32[]{:S(2)}) collective-permute-start(f32[104,128]{1,0:T(8,128)S(1)} %fusion.1.refs_4_), channel_id=1, source_target_pairs={{4,8},{8,4},{12,16},{16,12},{20,24},{24,20},{5,9},{9,5},{13,17},{1... | collective-permute-start | bytes 159752 | tf_op jit(solution)/shard_map/ppermute | solution.py:472
  53.0 3.8 %collective-permute-done.13.refs_3_ = f32[104,128]{1,0:T(8,128)S(1)} collective-permute-done((f32[104,128]{1,0:T(8,128)S(1)}, f32[104,128]{1,0:T(8,128)S(1)}, u32[]{:S(2)}, u32[]{:S(2)}) %collective-permute-start.13) | collective-permute-done | bytes 53280 | tf_op jit(solution)/shard_map/ppermute | solution.py:472
  56.8 1.0 %collective-permute-start.14 = (f32[8,128]{1,0:T(8,128)S(1)}, f32[8,128]{1,0:T(8,128)S(1)}, u32[]{:S(2)}, u32[]{:S(2)}) collective-permute-start(f32[8,128]{1,0:T(8,128)S(1)} %slice.61), channel_id=1, source_target_pairs={{0,4},{4,0},{8,12},{12,8},{16,20},{20,16},{24,28},{28,24},{1,5},{5... | collective-permute-start | bytes 12296 | tf_op jit(solution)/shard_map/ppermute | solution.py:472
  58.6 2.1 %filter_step_2.1 = (f32[12,16,128]{2,1,0:T(8,128)S(1)}, f32[104,128]{1,0:T(8,128)S(1)}, f32[104,128]{1,0:T(8,128)S(1)}) custom-call(bf16[128,512]{1,0:T(8,128)(2,1)S(1)} %get-tuple-element.44.refs_2_.refs_1_.refs_0_, bf16[128,512]{1,0:T(8,128)(2,1)S(1)} %get-tuple-element.45.refs_1_, f32[12,16,128]{2,1,0:T(8,128)S(1)} %local_2.1.refs_2_, ...), custom_call_target="tpu_custom_call" | custom-call | tf_op jit(solution)/shard_map/filter_step_2/pallas_call | solution.py:502
  61.1 0.9 %collective-permute-done.15.refs_4_ = f32[104,128]{1,0:T(8,128)S(1)} collective-permute-done((f32[104,128]{1,0:T(8,128)S(1)}, f32[104,128]{1,0:T(8,128)S(1)}, u32[]{:S(2)}, u32[]{:S(2)}) %collective-permute-start.15) | collective-permute-done | bytes 53280 | tf_op jit(solution)/shard_map/ppermute | solution.py:472
  62.0 1.9 %collective-permute-start.16 = (f32[104,128]{1,0:T(8,128)S(1)}, f32[104,128]{1,0:T(8,128)S(1)}, u32[]{:S(2)}, u32[]{:S(2)}) collective-permute-start(f32[104,128]{1,0:T(8,128)S(1)} %fusion.refs_4_), channel_id=1, source_target_pairs={{4,8},{8,4},{12,16},{16,12},{20,24},{24,20},{5,9},{9,5},{13,17},{1... | collective-permute-start | bytes 159752 | tf_op jit(solution)/shard_map/ppermute | solution.py:472
  63.9 3.8 %collective-permute-done.16.refs_3_ = f32[104,128]{1,0:T(8,128)S(1)} collective-permute-done((f32[104,128]{1,0:T(8,128)S(1)}, f32[104,128]{1,0:T(8,128)S(1)}, u32[]{:S(2)}, u32[]{:S(2)}) %collective-permute-start.16) | collective-permute-done | bytes 53280 | tf_op jit(solution)/shard_map/ppermute | solution.py:472
  67.7 0.9 %collective-permute-start.17 = (f32[8,128]{1,0:T(8,128)S(1)}, f32[8,128]{1,0:T(8,128)S(1)}, u32[]{:S(2)}, u32[]{:S(2)}) collective-permute-start(f32[8,128]{1,0:T(8,128)S(1)} %slice.63), channel_id=1, source_target_pairs={{0,4},{4,0},{8,12},{12,8},{16,20},{20,16},{24,28},{28,24},{1,5},{5... | collective-permute-start | bytes 12296 | tf_op jit(solution)/shard_map/ppermute | solution.py:472
  69.5 1.9 %filter_step_3.1 = f32[12,16,128]{2,1,0:T(8,128)} custom-call(bf16[128,512]{1,0:T(8,128)(2,1)S(1)} %get-tuple-element.44.refs_2_.refs_1_.refs_0_, bf16[128,512]{1,0:T(8,128)(2,1)S(1)} %get-tuple-element.45.refs_1_, f32[12,16,128]{2,1,0:T(8,128)S(1)} %local_3.1.refs_2_, f32[104,128]{1,0:T(8,128)S(1)} %collective-permute-done.16.refs_3_, ...), custom_call_target="tpu_custom_call" | custom-call | tf_op jit(solution)/shard_map/filter_step_3/pallas_call | solution.py:502
  (49 shorter events, 5.9 us)
Async XLA Ops:
  0.0 2.0 %copy-start = (f32[1,12,16,128]{3,2,1,0:T(8,128)S(1)}, f32[1,12,16,128]{3,2,1,0:T(8,128)}, u32[]{:S(2)}) copy-start(f32[1,12,16,128]{3,2,1,0:T(8,128)} %param.10) | copy-start | bytes 294916
  0.0 1.1 %copy-start.1 = (f32[32,8,512]{2,1,0:T(8,128)S(1)}, f32[32,8,512]{2,1,0:T(8,128)}, u32[]{:S(2)}) copy-start(f32[32,8,512]{2,1,0:T(8,128)} %refs_0_.6) | copy-start | bytes 1572868
  2.0 1.4 %copy-start.2 = (f32[32,8,512]{2,1,0:T(8,128)S(1)}, f32[32,8,512]{2,1,0:T(8,128)}, u32[]{:S(2)}) copy-start(f32[32,8,512]{2,1,0:T(8,128)} %refs_0_.6) | copy-start | bytes 1572868
  2.0 3.6 %copy-start.4 = (s32[3,32]{1,0:T(4,128)S(1)}, s32[3,32]{1,0:T(4,128)}, u32[]{:S(2)}) copy-start(s32[3,32]{1,0:T(4,128)} %refs_15_.5) | copy-start | bytes 1156
  2.0 10.2 %collective-permute-start = (f32[608,128]{1,0:T(8,128)S(1)}, f32[608,128]{1,0:T(8,128)S(1)}, u32[]{:S(2)}, u32[]{:S(2)}) collective-permute-start(f32[608,128]{1,0:T(8,128)S(1)} %add_window.1.refs_1_.refs_2_.refs_7_.refs_6_), channel_id=1, source_target_pairs={{0,1},{1,2},{2,3},{3,0},{4,5},{5,6},{6,7},{7,4},{8,9},{9,10},{10,1... | collective-permute-start | bytes 933896 | tf_op jit(solution)/shard_map/ppermute | solution.py:477
  4.3 13.6 %collective-permute-start.2 = (f32[512,128]{1,0:T(8,128)S(1)}, f32[512,128]{1,0:T(8,128)S(1)}, u32[]{:S(2)}, u32[]{:S(2)}) collective-permute-start(f32[512,128]{1,0:T(8,128)S(1)} %pack_high.1.refs_2_.refs_3_.refs_8_.refs_7_), channel_id=1, source_target_pairs={{0,1},{1,2},{2,3},{3,0},{4,5},{5,6},{6,7},{7,4},{8,9},{9,10},{10,1... | collective-permute-start | bytes 786440 | tf_op jit(solution)/shard_map/ppermute | solution.py:477
  13.1 5.6 %collective-permute-start.3 = (f32[4,8,128]{2,1,0:T(8,128)S(1)}, f32[4,8,128]{2,1,0:T(8,128)S(1)}, u32[]{:S(2)}, u32[]{:S(2)}) collective-permute-start(f32[4,8,128]{2,1,0:T(8,128)S(1)} %get-tuple-element.49), channel_id=1, source_target_pairs={{0,3},{1,0},{2,1},{3,2},{4,7},{5,4},{6,5},{7,6},{8,11},{9,8},{10,9... | collective-permute-start | bytes 49160 | tf_op jit(solution)/shard_map/ppermute | solution.py:477
  14.5 7.4 %collective-permute-start.1 = (f32[512,128]{1,0:T(8,128)S(1)}, f32[512,128]{1,0:T(8,128)S(1)}, u32[]{:S(2)}, u32[]{:S(2)}) collective-permute-start(f32[512,128]{1,0:T(8,128)S(1)} %get-tuple-element.48.refs_1_), channel_id=1, source_target_pairs={{0,1},{1,2},{2,3},{3,0},{4,5},{5,6},{6,7},{7,4},{8,9},{9,10},{10,1... | collective-permute-start | bytes 786440 | tf_op jit(solution)/shard_map/ppermute | solution.py:477
  14.6 0.7 copy-start.6
  14.6 0.8 %copy-start.5 = (f32[16,8]{0,1:T(8,128)S(1)}, f32[16,8]{0,1:T(8,128)}, u32[]{:S(2)}) copy-start(f32[16,8]{0,1:T(8,128)} %param.13) | copy-start | bytes 1540
  18.7 13.2 %collective-permute-start.6 = (f32[512,128]{1,0:T(8,128)S(1)}, f32[512,128]{1,0:T(8,128)S(1)}, u32[]{:S(2)}, u32[]{:S(2)}) collective-permute-start(f32[512,128]{1,0:T(8,128)S(1)} %hand_on.3.refs_1_), channel_id=1, source_target_pairs={{0,1},{1,2},{2,3},{3,0},{4,5},{5,6},{6,7},{7,4},{8,9},{9,10},{10,1... | collective-permute-start | bytes 786440 | tf_op jit(solution)/shard_map/ppermute | solution.py:477
  23.0 8.9 %collective-permute-start.4 = (f32[96,128]{1,0:T(8,128)S(1)}, f32[96,128]{1,0:T(8,128)S(1)}, u32[]{:S(2)}, u32[]{:S(2)}) collective-permute-start(f32[96,128]{1,0:T(8,128)S(1)} %get-tuple-element.50), channel_id=1, source_target_pairs={{0,4},{4,0},{8,12},{12,8},{16,20},{20,16},{24,28},{28,24},{1,5},{5... | collective-permute-start | bytes 147464 | tf_op jit(solution)/shard_map/ppermute | solution.py:472
  28.8 5.7 %collective-permute-start.5 = (f32[96,128]{1,0:T(8,128)S(1)}, f32[96,128]{1,0:T(8,128)S(1)}, u32[]{:S(2)}, u32[]{:S(2)}) collective-permute-start(f32[96,128]{1,0:T(8,128)S(1)} %get-tuple-element.51), channel_id=1, source_target_pairs={{4,8},{8,4},{12,16},{16,12},{20,24},{24,20},{5,9},{9,5},{13,17},{1... | collective-permute-start | bytes 147464 | tf_op jit(solution)/shard_map/ppermute | solution.py:472
  31.8 12.2 %collective-permute-start.10 = (f32[512,128]{1,0:T(8,128)S(1)}, f32[512,128]{1,0:T(8,128)S(1)}, u32[]{:S(2)}, u32[]{:S(2)}) collective-permute-start(f32[512,128]{1,0:T(8,128)S(1)} %hand_on.4.refs_1_), channel_id=1, source_target_pairs={{0,1},{1,2},{2,3},{3,0},{4,5},{5,6},{6,7},{7,4},{8,9},{9,10},{10,1... | collective-permute-start | bytes 786440 | tf_op jit(solution)/shard_map/ppermute | solution.py:477
  34.5 8.6 %copy-start.3 = (f32[12,16,128]{2,1,0:T(8,128)S(1)}, f32[12,16,128]{2,1,0:T(8,128)}, u32[]{:S(2)}) copy-start(f32[12,16,128]{2,1,0:T(8,128)} %refs_3_.5) | copy-start | bytes 294916
  34.5 12.2 %collective-permute-start.11 = (f32[512,128]{1,0:T(8,128)S(1)}, f32[512,128]{1,0:T(8,128)S(1)}, u32[]{:S(2)}, u32[]{:S(2)}) collective-permute-start(f32[512,128]{1,0:T(8,128)S(1)} %hand_on.5), channel_id=1, source_target_pairs={{0,1},{1,2},{2,3},{3,0},{4,5},{5,6},{6,7},{7,4},{8,9},{9,10},{10,1... | collective-permute-start | bytes 786440 | tf_op jit(solution)/shard_map/ppermute | solution.py:477
  35.5 1.5 %collective-permute-start.7 = (f32[16,128]{1,0:T(8,128)S(1)}, f32[16,128]{1,0:T(8,128)S(1)}, u32[]{:S(2)}, u32[]{:S(2)}) collective-permute-start(f32[16,128]{1,0:T(8,128)S(1)} %first_sums.1), channel_id=1, source_target_pairs={{0,4},{4,0},{8,12},{12,8},{16,20},{20,16},{24,28},{28,24},{1,5},{5... | collective-permute-start | bytes 24584 | tf_op jit(solution)/shard_map/ppermute | solution.py:472
  37.0 5.3 %collective-permute-start.8 = (f32[16,128]{1,0:T(8,128)S(1)}, f32[16,128]{1,0:T(8,128)S(1)}, u32[]{:S(2)}, u32[]{:S(2)}) collective-permute-start(f32[16,128]{1,0:T(8,128)S(1)} %add.52.refs_4_), channel_id=1, source_target_pairs={{4,8},{8,4},{12,16},{16,12},{20,24},{24,20},{5,9},{9,5},{13,17},{1... | collective-permute-start | bytes 24584 | tf_op jit(solution)/shard_map/ppermute | solution.py:472
  42.2 1.8 %collective-permute-start.9 = (f32[16,128]{1,0:T(8,128)S(1)}, f32[16,128]{1,0:T(8,128)S(1)}, u32[]{:S(2)}, u32[]{:S(2)}) collective-permute-start(f32[16,128]{1,0:T(8,128)S(1)} %collective-permute-done.8.refs_6_), channel_id=1, source_target_pairs={{0,4},{4,0},{8,12},{12,8},{16,20},{20,16},{24,28},{28,24},{1,5},{5... | collective-permute-start | bytes 24584 | tf_op jit(solution)/shard_map/ppermute | solution.py:472
  48.8 2.2 %collective-permute-start.12 = (f32[104,128]{1,0:T(8,128)S(1)}, f32[104,128]{1,0:T(8,128)S(1)}, u32[]{:S(2)}, u32[]{:S(2)}) collective-permute-start(f32[104,128]{1,0:T(8,128)S(1)} %get-tuple-element.53), channel_id=1, source_target_pairs={{0,4},{4,0},{8,12},{12,8},{16,20},{20,16},{24,28},{28,24},{1,5},{5... | collective-permute-start | bytes 159752 | tf_op jit(solution)/shard_map/ppermute | solution.py:472
  51.1 5.7 %collective-permute-start.13 = (f32[104,128]{1,0:T(8,128)S(1)}, f32[104,128]{1,0:T(8,128)S(1)}, u32[]{:S(2)}, u32[]{:S(2)}) collective-permute-start(f32[104,128]{1,0:T(8,128)S(1)} %fusion.1.refs_4_), channel_id=1, source_target_pairs={{4,8},{8,4},{12,16},{16,12},{20,24},{24,20},{5,9},{9,5},{13,17},{1... | collective-permute-start | bytes 159752 | tf_op jit(solution)/shard_map/ppermute | solution.py:472
  56.8 1.8 %collective-permute-start.14 = (f32[8,128]{1,0:T(8,128)S(1)}, f32[8,128]{1,0:T(8,128)S(1)}, u32[]{:S(2)}, u32[]{:S(2)}) collective-permute-start(f32[8,128]{1,0:T(8,128)S(1)} %slice.61), channel_id=1, source_target_pairs={{0,4},{4,0},{8,12},{12,8},{16,20},{20,16},{24,28},{28,24},{1,5},{5... | collective-permute-start | bytes 12296 | tf_op jit(solution)/shard_map/ppermute | solution.py:472
  60.7 1.3 %collective-permute-start.15 = (f32[104,128]{1,0:T(8,128)S(1)}, f32[104,128]{1,0:T(8,128)S(1)}, u32[]{:S(2)}, u32[]{:S(2)}) collective-permute-start(f32[104,128]{1,0:T(8,128)S(1)} %get-tuple-element.57), channel_id=1, source_target_pairs={{0,4},{4,0},{8,12},{12,8},{16,20},{20,16},{24,28},{28,24},{1,5},{5... | collective-permute-start | bytes 159752 | tf_op jit(solution)/shard_map/ppermute | solution.py:472
  62.0 5.7 %collective-permute-start.16 = (f32[104,128]{1,0:T(8,128)S(1)}, f32[104,128]{1,0:T(8,128)S(1)}, u32[]{:S(2)}, u32[]{:S(2)}) collective-permute-start(f32[104,128]{1,0:T(8,128)S(1)} %fusion.refs_4_), channel_id=1, source_target_pairs={{4,8},{8,4},{12,16},{16,12},{20,24},{24,20},{5,9},{9,5},{13,17},{1... | collective-permute-start | bytes 159752 | tf_op jit(solution)/shard_map/ppermute | solution.py:472
  67.7 1.8 %collective-permute-start.17 = (f32[8,128]{1,0:T(8,128)S(1)}, f32[8,128]{1,0:T(8,128)S(1)}, u32[]{:S(2)}, u32[]{:S(2)}) collective-permute-start(f32[8,128]{1,0:T(8,128)S(1)} %slice.63), channel_id=1, source_target_pairs={{0,4},{4,0},{8,12},{12,8},{16,20},{20,16},{24,28},{28,24},{1,5},{5... | collective-permute-start | bytes 12296 | tf_op jit(solution)/shard_map/ppermute | solution.py:472
